TPU v7x, 512 devices: a whole 4x4x16 slice. The times are simulated.
512 devices in a mesh: row: 16 (over z), col: 16 (over y, x_hi, core), layer: 2 (over x_lo).
Axes of the slice: x: 4 (x_hi: 2, x_lo: 2; x = x_hi * 2 + x_lo), y: 4, z: 16, core: 2. Of those that a mesh axis runs over, the one named last changes fastest.
Arguments:
- left_values: float32 [6144, 6144], P('row', 'col'), may hold values from -6 to 6
- left_mask: int32 [48, 48], P('row', 'col'), may hold values from 0 to 1, as said below
- right_values: float32 [6144, 6144], P('row', 'col'), may hold values from -0.125 to 0.125
- right_mask: int32 [48, 48], P('row', 'col'), may hold values from 0 to 1, as said below
- keep_mask: int32 [48, 48], P('row', 'col'), may hold values from 0 to 1, as said below
Outputs:
- product: float32 [6144, 6144], P(('row', 'layer'), 'col')
Inputs may be any that keep to these rules, and one draw needn't show every extreme that they name: `left_mask`: 0 or 1; every diagonal block is stored; the share of stored blocks differs from block row to block row. `right_mask`: 0 or 1; every diagonal block is stored; the share of stored blocks differs from block column to block column. `keep_mask`: 0 or 1; every diagonal block is retained.
All inputs are finite; a program needn't handle non-finite values.
Results may differ from a plain program's by a relative error of at most 0.00007.
Values sent between devices are 32-bit elements; how exact they have to be, the bound alone decides.
No kernel may reach another device: no remote copies, remote signals or barrier semaphores. Data moves between devices by JAX's collectives and lax.ppermute only.
A program may use at most 128 MiB of HBM per device.

v0:
```python
import jax
import jax.numpy as jnp
from jax import lax
from jax.sharding import PartitionSpec as P


def from_behind(value, axis, steps):
    count = lax.axis_size(axis)
    pairs = [(source, (source + steps) % count) for source in range(count)]
    return lax.ppermute(value, axis, pairs)


def spread(mask, block_size):
    return jnp.repeat(jnp.repeat(mask, block_size, 0), block_size, 1).astype(jnp.float32)


def whole_product(total, left_tile, right_tile):
    return total + jnp.dot(
        left_tile, right_tile, preferred_element_type=jnp.float32, precision=lax.Precision.HIGHEST
    )


def shards(left_values, left_mask, right_values, right_mask, keep_mask):
    tile_count = left_mask.shape[0]
    block_size = left_values.shape[0] // tile_count
    left_tile = left_values * spread(left_mask, block_size)
    right_tile = right_values * spread(right_mask, block_size)
    grid_size = lax.axis_size("col")
    layer_count = lax.axis_size("layer")
    step_count = grid_size // layer_count
    row_index = lax.axis_index("row")
    column_index = lax.axis_index("col")
    layer_index = lax.axis_index("layer")
    partial_value = jnp.zeros(left_values.shape, jnp.float32)
    left_offset = (row_index + layer_index * step_count) % grid_size
    right_offset = (column_index + layer_index * step_count) % grid_size
    for bit_number in range((grid_size - 1).bit_length()):
        moved_left = from_behind(left_tile, "col", -(1 << bit_number))
        moved_right = from_behind(right_tile, "row", -(1 << bit_number))
        left_tile = jnp.where((left_offset >> bit_number) % 2 == 1, moved_left, left_tile)
        right_tile = jnp.where((right_offset >> bit_number) % 2 == 1, moved_right, right_tile)
    for turn_index in range(step_count):
        partial_value = whole_product(partial_value, left_tile, right_tile)
        if turn_index + 1 < step_count:
            left_tile = from_behind(left_tile, "col", -1)
            right_tile = from_behind(right_tile, "row", -1)
    partial_value = partial_value * spread(keep_mask, block_size)
    return lax.psum_scatter(partial_value, "layer", scatter_dimension=0, tiled=True)


def solution(mesh):
    in_specs = (P("row", "col"), P("row", "col"), P("row", "col"), P("row", "col"), P("row", "col"))
    out_specs = P(("row", "layer"), "col")
    return jax.shard_map(shards, mesh=mesh, in_specs=in_specs, out_specs=out_specs, check_vma=False)
```

profile of v0, /device:TPU:1, one launch (start us, length us, event | category | flops | bytes accessed | tf_op | source)
XLA Modules:
  0.0 321.3 jit_solution(8035964802931044533)
XLA Ops:
  6.5 1.3 copy.9
  7.9 0.1 copy.8
  8.0 0.1 broadcast_bitcast_fusion.1
  8.1 0.0 copy-start.10
  8.1 12.1 %collective-permute-start.4 = (f32[384,384]{0,1:T(8,128)S(1)}, f32[384,384]{0,1:T(8,128)S(1)}, u32[]{:S(2)}, u32[]{:S(2)}) collective-permute-start(f32[384,384]{0,1:T(8,128)S(1)} %bitcast_multiply_fusion), channel_id=1, source_target_pairs={{0,480},{32,0},{64,32},{96,64},{128,96},{160,128},{192,160},{224,1... | collective-permute-start | bytes 1769480 | tf_op jit(solution)/shard_map/ppermute | solution.py:10
  20.2 0.2 copy.7
  20.5 0.1 copy.6
  20.6 0.1 broadcast_bitcast_fusion.2
  20.7 2.9 collective-permute-start
  23.6 8.6 %collective-permute-done.4 = f32[384,384]{0,1:T(8,128)S(1)} collective-permute-done((f32[384,384]{0,1:T(8,128)S(1)}, f32[384,384]{0,1:T(8,128)S(1)}, u32[]{:S(2)}, u32[]{:S(2)}) %collective-permute-start.4) | collective-permute-done | bytes 589856 | tf_op jit(solution)/shard_map/ppermute | solution.py:10
  32.2 0.1 broadcast_select_fusion
  32.2 4.6 %collective-permute-start.5 = (f32[384,384]{0,1:T(8,128)S(1)}, f32[384,384]{0,1:T(8,128)S(1)}, u32[]{:S(2)}, u32[]{:S(2)}) collective-permute-start(f32[384,384]{0,1:T(8,128)S(1)} %broadcast_select_fusion), channel_id=1, source_target_pairs={{0,448},{32,480},{64,0},{96,32},{128,64},{160,96},{192,128},{224,1... | collective-permute-start | bytes 1769480 | tf_op jit(solution)/shard_map/ppermute | solution.py:10
  36.8 0.1 broadcast_select_fusion.4
  36.9 7.1 %collective-permute-start.1 = (f32[384,384]{0,1:T(8,128)S(1)}, f32[384,384]{0,1:T(8,128)S(1)}, u32[]{:S(2)}, u32[]{:S(2)}) collective-permute-start(f32[384,384]{0,1:T(8,128)S(1)} %broadcast_select_fusion.4), channel_id=1, source_target_pairs={{0,28},{2,30},{4,0},{6,2},{8,4},{10,6},{12,8},{14,10},{16,12},{18,... | collective-permute-start | bytes 1769480 | tf_op jit(solution)/shard_map/ppermute | solution.py:10
  44.0 16.4 %collective-permute-done.5 = f32[384,384]{0,1:T(8,128)S(1)} collective-permute-done((f32[384,384]{0,1:T(8,128)S(1)}, f32[384,384]{0,1:T(8,128)S(1)}, u32[]{:S(2)}, u32[]{:S(2)}) %collective-permute-start.5) | collective-permute-done | bytes 589856 | tf_op jit(solution)/shard_map/ppermute | solution.py:10
  60.5 0.1 broadcast_select_fusion.1
  60.5 6.7 %collective-permute-start.6 = (f32[384,384]{0,1:T(8,128)S(1)}, f32[384,384]{0,1:T(8,128)S(1)}, u32[]{:S(2)}, u32[]{:S(2)}) collective-permute-start(f32[384,384]{0,1:T(8,128)S(1)} %broadcast_select_fusion.1), channel_id=1, source_target_pairs={{0,384},{32,416},{64,448},{96,480},{128,0},{160,32},{192,64},{224,... | collective-permute-start | bytes 1769480 | tf_op jit(solution)/shard_map/ppermute | solution.py:10
  67.2 0.1 broadcast_select_fusion.5
  67.3 4.6 %collective-permute-start.2 = (f32[384,384]{0,1:T(8,128)S(1)}, f32[384,384]{0,1:T(8,128)}, u32[]{:S(2)}, u32[]{:S(2)}) collective-permute-start(f32[384,384]{0,1:T(8,128)S(1)} %broadcast_select_fusion.5), channel_id=1, source_target_pairs={{0,24},{2,26},{4,28},{6,30},{8,0},{10,2},{12,4},{14,6},{16,8},{18,... | collective-permute-start | bytes 1769480 | tf_op jit(solution)/shard_map/ppermute | solution.py:10
  72.0 27.9 %collective-permute-done.6 = f32[384,384]{0,1:T(8,128)S(1)} collective-permute-done((f32[384,384]{0,1:T(8,128)S(1)}, f32[384,384]{0,1:T(8,128)S(1)}, u32[]{:S(2)}, u32[]{:S(2)}) %collective-permute-start.6) | collective-permute-done | bytes 589856 | tf_op jit(solution)/shard_map/ppermute | solution.py:10
  99.9 0.1 broadcast_select_fusion.2
  100.0 3.1 collective-permute-start.7
  103.1 0.1 broadcast_select_fusion.6
  103.2 4.8 %collective-permute-start.3 = (f32[384,384]{0,1:T(8,128)S(1)}, f32[384,384]{0,1:T(8,128)S(1)}, u32[]{:S(2)}, u32[]{:S(2)}) collective-permute-start(f32[384,384]{0,1:T(8,128)S(1)} %broadcast_select_fusion.6), channel_id=1, source_target_pairs={{0,16},{2,18},{4,20},{6,22},{8,24},{10,26},{12,28},{14,30},{16,0},... | collective-permute-start | bytes 1769480 | tf_op jit(solution)/shard_map/ppermute | solution.py:10
  108.1 32.0 %collective-permute-done.7 = f32[384,384]{0,1:T(8,128)S(1)} collective-permute-done((f32[384,384]{0,1:T(8,128)S(1)}, f32[384,384]{0,1:T(8,128)S(1)}, u32[]{:S(2)}, u32[]{:S(2)}) %collective-permute-start.7) | collective-permute-done | bytes 589856 | tf_op jit(solution)/shard_map/ppermute | solution.py:10
  140.1 0.1 broadcast_select_fusion.3
  140.1 0.0 copy-start.11
  140.1 30.7 %collective-permute-start.9 = (f32[384,384]{0,1:T(8,128)S(1)}, f32[384,384]{0,1:T(8,128)S(1)}, u32[]{:S(2)}, u32[]{:S(2)}) collective-permute-start(f32[384,384]{0,1:T(8,128)S(1)} %broadcast_select_fusion.3), channel_id=1, source_target_pairs={{0,480},{32,0},{64,32},{96,64},{128,96},{160,128},{192,160},{224,1... | collective-permute-start | bytes 1769480 | tf_op jit(solution)/shard_map/ppermute | solution.py:10
  170.9 0.1 broadcast_select_fusion.7
  170.9 3.2 collective-permute-start.8
  174.1 16.8 %collective-permute-done.9 = f32[384,384]{0,1:T(8,128)S(1)} collective-permute-done((f32[384,384]{0,1:T(8,128)S(1)}, f32[384,384]{0,1:T(8,128)S(1)}, u32[]{:S(2)}, u32[]{:S(2)}) %collective-permute-start.9) | collective-permute-done | bytes 589856 | tf_op jit(solution)/shard_map/ppermute | solution.py:10
  190.9 5.3 %collective-permute-start.11 = (f32[384,384]{0,1:T(8,128)S(1)}, f32[384,384]{0,1:T(8,128)S(1)}, u32[]{:S(2)}, u32[]{:S(2)}) collective-permute-start(f32[384,384]{0,1:T(8,128)S(1)} %collective-permute-done.9), channel_id=1, source_target_pairs={{0,480},{32,0},{64,32},{96,64},{128,96},{160,128},{192,160},{224,1... | collective-permute-start | bytes 1769480 | tf_op jit(solution)/shard_map/ppermute | solution.py:10
  196.3 0.0 collective-permute-done.8
  196.3 2.7 collective-permute-start.10
  199.0 9.5 %collective-permute-done.11 = f32[384,384]{0,1:T(8,128)S(1)} collective-permute-done((f32[384,384]{0,1:T(8,128)S(1)}, f32[384,384]{0,1:T(8,128)S(1)}, u32[]{:S(2)}, u32[]{:S(2)}) %collective-permute-start.11) | collective-permute-done | bytes 589856 | tf_op jit(solution)/shard_map/ppermute | solution.py:10
  208.4 5.3 %collective-permute-start.13 = (f32[384,384]{0,1:T(8,128)S(1)}, f32[384,384]{0,1:T(8,128)S(1)}, u32[]{:S(2)}, u32[]{:S(2)}) collective-permute-start(f32[384,384]{0,1:T(8,128)S(1)} %collective-permute-done.11), channel_id=1, source_target_pairs={{0,480},{32,0},{64,32},{96,64},{128,96},{160,128},{192,160},{224,1... | collective-permute-start | bytes 1769480 | tf_op jit(solution)/shard_map/ppermute | solution.py:10
  213.8 3.5 %collective-permute-start.12 = (f32[384,384]{0,1:T(8,128)S(1)}, f32[384,384]{0,1:T(8,128)S(1)}, u32[]{:S(2)}, u32[]{:S(2)}) collective-permute-start(f32[384,384]{0,1:T(8,128)S(1)} %collective-permute-done.10), channel_id=1, source_target_pairs={{0,30},{2,0},{4,2},{6,4},{8,6},{10,8},{12,10},{14,12},{16,14},{18,... | collective-permute-start | bytes 1769480 | tf_op jit(solution)/shard_map/ppermute | solution.py:10
  217.3 7.7 %collective-permute-done.13 = f32[384,384]{0,1:T(8,128)S(1)} collective-permute-done((f32[384,384]{0,1:T(8,128)S(1)}, f32[384,384]{0,1:T(8,128)S(1)}, u32[]{:S(2)}, u32[]{:S(2)}) %collective-permute-start.13) | collective-permute-done | bytes 589856 | tf_op jit(solution)/shard_map/ppermute | solution.py:10
  225.0 5.3 %collective-permute-start.15 = (f32[384,384]{0,1:T(8,128)S(1)}, f32[384,384]{0,1:T(8,128)}, u32[]{:S(2)}, u32[]{:S(2)}) collective-permute-start(f32[384,384]{0,1:T(8,128)S(1)} %collective-permute-done.13), channel_id=1, source_target_pairs={{0,480},{32,0},{64,32},{96,64},{128,96},{160,128},{192,160},{224,1... | collective-permute-start | bytes 1769480 | tf_op jit(solution)/shard_map/ppermute | solution.py:10
  230.4 4.5 %collective-permute-start.14 = (f32[384,384]{0,1:T(8,128)S(1)}, f32[384,384]{0,1:T(8,128)}, u32[]{:S(2)}, u32[]{:S(2)}) collective-permute-start(f32[384,384]{0,1:T(8,128)S(1)} %collective-permute-done.12), channel_id=1, source_target_pairs={{0,30},{2,0},{4,2},{6,4},{8,6},{10,8},{12,10},{14,12},{16,14},{18,... | collective-permute-start | bytes 1769480 | tf_op jit(solution)/shard_map/ppermute | solution.py:10
  234.8 5.8 %collective-permute-done.15 = f32[384,384]{0,1:T(8,128)} collective-permute-done((f32[384,384]{0,1:T(8,128)S(1)}, f32[384,384]{0,1:T(8,128)}, u32[]{:S(2)}, u32[]{:S(2)}) %collective-permute-start.15) | collective-permute-done | bytes 589856 | tf_op jit(solution)/shard_map/ppermute | solution.py:10
  240.7 5.4 %collective-permute-start.17 = (f32[384,384]{0,1:T(8,128)}, f32[384,384]{0,1:T(8,128)}, u32[]{:S(2)}, u32[]{:S(2)}) collective-permute-start(f32[384,384]{0,1:T(8,128)} %collective-permute-done.15), channel_id=1, source_target_pairs={{0,480},{32,0},{64,32},{96,64},{128,96},{160,128},{192,160},{224,1... | collective-permute-start | bytes 1769480 | tf_op jit(solution)/shard_map/ppermute | solution.py:10
  246.1 5.4 %collective-permute-start.16 = (f32[384,384]{0,1:T(8,128)}, f32[384,384]{0,1:T(8,128)}, u32[]{:S(2)}, u32[]{:S(2)}) collective-permute-start(f32[384,384]{0,1:T(8,128)} %collective-permute-done.14), channel_id=1, source_target_pairs={{0,30},{2,0},{4,2},{6,4},{8,6},{10,8},{12,10},{14,12},{16,14},{18,... | collective-permute-start | bytes 1769480 | tf_op jit(solution)/shard_map/ppermute | solution.py:10
  251.5 0.1 copy.10
  251.6 0.1 broadcast_bitcast_fusion
  251.7 0.2 copy.11
  252.0 2.0 fusion.1
  254.0 1.8 collective-permute-done.17
  255.8 5.3 %collective-permute-start.19 = (f32[384,384]{0,1:T(8,128)}, f32[384,384]{0,1:T(8,128)S(1)}, u32[]{:S(2)}, u32[]{:S(2)}) collective-permute-start(f32[384,384]{0,1:T(8,128)} %collective-permute-done.17), channel_id=1, source_target_pairs={{0,480},{32,0},{64,32},{96,64},{128,96},{160,128},{192,160},{224,1... | collective-permute-start | bytes 1769480 | tf_op jit(solution)/shard_map/ppermute | solution.py:10
  261.1 0.8 collective-permute-done.16
  262.0 5.6 %collective-permute-start.18 = (f32[384,384]{0,1:T(8,128)}, f32[384,384]{0,1:T(8,128)S(1)}, u32[]{:S(2)}, u32[]{:S(2)}) collective-permute-start(f32[384,384]{0,1:T(8,128)} %collective-permute-done.16), channel_id=1, source_target_pairs={{0,30},{2,0},{4,2},{6,4},{8,6},{10,8},{12,10},{14,12},{16,14},{18,... | collective-permute-start | bytes 1769480 | tf_op jit(solution)/shard_map/ppermute | solution.py:10
  267.6 2.0 convolution_add_fusion.6
  269.7 2.0 convolution_add_fusion.5
  271.8 2.0 convolution_add_fusion.4
  273.8 1.9 collective-permute-start.21
  275.8 2.1 collective-permute-done.18
  277.8 4.8 %collective-permute-start.20 = (f32[384,384]{0,1:T(8,128)S(1)}, f32[384,384]{0,1:T(8,128)S(1)}, u32[]{:S(2)}, u32[]{:S(2)}) collective-permute-start(f32[384,384]{0,1:T(8,128)S(1)} %collective-permute-done.18), channel_id=1, source_target_pairs={{0,30},{2,0},{4,2},{6,4},{8,6},{10,8},{12,10},{14,12},{16,14},{18,... | collective-permute-start | bytes 1769480 | tf_op jit(solution)/shard_map/ppermute | solution.py:10
  282.6 3.3 %convolution_add_fusion.3 = f32[384,384]{1,0:T(8,128)S(1)} fusion(f32[384,384]{1,0:T(8,128)S(1)} %convolution_add_fusion.4, f32[384,384]{0,1:T(8,128)} %collective-permute-done.14, f32[384,384]{0,1:T(8,128)} %collective-permute-done.15), kind=kOutput, calls=%fused_computation.3 | convolution fusion | flops 679624704 | bytes 2359296 | tf_op jit(solution)/shard_map/dot_general | solution.py:18
  285.9 3.3 %convolution_add_fusion.2 = f32[384,384]{1,0:T(8,128)S(1)} fusion(f32[384,384]{1,0:T(8,128)S(1)} %convolution_add_fusion.3, f32[384,384]{0,1:T(8,128)} %collective-permute-done.16, f32[384,384]{0,1:T(8,128)} %collective-permute-done.17), kind=kOutput, calls=%fused_computation.2 | convolution fusion | flops 679624704 | bytes 2359296 | tf_op jit(solution)/shard_map/dot_general | solution.py:18
  289.2 2.0 convolution_add_fusion.1
  291.2 1.3 collective-permute-done.20
  292.6 2.9 fusion
  295.4 0.0 reduce-scatter.2.cloned.1.call-update
  295.5 19.0 %reduce-scatter.2.cloned.1.call-done = f32[192,384]{1,0:T(8,128)} async-done(((f32[384,384]{1,0:T(8,128)}), f32[192,384]{1,0:T(8,128)}) %reduce-scatter.2.cloned.1.call-update) | async-done | bytes 294928 | tf_op jit(solution)/shard_map/reduce_scatter | solution.py:48
  (41 shorter events, 0.2 us)
Async XLA Ops:
  6.5 1.3 copy-start.9
  6.5 307.9 %reduce-scatter.2.cloned.1.call-start = ((), (), s32[]{:S(2)}) async-start(), calls=%async_computation.1 | async-start | bytes 884736 | tf_op jit(solution)/shard_map/reduce_scatter | solution.py:48
  8.0 12.2 %copy-start = (f32[384,384]{1,0:T(8,128)S(1)}, f32[384,384]{1,0:T(8,128)}, u32[]{:S(2)}) copy-start(f32[384,384]{1,0:T(8,128)} %param.5) | copy-start | bytes 1769476
  8.1 12.3 %copy-start.10 = (s32[3,3]{1,0:T(4,128)S(1)}, s32[3,3]{1,0:T(4,128)}, u32[]{:S(2)}) copy-start(s32[3,3]{1,0:T(4,128)} %param.6) | copy-start | bytes 112
  8.1 24.1 %collective-permute-start.4 = (f32[384,384]{0,1:T(8,128)S(1)}, f32[384,384]{0,1:T(8,128)S(1)}, u32[]{:S(2)}, u32[]{:S(2)}) collective-permute-start(f32[384,384]{0,1:T(8,128)S(1)} %bitcast_multiply_fusion), channel_id=1, source_target_pairs={{0,480},{32,0},{64,32},{96,64},{128,96},{160,128},{192,160},{224,1... | collective-permute-start | bytes 1769480 | tf_op jit(solution)/shard_map/ppermute | solution.py:10
  20.7 16.1 %collective-permute-start = (f32[384,384]{0,1:T(8,128)S(1)}, f32[384,384]{0,1:T(8,128)S(1)}, u32[]{:S(2)}, u32[]{:S(2)}) collective-permute-start(f32[384,384]{0,1:T(8,128)S(1)} %bitcast_multiply_fusion.1), channel_id=1, source_target_pairs={{0,30},{2,0},{4,2},{6,4},{8,6},{10,8},{12,10},{14,12},{16,14},{18,... | collective-permute-start | bytes 1769480 | tf_op jit(solution)/shard_map/ppermute | solution.py:10
  32.2 28.2 %collective-permute-start.5 = (f32[384,384]{0,1:T(8,128)S(1)}, f32[384,384]{0,1:T(8,128)S(1)}, u32[]{:S(2)}, u32[]{:S(2)}) collective-permute-start(f32[384,384]{0,1:T(8,128)S(1)} %broadcast_select_fusion), channel_id=1, source_target_pairs={{0,448},{32,480},{64,0},{96,32},{128,64},{160,96},{192,128},{224,1... | collective-permute-start | bytes 1769480 | tf_op jit(solution)/shard_map/ppermute | solution.py:10
  36.9 30.4 %collective-permute-start.1 = (f32[384,384]{0,1:T(8,128)S(1)}, f32[384,384]{0,1:T(8,128)S(1)}, u32[]{:S(2)}, u32[]{:S(2)}) collective-permute-start(f32[384,384]{0,1:T(8,128)S(1)} %broadcast_select_fusion.4), channel_id=1, source_target_pairs={{0,28},{2,30},{4,0},{6,2},{8,4},{10,6},{12,8},{14,10},{16,12},{18,... | collective-permute-start | bytes 1769480 | tf_op jit(solution)/shard_map/ppermute | solution.py:10
  60.5 39.4 %collective-permute-start.6 = (f32[384,384]{0,1:T(8,128)S(1)}, f32[384,384]{0,1:T(8,128)S(1)}, u32[]{:S(2)}, u32[]{:S(2)}) collective-permute-start(f32[384,384]{0,1:T(8,128)S(1)} %broadcast_select_fusion.1), channel_id=1, source_target_pairs={{0,384},{32,416},{64,448},{96,480},{128,0},{160,32},{192,64},{224,... | collective-permute-start | bytes 1769480 | tf_op jit(solution)/shard_map/ppermute | solution.py:10
  67.3 35.8 %collective-permute-start.2 = (f32[384,384]{0,1:T(8,128)S(1)}, f32[384,384]{0,1:T(8,128)}, u32[]{:S(2)}, u32[]{:S(2)}) collective-permute-start(f32[384,384]{0,1:T(8,128)S(1)} %broadcast_select_fusion.5), channel_id=1, source_target_pairs={{0,24},{2,26},{4,28},{6,30},{8,0},{10,2},{12,4},{14,6},{16,8},{18,... | collective-permute-start | bytes 1769480 | tf_op jit(solution)/shard_map/ppermute | solution.py:10
  100.0 40.1 %collective-permute-start.7 = (f32[384,384]{0,1:T(8,128)S(1)}, f32[384,384]{0,1:T(8,128)S(1)}, u32[]{:S(2)}, u32[]{:S(2)}) collective-permute-start(f32[384,384]{0,1:T(8,128)S(1)} %broadcast_select_fusion.2), channel_id=1, source_target_pairs={{0,256},{32,288},{64,320},{96,352},{128,384},{160,416},{192,448},{... | collective-permute-start | bytes 1769480 | tf_op jit(solution)/shard_map/ppermute | solution.py:10
  103.2 67.6 %collective-permute-start.3 = (f32[384,384]{0,1:T(8,128)S(1)}, f32[384,384]{0,1:T(8,128)S(1)}, u32[]{:S(2)}, u32[]{:S(2)}) collective-permute-start(f32[384,384]{0,1:T(8,128)S(1)} %broadcast_select_fusion.6), channel_id=1, source_target_pairs={{0,16},{2,18},{4,20},{6,22},{8,24},{10,26},{12,28},{14,30},{16,0},... | collective-permute-start | bytes 1769480 | tf_op jit(solution)/shard_map/ppermute | solution.py:10
  140.1 111.4 %copy-start.11 = (s32[3,3]{1,0:T(4,128)S(1)}, s32[3,3]{1,0:T(4,128)}, u32[]{:S(2)}) copy-start(s32[3,3]{1,0:T(4,128)} %param.9) | copy-start | bytes 112
  140.1 50.8 %collective-permute-start.9 = (f32[384,384]{0,1:T(8,128)S(1)}, f32[384,384]{0,1:T(8,128)S(1)}, u32[]{:S(2)}, u32[]{:S(2)}) collective-permute-start(f32[384,384]{0,1:T(8,128)S(1)} %broadcast_select_fusion.3), channel_id=1, source_target_pairs={{0,480},{32,0},{64,32},{96,64},{128,96},{160,128},{192,160},{224,1... | collective-permute-start | bytes 1769480 | tf_op jit(solution)/shard_map/ppermute | solution.py:10
  170.9 25.3 %collective-permute-start.8 = (f32[384,384]{0,1:T(8,128)S(1)}, f32[384,384]{0,1:T(8,128)S(1)}, u32[]{:S(2)}, u32[]{:S(2)}) collective-permute-start(f32[384,384]{0,1:T(8,128)S(1)} %broadcast_select_fusion.7), channel_id=1, source_target_pairs={{0,30},{2,0},{4,2},{6,4},{8,6},{10,8},{12,10},{14,12},{16,14},{18,... | collective-permute-start | bytes 1769480 | tf_op jit(solution)/shard_map/ppermute | solution.py:10
  190.9 17.5 %collective-permute-start.11 = (f32[384,384]{0,1:T(8,128)S(1)}, f32[384,384]{0,1:T(8,128)S(1)}, u32[]{:S(2)}, u32[]{:S(2)}) collective-permute-start(f32[384,384]{0,1:T(8,128)S(1)} %collective-permute-done.9), channel_id=1, source_target_pairs={{0,480},{32,0},{64,32},{96,64},{128,96},{160,128},{192,160},{224,1... | collective-permute-start | bytes 1769480 | tf_op jit(solution)/shard_map/ppermute | solution.py:10
  196.3 17.5 %collective-permute-start.10 = (f32[384,384]{0,1:T(8,128)S(1)}, f32[384,384]{0,1:T(8,128)S(1)}, u32[]{:S(2)}, u32[]{:S(2)}) collective-permute-start(f32[384,384]{0,1:T(8,128)S(1)} %collective-permute-done.8), channel_id=1, source_target_pairs={{0,30},{2,0},{4,2},{6,4},{8,6},{10,8},{12,10},{14,12},{16,14},{18,... | collective-permute-start | bytes 1769480 | tf_op jit(solution)/shard_map/ppermute | solution.py:10
  208.4 5.3 %copy-start.1 = (f32[384,384]{0,1:T(8,128)}, f32[384,384]{0,1:T(8,128)S(1)}, u32[]{:S(2)}) copy-start(f32[384,384]{0,1:T(8,128)S(1)} %collective-permute-done.11) | copy-start | bytes 1769476
  208.4 16.6 %collective-permute-start.13 = (f32[384,384]{0,1:T(8,128)S(1)}, f32[384,384]{0,1:T(8,128)S(1)}, u32[]{:S(2)}, u32[]{:S(2)}) collective-permute-start(f32[384,384]{0,1:T(8,128)S(1)} %collective-permute-done.11), channel_id=1, source_target_pairs={{0,480},{32,0},{64,32},{96,64},{128,96},{160,128},{192,160},{224,1... | collective-permute-start | bytes 1769480 | tf_op jit(solution)/shard_map/ppermute | solution.py:10
  213.8 11.2 %copy-start.3 = (f32[384,384]{0,1:T(8,128)}, f32[384,384]{0,1:T(8,128)S(1)}, u32[]{:S(2)}) copy-start(f32[384,384]{0,1:T(8,128)S(1)} %collective-permute-done.10) | copy-start | bytes 1769476
  213.8 16.5 %collective-permute-start.12 = (f32[384,384]{0,1:T(8,128)S(1)}, f32[384,384]{0,1:T(8,128)S(1)}, u32[]{:S(2)}, u32[]{:S(2)}) collective-permute-start(f32[384,384]{0,1:T(8,128)S(1)} %collective-permute-done.10), channel_id=1, source_target_pairs={{0,30},{2,0},{4,2},{6,4},{8,6},{10,8},{12,10},{14,12},{16,14},{18,... | collective-permute-start | bytes 1769480 | tf_op jit(solution)/shard_map/ppermute | solution.py:10
  225.0 5.3 %copy-start.5 = (f32[384,384]{0,1:T(8,128)}, f32[384,384]{0,1:T(8,128)S(1)}, u32[]{:S(2)}) copy-start(f32[384,384]{0,1:T(8,128)S(1)} %collective-permute-done.13) | copy-start | bytes 1769476
  225.0 15.7 %collective-permute-start.15 = (f32[384,384]{0,1:T(8,128)S(1)}, f32[384,384]{0,1:T(8,128)}, u32[]{:S(2)}, u32[]{:S(2)}) collective-permute-start(f32[384,384]{0,1:T(8,128)S(1)} %collective-permute-done.13), channel_id=1, source_target_pairs={{0,480},{32,0},{64,32},{96,64},{128,96},{160,128},{192,160},{224,1... | collective-permute-start | bytes 1769480 | tf_op jit(solution)/shard_map/ppermute | solution.py:10
  230.4 10.3 %copy-start.7 = (f32[384,384]{0,1:T(8,128)}, f32[384,384]{0,1:T(8,128)S(1)}, u32[]{:S(2)}) copy-start(f32[384,384]{0,1:T(8,128)S(1)} %collective-permute-done.12) | copy-start | bytes 1769476
  230.4 15.7 %collective-permute-start.14 = (f32[384,384]{0,1:T(8,128)S(1)}, f32[384,384]{0,1:T(8,128)}, u32[]{:S(2)}, u32[]{:S(2)}) collective-permute-start(f32[384,384]{0,1:T(8,128)S(1)} %collective-permute-done.12), channel_id=1, source_target_pairs={{0,30},{2,0},{4,2},{6,4},{8,6},{10,8},{12,10},{14,12},{16,14},{18,... | collective-permute-start | bytes 1769480 | tf_op jit(solution)/shard_map/ppermute | solution.py:10
  240.7 15.1 %collective-permute-start.17 = (f32[384,384]{0,1:T(8,128)}, f32[384,384]{0,1:T(8,128)}, u32[]{:S(2)}, u32[]{:S(2)}) collective-permute-start(f32[384,384]{0,1:T(8,128)} %collective-permute-done.15), channel_id=1, source_target_pairs={{0,480},{32,0},{64,32},{96,64},{128,96},{160,128},{192,160},{224,1... | collective-permute-start | bytes 1769480 | tf_op jit(solution)/shard_map/ppermute | solution.py:10
  246.1 15.9 %collective-permute-start.16 = (f32[384,384]{0,1:T(8,128)}, f32[384,384]{0,1:T(8,128)}, u32[]{:S(2)}, u32[]{:S(2)}) collective-permute-start(f32[384,384]{0,1:T(8,128)} %collective-permute-done.14), channel_id=1, source_target_pairs={{0,30},{2,0},{4,2},{6,4},{8,6},{10,8},{12,10},{14,12},{16,14},{18,... | collective-permute-start | bytes 1769480 | tf_op jit(solution)/shard_map/ppermute | solution.py:10
  254.0 15.7 %copy-start.2 = (f32[384,384]{0,1:T(8,128)S(1)}, f32[384,384]{0,1:T(8,128)}, u32[]{:S(2)}) copy-start(f32[384,384]{0,1:T(8,128)} %copy-done.1) | copy-start | bytes 1769476
  254.0 15.7 %copy-start.4 = (f32[384,384]{0,1:T(8,128)S(1)}, f32[384,384]{0,1:T(8,128)}, u32[]{:S(2)}) copy-start(f32[384,384]{0,1:T(8,128)} %copy-done.3) | copy-start | bytes 1769476
  255.8 18.0 %collective-permute-start.19 = (f32[384,384]{0,1:T(8,128)}, f32[384,384]{0,1:T(8,128)S(1)}, u32[]{:S(2)}, u32[]{:S(2)}) collective-permute-start(f32[384,384]{0,1:T(8,128)} %collective-permute-done.17), channel_id=1, source_target_pairs={{0,480},{32,0},{64,32},{96,64},{128,96},{160,128},{192,160},{224,1... | collective-permute-start | bytes 1769480 | tf_op jit(solution)/shard_map/ppermute | solution.py:10
  262.0 15.9 %collective-permute-start.18 = (f32[384,384]{0,1:T(8,128)}, f32[384,384]{0,1:T(8,128)S(1)}, u32[]{:S(2)}, u32[]{:S(2)}) collective-permute-start(f32[384,384]{0,1:T(8,128)} %collective-permute-done.16), channel_id=1, source_target_pairs={{0,30},{2,0},{4,2},{6,4},{8,6},{10,8},{12,10},{14,12},{16,14},{18,... | collective-permute-start | bytes 1769480 | tf_op jit(solution)/shard_map/ppermute | solution.py:10
  269.7 2.1 copy-start.6
  269.7 2.1 copy-start.8
  273.8 17.4 %collective-permute-start.21 = (f32[384,384]{0,1:T(8,128)S(1)}, f32[384,384]{0,1:T(8,128)S(1)}, u32[]{:S(2)}, u32[]{:S(2)}) collective-permute-start(f32[384,384]{0,1:T(8,128)S(1)} %collective-permute-done.19), channel_id=1, source_target_pairs={{0,480},{32,0},{64,32},{96,64},{128,96},{160,128},{192,160},{224,1... | collective-permute-start | bytes 1769480 | tf_op jit(solution)/shard_map/ppermute | solution.py:10
  277.8 14.7 %collective-permute-start.20 = (f32[384,384]{0,1:T(8,128)S(1)}, f32[384,384]{0,1:T(8,128)S(1)}, u32[]{:S(2)}, u32[]{:S(2)}) collective-permute-start(f32[384,384]{0,1:T(8,128)S(1)} %collective-permute-done.18), channel_id=1, source_target_pairs={{0,30},{2,0},{4,2},{6,4},{8,6},{10,8},{12,10},{14,12},{16,14},{18,... | collective-permute-start | bytes 1769480 | tf_op jit(solution)/shard_map/ppermute | solution.py:10
Sparse Core Ops, SparseCore 0:
  295.6 18.8 reduce-scatter.1
where the time goes:
time: 322 us; the launch traced here: 321 us
  waiting for transfers between devices  150 us (47%)
  starting transfers between devices  135 us (42%)
  matrix products  19.6 us (6%)
  between operations  14.1 us (4%)
    ppermute x22, starting transfers between devices, from_behind(): return lax.ppermute(value, axis, pairs)  135 us
    ppermute x22, waiting for transfers between devices, from_behind(): return lax.ppermute(value, axis, pairs)  131 us
    dot_general x8, matrix products, whole_product(): jnp.dot(left_tile, right_tile, preferred_element_type=jnp.float32, precis...  19.6 us
    reduce_scatter x1, waiting for transfers between devices, shards(): lax.psum_scatter(partial_value, 'layer', scatter_dimension=0, tiled=True)  19 us
  transfers between devices with their start and end apart: 23, of which 13 were waited for; matrix products, arithmetic and copies ran while one was open for 6% of the time, Pallas kernels for 0%

commit v1 on v0

v1 whole, which is shorter than its diff:
```python
import functools

import jax
import jax.numpy as jnp
from jax import lax
from jax.experimental import pallas as pl
from jax.experimental.pallas import tpu as pltpu
from jax.sharding import PartitionSpec as P

BLK = 128
HALF = 64
TILE = 3 * BLK
PART = TILE // 2
F32 = jnp.float32
BF16 = jnp.bfloat16
VMEM = pl.BlockSpec(memory_space=pltpu.VMEM)
SMEM = pl.BlockSpec(memory_space=pltpu.SMEM)


def call(kernel, out_shapes, in_specs, scratch=(), flops=0, nbytes=0):
    return pl.pallas_call(
        kernel,
        out_shape=out_shapes,
        in_specs=in_specs,
        out_specs=jax.tree.map(lambda _: VMEM, out_shapes),
        scratch_shapes=scratch,
        compiler_params=pltpu.CompilerParams(vmem_limit_bytes=40 * 2**20),
        cost_estimate=pl.CostEstimate(flops=flops, bytes_accessed=nbytes, transcendentals=0),
    )


def swap_halves(value):
    return pltpu.roll(value, HALF, 1)


def low_lanes(shape):
    return lax.broadcasted_iota(jnp.int32, shape, 1) < HALF


def prep_kernel(place, left_mask, right_mask, left, right, left_out, right_out):
    layer = place[2]

    def masked(values, mask, p, q, rows=slice(0, BLK)):
        block = values[p * BLK + rows.start : p * BLK + rows.stop, q * BLK : (q + 1) * BLK]
        return block * mask[p, q].astype(F32)

    def side(outer, near):
        for p in range(3):
            left_out[p * BLK : (p + 1) * BLK, :] = masked(left, left_mask, p, outer)
        middle = jnp.concatenate([masked(left, left_mask, p, 1) for p in range(3)], 0)
        top, bottom = middle[:PART], middle[PART:]
        keep_low = low_lanes((PART, BLK))
        if near == 0:
            left_out[TILE:, :] = jnp.where(keep_low, top, swap_halves(bottom))
        else:
            left_out[TILE:, :] = jnp.where(keep_low, swap_halves(top), bottom)
        rows = slice(near * HALF, (near + 1) * HALF)
        for q in range(3):
            lanes = slice(q * BLK, (q + 1) * BLK)
            right_out[:BLK, lanes] = masked(right, right_mask, outer, q)
            right_out[BLK:, lanes] = masked(right, right_mask, 1, q, rows)

    @pl.when(layer == 0)
    def _():
        side(0, 0)

    @pl.when(layer == 1)
    def _():
        side(2, 1)


def split(value):
    high = value.astype(BF16)
    return high, (value - high.astype(F32)).astype(BF16)


def triple(left, right):
    (lh, ll), (rh, rl) = left, right
    dot = functools.partial(jnp.dot, preferred_element_type=F32)
    return dot(lh, rh) + (dot(lh, rl) + dot(ll, rh))


def join_left(one, two):
    m1, m2 = one[TILE:], two[TILE:]
    keep_low = low_lanes((PART, BLK))
    top = jnp.where(keep_low, m1, swap_halves(m2))
    bottom = jnp.where(keep_low, swap_halves(m1), m2)
    return jnp.concatenate([one[:TILE], two[:TILE], jnp.concatenate([top, bottom], 0)], 1)


def join_right(one, two):
    return jnp.concatenate([one[:BLK], two[:BLK], one[BLK:], two[BLK:]], 0)


def panel_index(place, k):
    col = place[1]
    return lax.rem(k, 2) == lax.rem(col, 2), k // 4, lax.bitwise_xor(lax.rem(k // 2, 2), lax.rem(col // 2, 2))


def fill(place, same, other, step, rights, lh, ll, rh, rl, column):
    z = place[0]
    behind, ahead = lax.rem(z - step + 16, 16), lax.rem(z + step, 16)
    mine, y1, x1 = panel_index(place, behind)
    _, y2, x2 = panel_index(place, ahead)
    span = slice(column, column + TILE)

    def put(panel):
        one, two = panel[y1, x1], panel[y2, x2]
        if step == 0:
            two = jnp.zeros_like(two)
        lh[:, span], ll[:, span] = split(join_left(one, two))

    pl.when(mine)(lambda: put(same))
    pl.when(jnp.logical_not(mine))(lambda: put(other))
    one = rights[0][...]
    two = jnp.zeros_like(one) if step == 0 else rights[1][...]
    rh[span, :], rl[span, :] = split(join_right(one, two))


def main_kernel(steps, place, same, other, *refs):
    rights, (total, lh, ll, rh, rl) = refs[:-5], refs[-5:]
    for number, step in enumerate(steps):
        pair = rights[:1] if step == 0 else rights[2 * step - 1 : 2 * step + 1]
        fill(place, same, other, step, pair, lh, ll, rh, rl, number * TILE)
    total[...] = triple((lh[...], ll[...]), (rh[...], rl[...]))


def near_kernel(step, place, same, other, behind, ahead, total, own, away, lh, ll, rh, rl):
    fill(place, same, other, step, (behind, ahead), lh, ll, rh, rl, 0)
    value = total[...] + triple((lh[...], ll[...]), (rh[...], rl[...]))
    layer = place[2]

    @pl.when(layer == 0)
    def _():
        own[...] = value[:PART]
        away[...] = value[PART:]

    @pl.when(layer == 1)
    def _():
        own[...] = value[PART:]
        away[...] = value[:PART]


def last_kernel(place, keep, own, came, left_own, left_other, right_own, right_other, out):
    layer = place[2]
    first = layer == 0

    def rows_of(packed):
        outer = jnp.where(first, packed[:PART], packed[PART:TILE])
        middle = jnp.where(first, packed[TILE:], swap_halves(packed[TILE:]))
        return outer, middle

    outer1, middle1 = rows_of(left_own[...])
    outer2, middle2 = rows_of(left_other[...])
    middle = jnp.where(low_lanes((PART, BLK)), middle1, swap_halves(middle2))
    left = jnp.concatenate([outer1, outer2, middle], 1)
    right = join_right(right_own[...], right_other[...])
    value = own[...] + came[...] + triple(split(left), split(right))
    for q in range(3):
        lanes = slice(q * BLK, (q + 1) * BLK)
        ends = jnp.where(first, keep[0, q], keep[2, q]).astype(F32)
        centre = keep[1, q].astype(F32)
        row = lax.broadcasted_iota(jnp.int32, (PART, BLK), 0) + layer * PART
        scale = jnp.where((row >= BLK) & (row < 2 * BLK), centre, ends)
        out[:, lanes] = value[:, lanes] * scale


def shift(value, axis, steps):
    count = lax.axis_size(axis)
    return lax.ppermute(value, axis, [(i, (i + steps) % count) for i in range(count)])


def shards(left_values, left_mask, right_values, right_mask, keep_mask):
    count = lax.axis_size("row")
    cols = lax.axis_size("col")
    z, col, layer = lax.axis_index("row"), lax.axis_index("col"), lax.axis_index("layer")
    place = jnp.stack([z, col, layer]).astype(jnp.int32)
    packed = jax.ShapeDtypeStruct((TILE + PART, BLK), F32)
    half = jax.ShapeDtypeStruct((PART, TILE), F32)
    whole = jax.ShapeDtypeStruct((TILE, TILE), F32)

    left, right = call(prep_kernel, (packed, half), [SMEM] * 3 + [VMEM] * 2)(
        place, left_mask, right_mask, left_values, right_values
    )

    left_x = lax.ppermute(left, "col", [(i, i ^ 2) for i in range(cols)])
    groups = [[j + 4 * y for y in range(4)] for j in range(4)]
    same = lax.all_gather(jnp.stack([left, left_x]), "col", axis_index_groups=groups)
    other = lax.ppermute(same, "col", [(i, i ^ 1) for i in range(cols)])

    reach = count // 2
    rights, behind, ahead = [right], right, right
    for _ in range(1, reach):
        behind, ahead = shift(behind, "row", 1), shift(ahead, "row", -1)
        rights += [behind, ahead]
    far_own = shift(behind, "row", 1)
    cross = [(z0 * 2 + l0, (z0 - 1) % count * 2 + 1 - l0) for z0 in range(count) for l0 in range(2)]
    far_other = lax.ppermute(ahead, ("row", "layer"), cross)

    def parts(n):
        return [
            pltpu.VMEM((TILE, n * TILE), BF16), pltpu.VMEM((TILE, n * TILE), BF16),
            pltpu.VMEM((n * TILE, TILE), BF16), pltpu.VMEM((n * TILE, TILE), BF16),
        ]

    steps = tuple(range(reach - 1))
    first = rights[: 2 * len(steps) - 1]
    total = call(
        functools.partial(main_kernel, steps), whole, [SMEM] + [VMEM] * (2 + len(first)), parts(len(steps)),
        flops=6 * TILE * TILE * TILE * len(steps), nbytes=10 * 2**20,
    )(place, same, other, *first)
    own, away = call(
        functools.partial(near_kernel, reach - 1), (half, half), [SMEM] + [VMEM] * 5, parts(1),
        flops=6 * TILE * TILE * TILE, nbytes=2**20,
    )(place, same, other, *rights[-2:], total)
    came = shift(away, "layer", 1)

    far = (z + reach) % count
    mine, y, x = panel_index(place, far)
    left_own = jnp.where(mine, same[y, x], other[y, x])
    left_other = shift(left_own, "layer", 1)
    return call(last_kernel, half, [SMEM] * 2 + [VMEM] * 6, flops=6 * PART * TILE * TILE, nbytes=2**20)(
        place, keep_mask, own, came, left_own, left_other, far_own, far_other
    )


def solution(mesh):
    specs = (P("row", "col"),) * 5
    return jax.shard_map(shards, mesh=mesh, in_specs=specs, out_specs=P(("row", "layer"), "col"), check_vma=False)
```

time: 322 us -> 196 us (0.61)
  the two profiles are of different devices: /device:TPU:1 before, /device:TPU:2 now
where the time goes in v1:
time: 196 us; the launch traced here: 195 us
  waiting for transfers between devices  81.4 us (42%)
  starting transfers between devices  69.5 us (35%)
  local copies, waits for them, and re-layouts  16.9 us (9%)
  between operations  13.8 us (7%)
  Pallas kernels  11.1 us (6%)
  other arithmetic  1.96 us (1%)
    ppermute x17, starting transfers between devices, shift(): lax.ppermute(value, axis, [(i, (i + steps) % count) for i in range(count)])  58.4 us
    all_gather x1, waiting for transfers between devices, shards(): lax.all_gather(jnp.stack([left, left_x]), 'col', axis_index_groups=groups)  45.3 us
    ppermute x17, waiting for transfers between devices, shift(): lax.ppermute(value, axis, [(i, (i + steps) % count) for i in range(count)])  28 us
    unnamed x42, local copies, waits for them, and re-layouts  16.9 us
    ppermute x1, waiting for transfers between devices, shards(): left_x = lax.ppermute(left, 'col', [(i, i ^ 2) for i in range(cols)])  8.1 us
    pallas_call x1, Pallas kernels, shards(): call(functools.partial(main_kernel, steps), whole, [SMEM] + [VMEM] * (2 +...  6.49 us
    ppermute x1, starting transfers between devices, shards(): far_other = lax.ppermute(ahead, ('row', 'layer'), cross)  5.13 us
    ppermute x1, starting transfers between devices, shards(): left_x = lax.ppermute(left, 'col', [(i, i ^ 2) for i in range(cols)])  4.03 us
  transfers between devices with their start and end apart: 21, of which 12 were waited for; matrix products, arithmetic and copies ran while one was open for 1% of the time, Pallas kernels for 4%

profile of v1, /device:TPU:2, one launch (start us, length us, event | category | flops | bytes accessed | tf_op | source)
XLA Modules:
  0.0 194.6 jit_solution(2720500944076628239)
XLA Ops:
  6.5 0.1 pad_add_fusion.place
  6.6 1.1 copy-done.2
  7.7 1.1 copy-done.3
  8.7 0.7 copy-done.18
  9.4 0.7 copy-done.19
  10.1 0.7 shard_map.55
  10.8 4.0 %collective-permute-start = (f32[576,128]{1,0:T(8,128)S(1)}, f32[576,128]{1,0:T(8,128)S(1)}, u32[]{:S(2)}, u32[]{:S(2)}) collective-permute-start(f32[576,128]{1,0:T(8,128)S(1)} %get-tuple-element.9), channel_id=1, source_target_pairs={{0,4},{2,6},{4,0},{6,2},{8,12},{10,14},{12,8},{14,10},{16,20},{18,... | collective-permute-start | bytes 884744 | tf_op jit(solution)/shard_map/ppermute | solution.py:186
  14.9 8.1 %collective-permute-done = f32[576,128]{1,0:T(8,128)S(1)} collective-permute-done((f32[576,128]{1,0:T(8,128)S(1)}, f32[576,128]{1,0:T(8,128)S(1)}, u32[]{:S(2)}, u32[]{:S(2)}) %collective-permute-start) | collective-permute-done | bytes 294944 | tf_op jit(solution)/shard_map/ppermute | solution.py:186
  23.0 0.9 pad_maximum_fusion
  23.8 0.0 all-gather.3.cloned.1.call-update
  23.9 45.3 %all-gather.3.cloned.1.call-done = f32[8,576,128]{2,1,0:T(8,128)} async-done(((f32[2,576,128]{2,1,0:T(8,128)}), f32[8,576,128]{2,1,0:T(8,128)}) %all-gather.3.cloned.1.call-update) | async-done | bytes 2359312 | tf_op jit(solution)/shard_map/all_gather | solution.py:188
  69.2 1.9 collective-permute-start.1
  71.1 3.5 %collective-permute-start.2 = (f32[192,384]{1,0:T(8,128)S(1)}, f32[192,384]{1,0:T(8,128)S(1)}, u32[]{:S(2)}, u32[]{:S(2)}) collective-permute-start(f32[192,384]{1,0:T(8,128)S(1)} %get-tuple-element.10.refs_0_), channel_id=1, source_target_pairs={{0,32},{32,64},{64,96},{96,128},{128,160},{160,192},{192,224},{224... | collective-permute-start | bytes 884744 | tf_op jit(solution)/shard_map/ppermute | solution.py:170
  74.6 4.4 %collective-permute-start.9 = (f32[192,384]{1,0:T(8,128)S(1)}, f32[192,384]{1,0:T(8,128)S(1)}, u32[]{:S(2)}, u32[]{:S(2)}) collective-permute-start(f32[192,384]{1,0:T(8,128)S(1)} %get-tuple-element.10.refs_0_), channel_id=1, source_target_pairs={{0,480},{32,0},{64,32},{96,64},{128,96},{160,128},{192,160},{224,1... | collective-permute-start | bytes 884744 | tf_op jit(solution)/shard_map/ppermute | solution.py:170
  79.0 5.7 %collective-permute-done.2.refs_1_ = f32[192,384]{1,0:T(8,128)S(1)} collective-permute-done((f32[192,384]{1,0:T(8,128)S(1)}, f32[192,384]{1,0:T(8,128)S(1)}, u32[]{:S(2)}, u32[]{:S(2)}) %collective-permute-start.2) | collective-permute-done | bytes 294944 | tf_op jit(solution)/shard_map/ppermute | solution.py:170
  84.7 1.9 collective-permute-start.3
  86.7 5.1 %collective-permute-start.10 = (f32[192,384]{1,0:T(8,128)S(1)}, f32[192,384]{1,0:T(8,128)S(1)}, u32[]{:S(2)}, u32[]{:S(2)}) collective-permute-start(f32[192,384]{1,0:T(8,128)S(1)} %collective-permute-done.9.refs_2_), channel_id=1, source_target_pairs={{0,480},{32,0},{64,32},{96,64},{128,96},{160,128},{192,160},{224,1... | collective-permute-start | bytes 884744 | tf_op jit(solution)/shard_map/ppermute | solution.py:170
  91.8 4.9 %collective-permute-done.3.refs_3_ = f32[192,384]{1,0:T(8,128)S(1)} collective-permute-done((f32[192,384]{1,0:T(8,128)S(1)}, f32[192,384]{1,0:T(8,128)S(1)}, u32[]{:S(2)}, u32[]{:S(2)}) %collective-permute-start.3) | collective-permute-done | bytes 294944 | tf_op jit(solution)/shard_map/ppermute | solution.py:170
  96.7 1.9 collective-permute-start.4
  98.6 0.0 collective-permute-done.10.refs_4_
  98.6 5.1 %collective-permute-start.11 = (f32[192,384]{1,0:T(8,128)S(1)}, f32[192,384]{1,0:T(8,128)S(1)}, u32[]{:S(2)}, u32[]{:S(2)}) collective-permute-start(f32[192,384]{1,0:T(8,128)S(1)} %collective-permute-done.10.refs_4_), channel_id=1, source_target_pairs={{0,480},{32,0},{64,32},{96,64},{128,96},{160,128},{192,160},{224,1... | collective-permute-start | bytes 884744 | tf_op jit(solution)/shard_map/ppermute | solution.py:170
  103.7 0.0 copy-start.4
  103.7 0.7 copy-done.4
  104.4 3.3 %collective-permute-done.4.refs_5_ = f32[192,384]{1,0:T(8,128)S(1)} collective-permute-done((f32[192,384]{1,0:T(8,128)S(1)}, f32[192,384]{1,0:T(8,128)S(1)}, u32[]{:S(2)}, u32[]{:S(2)}) %collective-permute-start.4) | collective-permute-done | bytes 294944 | tf_op jit(solution)/shard_map/ppermute | solution.py:170
  107.7 1.9 collective-permute-start.5
  109.6 0.7 copy-done.6
  110.3 0.0 collective-permute-done.11.refs_6_
  110.3 5.1 %collective-permute-start.12 = (f32[192,384]{1,0:T(8,128)S(1)}, f32[192,384]{1,0:T(8,128)S(1)}, u32[]{:S(2)}, u32[]{:S(2)}) collective-permute-start(f32[192,384]{1,0:T(8,128)S(1)} %collective-permute-done.11.refs_6_), channel_id=1, source_target_pairs={{0,480},{32,0},{64,32},{96,64},{128,96},{160,128},{192,160},{224,1... | collective-permute-start | bytes 884744 | tf_op jit(solution)/shard_map/ppermute | solution.py:170
  115.5 0.7 copy-done.8
  116.2 1.6 collective-permute-done.5.refs_7_
  117.9 1.9 collective-permute-start.6
  119.8 0.7 copy-done.10
  120.5 5.1 %collective-permute-start.13 = (f32[192,384]{1,0:T(8,128)S(1)}, f32[192,384]{1,0:T(8,128)S(1)}, u32[]{:S(2)}, u32[]{:S(2)}) collective-permute-start(f32[192,384]{1,0:T(8,128)S(1)} %collective-permute-done.12.refs_8_), channel_id=1, source_target_pairs={{0,480},{32,0},{64,32},{96,64},{128,96},{160,128},{192,160},{224,1... | collective-permute-start | bytes 884744 | tf_op jit(solution)/shard_map/ppermute | solution.py:170
  125.6 0.7 copy-done.12
  126.3 1.3 collective-permute-done.6.refs_9_
  127.7 1.9 collective-permute-start.7
  129.6 0.7 copy-done.14
  130.3 0.0 collective-permute-done.13.refs_10_
  130.3 5.1 %collective-permute-start.14 = (f32[192,384]{1,0:T(8,128)S(1)}, f32[192,384]{1,0:T(8,128)}, u32[]{:S(2)}, u32[]{:S(2)}) collective-permute-start(f32[192,384]{1,0:T(8,128)S(1)} %collective-permute-done.13.refs_10_), channel_id=1, source_target_pairs={{0,480},{32,0},{64,32},{96,64},{128,96},{160,128},{192,160},{224,1... | collective-permute-start | bytes 884744 | tf_op jit(solution)/shard_map/ppermute | solution.py:170
  135.5 0.7 copy-done.16
  136.2 1.4 collective-permute-done.7.refs_11_
  137.6 1.9 collective-permute-start.8
  139.5 0.2 collective-permute-done.14.refs_12_
  139.7 5.7 %collective-permute-start.15 = (f32[192,384]{1,0:T(8,128)}, f32[192,384]{1,0:T(8,128)}, u32[]{:S(2)}, u32[]{:S(2)}) collective-permute-start(f32[192,384]{1,0:T(8,128)} %collective-permute-done.14.refs_12_), channel_id=1, source_target_pairs={{0,480},{32,0},{64,32},{96,64},{128,96},{160,128},{192,160},{224,1... | collective-permute-start | bytes 884744 | tf_op jit(solution)/shard_map/ppermute | solution.py:170
  145.5 2.4 %collective-permute-done.8.behind = f32[192,384]{1,0:T(8,128)} collective-permute-done((f32[192,384]{1,0:T(8,128)}, f32[192,384]{1,0:T(8,128)}, u32[]{:S(2)}, u32[]{:S(2)}) %collective-permute-start.8) | collective-permute-done | bytes 294944 | tf_op jit(solution)/shard_map/ppermute | solution.py:170
  147.9 1.9 collective-permute-start.18
  149.8 0.6 collective-permute-done.15.ahead
  150.4 5.1 %collective-permute-start.19 = (f32[192,384]{1,0:T(8,128)}, f32[192,384]{1,0:T(8,128)S(1)}, u32[]{:S(2)}, u32[]{:S(2)}) collective-permute-start(f32[192,384]{1,0:T(8,128)} %collective-permute-done.15.ahead), channel_id=1, source_target_pairs={{0,481},{1,480},{32,1},{33,0},{64,33},{65,32},{96,65},{97,64},{128... | collective-permute-start | bytes 884744 | tf_op jit(solution)/shard_map/ppermute | solution.py:198
  155.5 1.0 select_bitcast_fusion.left_own
  156.5 3.8 %collective-permute-start.17 = (f32[576,128]{1,0:T(8,128)S(1)}, f32[576,128]{1,0:T(8,128)S(1)}, u32[]{:S(2)}, u32[]{:S(2)}) collective-permute-start(f32[576,128]{1,0:T(8,128)S(1)} %select_bitcast_fusion.left_own), channel_id=1, source_target_pairs={{0,1},{1,0},{2,3},{3,2},{4,5},{5,4},{6,7},{7,6},{8,9},{9,8},{10,11... | collective-permute-start | bytes 884744 | tf_op jit(solution)/shard_map/ppermute | solution.py:170
  160.4 1.7 copy-done
  162.0 1.0 copy-done.5
  163.0 1.0 copy-done.7
  163.9 1.0 copy-done.9
  164.9 1.0 copy-done.11
  165.9 1.0 copy-done.13
  166.8 1.0 copy-done.15
  167.8 1.0 copy-done.17
  168.8 6.5 %shard_map.56.total = f32[384,384]{1,0:T(8,128)S(1)} custom-call(s32[3]{0:T(128)S(1)} %pad_add_fusion.place, f32[4,2,576,128]{3,2,1,0:T(8,128)S(1)} %bitcast.10, f32[4,2,576,128]{3,2,1,0:T(8,128)S(1)} %collective-permute-done.1.other, f32[192,384]{1,0:T(8,128)S(1)} %get-tuple-element.10.refs_0_, f32[192,384]{1,0:T(8,128)S(1)} %collective-permute-done.2.refs_1_, ...), custom_call_target="tpu_custom_call" | custom-call | flops 2378170368 | bytes 10485760 | tf_op jit(solution)/shard_map/pallas_call | solution.py:208
  175.3 0.0 copy-start.20
  175.3 2.0 %shard_map.57 = (f32[192,384]{1,0:T(8,128)S(1)}, f32[192,384]{1,0:T(8,128)S(1)}) custom-call(s32[3]{0:T(128)S(1)} %pad_add_fusion.place, f32[4,2,576,128]{3,2,1,0:T(8,128)S(1)} %bitcast.11, f32[4,2,576,128]{3,2,1,0:T(8,128)S(1)} %collective-permute-done.1.other, f32[192,384]{1,0:T(8,128)} %collective-permute-done.8.behind, ...), custom_call_target="tpu_custom_call" | custom-call | flops 339738624 | bytes 1048576 | tf_op jit(solution)/shard_map/pallas_call | solution.py:212
  177.3 2.0 %collective-permute-start.16 = (f32[192,384]{1,0:T(8,128)S(1)}, f32[192,384]{1,0:T(8,128)S(1)}, u32[]{:S(2)}, u32[]{:S(2)}) collective-permute-start(f32[192,384]{1,0:T(8,128)S(1)} %get-tuple-element.12), channel_id=1, source_target_pairs={{0,1},{1,0},{2,3},{3,2},{4,5},{5,4},{6,7},{7,6},{8,9},{9,8},{10,11... | collective-permute-start | bytes 884744 | tf_op jit(solution)/shard_map/ppermute | solution.py:170
  179.4 6.6 %collective-permute-done.16.came = f32[192,384]{1,0:T(8,128)S(1)} collective-permute-done((f32[192,384]{1,0:T(8,128)S(1)}, f32[192,384]{1,0:T(8,128)S(1)}, u32[]{:S(2)}, u32[]{:S(2)}) %collective-permute-start.16) | collective-permute-done | bytes 294944 | tf_op jit(solution)/shard_map/ppermute | solution.py:170
  185.9 1.8 shard_map.58
  (28 shorter events, 0.1 us)
Async XLA Ops:
  6.5 62.7 %all-gather.3.cloned.1.call-start = ((), (), s32[]{:S(2)}) async-start(), calls=%async_computation | async-start | bytes 2949120 | tf_op jit(solution)/shard_map/all_gather | solution.py:188
  6.6 1.1 copy-start.2
  7.7 1.1 copy-start.3
  8.7 0.7 copy-start.18
  9.4 0.7 copy-start.19
  10.8 12.1 %collective-permute-start = (f32[576,128]{1,0:T(8,128)S(1)}, f32[576,128]{1,0:T(8,128)S(1)}, u32[]{:S(2)}, u32[]{:S(2)}) collective-permute-start(f32[576,128]{1,0:T(8,128)S(1)} %get-tuple-element.9), channel_id=1, source_target_pairs={{0,4},{2,6},{4,0},{6,2},{8,12},{10,14},{12,8},{14,10},{16,20},{18,... | collective-permute-start | bytes 884744 | tf_op jit(solution)/shard_map/ppermute | solution.py:186
  69.2 86.3 %collective-permute-start.1 = (f32[4,2,576,128]{3,2,1,0:T(8,128)}, f32[4,2,576,128]{3,2,1,0:T(8,128)S(1)}, u32[]{:S(2)}, u32[]{:S(2)}) collective-permute-start(f32[4,2,576,128]{3,2,1,0:T(8,128)} %bitcast.8), channel_id=1, source_target_pairs={{0,2},{2,0},{4,6},{6,4},{8,10},{10,8},{12,14},{14,12},{16,18},{18,... | collective-permute-start | bytes 7077896 | tf_op jit(solution)/shard_map/ppermute | solution.py:189
  71.1 13.6 %collective-permute-start.2 = (f32[192,384]{1,0:T(8,128)S(1)}, f32[192,384]{1,0:T(8,128)S(1)}, u32[]{:S(2)}, u32[]{:S(2)}) collective-permute-start(f32[192,384]{1,0:T(8,128)S(1)} %get-tuple-element.10.refs_0_), channel_id=1, source_target_pairs={{0,32},{32,64},{64,96},{96,128},{128,160},{160,192},{192,224},{224... | collective-permute-start | bytes 884744 | tf_op jit(solution)/shard_map/ppermute | solution.py:170
  74.6 12.1 %collective-permute-start.9 = (f32[192,384]{1,0:T(8,128)S(1)}, f32[192,384]{1,0:T(8,128)S(1)}, u32[]{:S(2)}, u32[]{:S(2)}) collective-permute-start(f32[192,384]{1,0:T(8,128)S(1)} %get-tuple-element.10.refs_0_), channel_id=1, source_target_pairs={{0,480},{32,0},{64,32},{96,64},{128,96},{160,128},{192,160},{224,1... | collective-permute-start | bytes 884744 | tf_op jit(solution)/shard_map/ppermute | solution.py:170
  84.7 11.9 %collective-permute-start.3 = (f32[192,384]{1,0:T(8,128)S(1)}, f32[192,384]{1,0:T(8,128)S(1)}, u32[]{:S(2)}, u32[]{:S(2)}) collective-permute-start(f32[192,384]{1,0:T(8,128)S(1)} %collective-permute-done.2.refs_1_), channel_id=1, source_target_pairs={{0,32},{32,64},{64,96},{96,128},{128,160},{160,192},{192,224},{224... | collective-permute-start | bytes 884744 | tf_op jit(solution)/shard_map/ppermute | solution.py:170
  86.7 11.9 %collective-permute-start.10 = (f32[192,384]{1,0:T(8,128)S(1)}, f32[192,384]{1,0:T(8,128)S(1)}, u32[]{:S(2)}, u32[]{:S(2)}) collective-permute-start(f32[192,384]{1,0:T(8,128)S(1)} %collective-permute-done.9.refs_2_), channel_id=1, source_target_pairs={{0,480},{32,0},{64,32},{96,64},{128,96},{160,128},{192,160},{224,1... | collective-permute-start | bytes 884744 | tf_op jit(solution)/shard_map/ppermute | solution.py:170
  96.7 11.1 %collective-permute-start.4 = (f32[192,384]{1,0:T(8,128)S(1)}, f32[192,384]{1,0:T(8,128)S(1)}, u32[]{:S(2)}, u32[]{:S(2)}) collective-permute-start(f32[192,384]{1,0:T(8,128)S(1)} %collective-permute-done.3.refs_3_), channel_id=1, source_target_pairs={{0,32},{32,64},{64,96},{96,128},{128,160},{160,192},{192,224},{224... | collective-permute-start | bytes 884744 | tf_op jit(solution)/shard_map/ppermute | solution.py:170
  98.6 11.8 %collective-permute-start.11 = (f32[192,384]{1,0:T(8,128)S(1)}, f32[192,384]{1,0:T(8,128)S(1)}, u32[]{:S(2)}, u32[]{:S(2)}) collective-permute-start(f32[192,384]{1,0:T(8,128)S(1)} %collective-permute-done.10.refs_4_), channel_id=1, source_target_pairs={{0,480},{32,0},{64,32},{96,64},{128,96},{160,128},{192,160},{224,1... | collective-permute-start | bytes 884744 | tf_op jit(solution)/shard_map/ppermute | solution.py:170
  103.7 0.7 copy-start.4
  107.7 10.1 %collective-permute-start.5 = (f32[192,384]{1,0:T(8,128)S(1)}, f32[192,384]{1,0:T(8,128)S(1)}, u32[]{:S(2)}, u32[]{:S(2)}) collective-permute-start(f32[192,384]{1,0:T(8,128)S(1)} %collective-permute-done.4.refs_5_), channel_id=1, source_target_pairs={{0,32},{32,64},{64,96},{96,128},{128,160},{160,192},{192,224},{224... | collective-permute-start | bytes 884744 | tf_op jit(solution)/shard_map/ppermute | solution.py:170
  109.6 0.7 copy-start.6
  110.3 10.2 %collective-permute-start.12 = (f32[192,384]{1,0:T(8,128)S(1)}, f32[192,384]{1,0:T(8,128)S(1)}, u32[]{:S(2)}, u32[]{:S(2)}) collective-permute-start(f32[192,384]{1,0:T(8,128)S(1)} %collective-permute-done.11.refs_6_), channel_id=1, source_target_pairs={{0,480},{32,0},{64,32},{96,64},{128,96},{160,128},{192,160},{224,1... | collective-permute-start | bytes 884744 | tf_op jit(solution)/shard_map/ppermute | solution.py:170
  115.5 0.7 copy-start.8
  117.9 9.8 %collective-permute-start.6 = (f32[192,384]{1,0:T(8,128)S(1)}, f32[192,384]{1,0:T(8,128)S(1)}, u32[]{:S(2)}, u32[]{:S(2)}) collective-permute-start(f32[192,384]{1,0:T(8,128)S(1)} %collective-permute-done.5.refs_7_), channel_id=1, source_target_pairs={{0,32},{32,64},{64,96},{96,128},{128,160},{160,192},{192,224},{224... | collective-permute-start | bytes 884744 | tf_op jit(solution)/shard_map/ppermute | solution.py:170
  119.8 0.7 copy-start.10
  120.5 9.8 %collective-permute-start.13 = (f32[192,384]{1,0:T(8,128)S(1)}, f32[192,384]{1,0:T(8,128)S(1)}, u32[]{:S(2)}, u32[]{:S(2)}) collective-permute-start(f32[192,384]{1,0:T(8,128)S(1)} %collective-permute-done.12.refs_8_), channel_id=1, source_target_pairs={{0,480},{32,0},{64,32},{96,64},{128,96},{160,128},{192,160},{224,1... | collective-permute-start | bytes 884744 | tf_op jit(solution)/shard_map/ppermute | solution.py:170
  125.6 0.7 copy-start.12
  127.7 9.9 %collective-permute-start.7 = (f32[192,384]{1,0:T(8,128)S(1)}, f32[192,384]{1,0:T(8,128)}, u32[]{:S(2)}, u32[]{:S(2)}) collective-permute-start(f32[192,384]{1,0:T(8,128)S(1)} %collective-permute-done.6.refs_9_), channel_id=1, source_target_pairs={{0,32},{32,64},{64,96},{96,128},{128,160},{160,192},{192,224},{224... | collective-permute-start | bytes 884744 | tf_op jit(solution)/shard_map/ppermute | solution.py:170
  129.6 0.7 copy-start.14
  130.3 9.3 %collective-permute-start.14 = (f32[192,384]{1,0:T(8,128)S(1)}, f32[192,384]{1,0:T(8,128)}, u32[]{:S(2)}, u32[]{:S(2)}) collective-permute-start(f32[192,384]{1,0:T(8,128)S(1)} %collective-permute-done.13.refs_10_), channel_id=1, source_target_pairs={{0,480},{32,0},{64,32},{96,64},{128,96},{160,128},{192,160},{224,1... | collective-permute-start | bytes 884744 | tf_op jit(solution)/shard_map/ppermute | solution.py:170
  135.5 0.7 copy-start.16
  137.6 10.3 %collective-permute-start.8 = (f32[192,384]{1,0:T(8,128)}, f32[192,384]{1,0:T(8,128)}, u32[]{:S(2)}, u32[]{:S(2)}) collective-permute-start(f32[192,384]{1,0:T(8,128)} %collective-permute-done.7.refs_11_), channel_id=1, source_target_pairs={{0,32},{32,64},{64,96},{96,128},{128,160},{160,192},{192,224},{224... | collective-permute-start | bytes 884744 | tf_op jit(solution)/shard_map/ppermute | solution.py:170
  139.7 10.7 %collective-permute-start.15 = (f32[192,384]{1,0:T(8,128)}, f32[192,384]{1,0:T(8,128)}, u32[]{:S(2)}, u32[]{:S(2)}) collective-permute-start(f32[192,384]{1,0:T(8,128)} %collective-permute-done.14.refs_12_), channel_id=1, source_target_pairs={{0,480},{32,0},{64,32},{96,64},{128,96},{160,128},{192,160},{224,1... | collective-permute-start | bytes 884744 | tf_op jit(solution)/shard_map/ppermute | solution.py:170
  147.9 31.5 %collective-permute-start.18 = (f32[192,384]{1,0:T(8,128)}, f32[192,384]{1,0:T(8,128)S(1)}, u32[]{:S(2)}, u32[]{:S(2)}) collective-permute-start(f32[192,384]{1,0:T(8,128)} %collective-permute-done.8.behind), channel_id=1, source_target_pairs={{0,32},{32,64},{64,96},{96,128},{128,160},{160,192},{192,224},{224... | collective-permute-start | bytes 884744 | tf_op jit(solution)/shard_map/ppermute | solution.py:170
  150.4 29.0 %collective-permute-start.19 = (f32[192,384]{1,0:T(8,128)}, f32[192,384]{1,0:T(8,128)S(1)}, u32[]{:S(2)}, u32[]{:S(2)}) collective-permute-start(f32[192,384]{1,0:T(8,128)} %collective-permute-done.15.ahead), channel_id=1, source_target_pairs={{0,481},{1,480},{32,1},{33,0},{64,33},{65,32},{96,65},{97,64},{128... | collective-permute-start | bytes 884744 | tf_op jit(solution)/shard_map/ppermute | solution.py:198
  156.5 22.8 %collective-permute-start.17 = (f32[576,128]{1,0:T(8,128)S(1)}, f32[576,128]{1,0:T(8,128)S(1)}, u32[]{:S(2)}, u32[]{:S(2)}) collective-permute-start(f32[576,128]{1,0:T(8,128)S(1)} %select_bitcast_fusion.left_own), channel_id=1, source_target_pairs={{0,1},{1,0},{2,3},{3,2},{4,5},{5,4},{6,7},{7,6},{8,9},{9,8},{10,11... | collective-permute-start | bytes 884744 | tf_op jit(solution)/shard_map/ppermute | solution.py:170
  160.4 1.7 copy-start
  162.0 1.0 copy-start.5
  163.0 1.0 copy-start.7
  163.9 1.0 copy-start.9
  164.9 1.0 copy-start.11
  165.9 1.0 copy-start.13
  166.8 1.0 copy-start.15
  167.8 1.0 copy-start.17
  168.8 6.5 %copy-start.1 = (f32[8,576,128]{2,1,0:T(8,128)S(1)}, f32[8,576,128]{2,1,0:T(8,128)}, u32[]{:S(2)}) copy-start(f32[8,576,128]{2,1,0:T(8,128)} %all-gather.3.cloned.1.call-done) | copy-start | bytes 7077892
  175.3 10.7 %copy-start.20 = (s32[3,3]{1,0:T(4,128)S(1)}, s32[3,3]{1,0:T(4,128)}, u32[]{:S(2)}) copy-start(s32[3,3]{1,0:T(4,128)} %keep.1) | copy-start | bytes 112
  177.3 8.6 %collective-permute-start.16 = (f32[192,384]{1,0:T(8,128)S(1)}, f32[192,384]{1,0:T(8,128)S(1)}, u32[]{:S(2)}, u32[]{:S(2)}) collective-permute-start(f32[192,384]{1,0:T(8,128)S(1)} %get-tuple-element.12), channel_id=1, source_target_pairs={{0,1},{1,0},{2,3},{3,2},{4,5},{5,4},{6,7},{7,6},{8,9},{9,8},{10,11... | collective-permute-start | bytes 884744 | tf_op jit(solution)/shard_map/ppermute | solution.py:170
Sparse Core Ops, SparseCore 0:
  24.0 45.1 all-gather.2

commit v2 on v1

--- a/solution.py
+++ b/solution.py
@@ -24,7 +24,7 @@
         in_specs=in_specs,
         out_specs=jax.tree.map(lambda _: VMEM, out_shapes),
         scratch_shapes=scratch,
-        compiler_params=pltpu.CompilerParams(vmem_limit_bytes=40 * 2**20),
+        compiler_params=pltpu.CompilerParams(vmem_limit_bytes=20 * 2**20),
         cost_estimate=pl.CostEstimate(flops=flops, bytes_accessed=nbytes, transcendentals=0),
     )
 
@@ -125,8 +125,10 @@
     total[...] = triple((lh[...], ll[...]), (rh[...], rl[...]))
 
 
-def near_kernel(step, place, same, other, behind, ahead, total, own, away, lh, ll, rh, rl):
-    fill(place, same, other, step, (behind, ahead), lh, ll, rh, rl, 0)
+def near_kernel(steps, place, same, other, *refs):
+    rights, (total, own, away, lh, ll, rh, rl) = refs[:-7], refs[-7:]
+    for number, step in enumerate(steps):
+        fill(place, same, other, step, rights[2 * number : 2 * number + 2], lh, ll, rh, rl, number * TILE)
     value = total[...] + triple((lh[...], ll[...]), (rh[...], rl[...]))
     layer = place[2]
 
@@ -170,6 +172,10 @@
     return lax.ppermute(value, axis, [(i, (i + steps) % count) for i in range(count)])
 
 
+def after(value, *earlier):
+    return lax.optimization_barrier((value, *earlier))[0]
+
+
 def shards(left_values, left_mask, right_values, right_mask, keep_mask):
     count = lax.axis_size("row")
     cols = lax.axis_size("col")
@@ -186,16 +192,6 @@
     left_x = lax.ppermute(left, "col", [(i, i ^ 2) for i in range(cols)])
     groups = [[j + 4 * y for y in range(4)] for j in range(4)]
     same = lax.all_gather(jnp.stack([left, left_x]), "col", axis_index_groups=groups)
-    other = lax.ppermute(same, "col", [(i, i ^ 1) for i in range(cols)])
-
-    reach = count // 2
-    rights, behind, ahead = [right], right, right
-    for _ in range(1, reach):
-        behind, ahead = shift(behind, "row", 1), shift(ahead, "row", -1)
-        rights += [behind, ahead]
-    far_own = shift(behind, "row", 1)
-    cross = [(z0 * 2 + l0, (z0 - 1) % count * 2 + 1 - l0) for z0 in range(count) for l0 in range(2)]
-    far_other = lax.ppermute(ahead, ("row", "layer"), cross)
 
     def parts(n):
         return [
@@ -203,22 +199,35 @@
             pltpu.VMEM((n * TILE, TILE), BF16), pltpu.VMEM((n * TILE, TILE), BF16),
         ]
 
-    steps = tuple(range(reach - 1))
-    first = rights[: 2 * len(steps) - 1]
-    total = call(
-        functools.partial(main_kernel, steps), whole, [SMEM] + [VMEM] * (2 + len(first)), parts(len(steps)),
-        flops=6 * TILE * TILE * TILE * len(steps), nbytes=10 * 2**20,
-    )(place, same, other, *first)
+    reach = count // 2
+    rights, behind, ahead = [right], right, right
+    for step in range(1, reach):
+        if step == reach - 1:
+            steps = tuple(range(reach - 2))
+            first = rights[: 2 * len(steps) - 1]
+            total = call(
+                functools.partial(main_kernel, steps), whole, [SMEM] + [VMEM] * (2 + len(first)), parts(len(steps)),
+                flops=6 * TILE * TILE * TILE * len(steps), nbytes=10 * 2**20,
+            )(place, same, other, *first)
+            far = (z + reach) % count
+            mine, y, x = panel_index(place, far)
+            left_own = jnp.where(mine, same[y, x], other[y, x])
+            left_other = shift(left_own, "layer", 1)
+            behind, ahead = after(behind, total, left_other), after(ahead, total, left_other)
+        behind, ahead = shift(behind, "row", 1), shift(ahead, "row", -1)
+        rights += [behind, ahead]
+        if step == reach - 3:
+            same = after(same, behind, ahead)
+            other = lax.ppermute(same, "col", [(i, i ^ 1) for i in range(cols)])
     own, away = call(
-        functools.partial(near_kernel, reach - 1), (half, half), [SMEM] + [VMEM] * 5, parts(1),
+        functools.partial(near_kernel, (reach - 2, reach - 1)), (half, half), [SMEM] + [VMEM] * 7, parts(2),
         flops=6 * TILE * TILE * TILE, nbytes=2**20,
-    )(place, same, other, *rights[-2:], total)
+    )(place, same, other, *rights[-4:], total)
     came = shift(away, "layer", 1)
-
-    far = (z + reach) % count
-    mine, y, x = panel_index(place, far)
-    left_own = jnp.where(mine, same[y, x], other[y, x])
-    left_other = shift(left_own, "layer", 1)
+    behind, ahead = after(behind, away), after(ahead, away)
+    far_own = shift(behind, "row", 1)
+    cross = [(z0 * 2 + l0, (z0 - 1) % count * 2 + 1 - l0) for z0 in range(count) for l0 in range(2)]
+    far_other = lax.ppermute(ahead, ("row", "layer"), cross)
     return call(last_kernel, half, [SMEM] * 2 + [VMEM] * 6, flops=6 * PART * TILE * TILE, nbytes=2**20)(
         place, keep_mask, own, came, left_own, left_other, far_own, far_other
     )

time: 196 us -> 157 us (0.80)
  the two profiles are of different devices: /device:TPU:2 before, /device:TPU:1 now
where the time goes in v2:
time: 157 us; the launch traced here: 156 us
  starting transfers between devices  80.4 us (51%)
  waiting for transfers between devices  35.3 us (22%)
  local copies, waits for them, and re-layouts  14.5 us (9%)
  between operations  13.8 us (9%)
  Pallas kernels  10.2 us (6%)
  other arithmetic  1.92 us (1%)
    ppermute x17, starting transfers between devices, shift(): lax.ppermute(value, axis, [(i, (i + steps) % count) for i in range(count)])  64.7 us
    ppermute x17, waiting for transfers between devices, shift(): lax.ppermute(value, axis, [(i, (i + steps) % count) for i in range(count)])  28.1 us
    unnamed x38, local copies, waits for them, and re-layouts  14.5 us
    ppermute x1, starting transfers between devices, shards(): other = lax.ppermute(same, 'col', [(i, i ^ 1) for i in range(cols)])  8.22 us
    pallas_call x1, Pallas kernels, shards(): call(functools.partial(main_kernel, steps), whole, [SMEM] + [VMEM] * (2 +...  5.53 us
    ppermute x1, starting transfers between devices, shards(): left_x = lax.ppermute(left, 'col', [(i, i ^ 2) for i in range(cols)])  5.48 us
    ppermute x1, waiting for transfers between devices, shards(): left_x = lax.ppermute(left, 'col', [(i, i ^ 2) for i in range(cols)])  4.1 us
  transfers between devices with their start and end apart: 21, of which 13 were waited for; matrix products, arithmetic and copies ran while one was open for 1% of the time, Pallas kernels for 4%

profile of v2, /device:TPU:1, one launch (start us, length us, event | category | flops | bytes accessed | tf_op | source)
XLA Modules:
  0.0 156.1 jit_solution(6713299729972602463)
XLA Ops:
  6.5 0.1 pad_add_fusion.place
  6.6 1.1 copy-done.2
  7.7 1.1 copy-done.3
  8.7 0.7 copy-done.16
  9.4 0.7 copy-done.17
  10.1 0.7 shard_map.55
  10.8 5.5 %collective-permute-start = (f32[576,128]{1,0:T(8,128)S(1)}, f32[576,128]{1,0:T(8,128)S(1)}, u32[]{:S(2)}, u32[]{:S(2)}) collective-permute-start(f32[576,128]{1,0:T(8,128)S(1)} %get-tuple-element.14), channel_id=1, source_target_pairs={{0,4},{2,6},{4,0},{6,2},{8,12},{10,14},{12,8},{14,10},{16,20},{18,... | collective-permute-start | bytes 884744 | tf_op jit(solution)/shard_map/ppermute | solution.py:192
  16.3 4.1 %collective-permute-done = f32[576,128]{1,0:T(8,128)S(1)} collective-permute-done((f32[576,128]{1,0:T(8,128)S(1)}, f32[576,128]{1,0:T(8,128)S(1)}, u32[]{:S(2)}, u32[]{:S(2)}) %collective-permute-start) | collective-permute-done | bytes 294944 | tf_op jit(solution)/shard_map/ppermute | solution.py:192
  20.4 0.9 pad_maximum_fusion
  21.3 0.0 all-gather.3.cloned.1.call-update
  21.3 13.6 %collective-permute-start.6 = (f32[192,384]{1,0:T(8,128)S(1)}, f32[192,384]{1,0:T(8,128)S(1)}, u32[]{:S(2)}, u32[]{:S(2)}) collective-permute-start(f32[192,384]{1,0:T(8,128)S(1)} %get-tuple-element.15.refs_0_), channel_id=1, source_target_pairs={{0,480},{32,0},{64,32},{96,64},{128,96},{160,128},{192,160},{224,1... | collective-permute-start | bytes 884744 | tf_op jit(solution)/shard_map/ppermute | solution.py:172
  34.9 1.9 %collective-permute-start.1 = (f32[192,384]{1,0:T(8,128)S(1)}, f32[192,384]{1,0:T(8,128)S(1)}, u32[]{:S(2)}, u32[]{:S(2)}) collective-permute-start(f32[192,384]{1,0:T(8,128)S(1)} %get-tuple-element.15.refs_0_), channel_id=1, source_target_pairs={{0,32},{32,64},{64,96},{96,128},{128,160},{160,192},{192,224},{224... | collective-permute-start | bytes 884744 | tf_op jit(solution)/shard_map/ppermute | solution.py:172
  36.9 2.8 %collective-permute-done.6.refs_2_ = f32[192,384]{1,0:T(8,128)S(1)} collective-permute-done((f32[192,384]{1,0:T(8,128)S(1)}, f32[192,384]{1,0:T(8,128)S(1)}, u32[]{:S(2)}, u32[]{:S(2)}) %collective-permute-start.6) | collective-permute-done | bytes 294944 | tf_op jit(solution)/shard_map/ppermute | solution.py:172
  39.7 5.3 %collective-permute-start.7 = (f32[192,384]{1,0:T(8,128)S(1)}, f32[192,384]{1,0:T(8,128)S(1)}, u32[]{:S(2)}, u32[]{:S(2)}) collective-permute-start(f32[192,384]{1,0:T(8,128)S(1)} %collective-permute-done.6.refs_2_), channel_id=1, source_target_pairs={{0,480},{32,0},{64,32},{96,64},{128,96},{160,128},{192,160},{224,1... | collective-permute-start | bytes 884744 | tf_op jit(solution)/shard_map/ppermute | solution.py:172
  45.0 0.0 collective-permute-done.1.refs_1_
  45.0 1.9 %collective-permute-start.2 = (f32[192,384]{1,0:T(8,128)S(1)}, f32[192,384]{1,0:T(8,128)S(1)}, u32[]{:S(2)}, u32[]{:S(2)}) collective-permute-start(f32[192,384]{1,0:T(8,128)S(1)} %collective-permute-done.1.refs_1_), channel_id=1, source_target_pairs={{0,32},{32,64},{64,96},{96,128},{128,160},{160,192},{192,224},{224... | collective-permute-start | bytes 884744 | tf_op jit(solution)/shard_map/ppermute | solution.py:172
  46.9 1.7 %collective-permute-done.7.refs_4_ = f32[192,384]{1,0:T(8,128)S(1)} collective-permute-done((f32[192,384]{1,0:T(8,128)S(1)}, f32[192,384]{1,0:T(8,128)S(1)}, u32[]{:S(2)}, u32[]{:S(2)}) %collective-permute-start.7) | collective-permute-done | bytes 294944 | tf_op jit(solution)/shard_map/ppermute | solution.py:172
  48.6 5.5 %collective-permute-start.8 = (f32[192,384]{1,0:T(8,128)S(1)}, f32[192,384]{1,0:T(8,128)S(1)}, u32[]{:S(2)}, u32[]{:S(2)}) collective-permute-start(f32[192,384]{1,0:T(8,128)S(1)} %collective-permute-done.7.refs_4_), channel_id=1, source_target_pairs={{0,480},{32,0},{64,32},{96,64},{128,96},{160,128},{192,160},{224,1... | collective-permute-start | bytes 884744 | tf_op jit(solution)/shard_map/ppermute | solution.py:172
  54.1 0.0 collective-permute-done.2.refs_3_
  54.1 1.9 %collective-permute-start.3 = (f32[192,384]{1,0:T(8,128)S(1)}, f32[192,384]{1,0:T(8,128)S(1)}, u32[]{:S(2)}, u32[]{:S(2)}) collective-permute-start(f32[192,384]{1,0:T(8,128)S(1)} %collective-permute-done.2.refs_3_), channel_id=1, source_target_pairs={{0,32},{32,64},{64,96},{96,128},{128,160},{160,192},{192,224},{224... | collective-permute-start | bytes 884744 | tf_op jit(solution)/shard_map/ppermute | solution.py:172
  56.1 0.7 copy-done.4
  56.8 1.0 collective-permute-done.8.refs_6_
  57.7 5.4 %collective-permute-start.9 = (f32[192,384]{1,0:T(8,128)S(1)}, f32[192,384]{1,0:T(8,128)S(1)}, u32[]{:S(2)}, u32[]{:S(2)}) collective-permute-start(f32[192,384]{1,0:T(8,128)S(1)} %collective-permute-done.8.refs_6_), channel_id=1, source_target_pairs={{0,480},{32,0},{64,32},{96,64},{128,96},{160,128},{192,160},{224,1... | collective-permute-start | bytes 884744 | tf_op jit(solution)/shard_map/ppermute | solution.py:172
  63.2 0.7 copy-done.6
  63.9 0.0 collective-permute-done.3.refs_5_
  63.9 1.9 %collective-permute-start.4 = (f32[192,384]{1,0:T(8,128)S(1)}, f32[192,384]{1,0:T(8,128)S(1)}, u32[]{:S(2)}, u32[]{:S(2)}) collective-permute-start(f32[192,384]{1,0:T(8,128)S(1)} %collective-permute-done.3.refs_5_), channel_id=1, source_target_pairs={{0,32},{32,64},{64,96},{96,128},{128,160},{160,192},{192,224},{224... | collective-permute-start | bytes 884744 | tf_op jit(solution)/shard_map/ppermute | solution.py:172
  65.8 0.7 copy-done.8
  66.5 0.3 collective-permute-done.9.refs_8_
  66.8 5.4 %collective-permute-start.10 = (f32[192,384]{1,0:T(8,128)S(1)}, f32[192,384]{1,0:T(8,128)S(1)}, u32[]{:S(2)}, u32[]{:S(2)}) collective-permute-start(f32[192,384]{1,0:T(8,128)S(1)} %collective-permute-done.9.refs_8_), channel_id=1, source_target_pairs={{0,480},{32,0},{64,32},{96,64},{128,96},{160,128},{192,160},{224,1... | collective-permute-start | bytes 884744 | tf_op jit(solution)/shard_map/ppermute | solution.py:172
  72.2 0.7 copy-done.10
  73.0 0.0 collective-permute-done.4.refs_7_
  73.0 1.9 %collective-permute-start.5 = (f32[192,384]{1,0:T(8,128)S(1)}, f32[192,384]{1,0:T(8,128)}, u32[]{:S(2)}, u32[]{:S(2)}) collective-permute-start(f32[192,384]{1,0:T(8,128)S(1)} %collective-permute-done.4.refs_7_), channel_id=1, source_target_pairs={{0,32},{32,64},{64,96},{96,128},{128,160},{160,192},{192,224},{224... | collective-permute-start | bytes 884744 | tf_op jit(solution)/shard_map/ppermute | solution.py:172
  74.9 0.7 copy-done.12
  75.6 0.3 collective-permute-done.10.refs_10_
  75.9 5.9 %collective-permute-done.5.refs_9_ = f32[192,384]{1,0:T(8,128)} collective-permute-done((f32[192,384]{1,0:T(8,128)S(1)}, f32[192,384]{1,0:T(8,128)}, u32[]{:S(2)}, u32[]{:S(2)}) %collective-permute-start.5) | collective-permute-done | bytes 294944 | tf_op jit(solution)/shard_map/ppermute | solution.py:172
  81.7 8.2 %collective-permute-start.11 = (f32[4,2,576,128]{3,2,1,0:T(8,128)}, f32[4,2,576,128]{3,2,1,0:T(8,128)S(1)}, u32[]{:S(2)}, u32[]{:S(2)}) collective-permute-start(f32[4,2,576,128]{3,2,1,0:T(8,128)} %bitcast.8), channel_id=1, source_target_pairs={{0,2},{2,0},{4,6},{6,4},{8,10},{10,8},{12,14},{14,12},{16,18},{18,... | collective-permute-start | bytes 7077896 | tf_op jit(solution)/shard_map/ppermute | solution.py:221
  90.0 1.9 %collective-permute-start.13 = (f32[192,384]{1,0:T(8,128)}, f32[192,384]{1,0:T(8,128)S(1)}, u32[]{:S(2)}, u32[]{:S(2)}) collective-permute-start(f32[192,384]{1,0:T(8,128)} %copy-done.14), channel_id=1, source_target_pairs={{0,480},{32,0},{64,32},{96,64},{128,96},{160,128},{192,160},{224,1... | collective-permute-start | bytes 884744 | tf_op jit(solution)/shard_map/ppermute | solution.py:172
  92.0 2.3 %collective-permute-done.11.other = f32[4,2,576,128]{3,2,1,0:T(8,128)S(1)} collective-permute-done((f32[4,2,576,128]{3,2,1,0:T(8,128)}, f32[4,2,576,128]{3,2,1,0:T(8,128)S(1)}, u32[]{:S(2)}, u32[]{:S(2)}) %collective-permute-start.11) | collective-permute-done | bytes 2359328 | tf_op jit(solution)/shard_map/ppermute | solution.py:221
  94.3 1.0 select_bitcast_fusion.left_own
  95.3 3.1 %collective-permute-start.14 = (f32[576,128]{1,0:T(8,128)S(1)}, f32[576,128]{1,0:T(8,128)S(1)}, u32[]{:S(2)}, u32[]{:S(2)}) collective-permute-start(f32[576,128]{1,0:T(8,128)S(1)} %select_bitcast_fusion.left_own), channel_id=1, source_target_pairs={{0,1},{1,0},{2,3},{3,2},{4,5},{5,4},{6,7},{7,6},{8,9},{9,8},{10,11... | collective-permute-start | bytes 884744 | tf_op jit(solution)/shard_map/ppermute | solution.py:172
  98.4 1.9 %collective-permute-start.12 = (f32[192,384]{1,0:T(8,128)}, f32[192,384]{1,0:T(8,128)S(1)}, u32[]{:S(2)}, u32[]{:S(2)}) collective-permute-start(f32[192,384]{1,0:T(8,128)} %collective-permute-done.5.refs_9_), channel_id=1, source_target_pairs={{0,32},{32,64},{64,96},{96,128},{128,160},{160,192},{192,224},{224... | collective-permute-start | bytes 884744 | tf_op jit(solution)/shard_map/ppermute | solution.py:172
  100.4 1.7 %copy-done = f32[8,576,128]{2,1,0:T(8,128)S(1)} copy-done((f32[8,576,128]{2,1,0:T(8,128)S(1)}, f32[8,576,128]{2,1,0:T(8,128)}, u32[]{:S(2)}) %copy-start) | copy-done | bytes 2359320
  102.0 1.0 copy-done.5
  103.0 1.0 copy-done.7
  104.0 1.0 copy-done.9
  104.9 1.0 copy-done.11
  105.9 1.0 copy-done.13
  106.8 1.0 copy-done.15
  107.8 5.5 %shard_map.56.refs_4_ = f32[384,384]{1,0:T(8,128)S(1)} custom-call(s32[3]{0:T(128)S(1)} %pad_add_fusion.place, f32[4,2,576,128]{3,2,1,0:T(8,128)S(1)} %bitcast.10, f32[4,2,576,128]{3,2,1,0:T(8,128)S(1)} %collective-permute-done.11.other, f32[192,384]{1,0:T(8,128)S(1)} %get-tuple-element.15.refs_0_, f32[192,384]{1,0:T(8,128)S(1)} %collective-permute-done.1.refs_1_, ...), custom_call_target="tpu_custom_call" | custom-call | flops 2038431744 | bytes 10485760 | tf_op jit(solution)/shard_map/pallas_call | solution.py:208
  113.3 0.0 copy-start.18
  113.4 0.0 collective-permute-done.13.refs_1_
  113.4 4.6 %collective-permute-start.16 = (f32[192,384]{1,0:T(8,128)S(1)}, f32[192,384]{1,0:T(8,128)S(1)}, u32[]{:S(2)}, u32[]{:S(2)}) collective-permute-start(f32[192,384]{1,0:T(8,128)S(1)} %collective-permute-done.13.refs_1_), channel_id=1, source_target_pairs={{0,480},{32,0},{64,32},{96,64},{128,96},{160,128},{192,160},{224,1... | collective-permute-start | bytes 884744 | tf_op jit(solution)/shard_map/ppermute | solution.py:172
  118.0 0.0 collective-permute-done.12.refs_0_
  118.0 1.9 %collective-permute-start.15 = (f32[192,384]{1,0:T(8,128)S(1)}, f32[192,384]{1,0:T(8,128)S(1)}, u32[]{:S(2)}, u32[]{:S(2)}) collective-permute-start(f32[192,384]{1,0:T(8,128)S(1)} %collective-permute-done.12.refs_0_), channel_id=1, source_target_pairs={{0,32},{32,64},{64,96},{96,128},{128,160},{160,192},{192,224},{224... | collective-permute-start | bytes 884744 | tf_op jit(solution)/shard_map/ppermute | solution.py:172
  119.9 3.4 %collective-permute-done.16.refs_3_ = f32[192,384]{1,0:T(8,128)S(1)} collective-permute-done((f32[192,384]{1,0:T(8,128)S(1)}, f32[192,384]{1,0:T(8,128)S(1)}, u32[]{:S(2)}, u32[]{:S(2)}) %collective-permute-start.16) | collective-permute-done | bytes 294944 | tf_op jit(solution)/shard_map/ppermute | solution.py:172
  123.3 5.0 %collective-permute-done.15.refs_2_ = f32[192,384]{1,0:T(8,128)S(1)} collective-permute-done((f32[192,384]{1,0:T(8,128)S(1)}, f32[192,384]{1,0:T(8,128)S(1)}, u32[]{:S(2)}, u32[]{:S(2)}) %collective-permute-start.15) | collective-permute-done | bytes 294944 | tf_op jit(solution)/shard_map/ppermute | solution.py:172
  128.4 2.1 %shard_map.57 = (f32[192,384]{1,0:T(8,128)S(1)}, f32[192,384]{1,0:T(8,128)S(1)}) custom-call(s32[3]{0:T(128)S(1)} %pad_add_fusion.place, f32[4,2,576,128]{3,2,1,0:T(8,128)S(1)} %bitcast.11, f32[4,2,576,128]{3,2,1,0:T(8,128)S(1)} %collective-permute-done.11.other, f32[192,384]{1,0:T(8,128)S(1)} %collective-permute-done.12.refs_0_, ...), custom_call_target="tpu_custom_call" | custom-call | flops 339738624 | bytes 1048576 | tf_op jit(solution)/shard_map/pallas_call | solution.py:222
  130.5 1.9 %collective-permute-start.19 = (f32[192,384]{1,0:T(8,128)S(1)}, f32[192,384]{1,0:T(8,128)S(1)}, u32[]{:S(2)}, u32[]{:S(2)}) collective-permute-start(f32[192,384]{1,0:T(8,128)S(1)} %collective-permute-done.16.refs_3_), channel_id=1, source_target_pairs={{0,481},{1,480},{32,1},{33,0},{64,33},{65,32},{96,65},{97,64},{128... | collective-permute-start | bytes 884744 | tf_op jit(solution)/shard_map/ppermute | solution.py:230
  132.4 3.3 %collective-permute-start.18 = (f32[192,384]{1,0:T(8,128)S(1)}, f32[192,384]{1,0:T(8,128)S(1)}, u32[]{:S(2)}, u32[]{:S(2)}) collective-permute-start(f32[192,384]{1,0:T(8,128)S(1)} %collective-permute-done.15.refs_2_), channel_id=1, source_target_pairs={{0,32},{32,64},{64,96},{96,128},{128,160},{160,192},{192,224},{224... | collective-permute-start | bytes 884744 | tf_op jit(solution)/shard_map/ppermute | solution.py:172
  135.8 3.1 %collective-permute-start.17 = (f32[192,384]{1,0:T(8,128)S(1)}, f32[192,384]{1,0:T(8,128)S(1)}, u32[]{:S(2)}, u32[]{:S(2)}) collective-permute-start(f32[192,384]{1,0:T(8,128)S(1)} %get-tuple-element.20), channel_id=1, source_target_pairs={{0,1},{1,0},{2,3},{3,2},{4,5},{5,4},{6,7},{7,6},{8,9},{9,8},{10,11... | collective-permute-start | bytes 884744 | tf_op jit(solution)/shard_map/ppermute | solution.py:172
  138.9 0.8 collective-permute-done.19.right_other
  139.7 2.2 %collective-permute-done.18.right_own = f32[192,384]{1,0:T(8,128)S(1)} collective-permute-done((f32[192,384]{1,0:T(8,128)S(1)}, f32[192,384]{1,0:T(8,128)S(1)}, u32[]{:S(2)}, u32[]{:S(2)}) %collective-permute-start.18) | collective-permute-done | bytes 294944 | tf_op jit(solution)/shard_map/ppermute | solution.py:172
  141.9 5.5 %collective-permute-done.17.came = f32[192,384]{1,0:T(8,128)S(1)} collective-permute-done((f32[192,384]{1,0:T(8,128)S(1)}, f32[192,384]{1,0:T(8,128)S(1)}, u32[]{:S(2)}, u32[]{:S(2)}) %collective-permute-start.17) | collective-permute-done | bytes 294944 | tf_op jit(solution)/shard_map/ppermute | solution.py:172
  147.4 1.8 %shard_map.58 = f32[192,384]{1,0:T(8,128)} custom-call(s32[3]{0:T(128)S(1)} %pad_add_fusion.place, s32[3,3]{1,0:T(4,128)S(1)} %copy-done.18, f32[192,384]{1,0:T(8,128)S(1)} %get-tuple-element.19.own, f32[192,384]{1,0:T(8,128)S(1)} %collective-permute-done.17.came, f32[576,128]{1,0:T(8,128)S(1)} %select_bitcast_fusion.left_own, ...), custom_call_target="tpu_custom_call" | custom-call | flops 169869312 | bytes 1048576 | tf_op jit(solution)/shard_map/pallas_call | solution.py:231
  (24 shorter events, 0.0 us)
Async XLA Ops:
  6.5 75.2 %all-gather.3.cloned.1.call-start = ((), (), s32[]{:S(2)}) async-start(), calls=%async_computation | async-start | bytes 2949120 | tf_op jit(solution)/shard_map/all_gather | solution.py:194
  6.6 1.1 copy-start.2
  7.7 1.1 copy-start.3
  8.7 0.7 copy-start.16
  9.4 0.7 copy-start.17
  10.8 9.6 %collective-permute-start = (f32[576,128]{1,0:T(8,128)S(1)}, f32[576,128]{1,0:T(8,128)S(1)}, u32[]{:S(2)}, u32[]{:S(2)}) collective-permute-start(f32[576,128]{1,0:T(8,128)S(1)} %get-tuple-element.14), channel_id=1, source_target_pairs={{0,4},{2,6},{4,0},{6,2},{8,12},{10,14},{12,8},{14,10},{16,20},{18,... | collective-permute-start | bytes 884744 | tf_op jit(solution)/shard_map/ppermute | solution.py:192
  21.3 18.4 %collective-permute-start.6 = (f32[192,384]{1,0:T(8,128)S(1)}, f32[192,384]{1,0:T(8,128)S(1)}, u32[]{:S(2)}, u32[]{:S(2)}) collective-permute-start(f32[192,384]{1,0:T(8,128)S(1)} %get-tuple-element.15.refs_0_), channel_id=1, source_target_pairs={{0,480},{32,0},{64,32},{96,64},{128,96},{160,128},{192,160},{224,1... | collective-permute-start | bytes 884744 | tf_op jit(solution)/shard_map/ppermute | solution.py:172
  34.9 10.1 %collective-permute-start.1 = (f32[192,384]{1,0:T(8,128)S(1)}, f32[192,384]{1,0:T(8,128)S(1)}, u32[]{:S(2)}, u32[]{:S(2)}) collective-permute-start(f32[192,384]{1,0:T(8,128)S(1)} %get-tuple-element.15.refs_0_), channel_id=1, source_target_pairs={{0,32},{32,64},{64,96},{96,128},{128,160},{160,192},{192,224},{224... | collective-permute-start | bytes 884744 | tf_op jit(solution)/shard_map/ppermute | solution.py:172
  39.7 9.0 %collective-permute-start.7 = (f32[192,384]{1,0:T(8,128)S(1)}, f32[192,384]{1,0:T(8,128)S(1)}, u32[]{:S(2)}, u32[]{:S(2)}) collective-permute-start(f32[192,384]{1,0:T(8,128)S(1)} %collective-permute-done.6.refs_2_), channel_id=1, source_target_pairs={{0,480},{32,0},{64,32},{96,64},{128,96},{160,128},{192,160},{224,1... | collective-permute-start | bytes 884744 | tf_op jit(solution)/shard_map/ppermute | solution.py:172
  45.0 9.1 %collective-permute-start.2 = (f32[192,384]{1,0:T(8,128)S(1)}, f32[192,384]{1,0:T(8,128)S(1)}, u32[]{:S(2)}, u32[]{:S(2)}) collective-permute-start(f32[192,384]{1,0:T(8,128)S(1)} %collective-permute-done.1.refs_1_), channel_id=1, source_target_pairs={{0,32},{32,64},{64,96},{96,128},{128,160},{160,192},{192,224},{224... | collective-permute-start | bytes 884744 | tf_op jit(solution)/shard_map/ppermute | solution.py:172
  48.6 9.1 %collective-permute-start.8 = (f32[192,384]{1,0:T(8,128)S(1)}, f32[192,384]{1,0:T(8,128)S(1)}, u32[]{:S(2)}, u32[]{:S(2)}) collective-permute-start(f32[192,384]{1,0:T(8,128)S(1)} %collective-permute-done.7.refs_4_), channel_id=1, source_target_pairs={{0,480},{32,0},{64,32},{96,64},{128,96},{160,128},{192,160},{224,1... | collective-permute-start | bytes 884744 | tf_op jit(solution)/shard_map/ppermute | solution.py:172
  54.1 9.8 %collective-permute-start.3 = (f32[192,384]{1,0:T(8,128)S(1)}, f32[192,384]{1,0:T(8,128)S(1)}, u32[]{:S(2)}, u32[]{:S(2)}) collective-permute-start(f32[192,384]{1,0:T(8,128)S(1)} %collective-permute-done.2.refs_3_), channel_id=1, source_target_pairs={{0,32},{32,64},{64,96},{96,128},{128,160},{160,192},{192,224},{224... | collective-permute-start | bytes 884744 | tf_op jit(solution)/shard_map/ppermute | solution.py:172
  56.0 0.7 copy-start.4
  57.7 9.1 %collective-permute-start.9 = (f32[192,384]{1,0:T(8,128)S(1)}, f32[192,384]{1,0:T(8,128)S(1)}, u32[]{:S(2)}, u32[]{:S(2)}) collective-permute-start(f32[192,384]{1,0:T(8,128)S(1)} %collective-permute-done.8.refs_6_), channel_id=1, source_target_pairs={{0,480},{32,0},{64,32},{96,64},{128,96},{160,128},{192,160},{224,1... | collective-permute-start | bytes 884744 | tf_op jit(solution)/shard_map/ppermute | solution.py:172
  63.2 0.7 copy-start.6
  63.9 9.1 %collective-permute-start.4 = (f32[192,384]{1,0:T(8,128)S(1)}, f32[192,384]{1,0:T(8,128)S(1)}, u32[]{:S(2)}, u32[]{:S(2)}) collective-permute-start(f32[192,384]{1,0:T(8,128)S(1)} %collective-permute-done.3.refs_5_), channel_id=1, source_target_pairs={{0,32},{32,64},{64,96},{96,128},{128,160},{160,192},{192,224},{224... | collective-permute-start | bytes 884744 | tf_op jit(solution)/shard_map/ppermute | solution.py:172
  65.8 0.7 copy-start.8
  66.8 9.1 %collective-permute-start.10 = (f32[192,384]{1,0:T(8,128)S(1)}, f32[192,384]{1,0:T(8,128)S(1)}, u32[]{:S(2)}, u32[]{:S(2)}) collective-permute-start(f32[192,384]{1,0:T(8,128)S(1)} %collective-permute-done.9.refs_8_), channel_id=1, source_target_pairs={{0,480},{32,0},{64,32},{96,64},{128,96},{160,128},{192,160},{224,1... | collective-permute-start | bytes 884744 | tf_op jit(solution)/shard_map/ppermute | solution.py:172
  72.2 0.7 copy-start.10
  73.0 8.8 %collective-permute-start.5 = (f32[192,384]{1,0:T(8,128)S(1)}, f32[192,384]{1,0:T(8,128)}, u32[]{:S(2)}, u32[]{:S(2)}) collective-permute-start(f32[192,384]{1,0:T(8,128)S(1)} %collective-permute-done.4.refs_7_), channel_id=1, source_target_pairs={{0,32},{32,64},{64,96},{96,128},{128,160},{160,192},{192,224},{224... | collective-permute-start | bytes 884744 | tf_op jit(solution)/shard_map/ppermute | solution.py:172
  74.9 0.7 copy-start.12
  75.9 5.9 %copy-start.14 = (f32[192,384]{1,0:T(8,128)}, f32[192,384]{1,0:T(8,128)S(1)}, u32[]{:S(2)}) copy-start(f32[192,384]{1,0:T(8,128)S(1)} %collective-permute-done.10.refs_10_) | copy-start | bytes 884740
  81.7 12.6 %collective-permute-start.11 = (f32[4,2,576,128]{3,2,1,0:T(8,128)}, f32[4,2,576,128]{3,2,1,0:T(8,128)S(1)}, u32[]{:S(2)}, u32[]{:S(2)}) collective-permute-start(f32[4,2,576,128]{3,2,1,0:T(8,128)} %bitcast.8), channel_id=1, source_target_pairs={{0,2},{2,0},{4,6},{6,4},{8,10},{10,8},{12,14},{14,12},{16,18},{18,... | collective-permute-start | bytes 7077896 | tf_op jit(solution)/shard_map/ppermute | solution.py:221
  90.0 23.3 %collective-permute-start.13 = (f32[192,384]{1,0:T(8,128)}, f32[192,384]{1,0:T(8,128)S(1)}, u32[]{:S(2)}, u32[]{:S(2)}) collective-permute-start(f32[192,384]{1,0:T(8,128)} %copy-done.14), channel_id=1, source_target_pairs={{0,480},{32,0},{64,32},{96,64},{128,96},{160,128},{192,160},{224,1... | collective-permute-start | bytes 884744 | tf_op jit(solution)/shard_map/ppermute | solution.py:172
  95.3 18.1 %collective-permute-start.14 = (f32[576,128]{1,0:T(8,128)S(1)}, f32[576,128]{1,0:T(8,128)S(1)}, u32[]{:S(2)}, u32[]{:S(2)}) collective-permute-start(f32[576,128]{1,0:T(8,128)S(1)} %select_bitcast_fusion.left_own), channel_id=1, source_target_pairs={{0,1},{1,0},{2,3},{3,2},{4,5},{5,4},{6,7},{7,6},{8,9},{9,8},{10,11... | collective-permute-start | bytes 884744 | tf_op jit(solution)/shard_map/ppermute | solution.py:172
  98.4 19.5 %collective-permute-start.12 = (f32[192,384]{1,0:T(8,128)}, f32[192,384]{1,0:T(8,128)S(1)}, u32[]{:S(2)}, u32[]{:S(2)}) collective-permute-start(f32[192,384]{1,0:T(8,128)} %collective-permute-done.5.refs_9_), channel_id=1, source_target_pairs={{0,32},{32,64},{64,96},{96,128},{128,160},{160,192},{192,224},{224... | collective-permute-start | bytes 884744 | tf_op jit(solution)/shard_map/ppermute | solution.py:172
  100.4 1.7 %copy-start = (f32[8,576,128]{2,1,0:T(8,128)S(1)}, f32[8,576,128]{2,1,0:T(8,128)}, u32[]{:S(2)}) copy-start(f32[8,576,128]{2,1,0:T(8,128)} %all-gather.3.cloned.1.call-done) | copy-start | bytes 7077892
  102.0 1.0 copy-start.5
  103.0 1.0 copy-start.7
  104.0 1.0 copy-start.9
  104.9 1.0 copy-start.11
  105.9 1.0 copy-start.13
  106.8 1.0 copy-start.15
  107.8 20.6 %copy-start.1 = (f32[8,576,128]{2,1,0:T(8,128)S(1)}, f32[8,576,128]{2,1,0:T(8,128)}, u32[]{:S(2)}) copy-start(f32[8,576,128]{2,1,0:T(8,128)} %all-gather.3.cloned.1.call-done) | copy-start | bytes 7077892
  113.3 34.0 %copy-start.18 = (s32[3,3]{1,0:T(4,128)S(1)}, s32[3,3]{1,0:T(4,128)}, u32[]{:S(2)}) copy-start(s32[3,3]{1,0:T(4,128)} %keep.1) | copy-start | bytes 112
  113.4 9.9 %collective-permute-start.16 = (f32[192,384]{1,0:T(8,128)S(1)}, f32[192,384]{1,0:T(8,128)S(1)}, u32[]{:S(2)}, u32[]{:S(2)}) collective-permute-start(f32[192,384]{1,0:T(8,128)S(1)} %collective-permute-done.13.refs_1_), channel_id=1, source_target_pairs={{0,480},{32,0},{64,32},{96,64},{128,96},{160,128},{192,160},{224,1... | collective-permute-start | bytes 884744 | tf_op jit(solution)/shard_map/ppermute | solution.py:172
  118.0 10.4 %collective-permute-start.15 = (f32[192,384]{1,0:T(8,128)S(1)}, f32[192,384]{1,0:T(8,128)S(1)}, u32[]{:S(2)}, u32[]{:S(2)}) collective-permute-start(f32[192,384]{1,0:T(8,128)S(1)} %collective-permute-done.12.refs_0_), channel_id=1, source_target_pairs={{0,32},{32,64},{64,96},{96,128},{128,160},{160,192},{192,224},{224... | collective-permute-start | bytes 884744 | tf_op jit(solution)/shard_map/ppermute | solution.py:172
  130.5 9.2 %collective-permute-start.19 = (f32[192,384]{1,0:T(8,128)S(1)}, f32[192,384]{1,0:T(8,128)S(1)}, u32[]{:S(2)}, u32[]{:S(2)}) collective-permute-start(f32[192,384]{1,0:T(8,128)S(1)} %collective-permute-done.16.refs_3_), channel_id=1, source_target_pairs={{0,481},{1,480},{32,1},{33,0},{64,33},{65,32},{96,65},{97,64},{128... | collective-permute-start | bytes 884744 | tf_op jit(solution)/shard_map/ppermute | solution.py:230
  132.4 9.5 %collective-permute-start.18 = (f32[192,384]{1,0:T(8,128)S(1)}, f32[192,384]{1,0:T(8,128)S(1)}, u32[]{:S(2)}, u32[]{:S(2)}) collective-permute-start(f32[192,384]{1,0:T(8,128)S(1)} %collective-permute-done.15.refs_2_), channel_id=1, source_target_pairs={{0,32},{32,64},{64,96},{96,128},{128,160},{160,192},{192,224},{224... | collective-permute-start | bytes 884744 | tf_op jit(solution)/shard_map/ppermute | solution.py:172
  135.8 11.6 %collective-permute-start.17 = (f32[192,384]{1,0:T(8,128)S(1)}, f32[192,384]{1,0:T(8,128)S(1)}, u32[]{:S(2)}, u32[]{:S(2)}) collective-permute-start(f32[192,384]{1,0:T(8,128)S(1)} %get-tuple-element.20), channel_id=1, source_target_pairs={{0,1},{1,0},{2,3},{3,2},{4,5},{5,4},{6,7},{7,6},{8,9},{9,8},{10,11... | collective-permute-start | bytes 884744 | tf_op jit(solution)/shard_map/ppermute | solution.py:172
Sparse Core Ops, SparseCore 0:
  21.4 48.5 all-gather.2

commit v3 on v2

v3 whole, which is shorter than its diff:
```python
import functools

import jax
import jax.numpy as jnp
from jax import lax
from jax.experimental import pallas as pl
from jax.experimental.pallas import tpu as pltpu
from jax.sharding import PartitionSpec as P

BLK = 128
HALF = 64
TILE = 3 * BLK
PART = TILE // 2
F32 = jnp.float32
BF16 = jnp.bfloat16
VMEM = pl.BlockSpec(memory_space=pltpu.VMEM)
SMEM = pl.BlockSpec(memory_space=pltpu.SMEM)
ANY = pl.BlockSpec(memory_space=pl.ANY)
LIMIT = 20 * 2**20


def call(kernel, out_shapes, in_specs, scratch=(), flops=0, nbytes=0):
    return pl.pallas_call(
        kernel,
        out_shape=out_shapes,
        in_specs=in_specs,
        out_specs=jax.tree.map(lambda _: VMEM, out_shapes),
        scratch_shapes=scratch,
        compiler_params=pltpu.CompilerParams(vmem_limit_bytes=LIMIT),
        cost_estimate=pl.CostEstimate(flops=flops, bytes_accessed=nbytes, transcendentals=0),
    )


def swap_halves(value):
    return pltpu.roll(value, HALF, 1)


def low_lanes(shape):
    return lax.broadcasted_iota(jnp.int32, shape, 1) < HALF


def fetch(pairs, sems):
    copies = [pltpu.make_async_copy(src, dst, sems.at[i]) for i, (src, dst) in enumerate(pairs)]
    for copy in copies:
        copy.start()
    return copies


def masked(values, mask, p, q, rows=slice(0, BLK)):
    block = values[p * BLK + rows.start : p * BLK + rows.stop, q * BLK : (q + 1) * BLK]
    return block * mask[p : p + 1, q : q + 1].astype(F32)


def prep_kernel(place, lm_in, rm_in, left_in, right_in, left_out, right_out, lm, rm, left, right, sems):
    z, col, layer = place[0], place[1], place[2]
    for copy in fetch(((rm_in, rm), (right_in, right), (lm_in, lm), (left_in, left)), sems):
        copy.wait()
    far = lax.rem(z + 8, 16) == col

    def right_side(outer, near):
        rows = slice(near * HALF, (near + 1) * HALF)
        for q in range(3):
            lanes = slice(q * BLK, (q + 1) * BLK)
            right_out[:BLK, lanes] = masked(right, rm, outer, q)
            right_out[BLK:, lanes] = masked(right, rm, 1, q, rows)

    def left_side(outer, near):
        for p in range(3):
            left_out[p * BLK : (p + 1) * BLK, :] = masked(left, lm, p, outer)
        middle = jnp.concatenate([masked(left, lm, p, 1) for p in range(3)], 0)
        top, bottom = middle[:PART], middle[PART:]
        keep_low = low_lanes((PART, BLK))
        if near == 0:
            left_out[TILE:, :] = jnp.where(keep_low, top, swap_halves(bottom))
        else:
            left_out[TILE:, :] = jnp.where(keep_low, swap_halves(top), bottom)

    def left_far(outer, near):
        for q in range(3):
            start = q * PART
            end = masked(left, lm, outer, q)
            mid = masked(left, lm, 1, q, slice(near * HALF, (near + 1) * HALF))
            left_out[start : start + PART, :] = jnp.concatenate([end, mid] if near == 0 else [mid, end], 0)

    for side in (0, 1):

        @pl.when(layer == side)
        def _(outer=2 * side, near=side):
            right_side(outer, near)
            pl.when(far)(lambda: left_far(outer, near))
            pl.when(jnp.logical_not(far))(lambda: left_side(outer, near))


def split(value):
    high = value.astype(BF16)
    return high, (value - high.astype(F32)).astype(BF16)


def triple(left, right):
    (lh, ll), (rh, rl) = left, right
    dot = functools.partial(jnp.dot, preferred_element_type=F32)
    return dot(lh, rh) + (dot(lh, rl) + dot(ll, rh))


def join_left(one, two):
    m1, m2 = one[TILE:], two[TILE:]
    keep_low = low_lanes((PART, BLK))
    top = jnp.where(keep_low, m1, swap_halves(m2))
    bottom = jnp.where(keep_low, swap_halves(m1), m2)
    return jnp.concatenate([one[:TILE], two[:TILE], jnp.concatenate([top, bottom], 0)], 1)


def join_right(one, two):
    return jnp.concatenate([one[:BLK], two[:BLK], one[BLK:], two[BLK:]], 0)


def panel_index(place, k):
    col = place[1]
    mine = lax.rem(k, 2) == lax.rem(col, 2)
    return mine, lax.rem(col // 4 - k // 4 + 4, 4), lax.bitwise_xor(lax.rem(k // 2, 2), lax.rem(col // 2, 2))


def fill_left(place, same, other, step, lh, ll, column):
    z = place[0]
    mine, y1, x1 = panel_index(place, lax.rem(z - step + 16, 16))
    _, y2, x2 = panel_index(place, lax.rem(z + step, 16))
    span = slice(column, column + TILE)

    def put(panel):
        one, two = panel[y1, x1], panel[y2, x2]
        if step == 0:
            two = jnp.zeros_like(two)
        lh[:, span], ll[:, span] = split(join_left(one, two))

    pl.when(mine)(lambda: put(same))
    pl.when(jnp.logical_not(mine))(lambda: put(other))


def fill_right(one, two, rh, rl, column):
    span = slice(column, column + TILE)
    rh[span, :], rl[span, :] = split(join_right(one, two))


def main_kernel(early, late, place, same_in, other_in, *refs):
    n = 2 * len(early) - 1
    rights_in, (total, far, late_h, late_l, same, other, rights, lh, ll, rh, rl, sems) = refs[:n], refs[n:]
    pairs = [(same_in, same), (other_in, other)] + [(rights_in[i], rights.at[i]) for i in range(n)]
    copies = fetch(pairs, sems)
    copies[0].wait()
    copies[1].wait()
    for number, step in enumerate(early):
        fill_left(place, same, other, step, lh, ll, number * TILE)
    for number, step in enumerate(early):
        if step == 0:
            copies[2].wait()
            one, two = rights[0], jnp.zeros((PART, TILE), F32)
        else:
            copies[2 * step + 1].wait()
            copies[2 * step + 2].wait()
            one, two = rights[2 * step - 1], rights[2 * step]
        fill_right(one, two, rh, rl, number * TILE)
    total[...] = triple((lh[...], ll[...]), (rh[...], rl[...]))
    for number, step in enumerate(late):
        fill_left(place, same, other, step, late_h, late_l, number * TILE)
    mine, y, x = panel_index(place, lax.rem(place[0] + 8, 16))

    @pl.when(mine)
    def _():
        far[...] = same[y, x]

    @pl.when(jnp.logical_not(mine))
    def _():
        far[...] = other[y, x]


def near_kernel(place, total, late_h, late_l, *refs):
    rights, (own, away, rh, rl) = refs[:-4], refs[-4:]
    for number in range(len(rights) // 2):
        fill_right(rights[2 * number][...], rights[2 * number + 1][...], rh, rl, number * TILE)
    value = total[...] + triple((late_h[...], late_l[...]), (rh[...], rl[...]))
    layer = place[2]

    @pl.when(layer == 0)
    def _():
        own[...] = value[:PART]
        away[...] = value[PART:]

    @pl.when(layer == 1)
    def _():
        own[...] = value[PART:]
        away[...] = value[:PART]


def last_kernel(place, keep, own, came, far, right_own, right_other, out):
    layer = place[2]
    first = layer == 0
    mine, other = right_own[...], right_other[...]
    low, high = jnp.where(first, mine, other), jnp.where(first, other, mine)
    right = jnp.concatenate([low, high[BLK:], high[:BLK]], 0)
    left = jnp.concatenate([far[:PART], far[PART : 2 * PART], far[2 * PART :]], 1)
    value = own[...] + came[...] + triple(split(left), split(right))
    row = lax.broadcasted_iota(jnp.int32, (PART, BLK), 0) + layer * PART
    centre = (row >= BLK) & (row < 2 * BLK)
    for q in range(3):
        lanes = slice(q * BLK, (q + 1) * BLK)
        ends = jnp.where(first, keep[0:1, q : q + 1], keep[2:3, q : q + 1]).astype(F32)
        scale = jnp.where(centre, keep[1:2, q : q + 1].astype(F32), ends)
        out[:, lanes] = value[:, lanes] * scale


def shift(value, axis, steps):
    count = lax.axis_size(axis)
    return lax.ppermute(value, axis, [(i, (i + steps) % count) for i in range(count)])


def after(value, *earlier):
    return lax.optimization_barrier((value, *earlier))[0]


def shards(left_values, left_mask, right_values, right_mask, keep_mask):
    count = lax.axis_size("row")
    cols = lax.axis_size("col")
    z, col, layer = lax.axis_index("row"), lax.axis_index("col"), lax.axis_index("layer")
    place = jnp.stack([z, col, layer]).astype(jnp.int32)
    packed = jax.ShapeDtypeStruct((TILE + PART, BLK), F32)
    half = jax.ShapeDtypeStruct((PART, TILE), F32)
    whole = jax.ShapeDtypeStruct((TILE, TILE), F32)
    mask = pltpu.VMEM((3, 3), jnp.int32)

    left, right = call(
        prep_kernel, (packed, half), [SMEM] + [ANY] * 4,
        [mask, mask, pltpu.VMEM((TILE, TILE), F32), pltpu.VMEM((TILE, TILE), F32), pltpu.SemaphoreType.DMA((4,))],
        nbytes=2**21,
    )(place, left_mask, right_mask, left_values, right_values)

    left_x = lax.ppermute(left, "col", [(i, i ^ 2) for i in range(cols)])
    pair = jnp.stack([left, left_x])
    pieces = [pair]

    reach = count // 2
    early, late = tuple(range(reach - 2)), (reach - 2, reach - 1)
    rights, behind, ahead = [right], right, right
    for step in range(1, reach):
        if step > 1:
            behind, ahead = after(behind, rights[2 * step - 4]), after(ahead, behind)
        behind, ahead = shift(behind, "row", 1), shift(ahead, "row", -1)
        rights += [behind, ahead]
        if step <= 3:
            pair = after(pair, behind)
            pieces.append(lax.ppermute(pair, "col", [(i, (i + 4 * step) % cols) for i in range(cols)]))
        if step == reach - 3:
            same = after(jnp.stack(pieces), behind)
            other = lax.ppermute(same, "col", [(i, i ^ 1) for i in range(cols)])

    n = 2 * len(early) - 1
    panel = pltpu.VMEM((4, 2, TILE + PART, BLK), F32)
    part = jax.ShapeDtypeStruct((TILE, len(late) * TILE), BF16)
    lefts, downs = pltpu.VMEM((TILE, len(early) * TILE), BF16), pltpu.VMEM((len(early) * TILE, TILE), BF16)
    total, far, late_h, late_l = call(
        functools.partial(main_kernel, early, late), (whole, packed, part, part), [SMEM] + [ANY] * (2 + n),
        [panel, panel, pltpu.VMEM((n, PART, TILE), F32), lefts, lefts, downs, downs, pltpu.SemaphoreType.DMA((2 + n,))],
        flops=6 * TILE**3 * len(early), nbytes=10 * 2**20,
    )(place, same, other, *rights[:n])
    downs = pltpu.VMEM((len(late) * TILE, TILE), BF16)
    own, away = call(
        near_kernel, (half, half), [SMEM] + [VMEM] * (3 + 2 * len(late)), [downs, downs],
        flops=6 * TILE**3 * len(late), nbytes=2**21,
    )(place, total, late_h, late_l, *rights[n:])
    came = shift(away, "layer", 1)
    behind, ahead = after(behind, away), after(ahead, away)
    far_own = shift(behind, "row", 1)
    cross = [(z0 * 2 + l0, (z0 - 1) % count * 2 + 1 - l0) for z0 in range(count) for l0 in range(2)]
    far_other = lax.ppermute(ahead, ("row", "layer"), cross)
    return call(last_kernel, half, [SMEM] + [VMEM] * 6, flops=6 * PART * TILE * TILE, nbytes=2**20)(
        place, keep_mask, own, came, far, far_own, far_other
    )


def solution(mesh):
    specs = (P("row", "col"),) * 5
    return jax.shard_map(shards, mesh=mesh, in_specs=specs, out_specs=P(("row", "layer"), "col"), check_vma=False)
```

time: 157 us -> 140 us (0.89)
  the two profiles are of different devices: /device:TPU:1 before, /device:TPU:6 now
where the time goes in v3:
time: 140 us; the launch traced here: 139 us
  starting transfers between devices  78.1 us (56%)
  waiting for transfers between devices  46 us (33%)
  Pallas kernels  11.2 us (8%)
  local copies, waits for them, and re-layouts  3.5 us (2%)
    ppermute x16, starting transfers between devices, shift(): lax.ppermute(value, axis, [(i, (i + steps) % count) for i in range(count)])  55.5 us
    ppermute x16, waiting for transfers between devices, shift(): lax.ppermute(value, axis, [(i, (i + steps) % count) for i in range(count)])  40.7 us
    ppermute x3, starting transfers between devices, shards(): lax.ppermute(pair, 'col', [(i, (i + 4 * step) % cols) for i in range(cols)])  11.6 us
    pallas_call x1, Pallas kernels, shards(): call(functools.partial(main_kernel, early, late), (whole, packed, part, p...  6.6 us
    ppermute x1, starting transfers between devices, shards(): far_other = lax.ppermute(ahead, ('row', 'layer'), cross)  5.79 us
    ppermute x3, waiting for transfers between devices, shards(): lax.ppermute(pair, 'col', [(i, (i + 4 * step) % cols) for i in range(cols)])  5.32 us
    unnamed x10, local copies, waits for them, and re-layouts  3.5 us
    ppermute x1, starting transfers between devices, shards(): left_x = lax.ppermute(left, 'col', [(i, i ^ 2) for i in range(cols)])  3.31 us
  transfers between devices with their start and end apart: 22, of which 11 were waited for; matrix products, arithmetic and copies ran while one was open for 0% of the time, Pallas kernels for 5%

profile of v3, /device:TPU:6, one launch (start us, length us, event | category | flops | bytes accessed | tf_op | source)
XLA Modules:
  0.0 139.5 jit_solution(4544801046015793368)
XLA Ops:
  0.0 0.1 pad_add_fusion.place
  0.1 0.0 copy-start
  0.1 1.1 copy-done
  1.1 0.0 copy-start.1
  1.1 1.1 copy-done.1
  2.2 0.0 copy-start.2
  2.2 0.7 copy-done.2
  2.9 0.0 copy-start.3
  2.9 0.7 copy-done.3
  3.6 1.1 shard_map.55
  4.7 3.8 %collective-permute-start.1 = (f32[192,384]{1,0:T(8,128)S(1)}, f32[192,384]{1,0:T(8,128)S(1)}, u32[]{:S(2)}, u32[]{:S(2)}) collective-permute-start(f32[192,384]{1,0:T(8,128)S(1)} %get-tuple-element.32.refs_0_), channel_id=1, source_target_pairs={{0,32},{32,64},{64,96},{96,128},{128,160},{160,192},{192,224},{224... | collective-permute-start | bytes 884744 | tf_op jit(solution)/shard_map/ppermute | solution.py:213
  8.6 9.5 %collective-permute-start.5 = (f32[192,384]{1,0:T(8,128)S(1)}, f32[192,384]{1,0:T(8,128)S(1)}, u32[]{:S(2)}, u32[]{:S(2)}) collective-permute-start(f32[192,384]{1,0:T(8,128)S(1)} %get-tuple-element.32.refs_0_), channel_id=1, source_target_pairs={{0,480},{32,0},{64,32},{96,64},{128,96},{160,128},{192,160},{224,1... | collective-permute-start | bytes 884744 | tf_op jit(solution)/shard_map/ppermute | solution.py:213
  18.1 5.1 %collective-permute-done.1.refs_1_ = f32[192,384]{1,0:T(8,128)S(1)} collective-permute-done((f32[192,384]{1,0:T(8,128)S(1)}, f32[192,384]{1,0:T(8,128)S(1)}, u32[]{:S(2)}, u32[]{:S(2)}) %collective-permute-start.1) | collective-permute-done | bytes 294944 | tf_op jit(solution)/shard_map/ppermute | solution.py:213
  23.1 1.9 %collective-permute-start.3 = (f32[192,384]{1,0:T(8,128)S(1)}, f32[192,384]{1,0:T(8,128)S(1)}, u32[]{:S(2)}, u32[]{:S(2)}) collective-permute-start(f32[192,384]{1,0:T(8,128)S(1)} %collective-permute-done.1.refs_1_), channel_id=1, source_target_pairs={{0,32},{32,64},{64,96},{96,128},{128,160},{160,192},{192,224},{224... | collective-permute-start | bytes 884744 | tf_op jit(solution)/shard_map/ppermute | solution.py:213
  25.0 3.3 %collective-permute-start = (f32[576,128]{1,0:T(8,128)S(1)}, f32[576,128]{1,0:T(8,128)S(1)}, u32[]{:S(2)}, u32[]{:S(2)}) collective-permute-start(f32[576,128]{1,0:T(8,128)S(1)} %get-tuple-element.31), channel_id=1, source_target_pairs={{0,4},{2,6},{4,0},{6,2},{8,12},{10,14},{12,8},{14,10},{16,20},{18,... | collective-permute-start | bytes 884744 | tf_op jit(solution)/shard_map/ppermute | solution.py:236
  28.4 0.0 collective-permute-done.5.refs_2_
  28.4 6.0 %collective-permute-done.3.refs_3_ = f32[192,384]{1,0:T(8,128)S(1)} collective-permute-done((f32[192,384]{1,0:T(8,128)S(1)}, f32[192,384]{1,0:T(8,128)S(1)}, u32[]{:S(2)}, u32[]{:S(2)}) %collective-permute-start.3) | collective-permute-done | bytes 294944 | tf_op jit(solution)/shard_map/ppermute | solution.py:213
  34.4 1.9 %collective-permute-start.6 = (f32[192,384]{1,0:T(8,128)S(1)}, f32[192,384]{1,0:T(8,128)S(1)}, u32[]{:S(2)}, u32[]{:S(2)}) collective-permute-start(f32[192,384]{1,0:T(8,128)S(1)} %collective-permute-done.3.refs_3_), channel_id=1, source_target_pairs={{0,32},{32,64},{64,96},{96,128},{128,160},{160,192},{192,224},{224... | collective-permute-start | bytes 884744 | tf_op jit(solution)/shard_map/ppermute | solution.py:213
  36.3 5.1 %collective-permute-start.8 = (f32[192,384]{1,0:T(8,128)S(1)}, f32[192,384]{1,0:T(8,128)S(1)}, u32[]{:S(2)}, u32[]{:S(2)}) collective-permute-start(f32[192,384]{1,0:T(8,128)S(1)} %collective-permute-done.5.refs_2_), channel_id=1, source_target_pairs={{0,480},{32,0},{64,32},{96,64},{128,96},{160,128},{192,160},{224,1... | collective-permute-start | bytes 884744 | tf_op jit(solution)/shard_map/ppermute | solution.py:213
  41.5 0.0 collective-permute-done
  41.5 0.1 fusion
  41.6 3.3 %collective-permute-start.2 = (f32[2,576,128]{2,1,0:T(8,128)S(1)}, f32[2,576,128]{2,1,0:T(8,128)S(1)}, u32[]{:S(2)}, u32[]{:S(2)}) collective-permute-start(f32[2,576,128]{2,1,0:T(8,128)S(1)} %get-tuple-element.37), channel_id=1, source_target_pairs={{0,8},{2,10},{4,12},{6,14},{8,16},{10,18},{12,20},{14,22},{16,24},... | collective-permute-start | bytes 1769480 | tf_op jit(solution)/shard_map/ppermute | solution.py:250
  44.9 5.0 %collective-permute-start.4 = (f32[2,576,128]{2,1,0:T(8,128)S(1)}, f32[2,576,128]{2,1,0:T(8,128)S(1)}, u32[]{:S(2)}, u32[]{:S(2)}) collective-permute-start(f32[2,576,128]{2,1,0:T(8,128)S(1)} %get-tuple-element.37), channel_id=1, source_target_pairs={{0,16},{2,18},{4,20},{6,22},{8,24},{10,26},{12,28},{14,30},{16,0},... | collective-permute-start | bytes 1769480 | tf_op jit(solution)/shard_map/ppermute | solution.py:250
  49.9 0.0 collective-permute-done.6.refs_5_
  49.9 3.3 %collective-permute-start.7 = (f32[2,576,128]{2,1,0:T(8,128)S(1)}, f32[2,576,128]{2,1,0:T(8,128)S(1)}, u32[]{:S(2)}, u32[]{:S(2)}) collective-permute-start(f32[2,576,128]{2,1,0:T(8,128)S(1)} %get-tuple-element.37), channel_id=1, source_target_pairs={{0,24},{2,26},{4,28},{6,30},{8,0},{10,2},{12,4},{14,6},{16,8},{18,... | collective-permute-start | bytes 1769480 | tf_op jit(solution)/shard_map/ppermute | solution.py:250
  53.2 0.0 collective-permute-done.8.refs_4_
  53.2 1.9 %collective-permute-start.10 = (f32[192,384]{1,0:T(8,128)S(1)}, f32[192,384]{1,0:T(8,128)S(1)}, u32[]{:S(2)}, u32[]{:S(2)}) collective-permute-start(f32[192,384]{1,0:T(8,128)S(1)} %collective-permute-done.8.refs_4_), channel_id=1, source_target_pairs={{0,480},{32,0},{64,32},{96,64},{128,96},{160,128},{192,160},{224,1... | collective-permute-start | bytes 884744 | tf_op jit(solution)/shard_map/ppermute | solution.py:213
  55.1 3.9 %collective-permute-start.9 = (f32[192,384]{1,0:T(8,128)S(1)}, f32[192,384]{1,0:T(8,128)S(1)}, u32[]{:S(2)}, u32[]{:S(2)}) collective-permute-start(f32[192,384]{1,0:T(8,128)S(1)} %collective-permute-done.6.refs_5_), channel_id=1, source_target_pairs={{0,32},{32,64},{64,96},{96,128},{128,160},{160,192},{192,224},{224... | collective-permute-start | bytes 884744 | tf_op jit(solution)/shard_map/ppermute | solution.py:213
  59.0 2.8 %collective-permute-done.10.refs_6_ = f32[192,384]{1,0:T(8,128)S(1)} collective-permute-done((f32[192,384]{1,0:T(8,128)S(1)}, f32[192,384]{1,0:T(8,128)S(1)}, u32[]{:S(2)}, u32[]{:S(2)}) %collective-permute-start.10) | collective-permute-done | bytes 294944 | tf_op jit(solution)/shard_map/ppermute | solution.py:213
  61.8 3.1 %collective-permute-done.9.refs_7_ = f32[192,384]{1,0:T(8,128)S(1)} collective-permute-done((f32[192,384]{1,0:T(8,128)S(1)}, f32[192,384]{1,0:T(8,128)S(1)}, u32[]{:S(2)}, u32[]{:S(2)}) %collective-permute-start.9) | collective-permute-done | bytes 294944 | tf_op jit(solution)/shard_map/ppermute | solution.py:213
  64.9 2.7 %collective-permute-start.11 = (f32[192,384]{1,0:T(8,128)S(1)}, f32[192,384]{1,0:T(8,128)S(1)}, u32[]{:S(2)}, u32[]{:S(2)}) collective-permute-start(f32[192,384]{1,0:T(8,128)S(1)} %collective-permute-done.9.refs_7_), channel_id=1, source_target_pairs={{0,32},{32,64},{64,96},{96,128},{128,160},{160,192},{192,224},{224... | collective-permute-start | bytes 884744 | tf_op jit(solution)/shard_map/ppermute | solution.py:213
  67.6 0.0 collective-permute-done.2
  67.6 3.9 %collective-permute-done.4 = f32[2,576,128]{2,1,0:T(8,128)S(1)} collective-permute-done((f32[2,576,128]{2,1,0:T(8,128)S(1)}, f32[2,576,128]{2,1,0:T(8,128)S(1)}, u32[]{:S(2)}, u32[]{:S(2)}) %collective-permute-start.4) | collective-permute-done | bytes 589856 | tf_op jit(solution)/shard_map/ppermute | solution.py:250
  71.6 1.4 collective-permute-done.7
  73.0 0.2 pad_maximum_fusion.same_in
  73.2 1.6 %collective-permute-done.11.refs_9_ = f32[192,384]{1,0:T(8,128)S(1)} collective-permute-done((f32[192,384]{1,0:T(8,128)S(1)}, f32[192,384]{1,0:T(8,128)S(1)}, u32[]{:S(2)}, u32[]{:S(2)}) %collective-permute-start.11) | collective-permute-done | bytes 294944 | tf_op jit(solution)/shard_map/ppermute | solution.py:213
  74.7 1.9 %collective-permute-start.12 = (f32[4,2,576,128]{3,2,1,0:T(8,128)S(1)}, f32[4,2,576,128]{3,2,1,0:T(8,128)S(1)}, u32[]{:S(2)}, u32[]{:S(2)}) collective-permute-start(f32[4,2,576,128]{3,2,1,0:T(8,128)S(1)} %pad_maximum_fusion.same_in), channel_id=1, source_target_pairs={{0,2},{2,0},{4,6},{6,4},{8,10},{10,8},{12,14},{14,12},{16,18},{18,... | collective-permute-start | bytes 7077896 | tf_op jit(solution)/shard_map/ppermute | solution.py:253
  76.7 1.9 %collective-permute-start.13 = (f32[192,384]{1,0:T(8,128)S(1)}, f32[192,384]{1,0:T(8,128)S(1)}, u32[]{:S(2)}, u32[]{:S(2)}) collective-permute-start(f32[192,384]{1,0:T(8,128)S(1)} %collective-permute-done.10.refs_6_), channel_id=1, source_target_pairs={{0,480},{32,0},{64,32},{96,64},{128,96},{160,128},{192,160},{224,1... | collective-permute-start | bytes 884744 | tf_op jit(solution)/shard_map/ppermute | solution.py:213
  78.6 9.4 %collective-permute-done.13.refs_8_ = f32[192,384]{1,0:T(8,128)S(1)} collective-permute-done((f32[192,384]{1,0:T(8,128)S(1)}, f32[192,384]{1,0:T(8,128)S(1)}, u32[]{:S(2)}, u32[]{:S(2)}) %collective-permute-start.13) | collective-permute-done | bytes 294944 | tf_op jit(solution)/shard_map/ppermute | solution.py:213
  88.0 3.4 %collective-permute-start.14 = (f32[192,384]{1,0:T(8,128)S(1)}, f32[192,384]{1,0:T(8,128)S(1)}, u32[]{:S(2)}, u32[]{:S(2)}) collective-permute-start(f32[192,384]{1,0:T(8,128)S(1)} %collective-permute-done.13.refs_8_), channel_id=1, source_target_pairs={{0,480},{32,0},{64,32},{96,64},{128,96},{160,128},{192,160},{224,1... | collective-permute-start | bytes 884744 | tf_op jit(solution)/shard_map/ppermute | solution.py:213
  91.4 2.4 %collective-permute-start.15 = (f32[192,384]{1,0:T(8,128)S(1)}, f32[192,384]{1,0:T(8,128)S(1)}, u32[]{:S(2)}, u32[]{:S(2)}) collective-permute-start(f32[192,384]{1,0:T(8,128)S(1)} %collective-permute-done.11.refs_9_), channel_id=1, source_target_pairs={{0,32},{32,64},{64,96},{96,128},{128,160},{160,192},{192,224},{224... | collective-permute-start | bytes 884744 | tf_op jit(solution)/shard_map/ppermute | solution.py:213
  93.8 4.7 %collective-permute-done.14.refs_10_ = f32[192,384]{1,0:T(8,128)S(1)} collective-permute-done((f32[192,384]{1,0:T(8,128)S(1)}, f32[192,384]{1,0:T(8,128)S(1)}, u32[]{:S(2)}, u32[]{:S(2)}) %collective-permute-start.14) | collective-permute-done | bytes 294944 | tf_op jit(solution)/shard_map/ppermute | solution.py:213
  98.5 4.8 %collective-permute-start.16 = (f32[192,384]{1,0:T(8,128)S(1)}, f32[192,384]{1,0:T(8,128)S(1)}, u32[]{:S(2)}, u32[]{:S(2)}) collective-permute-start(f32[192,384]{1,0:T(8,128)S(1)} %collective-permute-done.14.refs_10_), channel_id=1, source_target_pairs={{0,480},{32,0},{64,32},{96,64},{128,96},{160,128},{192,160},{224,1... | collective-permute-start | bytes 884744 | tf_op jit(solution)/shard_map/ppermute | solution.py:213
  103.3 0.0 collective-permute-done.15.refs_0_
  103.3 1.9 %collective-permute-start.17 = (f32[192,384]{1,0:T(8,128)S(1)}, f32[192,384]{1,0:T(8,128)S(1)}, u32[]{:S(2)}, u32[]{:S(2)}) collective-permute-start(f32[192,384]{1,0:T(8,128)S(1)} %collective-permute-done.15.refs_0_), channel_id=1, source_target_pairs={{0,32},{32,64},{64,96},{96,128},{128,160},{160,192},{192,224},{224... | collective-permute-start | bytes 884744 | tf_op jit(solution)/shard_map/ppermute | solution.py:213
  105.2 3.5 %collective-permute-done.16.refs_1_ = f32[192,384]{1,0:T(8,128)S(1)} collective-permute-done((f32[192,384]{1,0:T(8,128)S(1)}, f32[192,384]{1,0:T(8,128)S(1)}, u32[]{:S(2)}, u32[]{:S(2)}) %collective-permute-start.16) | collective-permute-done | bytes 294944 | tf_op jit(solution)/shard_map/ppermute | solution.py:213
  108.8 5.6 %collective-permute-start.18 = (f32[192,384]{1,0:T(8,128)S(1)}, f32[192,384]{1,0:T(8,128)S(1)}, u32[]{:S(2)}, u32[]{:S(2)}) collective-permute-start(f32[192,384]{1,0:T(8,128)S(1)} %collective-permute-done.16.refs_1_), channel_id=1, source_target_pairs={{0,480},{32,0},{64,32},{96,64},{128,96},{160,128},{192,160},{224,1... | collective-permute-start | bytes 884744 | tf_op jit(solution)/shard_map/ppermute | solution.py:213
  114.4 0.0 collective-permute-done.12.other_in
  114.4 6.6 %shard_map.56 = (f32[384,384]{1,0:T(8,128)S(1)}, f32[576,128]{1,0:T(8,128)S(1)}, bf16[384,768]{1,0:T(8,128)(2,1)S(1)}, bf16[384,768]{1,0:T(8,128)(2,1)S(1)}) custom-call(s32[3]{0:T(128)S(1)} %pad_add_fusion.place, f32[4,2,576,128]{3,2,1,0:T(8,128)S(1)} %pad_maximum_fusion.same_in, f32[4,2,576,128]{3,2,1,0:T(8,128)S(1)} %collective-permute-done.12.other_in, ...), custom_call_target="tpu_custom_call" | custom-call | flops 2038431744 | bytes 10485760 | tf_op jit(solution)/shard_map/pallas_call | solution.py:259
  121.0 0.0 copy-start.4
  121.0 0.0 collective-permute-done.17.refs_2_
  121.0 0.0 collective-permute-done.18.refs_3_
  121.0 1.7 %shard_map.57 = (f32[192,384]{1,0:T(8,128)S(1)}, f32[192,384]{1,0:T(8,128)S(1)}) custom-call(s32[3]{0:T(128)S(1)} %pad_add_fusion.place, f32[384,384]{1,0:T(8,128)S(1)} %get-tuple-element.45.total, bf16[384,768]{1,0:T(8,128)(2,1)S(1)} %get-tuple-element.46.late_h, bf16[384,768]{1,0:T(8,128)(2,1)S(1)} %get-tuple-element.47.late_l, ...), custom_call_target="tpu_custom_call" | custom-call | flops 679477248 | bytes 2097152 | tf_op jit(solution)/shard_map/pallas_call | solution.py:265
  122.7 2.7 %collective-permute-start.19 = (f32[192,384]{1,0:T(8,128)S(1)}, f32[192,384]{1,0:T(8,128)S(1)}, u32[]{:S(2)}, u32[]{:S(2)}) collective-permute-start(f32[192,384]{1,0:T(8,128)S(1)} %get-tuple-element.53), channel_id=1, source_target_pairs={{0,1},{1,0},{2,3},{3,2},{4,5},{5,4},{6,7},{7,6},{8,9},{9,8},{10,11... | collective-permute-start | bytes 884744 | tf_op jit(solution)/shard_map/ppermute | solution.py:213
  125.5 1.9 %collective-permute-start.20 = (f32[192,384]{1,0:T(8,128)S(1)}, f32[192,384]{1,0:T(8,128)S(1)}, u32[]{:S(2)}, u32[]{:S(2)}) collective-permute-start(f32[192,384]{1,0:T(8,128)S(1)} %collective-permute-done.17.refs_2_), channel_id=1, source_target_pairs={{0,32},{32,64},{64,96},{96,128},{128,160},{160,192},{192,224},{224... | collective-permute-start | bytes 884744 | tf_op jit(solution)/shard_map/ppermute | solution.py:213
  127.4 5.8 %collective-permute-start.21 = (f32[192,384]{1,0:T(8,128)S(1)}, f32[192,384]{1,0:T(8,128)S(1)}, u32[]{:S(2)}, u32[]{:S(2)}) collective-permute-start(f32[192,384]{1,0:T(8,128)S(1)} %collective-permute-done.18.refs_3_), channel_id=1, source_target_pairs={{0,481},{1,480},{32,1},{33,0},{64,33},{65,32},{96,65},{97,64},{128... | collective-permute-start | bytes 884744 | tf_op jit(solution)/shard_map/ppermute | solution.py:273
  133.2 4.5 %collective-permute-done.19.came = f32[192,384]{1,0:T(8,128)S(1)} collective-permute-done((f32[192,384]{1,0:T(8,128)S(1)}, f32[192,384]{1,0:T(8,128)S(1)}, u32[]{:S(2)}, u32[]{:S(2)}) %collective-permute-start.19) | collective-permute-done | bytes 294944 | tf_op jit(solution)/shard_map/ppermute | solution.py:213
  137.7 0.0 collective-permute-done.20.right_own
  137.7 0.0 collective-permute-done.21.right_other
  137.7 0.0 copy-done.4
  137.7 1.7 %shard_map.58 = f32[192,384]{1,0:T(8,128)} custom-call(s32[3]{0:T(128)S(1)} %pad_add_fusion.place, s32[3,3]{1,0:T(4,128)S(1)} %copy-done.4, f32[192,384]{1,0:T(8,128)S(1)} %get-tuple-element.52.own, f32[192,384]{1,0:T(8,128)S(1)} %collective-permute-done.19.came, f32[576,128]{1,0:T(8,128)S(1)} %get-tuple-element.54.far, ...), custom_call_target="tpu_custom_call" | custom-call | flops 169869312 | bytes 1048576 | tf_op jit(solution)/shard_map/pallas_call | solution.py:274
Async XLA Ops:
  0.1 1.1 copy-start
  1.1 1.1 copy-start.1
  2.2 0.7 copy-start.2
  2.9 0.7 copy-start.3
  4.7 18.4 %collective-permute-start.1 = (f32[192,384]{1,0:T(8,128)S(1)}, f32[192,384]{1,0:T(8,128)S(1)}, u32[]{:S(2)}, u32[]{:S(2)}) collective-permute-start(f32[192,384]{1,0:T(8,128)S(1)} %get-tuple-element.32.refs_0_), channel_id=1, source_target_pairs={{0,32},{32,64},{64,96},{96,128},{128,160},{160,192},{192,224},{224... | collective-permute-start | bytes 884744 | tf_op jit(solution)/shard_map/ppermute | solution.py:213
  8.6 19.8 %collective-permute-start.5 = (f32[192,384]{1,0:T(8,128)S(1)}, f32[192,384]{1,0:T(8,128)S(1)}, u32[]{:S(2)}, u32[]{:S(2)}) collective-permute-start(f32[192,384]{1,0:T(8,128)S(1)} %get-tuple-element.32.refs_0_), channel_id=1, source_target_pairs={{0,480},{32,0},{64,32},{96,64},{128,96},{160,128},{192,160},{224,1... | collective-permute-start | bytes 884744 | tf_op jit(solution)/shard_map/ppermute | solution.py:213
  23.1 11.3 %collective-permute-start.3 = (f32[192,384]{1,0:T(8,128)S(1)}, f32[192,384]{1,0:T(8,128)S(1)}, u32[]{:S(2)}, u32[]{:S(2)}) collective-permute-start(f32[192,384]{1,0:T(8,128)S(1)} %collective-permute-done.1.refs_1_), channel_id=1, source_target_pairs={{0,32},{32,64},{64,96},{96,128},{128,160},{160,192},{192,224},{224... | collective-permute-start | bytes 884744 | tf_op jit(solution)/shard_map/ppermute | solution.py:213
  25.0 16.4 %collective-permute-start = (f32[576,128]{1,0:T(8,128)S(1)}, f32[576,128]{1,0:T(8,128)S(1)}, u32[]{:S(2)}, u32[]{:S(2)}) collective-permute-start(f32[576,128]{1,0:T(8,128)S(1)} %get-tuple-element.31), channel_id=1, source_target_pairs={{0,4},{2,6},{4,0},{6,2},{8,12},{10,14},{12,8},{14,10},{16,20},{18,... | collective-permute-start | bytes 884744 | tf_op jit(solution)/shard_map/ppermute | solution.py:236
  34.4 15.5 %collective-permute-start.6 = (f32[192,384]{1,0:T(8,128)S(1)}, f32[192,384]{1,0:T(8,128)S(1)}, u32[]{:S(2)}, u32[]{:S(2)}) collective-permute-start(f32[192,384]{1,0:T(8,128)S(1)} %collective-permute-done.3.refs_3_), channel_id=1, source_target_pairs={{0,32},{32,64},{64,96},{96,128},{128,160},{160,192},{192,224},{224... | collective-permute-start | bytes 884744 | tf_op jit(solution)/shard_map/ppermute | solution.py:213
  36.3 16.8 %collective-permute-start.8 = (f32[192,384]{1,0:T(8,128)S(1)}, f32[192,384]{1,0:T(8,128)S(1)}, u32[]{:S(2)}, u32[]{:S(2)}) collective-permute-start(f32[192,384]{1,0:T(8,128)S(1)} %collective-permute-done.5.refs_2_), channel_id=1, source_target_pairs={{0,480},{32,0},{64,32},{96,64},{128,96},{160,128},{192,160},{224,1... | collective-permute-start | bytes 884744 | tf_op jit(solution)/shard_map/ppermute | solution.py:213
  41.6 26.1 %collective-permute-start.2 = (f32[2,576,128]{2,1,0:T(8,128)S(1)}, f32[2,576,128]{2,1,0:T(8,128)S(1)}, u32[]{:S(2)}, u32[]{:S(2)}) collective-permute-start(f32[2,576,128]{2,1,0:T(8,128)S(1)} %get-tuple-element.37), channel_id=1, source_target_pairs={{0,8},{2,10},{4,12},{6,14},{8,16},{10,18},{12,20},{14,22},{16,24},... | collective-permute-start | bytes 1769480 | tf_op jit(solution)/shard_map/ppermute | solution.py:250
  44.9 26.7 %collective-permute-start.4 = (f32[2,576,128]{2,1,0:T(8,128)S(1)}, f32[2,576,128]{2,1,0:T(8,128)S(1)}, u32[]{:S(2)}, u32[]{:S(2)}) collective-permute-start(f32[2,576,128]{2,1,0:T(8,128)S(1)} %get-tuple-element.37), channel_id=1, source_target_pairs={{0,16},{2,18},{4,20},{6,22},{8,24},{10,26},{12,28},{14,30},{16,0},... | collective-permute-start | bytes 1769480 | tf_op jit(solution)/shard_map/ppermute | solution.py:250
  49.9 23.1 %collective-permute-start.7 = (f32[2,576,128]{2,1,0:T(8,128)S(1)}, f32[2,576,128]{2,1,0:T(8,128)S(1)}, u32[]{:S(2)}, u32[]{:S(2)}) collective-permute-start(f32[2,576,128]{2,1,0:T(8,128)S(1)} %get-tuple-element.37), channel_id=1, source_target_pairs={{0,24},{2,26},{4,28},{6,30},{8,0},{10,2},{12,4},{14,6},{16,8},{18,... | collective-permute-start | bytes 1769480 | tf_op jit(solution)/shard_map/ppermute | solution.py:250
  53.2 8.6 %collective-permute-start.10 = (f32[192,384]{1,0:T(8,128)S(1)}, f32[192,384]{1,0:T(8,128)S(1)}, u32[]{:S(2)}, u32[]{:S(2)}) collective-permute-start(f32[192,384]{1,0:T(8,128)S(1)} %collective-permute-done.8.refs_4_), channel_id=1, source_target_pairs={{0,480},{32,0},{64,32},{96,64},{128,96},{160,128},{192,160},{224,1... | collective-permute-start | bytes 884744 | tf_op jit(solution)/shard_map/ppermute | solution.py:213
  55.1 9.8 %collective-permute-start.9 = (f32[192,384]{1,0:T(8,128)S(1)}, f32[192,384]{1,0:T(8,128)S(1)}, u32[]{:S(2)}, u32[]{:S(2)}) collective-permute-start(f32[192,384]{1,0:T(8,128)S(1)} %collective-permute-done.6.refs_5_), channel_id=1, source_target_pairs={{0,32},{32,64},{64,96},{96,128},{128,160},{160,192},{192,224},{224... | collective-permute-start | bytes 884744 | tf_op jit(solution)/shard_map/ppermute | solution.py:213
  64.9 9.8 %collective-permute-start.11 = (f32[192,384]{1,0:T(8,128)S(1)}, f32[192,384]{1,0:T(8,128)S(1)}, u32[]{:S(2)}, u32[]{:S(2)}) collective-permute-start(f32[192,384]{1,0:T(8,128)S(1)} %collective-permute-done.9.refs_7_), channel_id=1, source_target_pairs={{0,32},{32,64},{64,96},{96,128},{128,160},{160,192},{192,224},{224... | collective-permute-start | bytes 884744 | tf_op jit(solution)/shard_map/ppermute | solution.py:213
  74.7 39.6 %collective-permute-start.12 = (f32[4,2,576,128]{3,2,1,0:T(8,128)S(1)}, f32[4,2,576,128]{3,2,1,0:T(8,128)S(1)}, u32[]{:S(2)}, u32[]{:S(2)}) collective-permute-start(f32[4,2,576,128]{3,2,1,0:T(8,128)S(1)} %pad_maximum_fusion.same_in), channel_id=1, source_target_pairs={{0,2},{2,0},{4,6},{6,4},{8,10},{10,8},{12,14},{14,12},{16,18},{18,... | collective-permute-start | bytes 7077896 | tf_op jit(solution)/shard_map/ppermute | solution.py:253
  76.7 11.3 %collective-permute-start.13 = (f32[192,384]{1,0:T(8,128)S(1)}, f32[192,384]{1,0:T(8,128)S(1)}, u32[]{:S(2)}, u32[]{:S(2)}) collective-permute-start(f32[192,384]{1,0:T(8,128)S(1)} %collective-permute-done.10.refs_6_), channel_id=1, source_target_pairs={{0,480},{32,0},{64,32},{96,64},{128,96},{160,128},{192,160},{224,1... | collective-permute-start | bytes 884744 | tf_op jit(solution)/shard_map/ppermute | solution.py:213
  88.0 10.5 %collective-permute-start.14 = (f32[192,384]{1,0:T(8,128)S(1)}, f32[192,384]{1,0:T(8,128)S(1)}, u32[]{:S(2)}, u32[]{:S(2)}) collective-permute-start(f32[192,384]{1,0:T(8,128)S(1)} %collective-permute-done.13.refs_8_), channel_id=1, source_target_pairs={{0,480},{32,0},{64,32},{96,64},{128,96},{160,128},{192,160},{224,1... | collective-permute-start | bytes 884744 | tf_op jit(solution)/shard_map/ppermute | solution.py:213
  91.4 11.9 %collective-permute-start.15 = (f32[192,384]{1,0:T(8,128)S(1)}, f32[192,384]{1,0:T(8,128)S(1)}, u32[]{:S(2)}, u32[]{:S(2)}) collective-permute-start(f32[192,384]{1,0:T(8,128)S(1)} %collective-permute-done.11.refs_9_), channel_id=1, source_target_pairs={{0,32},{32,64},{64,96},{96,128},{128,160},{160,192},{192,224},{224... | collective-permute-start | bytes 884744 | tf_op jit(solution)/shard_map/ppermute | solution.py:213
  98.5 10.3 %collective-permute-start.16 = (f32[192,384]{1,0:T(8,128)S(1)}, f32[192,384]{1,0:T(8,128)S(1)}, u32[]{:S(2)}, u32[]{:S(2)}) collective-permute-start(f32[192,384]{1,0:T(8,128)S(1)} %collective-permute-done.14.refs_10_), channel_id=1, source_target_pairs={{0,480},{32,0},{64,32},{96,64},{128,96},{160,128},{192,160},{224,1... | collective-permute-start | bytes 884744 | tf_op jit(solution)/shard_map/ppermute | solution.py:213
  103.3 17.7 %collective-permute-start.17 = (f32[192,384]{1,0:T(8,128)S(1)}, f32[192,384]{1,0:T(8,128)S(1)}, u32[]{:S(2)}, u32[]{:S(2)}) collective-permute-start(f32[192,384]{1,0:T(8,128)S(1)} %collective-permute-done.15.refs_0_), channel_id=1, source_target_pairs={{0,32},{32,64},{64,96},{96,128},{128,160},{160,192},{192,224},{224... | collective-permute-start | bytes 884744 | tf_op jit(solution)/shard_map/ppermute | solution.py:213
  108.8 12.2 %collective-permute-start.18 = (f32[192,384]{1,0:T(8,128)S(1)}, f32[192,384]{1,0:T(8,128)S(1)}, u32[]{:S(2)}, u32[]{:S(2)}) collective-permute-start(f32[192,384]{1,0:T(8,128)S(1)} %collective-permute-done.16.refs_1_), channel_id=1, source_target_pairs={{0,480},{32,0},{64,32},{96,64},{128,96},{160,128},{192,160},{224,1... | collective-permute-start | bytes 884744 | tf_op jit(solution)/shard_map/ppermute | solution.py:213
  121.0 16.7 %copy-start.4 = (s32[3,3]{1,0:T(4,128)S(1)}, s32[3,3]{1,0:T(4,128)}, u32[]{:S(2)}) copy-start(s32[3,3]{1,0:T(4,128)} %keep.1) | copy-start | bytes 112
  122.7 15.0 %collective-permute-start.19 = (f32[192,384]{1,0:T(8,128)S(1)}, f32[192,384]{1,0:T(8,128)S(1)}, u32[]{:S(2)}, u32[]{:S(2)}) collective-permute-start(f32[192,384]{1,0:T(8,128)S(1)} %get-tuple-element.53), channel_id=1, source_target_pairs={{0,1},{1,0},{2,3},{3,2},{4,5},{5,4},{6,7},{7,6},{8,9},{9,8},{10,11... | collective-permute-start | bytes 884744 | tf_op jit(solution)/shard_map/ppermute | solution.py:213
  125.5 12.3 %collective-permute-start.20 = (f32[192,384]{1,0:T(8,128)S(1)}, f32[192,384]{1,0:T(8,128)S(1)}, u32[]{:S(2)}, u32[]{:S(2)}) collective-permute-start(f32[192,384]{1,0:T(8,128)S(1)} %collective-permute-done.17.refs_2_), channel_id=1, source_target_pairs={{0,32},{32,64},{64,96},{96,128},{128,160},{160,192},{192,224},{224... | collective-permute-start | bytes 884744 | tf_op jit(solution)/shard_map/ppermute | solution.py:213
  127.4 10.3 %collective-permute-start.21 = (f32[192,384]{1,0:T(8,128)S(1)}, f32[192,384]{1,0:T(8,128)S(1)}, u32[]{:S(2)}, u32[]{:S(2)}) collective-permute-start(f32[192,384]{1,0:T(8,128)S(1)} %collective-permute-done.18.refs_3_), channel_id=1, source_target_pairs={{0,481},{1,480},{32,1},{33,0},{64,33},{65,32},{96,65},{97,64},{128... | collective-permute-start | bytes 884744 | tf_op jit(solution)/shard_map/ppermute | solution.py:273

commit v4 on v3

--- a/solution.py
+++ b/solution.py
@@ -16,17 +16,16 @@
 VMEM = pl.BlockSpec(memory_space=pltpu.VMEM)
 SMEM = pl.BlockSpec(memory_space=pltpu.SMEM)
 ANY = pl.BlockSpec(memory_space=pl.ANY)
-LIMIT = 20 * 2**20
-
-
-def call(kernel, out_shapes, in_specs, scratch=(), flops=0, nbytes=0):
+
+
+def call(kernel, out_shapes, in_specs, scratch=(), flops=0, nbytes=0, limit=20):
     return pl.pallas_call(
         kernel,
         out_shape=out_shapes,
         in_specs=in_specs,
         out_specs=jax.tree.map(lambda _: VMEM, out_shapes),
         scratch_shapes=scratch,
-        compiler_params=pltpu.CompilerParams(vmem_limit_bytes=LIMIT),
+        compiler_params=pltpu.CompilerParams(vmem_limit_bytes=limit * 2**20),
         cost_estimate=pl.CostEstimate(flops=flops, bytes_accessed=nbytes, transcendentals=0),
     )
 
@@ -141,23 +140,13 @@
     rh[span, :], rl[span, :] = split(join_right(one, two))
 
 
-def main_kernel(early, late, place, same_in, other_in, *refs):
+def main_kernel(early, late, place, same, other, *refs):
     n = 2 * len(early) - 1
-    rights_in, (total, far, late_h, late_l, same, other, rights, lh, ll, rh, rl, sems) = refs[:n], refs[n:]
-    pairs = [(same_in, same), (other_in, other)] + [(rights_in[i], rights.at[i]) for i in range(n)]
-    copies = fetch(pairs, sems)
-    copies[0].wait()
-    copies[1].wait()
+    rights, (total, far, late_h, late_l, lh, ll, rh, rl) = refs[:n], refs[n:]
     for number, step in enumerate(early):
         fill_left(place, same, other, step, lh, ll, number * TILE)
-    for number, step in enumerate(early):
-        if step == 0:
-            copies[2].wait()
-            one, two = rights[0], jnp.zeros((PART, TILE), F32)
-        else:
-            copies[2 * step + 1].wait()
-            copies[2 * step + 2].wait()
-            one, two = rights[2 * step - 1], rights[2 * step]
+        one = rights[0 if step == 0 else 2 * step - 1][...]
+        two = jnp.zeros_like(one) if step == 0 else rights[2 * step][...]
         fill_right(one, two, rh, rl, number * TILE)
     total[...] = triple((lh[...], ll[...]), (rh[...], rl[...]))
     for number, step in enumerate(late):
@@ -230,10 +219,11 @@
     left, right = call(
         prep_kernel, (packed, half), [SMEM] + [ANY] * 4,
         [mask, mask, pltpu.VMEM((TILE, TILE), F32), pltpu.VMEM((TILE, TILE), F32), pltpu.SemaphoreType.DMA((4,))],
-        nbytes=2**21,
+        nbytes=2**21, limit=60,
     )(place, left_mask, right_mask, left_values, right_values)
 
-    left_x = lax.ppermute(left, "col", [(i, i ^ 2) for i in range(cols)])
+    with jax.named_scope("left_x"):
+        left_x = lax.ppermute(left, "col", [(i, i ^ 2) for i in range(cols)])
     pair = jnp.stack([left, left_x])
     pieces = [pair]
 
@@ -241,24 +231,28 @@
     early, late = tuple(range(reach - 2)), (reach - 2, reach - 1)
     rights, behind, ahead = [right], right, right
     for step in range(1, reach):
-        if step > 1:
-            behind, ahead = after(behind, rights[2 * step - 4]), after(ahead, behind)
-        behind, ahead = shift(behind, "row", 1), shift(ahead, "row", -1)
+        if 4 <= step <= 6:
+            behind, ahead = after(behind, pieces[step - 3]), after(ahead, pieces[step - 3])
+        with jax.named_scope(f"behind{step}"):
+            behind = shift(behind, "row", 1)
+        with jax.named_scope(f"ahead{step}"):
+            ahead = shift(ahead, "row", -1)
         rights += [behind, ahead]
         if step <= 3:
-            pair = after(pair, behind)
-            pieces.append(lax.ppermute(pair, "col", [(i, (i + 4 * step) % cols) for i in range(cols)]))
+            with jax.named_scope(f"left_y{step}"):
+                pair = after(pair, behind, ahead)
+                pieces.append(lax.ppermute(pair, "col", [(i, (i + 4 * step) % cols) for i in range(cols)]))
         if step == reach - 3:
-            same = after(jnp.stack(pieces), behind)
-            other = lax.ppermute(same, "col", [(i, i ^ 1) for i in range(cols)])
+            with jax.named_scope("left_core"):
+                same = after(jnp.stack(pieces), behind, ahead)
+                other = lax.ppermute(same, "col", [(i, i ^ 1) for i in range(cols)])
 
     n = 2 * len(early) - 1
-    panel = pltpu.VMEM((4, 2, TILE + PART, BLK), F32)
     part = jax.ShapeDtypeStruct((TILE, len(late) * TILE), BF16)
     lefts, downs = pltpu.VMEM((TILE, len(early) * TILE), BF16), pltpu.VMEM((len(early) * TILE, TILE), BF16)
     total, far, late_h, late_l = call(
-        functools.partial(main_kernel, early, late), (whole, packed, part, part), [SMEM] + [ANY] * (2 + n),
-        [panel, panel, pltpu.VMEM((n, PART, TILE), F32), lefts, lefts, downs, downs, pltpu.SemaphoreType.DMA((2 + n,))],
+        functools.partial(main_kernel, early, late), (whole, packed, part, part), [SMEM] + [VMEM] * (2 + n),
+        [lefts, lefts, downs, downs],
         flops=6 * TILE**3 * len(early), nbytes=10 * 2**20,
     )(place, same, other, *rights[:n])
     downs = pltpu.VMEM((len(late) * TILE, TILE), BF16)
@@ -266,11 +260,14 @@
         near_kernel, (half, half), [SMEM] + [VMEM] * (3 + 2 * len(late)), [downs, downs],
         flops=6 * TILE**3 * len(late), nbytes=2**21,
     )(place, total, late_h, late_l, *rights[n:])
-    came = shift(away, "layer", 1)
+    with jax.named_scope("away"):
+        came = shift(away, "layer", 1)
     behind, ahead = after(behind, away), after(ahead, away)
-    far_own = shift(behind, "row", 1)
+    with jax.named_scope("behind8"):
+        far_own = shift(behind, "row", 1)
     cross = [(z0 * 2 + l0, (z0 - 1) % count * 2 + 1 - l0) for z0 in range(count) for l0 in range(2)]
-    far_other = lax.ppermute(ahead, ("row", "layer"), cross)
+    with jax.named_scope("ahead8"):
+        far_other = lax.ppermute(ahead, ("row", "layer"), cross)
     return call(last_kernel, half, [SMEM] + [VMEM] * 6, flops=6 * PART * TILE * TILE, nbytes=2**20)(
         place, keep_mask, own, came, far, far_own, far_other
     )

time: 140 us -> 129 us (0.921)
  the two profiles are of different devices: /device:TPU:6 before, /device:TPU:18 now
where the time goes in v4:
time: 129 us; the launch traced here: 128 us
  starting transfers between devices  81.4 us (63%)
  waiting for transfers between devices  33 us (26%)
  Pallas kernels  11.9 us (9%)
  other arithmetic  1.75 us (1%)
    ppermute x16, starting transfers between devices, shift(): lax.ppermute(value, axis, [(i, (i + steps) % count) for i in range(count)])  60.5 us
    ppermute x16, waiting for transfers between devices, shift(): lax.ppermute(value, axis, [(i, (i + steps) % count) for i in range(count)])  22 us
    ppermute x3, waiting for transfers between devices, shards(): lax.ppermute(pair, 'col', [(i, (i + 4 * step) % cols) for i in range(cols)])  11 us
    ppermute x3, starting transfers between devices, shards(): lax.ppermute(pair, 'col', [(i, (i + 4 * step) % cols) for i in range(cols)])  8.37 us
    ppermute x1, starting transfers between devices, shards(): far_other = lax.ppermute(ahead, ('row', 'layer'), cross)  6.54 us
    pallas_call x1, Pallas kernels, shards(): call(functools.partial(main_kernel, early, late), (whole, packed, part, p...  5.44 us
    ppermute x1, starting transfers between devices, shards(): left_x = lax.ppermute(left, 'col', [(i, i ^ 2) for i in range(cols)])  4.03 us
    pallas_call x1, Pallas kernels, shards(): call(prep_kernel, (packed, half), [SMEM] + [ANY] * 4, [mask, mask, pltpu....  3.02 us
  transfers between devices with their start and end apart: 22, of which 10 were waited for; matrix products, arithmetic and copies ran while one was open for 1% of the time, Pallas kernels for 4%

profile of v4, /device:TPU:18, one launch (start us, length us, event | category | flops | bytes accessed | tf_op | source)
XLA Modules:
  0.0 128.4 jit_solution(2561665664599484138)
XLA Ops:
  0.0 0.6 pad_add_fusion.place
  0.6 3.0 %shard_map.55 = (f32[576,128]{1,0:T(8,128)}, f32[192,384]{1,0:T(8,128)}) custom-call(s32[3]{0:T(128)} %pad_add_fusion.place, s32[3,3]{1,0:T(4,128)} %lm_in.1, s32[3,3]{1,0:T(4,128)} %rm_in.1, f32[384,384]{1,0:T(8,128)} %left_in.1, f32[384,384]{1,0:T(8,128)} %right_in.1), custom_call_target="tpu_custom_call" | custom-call | bytes 2097152 | tf_op jit(solution)/shard_map/pallas_call | solution.py:219
  3.6 3.9 %collective-permute-start.1 = (f32[192,384]{1,0:T(8,128)}, f32[192,384]{1,0:T(8,128)S(1)}, u32[]{:S(2)}, u32[]{:S(2)}) collective-permute-start(f32[192,384]{1,0:T(8,128)} %get-tuple-element.26.refs_0_), channel_id=1, source_target_pairs={{0,32},{32,64},{64,96},{96,128},{128,160},{160,192},{192,224},{224... | collective-permute-start | bytes 884744 | tf_op jit(solution)/shard_map/behind1/ppermute | solution.py:202
  7.5 9.5 %collective-permute-start.2 = (f32[192,384]{1,0:T(8,128)}, f32[192,384]{1,0:T(8,128)S(1)}, u32[]{:S(2)}, u32[]{:S(2)}) collective-permute-start(f32[192,384]{1,0:T(8,128)} %get-tuple-element.26.refs_0_), channel_id=1, source_target_pairs={{0,480},{32,0},{64,32},{96,64},{128,96},{160,128},{192,160},{224,1... | collective-permute-start | bytes 884744 | tf_op jit(solution)/shard_map/ahead1/ppermute | solution.py:202
  17.0 4.0 %collective-permute-start = (f32[576,128]{1,0:T(8,128)}, f32[576,128]{1,0:T(8,128)S(1)}, u32[]{:S(2)}, u32[]{:S(2)}) collective-permute-start(f32[576,128]{1,0:T(8,128)} %get-tuple-element.25), channel_id=1, source_target_pairs={{0,4},{2,6},{4,0},{6,2},{8,12},{10,14},{12,8},{14,10},{16,20},{18,... | collective-permute-start | bytes 884744 | tf_op jit(solution)/shard_map/left_x/ppermute | solution.py:226
  21.1 1.2 collective-permute-done.1.refs_1_
  22.3 1.9 %collective-permute-start.4 = (f32[192,384]{1,0:T(8,128)S(1)}, f32[192,384]{1,0:T(8,128)S(1)}, u32[]{:S(2)}, u32[]{:S(2)}) collective-permute-start(f32[192,384]{1,0:T(8,128)S(1)} %collective-permute-done.1.refs_1_), channel_id=1, source_target_pairs={{0,32},{32,64},{64,96},{96,128},{128,160},{160,192},{192,224},{224... | collective-permute-start | bytes 884744 | tf_op jit(solution)/shard_map/behind2/ppermute | solution.py:202
  24.2 0.0 collective-permute-done.2.refs_2_
  24.2 5.1 %collective-permute-start.5 = (f32[192,384]{1,0:T(8,128)S(1)}, f32[192,384]{1,0:T(8,128)S(1)}, u32[]{:S(2)}, u32[]{:S(2)}) collective-permute-start(f32[192,384]{1,0:T(8,128)S(1)} %collective-permute-done.2.refs_2_), channel_id=1, source_target_pairs={{0,480},{32,0},{64,32},{96,64},{128,96},{160,128},{192,160},{224,1... | collective-permute-start | bytes 884744 | tf_op jit(solution)/shard_map/ahead2/ppermute | solution.py:202
  29.4 0.0 collective-permute-done
  29.4 1.0 fusion
  30.4 3.2 %collective-permute-start.3 = (f32[2,576,128]{2,1,0:T(8,128)S(1)}, f32[2,576,128]{2,1,0:T(8,128)S(1)}, u32[]{:S(2)}, u32[]{:S(2)}) collective-permute-start(f32[2,576,128]{2,1,0:T(8,128)S(1)} %get-tuple-element.29), channel_id=1, source_target_pairs={{0,8},{2,10},{4,12},{6,14},{8,16},{10,18},{12,20},{14,22},{16,24},... | collective-permute-start | bytes 1769480 | tf_op jit(solution)/shard_map/left_y1/ppermute | solution.py:244
  33.6 0.0 collective-permute-done.4.refs_3_
  33.6 1.9 %collective-permute-start.7 = (f32[192,384]{1,0:T(8,128)S(1)}, f32[192,384]{1,0:T(8,128)S(1)}, u32[]{:S(2)}, u32[]{:S(2)}) collective-permute-start(f32[192,384]{1,0:T(8,128)S(1)} %collective-permute-done.4.refs_3_), channel_id=1, source_target_pairs={{0,32},{32,64},{64,96},{96,128},{128,160},{160,192},{192,224},{224... | collective-permute-start | bytes 884744 | tf_op jit(solution)/shard_map/behind3/ppermute | solution.py:202
  35.6 0.0 collective-permute-done.5.refs_4_
  35.6 5.1 %collective-permute-start.8 = (f32[192,384]{1,0:T(8,128)S(1)}, f32[192,384]{1,0:T(8,128)S(1)}, u32[]{:S(2)}, u32[]{:S(2)}) collective-permute-start(f32[192,384]{1,0:T(8,128)S(1)} %collective-permute-done.5.refs_4_), channel_id=1, source_target_pairs={{0,480},{32,0},{64,32},{96,64},{128,96},{160,128},{192,160},{224,1... | collective-permute-start | bytes 884744 | tf_op jit(solution)/shard_map/ahead3/ppermute | solution.py:202
  40.7 2.5 %collective-permute-start.6 = (f32[2,576,128]{2,1,0:T(8,128)S(1)}, f32[2,576,128]{2,1,0:T(8,128)S(1)}, u32[]{:S(2)}, u32[]{:S(2)}) collective-permute-start(f32[2,576,128]{2,1,0:T(8,128)S(1)} %get-tuple-element.29), channel_id=1, source_target_pairs={{0,16},{2,18},{4,20},{6,22},{8,24},{10,26},{12,28},{14,30},{16,0},... | collective-permute-start | bytes 1769480 | tf_op jit(solution)/shard_map/left_y2/ppermute | solution.py:244
  43.2 0.8 collective-permute-done.7.refs_5_
  44.1 1.2 collective-permute-done.8.refs_6_
  45.3 2.6 %collective-permute-start.9 = (f32[2,576,128]{2,1,0:T(8,128)S(1)}, f32[2,576,128]{2,1,0:T(8,128)S(1)}, u32[]{:S(2)}, u32[]{:S(2)}) collective-permute-start(f32[2,576,128]{2,1,0:T(8,128)S(1)} %get-tuple-element.29), channel_id=1, source_target_pairs={{0,24},{2,26},{4,28},{6,30},{8,0},{10,2},{12,4},{14,6},{16,8},{18,... | collective-permute-start | bytes 1769480 | tf_op jit(solution)/shard_map/left_y3/ppermute | solution.py:244
  47.9 11.0 %collective-permute-done.3 = f32[2,576,128]{2,1,0:T(8,128)S(1)} collective-permute-done((f32[2,576,128]{2,1,0:T(8,128)S(1)}, f32[2,576,128]{2,1,0:T(8,128)S(1)}, u32[]{:S(2)}, u32[]{:S(2)}) %collective-permute-start.3) | collective-permute-done | bytes 589856 | tf_op jit(solution)/shard_map/left_y1/ppermute | solution.py:244
  58.9 1.9 %collective-permute-start.10 = (f32[192,384]{1,0:T(8,128)S(1)}, f32[192,384]{1,0:T(8,128)S(1)}, u32[]{:S(2)}, u32[]{:S(2)}) collective-permute-start(f32[192,384]{1,0:T(8,128)S(1)} %collective-permute-done.7.refs_5_), channel_id=1, source_target_pairs={{0,32},{32,64},{64,96},{96,128},{128,160},{160,192},{192,224},{224... | collective-permute-start | bytes 884744 | tf_op jit(solution)/shard_map/behind4/ppermute | solution.py:202
  60.8 5.1 %collective-permute-start.12 = (f32[192,384]{1,0:T(8,128)S(1)}, f32[192,384]{1,0:T(8,128)S(1)}, u32[]{:S(2)}, u32[]{:S(2)}) collective-permute-start(f32[192,384]{1,0:T(8,128)S(1)} %collective-permute-done.8.refs_6_), channel_id=1, source_target_pairs={{0,480},{32,0},{64,32},{96,64},{128,96},{160,128},{192,160},{224,1... | collective-permute-start | bytes 884744 | tf_op jit(solution)/shard_map/ahead4/ppermute | solution.py:202
  66.0 0.0 collective-permute-done.6
  66.0 3.4 %collective-permute-done.10.refs_7_ = f32[192,384]{1,0:T(8,128)S(1)} collective-permute-done((f32[192,384]{1,0:T(8,128)S(1)}, f32[192,384]{1,0:T(8,128)S(1)}, u32[]{:S(2)}, u32[]{:S(2)}) %collective-permute-start.10) | collective-permute-done | bytes 294944 | tf_op jit(solution)/shard_map/behind4/ppermute | solution.py:202
  69.4 1.9 %collective-permute-start.11 = (f32[192,384]{1,0:T(8,128)S(1)}, f32[192,384]{1,0:T(8,128)S(1)}, u32[]{:S(2)}, u32[]{:S(2)}) collective-permute-start(f32[192,384]{1,0:T(8,128)S(1)} %collective-permute-done.10.refs_7_), channel_id=1, source_target_pairs={{0,32},{32,64},{64,96},{96,128},{128,160},{160,192},{192,224},{224... | collective-permute-start | bytes 884744 | tf_op jit(solution)/shard_map/behind5/ppermute | solution.py:202
  71.3 0.0 collective-permute-done.12.refs_8_
  71.3 5.1 %collective-permute-start.13 = (f32[192,384]{1,0:T(8,128)S(1)}, f32[192,384]{1,0:T(8,128)S(1)}, u32[]{:S(2)}, u32[]{:S(2)}) collective-permute-start(f32[192,384]{1,0:T(8,128)S(1)} %collective-permute-done.12.refs_8_), channel_id=1, source_target_pairs={{0,480},{32,0},{64,32},{96,64},{128,96},{160,128},{192,160},{224,1... | collective-permute-start | bytes 884744 | tf_op jit(solution)/shard_map/ahead5/ppermute | solution.py:202
  76.4 0.0 collective-permute-done.9
  76.5 0.0 copy-start
  76.5 0.0 copy-start.1
  76.5 0.2 pad_maximum_fusion.same
  76.6 2.6 %collective-permute-done.11.refs_9_ = f32[192,384]{1,0:T(8,128)S(1)} collective-permute-done((f32[192,384]{1,0:T(8,128)S(1)}, f32[192,384]{1,0:T(8,128)S(1)}, u32[]{:S(2)}, u32[]{:S(2)}) %collective-permute-start.11) | collective-permute-done | bytes 294944 | tf_op jit(solution)/shard_map/behind5/ppermute | solution.py:202
  79.2 1.5 %collective-permute-done.13.refs_10_ = f32[192,384]{1,0:T(8,128)S(1)} collective-permute-done((f32[192,384]{1,0:T(8,128)S(1)}, f32[192,384]{1,0:T(8,128)S(1)}, u32[]{:S(2)}, u32[]{:S(2)}) %collective-permute-start.13) | collective-permute-done | bytes 294944 | tf_op jit(solution)/shard_map/ahead5/ppermute | solution.py:202
  80.7 1.9 %collective-permute-start.14 = (f32[4,2,576,128]{3,2,1,0:T(8,128)S(1)}, f32[4,2,576,128]{3,2,1,0:T(8,128)S(1)}, u32[]{:S(2)}, u32[]{:S(2)}) collective-permute-start(f32[4,2,576,128]{3,2,1,0:T(8,128)S(1)} %pad_maximum_fusion.same), channel_id=1, source_target_pairs={{0,2},{2,0},{4,6},{6,4},{8,10},{10,8},{12,14},{14,12},{16,18},{18,... | collective-permute-start | bytes 7077896 | tf_op jit(solution)/shard_map/left_core/ppermute | solution.py:248
  82.6 1.9 %collective-permute-start.15 = (f32[192,384]{1,0:T(8,128)S(1)}, f32[192,384]{1,0:T(8,128)S(1)}, u32[]{:S(2)}, u32[]{:S(2)}) collective-permute-start(f32[192,384]{1,0:T(8,128)S(1)} %collective-permute-done.11.refs_9_), channel_id=1, source_target_pairs={{0,32},{32,64},{64,96},{96,128},{128,160},{160,192},{192,224},{224... | collective-permute-start | bytes 884744 | tf_op jit(solution)/shard_map/behind6/ppermute | solution.py:202
  84.5 5.6 %collective-permute-start.16 = (f32[192,384]{1,0:T(8,128)S(1)}, f32[192,384]{1,0:T(8,128)S(1)}, u32[]{:S(2)}, u32[]{:S(2)}) collective-permute-start(f32[192,384]{1,0:T(8,128)S(1)} %collective-permute-done.13.refs_10_), channel_id=1, source_target_pairs={{0,480},{32,0},{64,32},{96,64},{128,96},{160,128},{192,160},{224,1... | collective-permute-start | bytes 884744 | tf_op jit(solution)/shard_map/ahead6/ppermute | solution.py:202
  90.1 5.7 %collective-permute-done.15.refs_0_ = f32[192,384]{1,0:T(8,128)S(1)} collective-permute-done((f32[192,384]{1,0:T(8,128)S(1)}, f32[192,384]{1,0:T(8,128)S(1)}, u32[]{:S(2)}, u32[]{:S(2)}) %collective-permute-start.15) | collective-permute-done | bytes 294944 | tf_op jit(solution)/shard_map/behind6/ppermute | solution.py:202
  95.8 1.9 %collective-permute-start.17 = (f32[192,384]{1,0:T(8,128)S(1)}, f32[192,384]{1,0:T(8,128)S(1)}, u32[]{:S(2)}, u32[]{:S(2)}) collective-permute-start(f32[192,384]{1,0:T(8,128)S(1)} %collective-permute-done.15.refs_0_), channel_id=1, source_target_pairs={{0,32},{32,64},{64,96},{96,128},{128,160},{160,192},{192,224},{224... | collective-permute-start | bytes 884744 | tf_op jit(solution)/shard_map/behind7/ppermute | solution.py:202
  97.8 0.0 collective-permute-done.16.refs_1_
  97.8 5.1 %collective-permute-start.18 = (f32[192,384]{1,0:T(8,128)S(1)}, f32[192,384]{1,0:T(8,128)S(1)}, u32[]{:S(2)}, u32[]{:S(2)}) collective-permute-start(f32[192,384]{1,0:T(8,128)S(1)} %collective-permute-done.16.refs_1_), channel_id=1, source_target_pairs={{0,480},{32,0},{64,32},{96,64},{128,96},{160,128},{192,160},{224,1... | collective-permute-start | bytes 884744 | tf_op jit(solution)/shard_map/ahead7/ppermute | solution.py:202
  102.9 0.0 collective-permute-done.14.other
  102.9 0.0 copy-done
  102.9 0.0 copy-done.1
  102.9 5.4 %shard_map.56 = (f32[384,384]{1,0:T(8,128)S(1)}, f32[576,128]{1,0:T(8,128)S(1)}, bf16[384,768]{1,0:T(8,128)(2,1)S(1)}, bf16[384,768]{1,0:T(8,128)(2,1)S(1)}) custom-call(s32[3]{0:T(128)S(1)} %copy-done.1, f32[4,2,576,128]{3,2,1,0:T(8,128)S(1)} %pad_maximum_fusion.same, f32[4,2,576,128]{3,2,1,0:T(8,128)S(1)} %collective-permute-done.14.other, ...), custom_call_target="tpu_custom_call" | custom-call | flops 2038431744 | bytes 10485760 | tf_op jit(solution)/shard_map/pallas_call | solution.py:253
  108.4 0.0 copy-start.2
  108.4 0.0 collective-permute-done.17.refs_2_
  108.4 0.5 collective-permute-done.18.refs_3_
  109.0 1.7 %shard_map.57 = (f32[192,384]{1,0:T(8,128)S(1)}, f32[192,384]{1,0:T(8,128)S(1)}) custom-call(s32[3]{0:T(128)S(1)} %copy-done.1, f32[384,384]{1,0:T(8,128)S(1)} %get-tuple-element.35.total, bf16[384,768]{1,0:T(8,128)(2,1)S(1)} %get-tuple-element.36.late_h, bf16[384,768]{1,0:T(8,128)(2,1)S(1)} %get-tuple-element.37.late_l, ...), custom_call_target="tpu_custom_call" | custom-call | flops 679477248 | bytes 2097152 | tf_op jit(solution)/shard_map/pallas_call | solution.py:259
  110.7 2.4 %collective-permute-start.19 = (f32[192,384]{1,0:T(8,128)S(1)}, f32[192,384]{1,0:T(8,128)S(1)}, u32[]{:S(2)}, u32[]{:S(2)}) collective-permute-start(f32[192,384]{1,0:T(8,128)S(1)} %get-tuple-element.41), channel_id=1, source_target_pairs={{0,1},{1,0},{2,3},{3,2},{4,5},{5,4},{6,7},{7,6},{8,9},{9,8},{10,11... | collective-permute-start | bytes 884744 | tf_op jit(solution)/shard_map/away/ppermute | solution.py:202
  113.1 1.9 %collective-permute-start.20 = (f32[192,384]{1,0:T(8,128)S(1)}, f32[192,384]{1,0:T(8,128)S(1)}, u32[]{:S(2)}, u32[]{:S(2)}) collective-permute-start(f32[192,384]{1,0:T(8,128)S(1)} %collective-permute-done.17.refs_2_), channel_id=1, source_target_pairs={{0,32},{32,64},{64,96},{96,128},{128,160},{160,192},{192,224},{224... | collective-permute-start | bytes 884744 | tf_op jit(solution)/shard_map/behind8/ppermute | solution.py:202
  115.0 6.5 %collective-permute-start.21 = (f32[192,384]{1,0:T(8,128)S(1)}, f32[192,384]{1,0:T(8,128)S(1)}, u32[]{:S(2)}, u32[]{:S(2)}) collective-permute-start(f32[192,384]{1,0:T(8,128)S(1)} %collective-permute-done.18.refs_3_), channel_id=1, source_target_pairs={{0,481},{1,480},{32,1},{33,0},{64,33},{65,32},{96,65},{97,64},{128... | collective-permute-start | bytes 884744 | tf_op jit(solution)/shard_map/ahead8/ppermute | solution.py:270
  121.6 5.0 %collective-permute-done.19.came = f32[192,384]{1,0:T(8,128)S(1)} collective-permute-done((f32[192,384]{1,0:T(8,128)S(1)}, f32[192,384]{1,0:T(8,128)S(1)}, u32[]{:S(2)}, u32[]{:S(2)}) %collective-permute-start.19) | collective-permute-done | bytes 294944 | tf_op jit(solution)/shard_map/away/ppermute | solution.py:202
  126.6 0.0 collective-permute-done.20.right_own
  126.6 0.0 collective-permute-done.21.right_other
  126.6 0.0 copy-done.2
  126.6 1.7 %shard_map.58 = f32[192,384]{1,0:T(8,128)} custom-call(s32[3]{0:T(128)S(1)} %copy-done.1, s32[3,3]{1,0:T(4,128)S(1)} %copy-done.2, f32[192,384]{1,0:T(8,128)S(1)} %get-tuple-element.40.own, f32[192,384]{1,0:T(8,128)S(1)} %collective-permute-done.19.came, f32[576,128]{1,0:T(8,128)S(1)} %get-tuple-element.42.far, ...), custom_call_target="tpu_custom_call" | custom-call | flops 169869312 | bytes 1048576 | tf_op jit(solution)/shard_map/pallas_call | solution.py:271
Async XLA Ops:
  3.6 18.7 %collective-permute-start.1 = (f32[192,384]{1,0:T(8,128)}, f32[192,384]{1,0:T(8,128)S(1)}, u32[]{:S(2)}, u32[]{:S(2)}) collective-permute-start(f32[192,384]{1,0:T(8,128)} %get-tuple-element.26.refs_0_), channel_id=1, source_target_pairs={{0,32},{32,64},{64,96},{96,128},{128,160},{160,192},{192,224},{224... | collective-permute-start | bytes 884744 | tf_op jit(solution)/shard_map/behind1/ppermute | solution.py:202
  7.5 16.7 %collective-permute-start.2 = (f32[192,384]{1,0:T(8,128)}, f32[192,384]{1,0:T(8,128)S(1)}, u32[]{:S(2)}, u32[]{:S(2)}) collective-permute-start(f32[192,384]{1,0:T(8,128)} %get-tuple-element.26.refs_0_), channel_id=1, source_target_pairs={{0,480},{32,0},{64,32},{96,64},{128,96},{160,128},{192,160},{224,1... | collective-permute-start | bytes 884744 | tf_op jit(solution)/shard_map/ahead1/ppermute | solution.py:202
  17.0 12.3 %collective-permute-start = (f32[576,128]{1,0:T(8,128)}, f32[576,128]{1,0:T(8,128)S(1)}, u32[]{:S(2)}, u32[]{:S(2)}) collective-permute-start(f32[576,128]{1,0:T(8,128)} %get-tuple-element.25), channel_id=1, source_target_pairs={{0,4},{2,6},{4,0},{6,2},{8,12},{10,14},{12,8},{14,10},{16,20},{18,... | collective-permute-start | bytes 884744 | tf_op jit(solution)/shard_map/left_x/ppermute | solution.py:226
  22.3 11.3 %collective-permute-start.4 = (f32[192,384]{1,0:T(8,128)S(1)}, f32[192,384]{1,0:T(8,128)S(1)}, u32[]{:S(2)}, u32[]{:S(2)}) collective-permute-start(f32[192,384]{1,0:T(8,128)S(1)} %collective-permute-done.1.refs_1_), channel_id=1, source_target_pairs={{0,32},{32,64},{64,96},{96,128},{128,160},{160,192},{192,224},{224... | collective-permute-start | bytes 884744 | tf_op jit(solution)/shard_map/behind2/ppermute | solution.py:202
  24.2 11.3 %collective-permute-start.5 = (f32[192,384]{1,0:T(8,128)S(1)}, f32[192,384]{1,0:T(8,128)S(1)}, u32[]{:S(2)}, u32[]{:S(2)}) collective-permute-start(f32[192,384]{1,0:T(8,128)S(1)} %collective-permute-done.2.refs_2_), channel_id=1, source_target_pairs={{0,480},{32,0},{64,32},{96,64},{128,96},{160,128},{192,160},{224,1... | collective-permute-start | bytes 884744 | tf_op jit(solution)/shard_map/ahead2/ppermute | solution.py:202
  30.4 28.5 %collective-permute-start.3 = (f32[2,576,128]{2,1,0:T(8,128)S(1)}, f32[2,576,128]{2,1,0:T(8,128)S(1)}, u32[]{:S(2)}, u32[]{:S(2)}) collective-permute-start(f32[2,576,128]{2,1,0:T(8,128)S(1)} %get-tuple-element.29), channel_id=1, source_target_pairs={{0,8},{2,10},{4,12},{6,14},{8,16},{10,18},{12,20},{14,22},{16,24},... | collective-permute-start | bytes 1769480 | tf_op jit(solution)/shard_map/left_y1/ppermute | solution.py:244
  33.6 10.5 %collective-permute-start.7 = (f32[192,384]{1,0:T(8,128)S(1)}, f32[192,384]{1,0:T(8,128)S(1)}, u32[]{:S(2)}, u32[]{:S(2)}) collective-permute-start(f32[192,384]{1,0:T(8,128)S(1)} %collective-permute-done.4.refs_3_), channel_id=1, source_target_pairs={{0,32},{32,64},{64,96},{96,128},{128,160},{160,192},{192,224},{224... | collective-permute-start | bytes 884744 | tf_op jit(solution)/shard_map/behind3/ppermute | solution.py:202
  35.6 9.7 %collective-permute-start.8 = (f32[192,384]{1,0:T(8,128)S(1)}, f32[192,384]{1,0:T(8,128)S(1)}, u32[]{:S(2)}, u32[]{:S(2)}) collective-permute-start(f32[192,384]{1,0:T(8,128)S(1)} %collective-permute-done.5.refs_4_), channel_id=1, source_target_pairs={{0,480},{32,0},{64,32},{96,64},{128,96},{160,128},{192,160},{224,1... | collective-permute-start | bytes 884744 | tf_op jit(solution)/shard_map/ahead3/ppermute | solution.py:202
  40.7 25.3 %collective-permute-start.6 = (f32[2,576,128]{2,1,0:T(8,128)S(1)}, f32[2,576,128]{2,1,0:T(8,128)S(1)}, u32[]{:S(2)}, u32[]{:S(2)}) collective-permute-start(f32[2,576,128]{2,1,0:T(8,128)S(1)} %get-tuple-element.29), channel_id=1, source_target_pairs={{0,16},{2,18},{4,20},{6,22},{8,24},{10,26},{12,28},{14,30},{16,0},... | collective-permute-start | bytes 1769480 | tf_op jit(solution)/shard_map/left_y2/ppermute | solution.py:244
  45.3 31.2 %collective-permute-start.9 = (f32[2,576,128]{2,1,0:T(8,128)S(1)}, f32[2,576,128]{2,1,0:T(8,128)S(1)}, u32[]{:S(2)}, u32[]{:S(2)}) collective-permute-start(f32[2,576,128]{2,1,0:T(8,128)S(1)} %get-tuple-element.29), channel_id=1, source_target_pairs={{0,24},{2,26},{4,28},{6,30},{8,0},{10,2},{12,4},{14,6},{16,8},{18,... | collective-permute-start | bytes 1769480 | tf_op jit(solution)/shard_map/left_y3/ppermute | solution.py:244
  58.9 10.5 %collective-permute-start.10 = (f32[192,384]{1,0:T(8,128)S(1)}, f32[192,384]{1,0:T(8,128)S(1)}, u32[]{:S(2)}, u32[]{:S(2)}) collective-permute-start(f32[192,384]{1,0:T(8,128)S(1)} %collective-permute-done.7.refs_5_), channel_id=1, source_target_pairs={{0,32},{32,64},{64,96},{96,128},{128,160},{160,192},{192,224},{224... | collective-permute-start | bytes 884744 | tf_op jit(solution)/shard_map/behind4/ppermute | solution.py:202
  60.8 10.5 %collective-permute-start.12 = (f32[192,384]{1,0:T(8,128)S(1)}, f32[192,384]{1,0:T(8,128)S(1)}, u32[]{:S(2)}, u32[]{:S(2)}) collective-permute-start(f32[192,384]{1,0:T(8,128)S(1)} %collective-permute-done.8.refs_6_), channel_id=1, source_target_pairs={{0,480},{32,0},{64,32},{96,64},{128,96},{160,128},{192,160},{224,1... | collective-permute-start | bytes 884744 | tf_op jit(solution)/shard_map/ahead4/ppermute | solution.py:202
  69.4 9.8 %collective-permute-start.11 = (f32[192,384]{1,0:T(8,128)S(1)}, f32[192,384]{1,0:T(8,128)S(1)}, u32[]{:S(2)}, u32[]{:S(2)}) collective-permute-start(f32[192,384]{1,0:T(8,128)S(1)} %collective-permute-done.10.refs_7_), channel_id=1, source_target_pairs={{0,32},{32,64},{64,96},{96,128},{128,160},{160,192},{192,224},{224... | collective-permute-start | bytes 884744 | tf_op jit(solution)/shard_map/behind5/ppermute | solution.py:202
  71.3 9.4 %collective-permute-start.13 = (f32[192,384]{1,0:T(8,128)S(1)}, f32[192,384]{1,0:T(8,128)S(1)}, u32[]{:S(2)}, u32[]{:S(2)}) collective-permute-start(f32[192,384]{1,0:T(8,128)S(1)} %collective-permute-done.12.refs_8_), channel_id=1, source_target_pairs={{0,480},{32,0},{64,32},{96,64},{128,96},{160,128},{192,160},{224,1... | collective-permute-start | bytes 884744 | tf_op jit(solution)/shard_map/ahead5/ppermute | solution.py:202
  76.5 26.5 %copy-start = (f32[192,384]{1,0:T(8,128)S(1)}, f32[192,384]{1,0:T(8,128)}, u32[]{:S(2)}) copy-start(f32[192,384]{1,0:T(8,128)} %get-tuple-element.26.refs_0_) | copy-start | bytes 884740
  76.5 26.5 %copy-start.1 = (s32[3]{0:T(128)S(1)}, s32[3]{0:T(128)}, u32[]{:S(2)}) copy-start(s32[3]{0:T(128)} %pad_add_fusion.place) | copy-start | bytes 40
  80.7 22.3 %collective-permute-start.14 = (f32[4,2,576,128]{3,2,1,0:T(8,128)S(1)}, f32[4,2,576,128]{3,2,1,0:T(8,128)S(1)}, u32[]{:S(2)}, u32[]{:S(2)}) collective-permute-start(f32[4,2,576,128]{3,2,1,0:T(8,128)S(1)} %pad_maximum_fusion.same), channel_id=1, source_target_pairs={{0,2},{2,0},{4,6},{6,4},{8,10},{10,8},{12,14},{14,12},{16,18},{18,... | collective-permute-start | bytes 7077896 | tf_op jit(solution)/shard_map/left_core/ppermute | solution.py:248
  82.6 13.3 %collective-permute-start.15 = (f32[192,384]{1,0:T(8,128)S(1)}, f32[192,384]{1,0:T(8,128)S(1)}, u32[]{:S(2)}, u32[]{:S(2)}) collective-permute-start(f32[192,384]{1,0:T(8,128)S(1)} %collective-permute-done.11.refs_9_), channel_id=1, source_target_pairs={{0,32},{32,64},{64,96},{96,128},{128,160},{160,192},{192,224},{224... | collective-permute-start | bytes 884744 | tf_op jit(solution)/shard_map/behind6/ppermute | solution.py:202
  84.5 13.3 %collective-permute-start.16 = (f32[192,384]{1,0:T(8,128)S(1)}, f32[192,384]{1,0:T(8,128)S(1)}, u32[]{:S(2)}, u32[]{:S(2)}) collective-permute-start(f32[192,384]{1,0:T(8,128)S(1)} %collective-permute-done.13.refs_10_), channel_id=1, source_target_pairs={{0,480},{32,0},{64,32},{96,64},{128,96},{160,128},{192,160},{224,1... | collective-permute-start | bytes 884744 | tf_op jit(solution)/shard_map/ahead6/ppermute | solution.py:202
  95.8 12.6 %collective-permute-start.17 = (f32[192,384]{1,0:T(8,128)S(1)}, f32[192,384]{1,0:T(8,128)S(1)}, u32[]{:S(2)}, u32[]{:S(2)}) collective-permute-start(f32[192,384]{1,0:T(8,128)S(1)} %collective-permute-done.15.refs_0_), channel_id=1, source_target_pairs={{0,32},{32,64},{64,96},{96,128},{128,160},{160,192},{192,224},{224... | collective-permute-start | bytes 884744 | tf_op jit(solution)/shard_map/behind7/ppermute | solution.py:202
  97.8 11.2 %collective-permute-start.18 = (f32[192,384]{1,0:T(8,128)S(1)}, f32[192,384]{1,0:T(8,128)S(1)}, u32[]{:S(2)}, u32[]{:S(2)}) collective-permute-start(f32[192,384]{1,0:T(8,128)S(1)} %collective-permute-done.16.refs_1_), channel_id=1, source_target_pairs={{0,480},{32,0},{64,32},{96,64},{128,96},{160,128},{192,160},{224,1... | collective-permute-start | bytes 884744 | tf_op jit(solution)/shard_map/ahead7/ppermute | solution.py:202
  108.4 18.3 %copy-start.2 = (s32[3,3]{1,0:T(4,128)S(1)}, s32[3,3]{1,0:T(4,128)}, u32[]{:S(2)}) copy-start(s32[3,3]{1,0:T(4,128)} %keep.1) | copy-start | bytes 112
  110.7 16.0 %collective-permute-start.19 = (f32[192,384]{1,0:T(8,128)S(1)}, f32[192,384]{1,0:T(8,128)S(1)}, u32[]{:S(2)}, u32[]{:S(2)}) collective-permute-start(f32[192,384]{1,0:T(8,128)S(1)} %get-tuple-element.41), channel_id=1, source_target_pairs={{0,1},{1,0},{2,3},{3,2},{4,5},{5,4},{6,7},{7,6},{8,9},{9,8},{10,11... | collective-permute-start | bytes 884744 | tf_op jit(solution)/shard_map/away/ppermute | solution.py:202
  113.1 13.5 %collective-permute-start.20 = (f32[192,384]{1,0:T(8,128)S(1)}, f32[192,384]{1,0:T(8,128)S(1)}, u32[]{:S(2)}, u32[]{:S(2)}) collective-permute-start(f32[192,384]{1,0:T(8,128)S(1)} %collective-permute-done.17.refs_2_), channel_id=1, source_target_pairs={{0,32},{32,64},{64,96},{96,128},{128,160},{160,192},{192,224},{224... | collective-permute-start | bytes 884744 | tf_op jit(solution)/shard_map/behind8/ppermute | solution.py:202
  115.0 11.6 %collective-permute-start.21 = (f32[192,384]{1,0:T(8,128)S(1)}, f32[192,384]{1,0:T(8,128)S(1)}, u32[]{:S(2)}, u32[]{:S(2)}) collective-permute-start(f32[192,384]{1,0:T(8,128)S(1)} %collective-permute-done.18.refs_3_), channel_id=1, source_target_pairs={{0,481},{1,480},{32,1},{33,0},{64,33},{65,32},{96,65},{97,64},{128... | collective-permute-start | bytes 884744 | tf_op jit(solution)/shard_map/ahead8/ppermute | solution.py:270

commit v5 on v4

--- a/solution.py
+++ b/solution.py
@@ -1,4 +1,5 @@
 import functools
+import itertools
 
 import jax
 import jax.numpy as jnp
@@ -119,54 +120,66 @@
     return mine, lax.rem(col // 4 - k // 4 + 4, 4), lax.bitwise_xor(lax.rem(k // 2, 2), lax.rem(col // 2, 2))
 
 
-def fill_left(place, same, other, step, lh, ll, column):
-    z = place[0]
-    mine, y1, x1 = panel_index(place, lax.rem(z - step + 16, 16))
-    _, y2, x2 = panel_index(place, lax.rem(z + step, 16))
+def tile_at(place, step):
+    z, core = place[0], lax.rem(place[1], 2)
+    return lax.rem(z + (2 * core - 1) * step + 16, 16)
+
+
+def fill_left(place, same, other, one, two, lh, ll, column):
+    mine1, y1, x1 = panel_index(place, one)
+    mine2, y2, x2 = panel_index(place, one if two is None else two)
     span = slice(column, column + TILE)
 
-    def put(panel):
-        one, two = panel[y1, x1], panel[y2, x2]
-        if step == 0:
-            two = jnp.zeros_like(two)
-        lh[:, span], ll[:, span] = split(join_left(one, two))
-
-    pl.when(mine)(lambda: put(same))
-    pl.when(jnp.logical_not(mine))(lambda: put(other))
-
-
-def fill_right(one, two, rh, rl, column):
-    span = slice(column, column + TILE)
-    rh[span, :], rl[span, :] = split(join_right(one, two))
-
-
-def main_kernel(early, late, place, same, other, *refs):
-    n = 2 * len(early) - 1
-    rights, (total, far, late_h, late_l, lh, ll, rh, rl) = refs[:n], refs[n:]
-    for number, step in enumerate(early):
-        fill_left(place, same, other, step, lh, ll, number * TILE)
-        one = rights[0 if step == 0 else 2 * step - 1][...]
-        two = jnp.zeros_like(one) if step == 0 else rights[2 * step][...]
-        fill_right(one, two, rh, rl, number * TILE)
-    total[...] = triple((lh[...], ll[...]), (rh[...], rl[...]))
-    for number, step in enumerate(late):
-        fill_left(place, same, other, step, late_h, late_l, number * TILE)
-    mine, y, x = panel_index(place, lax.rem(place[0] + 8, 16))
-
-    @pl.when(mine)
+    def put(panel1, panel2):
+        first = panel1[y1, x1]
+        second = jnp.zeros_like(first) if two is None else panel2[y2, x2]
+        lh[:, span], ll[:, span] = split(join_left(first, second))
+
+    for is1 in (True, False):
+        for is2 in (True, False):
+            pl.when((mine1 == is1) & (mine2 == is2))(
+                functools.partial(put, same if is1 else other, same if is2 else other)
+            )
+
+
+def fill_right(one, two, rh, rl, row, lane=0):
+    rows, lanes = slice(row, row + TILE), slice(lane, lane + TILE)
+    rh[rows, lanes], rl[rows, lanes] = split(join_right(one, two))
+
+
+def main_kernel(steps, place, same, other, *refs):
+    mine, others = refs[:steps], refs[steps : 2 * steps]
+    total, spare, far, late_h, late_l, lh, ll, rh, rl = refs[2 * steps :]
+    core = lax.rem(place[1], 2)
+    for start in range(0, steps, 2):
+        column = start * PART
+        paired = start + 1 < steps
+        one, two = tile_at(place, start), tile_at(place, start + 1) if paired else None
+        fill_left(place, same, other, one, two, lh, ll, column)
+        for lane, tiles in ((0, mine), (TILE, others)):
+            one = tiles[start][...]
+            if start == 0:
+                one = jnp.where(core == 0, one, jnp.zeros_like(one))
+            two = tiles[start + 1][...] if paired else jnp.zeros_like(one)
+            fill_right(one, two, rh, rl, column, lane)
+    value = triple((lh[...], ll[...]), (rh[...], rl[...]))
+    total[...] = value[:, :TILE]
+    spare[...] = value[:, TILE:]
+    fill_left(place, same, other, tile_at(place, steps), tile_at(place, -steps), late_h, late_l, 0)
+    here, y, x = panel_index(place, lax.rem(place[0] + 8, 16))
+
+    @pl.when(here)
     def _():
         far[...] = same[y, x]
 
-    @pl.when(jnp.logical_not(mine))
+    @pl.when(jnp.logical_not(here))
     def _():
         far[...] = other[y, x]
 
 
-def near_kernel(place, total, late_h, late_l, *refs):
-    rights, (own, away, rh, rl) = refs[:-4], refs[-4:]
-    for number in range(len(rights) // 2):
-        fill_right(rights[2 * number][...], rights[2 * number + 1][...], rh, rl, number * TILE)
-    value = total[...] + triple((late_h[...], late_l[...]), (rh[...], rl[...]))
+def near_kernel(place, total, spare, late_h, late_l, one, two, own, away, rh, rl):
+    fill_right(one[...], two[...], rh, rl, 0)
+    value = total[...] + spare[...] + triple((late_h[...], late_l[...]), (rh[...], rl[...]))
     layer = place[2]
 
     @pl.when(layer == 0)
@@ -197,9 +210,19 @@
         out[:, lanes] = value[:, lanes] * scale
 
 
-def shift(value, axis, steps):
-    count = lax.axis_size(axis)
-    return lax.ppermute(value, axis, [(i, (i + steps) % count) for i in range(count)])
+def move(value, axes, target):
+    sizes = [lax.axis_size(axis) for axis in axes]
+    flat = lambda at: functools.reduce(lambda total, pair: total * pair[1] + pair[0] % pair[1], zip(at, sizes), 0)
+    points = list(itertools.product(*map(range, sizes)))
+    return lax.ppermute(value, axes, [(flat(at), flat(target(*at))) for at in points])
+
+
+def along(core):
+    return 1 - 2 * core
+
+
+def onward(value):
+    return move(value, ("row", "col"), lambda z, c: (z + along(c % 2), c))
 
 
 def after(value, *earlier):
@@ -222,52 +245,57 @@
         nbytes=2**21, limit=60,
     )(place, left_mask, right_mask, left_values, right_values)
 
+    with jax.named_scope("right_core"):
+        right_other = move(right, ("col",), lambda c: (c ^ 1,))
     with jax.named_scope("left_x"):
-        left_x = lax.ppermute(left, "col", [(i, i ^ 2) for i in range(cols)])
+        left_x = move(left, ("col",), lambda c: (c ^ 2,))
     pair = jnp.stack([left, left_x])
     pieces = [pair]
 
-    reach = count // 2
-    early, late = tuple(range(reach - 2)), (reach - 2, reach - 1)
-    rights, behind, ahead = [right], right, right
-    for step in range(1, reach):
+    steps = count // 2 - 1
+    mine, others = [right], [right_other]
+    one, two = right, right_other
+    for step in range(1, steps + 1):
         if 4 <= step <= 6:
-            behind, ahead = after(behind, pieces[step - 3]), after(ahead, pieces[step - 3])
-        with jax.named_scope(f"behind{step}"):
-            behind = shift(behind, "row", 1)
-        with jax.named_scope(f"ahead{step}"):
-            ahead = shift(ahead, "row", -1)
-        rights += [behind, ahead]
+            one, two = after(one, pieces[step - 3]), after(two, pieces[step - 3])
+        with jax.named_scope(f"own{step}"):
+            one = onward(one)
+        with jax.named_scope(f"other{step}"):
+            if step < steps:
+                two = onward(two)
+            else:
+                two = move(two, ("row", "col"), lambda z, c: (z + along(c % 2), c ^ 1))
+        mine.append(one)
+        others.append(two)
         if step <= 3:
             with jax.named_scope(f"left_y{step}"):
-                pair = after(pair, behind, ahead)
-                pieces.append(lax.ppermute(pair, "col", [(i, (i + 4 * step) % cols) for i in range(cols)]))
-        if step == reach - 3:
+                pair = after(pair, one, two)
+                pieces.append(move(pair, ("col",), lambda c: (c + 4 * step,)))
+        if step == steps - 2:
             with jax.named_scope("left_core"):
-                same = after(jnp.stack(pieces), behind, ahead)
-                other = lax.ppermute(same, "col", [(i, i ^ 1) for i in range(cols)])
-
-    n = 2 * len(early) - 1
-    part = jax.ShapeDtypeStruct((TILE, len(late) * TILE), BF16)
-    lefts, downs = pltpu.VMEM((TILE, len(early) * TILE), BF16), pltpu.VMEM((len(early) * TILE, TILE), BF16)
-    total, far, late_h, late_l = call(
-        functools.partial(main_kernel, early, late), (whole, packed, part, part), [SMEM] + [VMEM] * (2 + n),
-        [lefts, lefts, downs, downs],
-        flops=6 * TILE**3 * len(early), nbytes=10 * 2**20,
-    )(place, same, other, *rights[:n])
-    downs = pltpu.VMEM((len(late) * TILE, TILE), BF16)
+                same = after(jnp.stack(pieces), one, two)
+                other = move(same, ("col",), lambda c: (c ^ 1,))
+
+    span = (steps + 1) // 2 * TILE
+    part = jax.ShapeDtypeStruct((TILE, TILE), BF16)
+    lefts, rights = pltpu.VMEM((TILE, span), BF16), pltpu.VMEM((span, 2 * TILE), BF16)
+    total, spare, far, late_h, late_l = call(
+        functools.partial(main_kernel, steps), (whole, whole, packed, part, part), [SMEM] + [VMEM] * (2 + 2 * steps),
+        [lefts, lefts, rights, rights], flops=12 * span * TILE**2, nbytes=10 * 2**20,
+    )(place, same, other, *mine[:steps], *others[:steps])
+    with jax.named_scope("spare"):
+        spare = move(spare, ("col",), lambda c: (c ^ 1,))
+    rights = pltpu.VMEM((TILE, TILE), BF16)
     own, away = call(
-        near_kernel, (half, half), [SMEM] + [VMEM] * (3 + 2 * len(late)), [downs, downs],
-        flops=6 * TILE**3 * len(late), nbytes=2**21,
-    )(place, total, late_h, late_l, *rights[n:])
+        near_kernel, (half, half), [SMEM] + [VMEM] * 6, [rights, rights], flops=6 * TILE**3, nbytes=2**21
+    )(place, total, spare, late_h, late_l, one, two)
     with jax.named_scope("away"):
-        came = shift(away, "layer", 1)
-    behind, ahead = after(behind, away), after(ahead, away)
-    with jax.named_scope("behind8"):
-        far_own = shift(behind, "row", 1)
-    cross = [(z0 * 2 + l0, (z0 - 1) % count * 2 + 1 - l0) for z0 in range(count) for l0 in range(2)]
-    with jax.named_scope("ahead8"):
-        far_other = lax.ppermute(ahead, ("row", "layer"), cross)
+        came = move(away, ("layer",), lambda l: (1 - l,))
+    one, two = after(one, away), after(two, away)
+    with jax.named_scope("far_own"):
+        far_own = onward(one)
+    with jax.named_scope("far_other"):
+        far_other = move(two, ("row", "col", "layer"), lambda z, c, l: (z - along(c % 2), c, 1 - l))
     return call(last_kernel, half, [SMEM] + [VMEM] * 6, flops=6 * PART * TILE * TILE, nbytes=2**20)(
         place, keep_mask, own, came, far, far_own, far_other
     )

time: 129 us -> 139 us (1.078)
  the two profiles are of different devices: /device:TPU:18 before, /device:TPU:16 now
where the time goes in v5:
time: 139 us; the launch traced here: 138 us
  starting transfers between devices  77.8 us (56%)
  waiting for transfers between devices  47.4 us (34%)
  Pallas kernels  11.1 us (8%)
  other arithmetic  1.75 us (1%)
    ppermute x24, starting transfers between devices, move(): lax.ppermute(value, axes, [(flat(at), flat(target(*at))) for at in points])  77.8 us
    ppermute x24, waiting for transfers between devices, move(): lax.ppermute(value, axes, [(flat(at), flat(target(*at))) for at in points])  47.4 us
    pallas_call x1, Pallas kernels, shards(): call(functools.partial(main_kernel, steps), (whole, whole, packed, part,...  5.05 us
    pallas_call x1, Pallas kernels, shards(): call(prep_kernel, (packed, half), [SMEM] + [ANY] * 4, [mask, mask, pltpu....  3.01 us
  transfers between devices with their start and end apart: 24, of which 16 were waited for; matrix products, arithmetic and copies ran while one was open for 1% of the time, Pallas kernels for 0%

profile of v5, /device:TPU:16, one launch (start us, length us, event | category | flops | bytes accessed | tf_op | source)
XLA Modules:
  0.0 138.4 jit_solution(6995498531980283388)
XLA Ops:
  0.0 0.6 pad_add_fusion.place
  0.6 3.0 %shard_map.55 = (f32[576,128]{1,0:T(8,128)}, f32[192,384]{1,0:T(8,128)}) custom-call(s32[3]{0:T(128)} %pad_add_fusion.place, s32[3,3]{1,0:T(4,128)} %lm_in.1, s32[3,3]{1,0:T(4,128)} %rm_in.1, f32[384,384]{1,0:T(8,128)} %left_in.1, f32[384,384]{1,0:T(8,128)} %right_in.1), custom_call_target="tpu_custom_call" | custom-call | bytes 2097152 | tf_op jit(solution)/shard_map/pallas_call | solution.py:242
  3.6 1.9 %collective-permute-start.2 = (f32[192,384]{1,0:T(8,128)}, f32[192,384]{1,0:T(8,128)S(1)}, u32[]{:S(2)}, u32[]{:S(2)}) collective-permute-start(f32[192,384]{1,0:T(8,128)} %get-tuple-element.27.refs_0_), channel_id=1, source_target_pairs={{0,2},{2,0},{4,6},{6,4},{8,10},{10,8},{12,14},{14,12},{16,18},{18,... | collective-permute-start | bytes 884744 | tf_op jit(solution)/shard_map/right_core/ppermute | solution.py:217
  5.5 3.9 %collective-permute-start.1 = (f32[192,384]{1,0:T(8,128)}, f32[192,384]{1,0:T(8,128)S(1)}, u32[]{:S(2)}, u32[]{:S(2)}) collective-permute-start(f32[192,384]{1,0:T(8,128)} %get-tuple-element.27.refs_0_), channel_id=1, source_target_pairs={{0,32},{2,482},{4,36},{6,486},{8,40},{10,490},{12,44},{14,494},{16... | collective-permute-start | bytes 884744 | tf_op jit(solution)/shard_map/own1/ppermute | solution.py:217
  9.4 0.0 collective-permute-done.2.refs_7_
  9.4 3.8 %collective-permute-start.3 = (f32[192,384]{1,0:T(8,128)S(1)}, f32[192,384]{1,0:T(8,128)S(1)}, u32[]{:S(2)}, u32[]{:S(2)}) collective-permute-start(f32[192,384]{1,0:T(8,128)S(1)} %collective-permute-done.2.refs_7_), channel_id=1, source_target_pairs={{0,32},{2,482},{4,36},{6,486},{8,40},{10,490},{12,44},{14,494},{16... | collective-permute-start | bytes 884744 | tf_op jit(solution)/shard_map/other1/ppermute | solution.py:217
  13.3 4.9 %collective-permute-start = (f32[576,128]{1,0:T(8,128)}, f32[576,128]{1,0:T(8,128)S(1)}, u32[]{:S(2)}, u32[]{:S(2)}) collective-permute-start(f32[576,128]{1,0:T(8,128)} %get-tuple-element.26), channel_id=1, source_target_pairs={{0,4},{2,6},{4,0},{6,2},{8,12},{10,14},{12,8},{14,10},{16,20},{18,... | collective-permute-start | bytes 884744 | tf_op jit(solution)/shard_map/left_x/ppermute | solution.py:217
  18.1 3.8 %collective-permute-done.1.refs_1_ = f32[192,384]{1,0:T(8,128)S(1)} collective-permute-done((f32[192,384]{1,0:T(8,128)}, f32[192,384]{1,0:T(8,128)S(1)}, u32[]{:S(2)}, u32[]{:S(2)}) %collective-permute-start.1) | collective-permute-done | bytes 294944 | tf_op jit(solution)/shard_map/own1/ppermute | solution.py:217
  21.9 1.9 %collective-permute-start.5 = (f32[192,384]{1,0:T(8,128)S(1)}, f32[192,384]{1,0:T(8,128)S(1)}, u32[]{:S(2)}, u32[]{:S(2)}) collective-permute-start(f32[192,384]{1,0:T(8,128)S(1)} %collective-permute-done.1.refs_1_), channel_id=1, source_target_pairs={{0,32},{2,482},{4,36},{6,486},{8,40},{10,490},{12,44},{14,494},{16... | collective-permute-start | bytes 884744 | tf_op jit(solution)/shard_map/own2/ppermute | solution.py:217
  23.8 1.2 collective-permute-done.3.refs_8_
  25.1 2.0 %collective-permute-start.6 = (f32[192,384]{1,0:T(8,128)S(1)}, f32[192,384]{1,0:T(8,128)S(1)}, u32[]{:S(2)}, u32[]{:S(2)}) collective-permute-start(f32[192,384]{1,0:T(8,128)S(1)} %collective-permute-done.3.refs_8_), channel_id=1, source_target_pairs={{0,32},{2,482},{4,36},{6,486},{8,40},{10,490},{12,44},{14,494},{16... | collective-permute-start | bytes 884744 | tf_op jit(solution)/shard_map/other2/ppermute | solution.py:217
  27.1 0.0 collective-permute-done
  27.1 1.0 fusion
  28.2 3.2 %collective-permute-start.4 = (f32[2,576,128]{2,1,0:T(8,128)S(1)}, f32[2,576,128]{2,1,0:T(8,128)S(1)}, u32[]{:S(2)}, u32[]{:S(2)}) collective-permute-start(f32[2,576,128]{2,1,0:T(8,128)S(1)} %get-tuple-element.30), channel_id=1, source_target_pairs={{0,8},{2,10},{4,12},{6,14},{8,16},{10,18},{12,20},{14,22},{16,24},... | collective-permute-start | bytes 1769480 | tf_op jit(solution)/shard_map/left_y1/ppermute | solution.py:217
  31.4 0.4 collective-permute-done.5.refs_2_
  31.7 3.5 %collective-permute-start.8 = (f32[192,384]{1,0:T(8,128)S(1)}, f32[192,384]{1,0:T(8,128)S(1)}, u32[]{:S(2)}, u32[]{:S(2)}) collective-permute-start(f32[192,384]{1,0:T(8,128)S(1)} %collective-permute-done.5.refs_2_), channel_id=1, source_target_pairs={{0,32},{2,482},{4,36},{6,486},{8,40},{10,490},{12,44},{14,494},{16... | collective-permute-start | bytes 884744 | tf_op jit(solution)/shard_map/own3/ppermute | solution.py:217
  35.2 0.0 collective-permute-done.6.refs_9_
  35.2 3.7 %collective-permute-start.9 = (f32[192,384]{1,0:T(8,128)S(1)}, f32[192,384]{1,0:T(8,128)S(1)}, u32[]{:S(2)}, u32[]{:S(2)}) collective-permute-start(f32[192,384]{1,0:T(8,128)S(1)} %collective-permute-done.6.refs_9_), channel_id=1, source_target_pairs={{0,32},{2,482},{4,36},{6,486},{8,40},{10,490},{12,44},{14,494},{16... | collective-permute-start | bytes 884744 | tf_op jit(solution)/shard_map/other3/ppermute | solution.py:217
  39.0 2.6 %collective-permute-start.7 = (f32[2,576,128]{2,1,0:T(8,128)S(1)}, f32[2,576,128]{2,1,0:T(8,128)S(1)}, u32[]{:S(2)}, u32[]{:S(2)}) collective-permute-start(f32[2,576,128]{2,1,0:T(8,128)S(1)} %get-tuple-element.30), channel_id=1, source_target_pairs={{0,16},{2,18},{4,20},{6,22},{8,24},{10,26},{12,28},{14,30},{16,0},... | collective-permute-start | bytes 1769480 | tf_op jit(solution)/shard_map/left_y2/ppermute | solution.py:217
  41.6 0.7 collective-permute-done.8.refs_3_
  42.3 3.2 %collective-permute-done.9.refs_10_ = f32[192,384]{1,0:T(8,128)S(1)} collective-permute-done((f32[192,384]{1,0:T(8,128)S(1)}, f32[192,384]{1,0:T(8,128)S(1)}, u32[]{:S(2)}, u32[]{:S(2)}) %collective-permute-start.9) | collective-permute-done | bytes 294944 | tf_op jit(solution)/shard_map/other3/ppermute | solution.py:217
  45.5 2.6 %collective-permute-start.10 = (f32[2,576,128]{2,1,0:T(8,128)S(1)}, f32[2,576,128]{2,1,0:T(8,128)S(1)}, u32[]{:S(2)}, u32[]{:S(2)}) collective-permute-start(f32[2,576,128]{2,1,0:T(8,128)S(1)} %get-tuple-element.30), channel_id=1, source_target_pairs={{0,24},{2,26},{4,28},{6,30},{8,0},{10,2},{12,4},{14,6},{16,8},{18,... | collective-permute-start | bytes 1769480 | tf_op jit(solution)/shard_map/left_y3/ppermute | solution.py:217
  48.1 0.0 collective-permute-done.4
  48.2 2.2 %collective-permute-start.13 = (f32[192,384]{1,0:T(8,128)S(1)}, f32[192,384]{1,0:T(8,128)S(1)}, u32[]{:S(2)}, u32[]{:S(2)}) collective-permute-start(f32[192,384]{1,0:T(8,128)S(1)} %collective-permute-done.9.refs_10_), channel_id=1, source_target_pairs={{0,32},{2,482},{4,36},{6,486},{8,40},{10,490},{12,44},{14,494},{16... | collective-permute-start | bytes 884744 | tf_op jit(solution)/shard_map/other4/ppermute | solution.py:217
  50.3 16.2 %collective-permute-start.11 = (f32[192,384]{1,0:T(8,128)S(1)}, f32[192,384]{1,0:T(8,128)S(1)}, u32[]{:S(2)}, u32[]{:S(2)}) collective-permute-start(f32[192,384]{1,0:T(8,128)S(1)} %collective-permute-done.8.refs_3_), channel_id=1, source_target_pairs={{0,32},{2,482},{4,36},{6,486},{8,40},{10,490},{12,44},{14,494},{16... | collective-permute-start | bytes 884744 | tf_op jit(solution)/shard_map/own4/ppermute | solution.py:217
  66.5 0.0 collective-permute-done.7
  66.5 3.1 %collective-permute-done.13.refs_11_ = f32[192,384]{1,0:T(8,128)S(1)} collective-permute-done((f32[192,384]{1,0:T(8,128)S(1)}, f32[192,384]{1,0:T(8,128)S(1)}, u32[]{:S(2)}, u32[]{:S(2)}) %collective-permute-start.13) | collective-permute-done | bytes 294944 | tf_op jit(solution)/shard_map/other4/ppermute | solution.py:217
  69.7 1.9 %collective-permute-start.14 = (f32[192,384]{1,0:T(8,128)S(1)}, f32[192,384]{1,0:T(8,128)S(1)}, u32[]{:S(2)}, u32[]{:S(2)}) collective-permute-start(f32[192,384]{1,0:T(8,128)S(1)} %collective-permute-done.13.refs_11_), channel_id=1, source_target_pairs={{0,32},{2,482},{4,36},{6,486},{8,40},{10,490},{12,44},{14,494},{16... | collective-permute-start | bytes 884744 | tf_op jit(solution)/shard_map/other5/ppermute | solution.py:217
  71.6 1.2 collective-permute-done.11.refs_4_
  72.8 2.3 %collective-permute-start.12 = (f32[192,384]{1,0:T(8,128)S(1)}, f32[192,384]{1,0:T(8,128)S(1)}, u32[]{:S(2)}, u32[]{:S(2)}) collective-permute-start(f32[192,384]{1,0:T(8,128)S(1)} %collective-permute-done.11.refs_4_), channel_id=1, source_target_pairs={{0,32},{2,482},{4,36},{6,486},{8,40},{10,490},{12,44},{14,494},{16... | collective-permute-start | bytes 884744 | tf_op jit(solution)/shard_map/own5/ppermute | solution.py:217
  75.1 0.0 collective-permute-done.10
  75.1 0.0 copy-start
  75.2 0.0 copy-start.2
  75.2 0.2 pad_maximum_fusion.same
  75.3 4.2 %collective-permute-done.14.refs_12_ = f32[192,384]{1,0:T(8,128)S(1)} collective-permute-done((f32[192,384]{1,0:T(8,128)S(1)}, f32[192,384]{1,0:T(8,128)S(1)}, u32[]{:S(2)}, u32[]{:S(2)}) %collective-permute-start.14) | collective-permute-done | bytes 294944 | tf_op jit(solution)/shard_map/other5/ppermute | solution.py:217
  79.5 3.2 %collective-permute-done.12.refs_5_ = f32[192,384]{1,0:T(8,128)S(1)} collective-permute-done((f32[192,384]{1,0:T(8,128)S(1)}, f32[192,384]{1,0:T(8,128)S(1)}, u32[]{:S(2)}, u32[]{:S(2)}) %collective-permute-start.12) | collective-permute-done | bytes 294944 | tf_op jit(solution)/shard_map/own5/ppermute | solution.py:217
  82.6 1.9 %collective-permute-start.15 = (f32[4,2,576,128]{3,2,1,0:T(8,128)S(1)}, f32[4,2,576,128]{3,2,1,0:T(8,128)S(1)}, u32[]{:S(2)}, u32[]{:S(2)}) collective-permute-start(f32[4,2,576,128]{3,2,1,0:T(8,128)S(1)} %pad_maximum_fusion.same), channel_id=1, source_target_pairs={{0,2},{2,0},{4,6},{6,4},{8,10},{10,8},{12,14},{14,12},{16,18},{18,... | collective-permute-start | bytes 7077896 | tf_op jit(solution)/shard_map/left_core/ppermute | solution.py:217
  84.6 1.9 %collective-permute-start.17 = (f32[192,384]{1,0:T(8,128)S(1)}, f32[192,384]{1,0:T(8,128)S(1)}, u32[]{:S(2)}, u32[]{:S(2)}) collective-permute-start(f32[192,384]{1,0:T(8,128)S(1)} %collective-permute-done.14.refs_12_), channel_id=1, source_target_pairs={{0,32},{2,482},{4,36},{6,486},{8,40},{10,490},{12,44},{14,494},{16... | collective-permute-start | bytes 884744 | tf_op jit(solution)/shard_map/other6/ppermute | solution.py:217
  86.5 2.3 %collective-permute-start.16 = (f32[192,384]{1,0:T(8,128)S(1)}, f32[192,384]{1,0:T(8,128)S(1)}, u32[]{:S(2)}, u32[]{:S(2)}) collective-permute-start(f32[192,384]{1,0:T(8,128)S(1)} %collective-permute-done.12.refs_5_), channel_id=1, source_target_pairs={{0,32},{2,482},{4,36},{6,486},{8,40},{10,490},{12,44},{14,494},{16... | collective-permute-start | bytes 884744 | tf_op jit(solution)/shard_map/own6/ppermute | solution.py:217
  88.8 5.6 %collective-permute-done.17.refs_13_ = f32[192,384]{1,0:T(8,128)S(1)} collective-permute-done((f32[192,384]{1,0:T(8,128)S(1)}, f32[192,384]{1,0:T(8,128)S(1)}, u32[]{:S(2)}, u32[]{:S(2)}) %collective-permute-start.17) | collective-permute-done | bytes 294944 | tf_op jit(solution)/shard_map/other6/ppermute | solution.py:217
  94.4 3.2 %collective-permute-done.16.refs_6_ = f32[192,384]{1,0:T(8,128)S(1)} collective-permute-done((f32[192,384]{1,0:T(8,128)S(1)}, f32[192,384]{1,0:T(8,128)S(1)}, u32[]{:S(2)}, u32[]{:S(2)}) %collective-permute-start.16) | collective-permute-done | bytes 294944 | tf_op jit(solution)/shard_map/own6/ppermute | solution.py:217
  97.5 0.0 collective-permute-done.15.other
  97.5 0.0 copy-done
  97.5 0.0 copy-done.2
  97.6 5.0 %shard_map.56 = (f32[384,384]{1,0:T(8,128)S(1)}, f32[384,384]{1,0:T(8,128)S(1)}, f32[576,128]{1,0:T(8,128)S(1)}, bf16[384,384]{1,0:T(8,128)(2,1)S(1)}, bf16[384,384]{1,0:T(8,128)(2,1)S(1)}) custom-call(s32[3]{0:T(128)S(1)} %copy-done, f32[4,2,576,128]{3,2,1,0:T(8,128)S(1)} %pad_maximum_fusion.same, f32[4,2,576,128]{3,2,1,0:T(8,128)S(1)} %collective-permute-done.15.other, ...), custom_call_target="tpu_custom_call" | custom-call | flops 2717908992 | bytes 10485760 | tf_op jit(solution)/shard_map/pallas_call | solution.py:282
  102.6 0.0 copy-start.1
  102.6 1.9 %collective-permute-start.18 = (f32[384,384]{1,0:T(8,128)S(1)}, f32[384,384]{1,0:T(8,128)S(1)}, u32[]{:S(2)}, u32[]{:S(2)}) collective-permute-start(f32[384,384]{1,0:T(8,128)S(1)} %get-tuple-element.39), channel_id=1, source_target_pairs={{0,2},{2,0},{4,6},{6,4},{8,10},{10,8},{12,14},{14,12},{16,18},{18,... | collective-permute-start | bytes 1769480 | tf_op jit(solution)/shard_map/spare/ppermute | solution.py:217
  104.5 1.9 %collective-permute-start.20 = (f32[192,384]{1,0:T(8,128)S(1)}, f32[192,384]{1,0:T(8,128)S(1)}, u32[]{:S(2)}, u32[]{:S(2)}) collective-permute-start(f32[192,384]{1,0:T(8,128)S(1)} %collective-permute-done.17.refs_13_), channel_id=1, source_target_pairs={{0,34},{2,480},{4,38},{6,484},{8,42},{10,488},{12,46},{14,492},{16... | collective-permute-start | bytes 884744 | tf_op jit(solution)/shard_map/other7/ppermute | solution.py:217
  106.5 1.9 %collective-permute-start.19 = (f32[192,384]{1,0:T(8,128)S(1)}, f32[192,384]{1,0:T(8,128)S(1)}, u32[]{:S(2)}, u32[]{:S(2)}) collective-permute-start(f32[192,384]{1,0:T(8,128)S(1)} %collective-permute-done.16.refs_6_), channel_id=1, source_target_pairs={{0,32},{2,482},{4,36},{6,486},{8,40},{10,490},{12,44},{14,494},{16... | collective-permute-start | bytes 884744 | tf_op jit(solution)/shard_map/own7/ppermute | solution.py:217
  108.4 4.2 %collective-permute-done.20.two = f32[192,384]{1,0:T(8,128)S(1)} collective-permute-done((f32[192,384]{1,0:T(8,128)S(1)}, f32[192,384]{1,0:T(8,128)S(1)}, u32[]{:S(2)}, u32[]{:S(2)}) %collective-permute-start.20) | collective-permute-done | bytes 294944 | tf_op jit(solution)/shard_map/other7/ppermute | solution.py:217
  112.6 5.0 %collective-permute-done.19.one = f32[192,384]{1,0:T(8,128)S(1)} collective-permute-done((f32[192,384]{1,0:T(8,128)S(1)}, f32[192,384]{1,0:T(8,128)S(1)}, u32[]{:S(2)}, u32[]{:S(2)}) %collective-permute-start.19) | collective-permute-done | bytes 294944 | tf_op jit(solution)/shard_map/own7/ppermute | solution.py:217
  117.6 0.0 collective-permute-done.18.spare
  117.6 1.3 shard_map.57
  119.0 3.6 %collective-permute-start.23 = (f32[192,384]{1,0:T(8,128)S(1)}, f32[192,384]{1,0:T(8,128)S(1)}, u32[]{:S(2)}, u32[]{:S(2)}) collective-permute-start(f32[192,384]{1,0:T(8,128)S(1)} %collective-permute-done.20.two), channel_id=1, source_target_pairs={{0,481},{1,480},{2,35},{3,34},{4,485},{5,484},{6,39},{7,38},{8,489... | collective-permute-start | bytes 884744 | tf_op jit(solution)/shard_map/far_other/ppermute | solution.py:217
  122.6 3.2 %collective-permute-start.22 = (f32[192,384]{1,0:T(8,128)S(1)}, f32[192,384]{1,0:T(8,128)S(1)}, u32[]{:S(2)}, u32[]{:S(2)}) collective-permute-start(f32[192,384]{1,0:T(8,128)S(1)} %collective-permute-done.19.one), channel_id=1, source_target_pairs={{0,32},{2,482},{4,36},{6,486},{8,40},{10,490},{12,44},{14,494},{16... | collective-permute-start | bytes 884744 | tf_op jit(solution)/shard_map/far_own/ppermute | solution.py:217
  125.8 2.4 %collective-permute-start.21 = (f32[192,384]{1,0:T(8,128)S(1)}, f32[192,384]{1,0:T(8,128)S(1)}, u32[]{:S(2)}, u32[]{:S(2)}) collective-permute-start(f32[192,384]{1,0:T(8,128)S(1)} %get-tuple-element.43), channel_id=1, source_target_pairs={{0,1},{1,0},{2,3},{3,2},{4,5},{5,4},{6,7},{7,6},{8,9},{9,8},{10,11... | collective-permute-start | bytes 884744 | tf_op jit(solution)/shard_map/away/ppermute | solution.py:217
  128.2 2.9 %collective-permute-done.23.right_other = f32[192,384]{1,0:T(8,128)S(1)} collective-permute-done((f32[192,384]{1,0:T(8,128)S(1)}, f32[192,384]{1,0:T(8,128)S(1)}, u32[]{:S(2)}, u32[]{:S(2)}) %collective-permute-start.23) | collective-permute-done | bytes 294944 | tf_op jit(solution)/shard_map/far_other/ppermute | solution.py:217
  131.1 1.3 collective-permute-done.22.right_own
  132.4 4.2 %collective-permute-done.21.came = f32[192,384]{1,0:T(8,128)S(1)} collective-permute-done((f32[192,384]{1,0:T(8,128)S(1)}, f32[192,384]{1,0:T(8,128)S(1)}, u32[]{:S(2)}, u32[]{:S(2)}) %collective-permute-start.21) | collective-permute-done | bytes 294944 | tf_op jit(solution)/shard_map/away/ppermute | solution.py:217
  136.7 0.0 copy-done.1
  136.7 1.7 %shard_map.58 = f32[192,384]{1,0:T(8,128)} custom-call(s32[3]{0:T(128)S(1)} %copy-done, s32[3,3]{1,0:T(4,128)S(1)} %copy-done.1, f32[192,384]{1,0:T(8,128)S(1)} %get-tuple-element.42.own, f32[192,384]{1,0:T(8,128)S(1)} %collective-permute-done.21.came, f32[576,128]{1,0:T(8,128)S(1)} %get-tuple-element.44.far, ...), custom_call_target="tpu_custom_call" | custom-call | flops 169869312 | bytes 1048576 | tf_op jit(solution)/shard_map/pallas_call | solution.py:299
Async XLA Ops:
  3.6 5.8 %collective-permute-start.2 = (f32[192,384]{1,0:T(8,128)}, f32[192,384]{1,0:T(8,128)S(1)}, u32[]{:S(2)}, u32[]{:S(2)}) collective-permute-start(f32[192,384]{1,0:T(8,128)} %get-tuple-element.27.refs_0_), channel_id=1, source_target_pairs={{0,2},{2,0},{4,6},{6,4},{8,10},{10,8},{12,14},{14,12},{16,18},{18,... | collective-permute-start | bytes 884744 | tf_op jit(solution)/shard_map/right_core/ppermute | solution.py:217
  5.5 16.4 %collective-permute-start.1 = (f32[192,384]{1,0:T(8,128)}, f32[192,384]{1,0:T(8,128)S(1)}, u32[]{:S(2)}, u32[]{:S(2)}) collective-permute-start(f32[192,384]{1,0:T(8,128)} %get-tuple-element.27.refs_0_), channel_id=1, source_target_pairs={{0,32},{2,482},{4,36},{6,486},{8,40},{10,490},{12,44},{14,494},{16... | collective-permute-start | bytes 884744 | tf_op jit(solution)/shard_map/own1/ppermute | solution.py:217
  9.4 15.6 %collective-permute-start.3 = (f32[192,384]{1,0:T(8,128)S(1)}, f32[192,384]{1,0:T(8,128)S(1)}, u32[]{:S(2)}, u32[]{:S(2)}) collective-permute-start(f32[192,384]{1,0:T(8,128)S(1)} %collective-permute-done.2.refs_7_), channel_id=1, source_target_pairs={{0,32},{2,482},{4,36},{6,486},{8,40},{10,490},{12,44},{14,494},{16... | collective-permute-start | bytes 884744 | tf_op jit(solution)/shard_map/other1/ppermute | solution.py:217
  13.3 13.8 %collective-permute-start = (f32[576,128]{1,0:T(8,128)}, f32[576,128]{1,0:T(8,128)S(1)}, u32[]{:S(2)}, u32[]{:S(2)}) collective-permute-start(f32[576,128]{1,0:T(8,128)} %get-tuple-element.26), channel_id=1, source_target_pairs={{0,4},{2,6},{4,0},{6,2},{8,12},{10,14},{12,8},{14,10},{16,20},{18,... | collective-permute-start | bytes 884744 | tf_op jit(solution)/shard_map/left_x/ppermute | solution.py:217
  21.9 9.8 %collective-permute-start.5 = (f32[192,384]{1,0:T(8,128)S(1)}, f32[192,384]{1,0:T(8,128)S(1)}, u32[]{:S(2)}, u32[]{:S(2)}) collective-permute-start(f32[192,384]{1,0:T(8,128)S(1)} %collective-permute-done.1.refs_1_), channel_id=1, source_target_pairs={{0,32},{2,482},{4,36},{6,486},{8,40},{10,490},{12,44},{14,494},{16... | collective-permute-start | bytes 884744 | tf_op jit(solution)/shard_map/own2/ppermute | solution.py:217
  25.1 10.1 %collective-permute-start.6 = (f32[192,384]{1,0:T(8,128)S(1)}, f32[192,384]{1,0:T(8,128)S(1)}, u32[]{:S(2)}, u32[]{:S(2)}) collective-permute-start(f32[192,384]{1,0:T(8,128)S(1)} %collective-permute-done.3.refs_8_), channel_id=1, source_target_pairs={{0,32},{2,482},{4,36},{6,486},{8,40},{10,490},{12,44},{14,494},{16... | collective-permute-start | bytes 884744 | tf_op jit(solution)/shard_map/other2/ppermute | solution.py:217
  28.2 20.0 %collective-permute-start.4 = (f32[2,576,128]{2,1,0:T(8,128)S(1)}, f32[2,576,128]{2,1,0:T(8,128)S(1)}, u32[]{:S(2)}, u32[]{:S(2)}) collective-permute-start(f32[2,576,128]{2,1,0:T(8,128)S(1)} %get-tuple-element.30), channel_id=1, source_target_pairs={{0,8},{2,10},{4,12},{6,14},{8,16},{10,18},{12,20},{14,22},{16,24},... | collective-permute-start | bytes 1769480 | tf_op jit(solution)/shard_map/left_y1/ppermute | solution.py:217
  31.7 10.6 %collective-permute-start.8 = (f32[192,384]{1,0:T(8,128)S(1)}, f32[192,384]{1,0:T(8,128)S(1)}, u32[]{:S(2)}, u32[]{:S(2)}) collective-permute-start(f32[192,384]{1,0:T(8,128)S(1)} %collective-permute-done.5.refs_2_), channel_id=1, source_target_pairs={{0,32},{2,482},{4,36},{6,486},{8,40},{10,490},{12,44},{14,494},{16... | collective-permute-start | bytes 884744 | tf_op jit(solution)/shard_map/own3/ppermute | solution.py:217
  35.2 10.3 %collective-permute-start.9 = (f32[192,384]{1,0:T(8,128)S(1)}, f32[192,384]{1,0:T(8,128)S(1)}, u32[]{:S(2)}, u32[]{:S(2)}) collective-permute-start(f32[192,384]{1,0:T(8,128)S(1)} %collective-permute-done.6.refs_9_), channel_id=1, source_target_pairs={{0,32},{2,482},{4,36},{6,486},{8,40},{10,490},{12,44},{14,494},{16... | collective-permute-start | bytes 884744 | tf_op jit(solution)/shard_map/other3/ppermute | solution.py:217
  39.0 27.6 %collective-permute-start.7 = (f32[2,576,128]{2,1,0:T(8,128)S(1)}, f32[2,576,128]{2,1,0:T(8,128)S(1)}, u32[]{:S(2)}, u32[]{:S(2)}) collective-permute-start(f32[2,576,128]{2,1,0:T(8,128)S(1)} %get-tuple-element.30), channel_id=1, source_target_pairs={{0,16},{2,18},{4,20},{6,22},{8,24},{10,26},{12,28},{14,30},{16,0},... | collective-permute-start | bytes 1769480 | tf_op jit(solution)/shard_map/left_y2/ppermute | solution.py:217
  45.5 29.6 %collective-permute-start.10 = (f32[2,576,128]{2,1,0:T(8,128)S(1)}, f32[2,576,128]{2,1,0:T(8,128)S(1)}, u32[]{:S(2)}, u32[]{:S(2)}) collective-permute-start(f32[2,576,128]{2,1,0:T(8,128)S(1)} %get-tuple-element.30), channel_id=1, source_target_pairs={{0,24},{2,26},{4,28},{6,30},{8,0},{10,2},{12,4},{14,6},{16,8},{18,... | collective-permute-start | bytes 1769480 | tf_op jit(solution)/shard_map/left_y3/ppermute | solution.py:217
  48.2 21.5 %collective-permute-start.13 = (f32[192,384]{1,0:T(8,128)S(1)}, f32[192,384]{1,0:T(8,128)S(1)}, u32[]{:S(2)}, u32[]{:S(2)}) collective-permute-start(f32[192,384]{1,0:T(8,128)S(1)} %collective-permute-done.9.refs_10_), channel_id=1, source_target_pairs={{0,32},{2,482},{4,36},{6,486},{8,40},{10,490},{12,44},{14,494},{16... | collective-permute-start | bytes 884744 | tf_op jit(solution)/shard_map/other4/ppermute | solution.py:217
  50.3 22.5 %collective-permute-start.11 = (f32[192,384]{1,0:T(8,128)S(1)}, f32[192,384]{1,0:T(8,128)S(1)}, u32[]{:S(2)}, u32[]{:S(2)}) collective-permute-start(f32[192,384]{1,0:T(8,128)S(1)} %collective-permute-done.8.refs_3_), channel_id=1, source_target_pairs={{0,32},{2,482},{4,36},{6,486},{8,40},{10,490},{12,44},{14,494},{16... | collective-permute-start | bytes 884744 | tf_op jit(solution)/shard_map/own4/ppermute | solution.py:217
  69.7 9.8 %collective-permute-start.14 = (f32[192,384]{1,0:T(8,128)S(1)}, f32[192,384]{1,0:T(8,128)S(1)}, u32[]{:S(2)}, u32[]{:S(2)}) collective-permute-start(f32[192,384]{1,0:T(8,128)S(1)} %collective-permute-done.13.refs_11_), channel_id=1, source_target_pairs={{0,32},{2,482},{4,36},{6,486},{8,40},{10,490},{12,44},{14,494},{16... | collective-permute-start | bytes 884744 | tf_op jit(solution)/shard_map/other5/ppermute | solution.py:217
  72.8 9.8 %collective-permute-start.12 = (f32[192,384]{1,0:T(8,128)S(1)}, f32[192,384]{1,0:T(8,128)S(1)}, u32[]{:S(2)}, u32[]{:S(2)}) collective-permute-start(f32[192,384]{1,0:T(8,128)S(1)} %collective-permute-done.11.refs_4_), channel_id=1, source_target_pairs={{0,32},{2,482},{4,36},{6,486},{8,40},{10,490},{12,44},{14,494},{16... | collective-permute-start | bytes 884744 | tf_op jit(solution)/shard_map/own5/ppermute | solution.py:217
  75.1 22.4 %copy-start = (s32[3]{0:T(128)S(1)}, s32[3]{0:T(128)}, u32[]{:S(2)}) copy-start(s32[3]{0:T(128)} %pad_add_fusion.place) | copy-start | bytes 40
  75.2 22.4 %copy-start.2 = (f32[192,384]{1,0:T(8,128)S(1)}, f32[192,384]{1,0:T(8,128)}, u32[]{:S(2)}) copy-start(f32[192,384]{1,0:T(8,128)} %get-tuple-element.27.refs_0_) | copy-start | bytes 884740
  82.6 14.9 %collective-permute-start.15 = (f32[4,2,576,128]{3,2,1,0:T(8,128)S(1)}, f32[4,2,576,128]{3,2,1,0:T(8,128)S(1)}, u32[]{:S(2)}, u32[]{:S(2)}) collective-permute-start(f32[4,2,576,128]{3,2,1,0:T(8,128)S(1)} %pad_maximum_fusion.same), channel_id=1, source_target_pairs={{0,2},{2,0},{4,6},{6,4},{8,10},{10,8},{12,14},{14,12},{16,18},{18,... | collective-permute-start | bytes 7077896 | tf_op jit(solution)/shard_map/left_core/ppermute | solution.py:217
  84.6 9.8 %collective-permute-start.17 = (f32[192,384]{1,0:T(8,128)S(1)}, f32[192,384]{1,0:T(8,128)S(1)}, u32[]{:S(2)}, u32[]{:S(2)}) collective-permute-start(f32[192,384]{1,0:T(8,128)S(1)} %collective-permute-done.14.refs_12_), channel_id=1, source_target_pairs={{0,32},{2,482},{4,36},{6,486},{8,40},{10,490},{12,44},{14,494},{16... | collective-permute-start | bytes 884744 | tf_op jit(solution)/shard_map/other6/ppermute | solution.py:217
  86.5 11.1 %collective-permute-start.16 = (f32[192,384]{1,0:T(8,128)S(1)}, f32[192,384]{1,0:T(8,128)S(1)}, u32[]{:S(2)}, u32[]{:S(2)}) collective-permute-start(f32[192,384]{1,0:T(8,128)S(1)} %collective-permute-done.12.refs_5_), channel_id=1, source_target_pairs={{0,32},{2,482},{4,36},{6,486},{8,40},{10,490},{12,44},{14,494},{16... | collective-permute-start | bytes 884744 | tf_op jit(solution)/shard_map/own6/ppermute | solution.py:217
  102.6 34.1 %copy-start.1 = (s32[3,3]{1,0:T(4,128)S(1)}, s32[3,3]{1,0:T(4,128)}, u32[]{:S(2)}) copy-start(s32[3,3]{1,0:T(4,128)} %keep.1) | copy-start | bytes 112
  102.6 15.0 %collective-permute-start.18 = (f32[384,384]{1,0:T(8,128)S(1)}, f32[384,384]{1,0:T(8,128)S(1)}, u32[]{:S(2)}, u32[]{:S(2)}) collective-permute-start(f32[384,384]{1,0:T(8,128)S(1)} %get-tuple-element.39), channel_id=1, source_target_pairs={{0,2},{2,0},{4,6},{6,4},{8,10},{10,8},{12,14},{14,12},{16,18},{18,... | collective-permute-start | bytes 1769480 | tf_op jit(solution)/shard_map/spare/ppermute | solution.py:217
  104.5 8.0 %collective-permute-start.20 = (f32[192,384]{1,0:T(8,128)S(1)}, f32[192,384]{1,0:T(8,128)S(1)}, u32[]{:S(2)}, u32[]{:S(2)}) collective-permute-start(f32[192,384]{1,0:T(8,128)S(1)} %collective-permute-done.17.refs_13_), channel_id=1, source_target_pairs={{0,34},{2,480},{4,38},{6,484},{8,42},{10,488},{12,46},{14,492},{16... | collective-permute-start | bytes 884744 | tf_op jit(solution)/shard_map/other7/ppermute | solution.py:217
  106.5 11.2 %collective-permute-start.19 = (f32[192,384]{1,0:T(8,128)S(1)}, f32[192,384]{1,0:T(8,128)S(1)}, u32[]{:S(2)}, u32[]{:S(2)}) collective-permute-start(f32[192,384]{1,0:T(8,128)S(1)} %collective-permute-done.16.refs_6_), channel_id=1, source_target_pairs={{0,32},{2,482},{4,36},{6,486},{8,40},{10,490},{12,44},{14,494},{16... | collective-permute-start | bytes 884744 | tf_op jit(solution)/shard_map/own7/ppermute | solution.py:217
  119.0 12.2 %collective-permute-start.23 = (f32[192,384]{1,0:T(8,128)S(1)}, f32[192,384]{1,0:T(8,128)S(1)}, u32[]{:S(2)}, u32[]{:S(2)}) collective-permute-start(f32[192,384]{1,0:T(8,128)S(1)} %collective-permute-done.20.two), channel_id=1, source_target_pairs={{0,481},{1,480},{2,35},{3,34},{4,485},{5,484},{6,39},{7,38},{8,489... | collective-permute-start | bytes 884744 | tf_op jit(solution)/shard_map/far_other/ppermute | solution.py:217
  122.6 9.8 %collective-permute-start.22 = (f32[192,384]{1,0:T(8,128)S(1)}, f32[192,384]{1,0:T(8,128)S(1)}, u32[]{:S(2)}, u32[]{:S(2)}) collective-permute-start(f32[192,384]{1,0:T(8,128)S(1)} %collective-permute-done.19.one), channel_id=1, source_target_pairs={{0,32},{2,482},{4,36},{6,486},{8,40},{10,490},{12,44},{14,494},{16... | collective-permute-start | bytes 884744 | tf_op jit(solution)/shard_map/far_own/ppermute | solution.py:217
  125.8 10.9 %collective-permute-start.21 = (f32[192,384]{1,0:T(8,128)S(1)}, f32[192,384]{1,0:T(8,128)S(1)}, u32[]{:S(2)}, u32[]{:S(2)}) collective-permute-start(f32[192,384]{1,0:T(8,128)S(1)} %get-tuple-element.43), channel_id=1, source_target_pairs={{0,1},{1,0},{2,3},{3,2},{4,5},{5,4},{6,7},{7,6},{8,9},{9,8},{10,11... | collective-permute-start | bytes 884744 | tf_op jit(solution)/shard_map/away/ppermute | solution.py:217

commit v6 on v5

--- a/solution.py
+++ b/solution.py
@@ -15,7 +15,6 @@
 F32 = jnp.float32
 BF16 = jnp.bfloat16
 VMEM = pl.BlockSpec(memory_space=pltpu.VMEM)
-SMEM = pl.BlockSpec(memory_space=pltpu.SMEM)
 ANY = pl.BlockSpec(memory_space=pl.ANY)
 
 
@@ -51,10 +50,14 @@
     return block * mask[p : p + 1, q : q + 1].astype(F32)
 
 
-def prep_kernel(place, lm_in, rm_in, left_in, right_in, left_out, right_out, lm, rm, left, right, sems):
+def coordinates():
+    return lax.axis_index("row"), lax.axis_index("col"), lax.axis_index("layer")
+
+
+def prep_kernel(lm_in, rm_in, left_in, right_in, left_out, right_out, lm, rm, left, right, sems):
+    place = coordinates()
     z, col, layer = place[0], place[1], place[2]
-    for copy in fetch(((rm_in, rm), (right_in, right), (lm_in, lm), (left_in, left)), sems):
-        copy.wait()
+    copies = fetch(((rm_in, rm), (right_in, right), (lm_in, lm), (left_in, left)), sems)
     far = lax.rem(z + 8, 16) == col
 
     def right_side(outer, near):
@@ -82,13 +85,15 @@
             mid = masked(left, lm, 1, q, slice(near * HALF, (near + 1) * HALF))
             left_out[start : start + PART, :] = jnp.concatenate([end, mid] if near == 0 else [mid, end], 0)
 
+    copies[0].wait()
+    copies[1].wait()
     for side in (0, 1):
-
-        @pl.when(layer == side)
-        def _(outer=2 * side, near=side):
-            right_side(outer, near)
-            pl.when(far)(lambda: left_far(outer, near))
-            pl.when(jnp.logical_not(far))(lambda: left_side(outer, near))
+        pl.when(layer == side)(functools.partial(right_side, 2 * side, side))
+    copies[2].wait()
+    copies[3].wait()
+    for side in (0, 1):
+        pl.when((layer == side) & far)(functools.partial(left_far, 2 * side, side))
+        pl.when((layer == side) & jnp.logical_not(far))(functools.partial(left_side, 2 * side, side))
 
 
 def split(value):
@@ -114,10 +119,14 @@
     return jnp.concatenate([one[:BLK], two[:BLK], one[BLK:], two[BLK:]], 0)
 
 
+def along(core):
+    return 1 - 2 * core
+
+
 def panel_index(place, k):
-    col = place[1]
-    mine = lax.rem(k, 2) == lax.rem(col, 2)
-    return mine, lax.rem(col // 4 - k // 4 + 4, 4), lax.bitwise_xor(lax.rem(k // 2, 2), lax.rem(col // 2, 2))
+    col, core = place[1], lax.rem(k, 2)
+    hops = lax.rem((col // 4 - k // 4) * along(core) + 4, 4)
+    return core == lax.rem(col, 2), hops, lax.bitwise_xor(lax.rem(k // 2, 2), lax.rem(col // 2, 2))
 
 
 def tile_at(place, step):
@@ -147,25 +156,26 @@
     rh[rows, lanes], rl[rows, lanes] = split(join_right(one, two))
 
 
-def main_kernel(steps, place, same, other, *refs):
-    mine, others = refs[:steps], refs[steps : 2 * steps]
-    total, spare, far, late_h, late_l, lh, ll, rh, rl = refs[2 * steps :]
+def fill_rights(place, tiles, rh, rl):
     core = lax.rem(place[1], 2)
+    for start in range(0, len(tiles), 2):
+        one = tiles[start][...]
+        if start == 0:
+            one = jnp.where(core == 0, one, jnp.zeros_like(one))
+        two = tiles[start + 1][...] if start + 1 < len(tiles) else jnp.zeros_like(one)
+        fill_right(one, two, rh, rl, start * PART)
+
+
+def spare_kernel(steps, same, other, *refs):
+    place = coordinates()
+    tiles, (spare, lh, ll, far, late_h, late_l, rh, rl) = refs[:steps], refs[steps:]
     for start in range(0, steps, 2):
-        column = start * PART
-        paired = start + 1 < steps
-        one, two = tile_at(place, start), tile_at(place, start + 1) if paired else None
-        fill_left(place, same, other, one, two, lh, ll, column)
-        for lane, tiles in ((0, mine), (TILE, others)):
-            one = tiles[start][...]
-            if start == 0:
-                one = jnp.where(core == 0, one, jnp.zeros_like(one))
-            two = tiles[start + 1][...] if paired else jnp.zeros_like(one)
-            fill_right(one, two, rh, rl, column, lane)
-    value = triple((lh[...], ll[...]), (rh[...], rl[...]))
-    total[...] = value[:, :TILE]
-    spare[...] = value[:, TILE:]
-    fill_left(place, same, other, tile_at(place, steps), tile_at(place, -steps), late_h, late_l, 0)
+        two = tile_at(place, start + 1) if start + 1 < steps else None
+        fill_left(place, same, other, tile_at(place, start), two, lh, ll, start * PART)
+    fill_rights(place, tiles, rh, rl)
+    spare[...] = triple((lh[...], ll[...]), (rh[...], rl[...]))
+    for number, step in enumerate((steps, steps + 1)):
+        fill_left(place, same, other, tile_at(place, step), tile_at(place, -step), late_h, late_l, number * TILE)
     here, y, x = panel_index(place, lax.rem(place[0] + 8, 16))
 
     @pl.when(here)
@@ -177,30 +187,41 @@
         far[...] = other[y, x]
 
 
-def near_kernel(place, total, spare, late_h, late_l, one, two, own, away, rh, rl):
+def main_kernel(steps, lh, ll, *refs):
+    place = coordinates()
+    tiles, (total, rh, rl) = refs[:steps], refs[steps:]
+    fill_rights(place, tiles, rh, rl)
+    total[...] = triple((lh[...], ll[...]), (rh[...], rl[...]))
+
+
+def near_kernel(total, spare, late_h, late_l, one, two, three, four, own, away, rh, rl):
+    place = coordinates()
     fill_right(one[...], two[...], rh, rl, 0)
+    fill_right(three[...], four[...], rh, rl, TILE)
     value = total[...] + spare[...] + triple((late_h[...], late_l[...]), (rh[...], rl[...]))
     layer = place[2]
+    away[PART:] = jnp.zeros((8, TILE), F32)
 
     @pl.when(layer == 0)
     def _():
         own[...] = value[:PART]
-        away[...] = value[PART:]
+        away[:PART] = value[PART:]
 
     @pl.when(layer == 1)
     def _():
         own[...] = value[PART:]
-        away[...] = value[:PART]
-
-
-def last_kernel(place, keep, own, came, far, right_own, right_other, out):
+        away[:PART] = value[:PART]
+
+
+def last_kernel(keep, own, came, far, right_own, right_other, out):
+    place = coordinates()
     layer = place[2]
     first = layer == 0
     mine, other = right_own[...], right_other[...]
     low, high = jnp.where(first, mine, other), jnp.where(first, other, mine)
     right = jnp.concatenate([low, high[BLK:], high[:BLK]], 0)
     left = jnp.concatenate([far[:PART], far[PART : 2 * PART], far[2 * PART :]], 1)
-    value = own[...] + came[...] + triple(split(left), split(right))
+    value = own[...] + came[:PART] + triple(split(left), split(right))
     row = lax.broadcasted_iota(jnp.int32, (PART, BLK), 0) + layer * PART
     centre = (row >= BLK) & (row < 2 * BLK)
     for q in range(3):
@@ -217,10 +238,6 @@
     return lax.ppermute(value, axes, [(flat(at), flat(target(*at))) for at in points])
 
 
-def along(core):
-    return 1 - 2 * core
-
-
 def onward(value):
     return move(value, ("row", "col"), lambda z, c: (z + along(c % 2), c))
 
@@ -231,33 +248,29 @@
 
 def shards(left_values, left_mask, right_values, right_mask, keep_mask):
     count = lax.axis_size("row")
-    cols = lax.axis_size("col")
-    z, col, layer = lax.axis_index("row"), lax.axis_index("col"), lax.axis_index("layer")
-    place = jnp.stack([z, col, layer]).astype(jnp.int32)
     packed = jax.ShapeDtypeStruct((TILE + PART, BLK), F32)
     half = jax.ShapeDtypeStruct((PART, TILE), F32)
     whole = jax.ShapeDtypeStruct((TILE, TILE), F32)
     mask = pltpu.VMEM((3, 3), jnp.int32)
 
     left, right = call(
-        prep_kernel, (packed, half), [SMEM] + [ANY] * 4,
+        prep_kernel, (packed, half), [ANY] * 4,
         [mask, mask, pltpu.VMEM((TILE, TILE), F32), pltpu.VMEM((TILE, TILE), F32), pltpu.SemaphoreType.DMA((4,))],
         nbytes=2**21, limit=60,
-    )(place, left_mask, right_mask, left_values, right_values)
+    )(left_mask, right_mask, left_values, right_values)
 
     with jax.named_scope("right_core"):
         right_other = move(right, ("col",), lambda c: (c ^ 1,))
     with jax.named_scope("left_x"):
         left_x = move(left, ("col",), lambda c: (c ^ 2,))
     pair = jnp.stack([left, left_x])
-    pieces = [pair]
 
     steps = count // 2 - 1
     mine, others = [right], [right_other]
     one, two = right, right_other
     for step in range(1, steps + 1):
-        if 4 <= step <= 6:
-            one, two = after(one, pieces[step - 3]), after(two, pieces[step - 3])
+        if step == 3:
+            one, two = after(one, pair), after(two, pair)
         with jax.named_scope(f"own{step}"):
             one = onward(one)
         with jax.named_scope(f"other{step}"):
@@ -267,28 +280,41 @@
                 two = move(two, ("row", "col"), lambda z, c: (z + along(c % 2), c ^ 1))
         mine.append(one)
         others.append(two)
-        if step <= 3:
-            with jax.named_scope(f"left_y{step}"):
-                pair = after(pair, one, two)
-                pieces.append(move(pair, ("col",), lambda c: (c + 4 * step,)))
-        if step == steps - 2:
+        if step == 1:
+            with jax.named_scope("left_y1"):
+                left_y1 = move(after(pair, one, two), ("col",), lambda c: (c + 4 * along(c % 2),))
+        if step == 2:
+            with jax.named_scope("left_y3"):
+                left_y3 = move(after(pair, one, two), ("col",), lambda c: (c - 4 * along(c % 2),))
+        if step == 3:
+            with jax.named_scope("left_y2"):
+                left_y2 = move(after(left_y1, one), ("col",), lambda c: (c + 4 * along(c % 2),))
+        if step == 5:
             with jax.named_scope("left_core"):
-                same = after(jnp.stack(pieces), one, two)
+                same = after(jnp.stack([pair, left_y1, left_y2, left_y3]), one, two)
                 other = move(same, ("col",), lambda c: (c ^ 1,))
 
-    span = (steps + 1) // 2 * TILE
-    part = jax.ShapeDtypeStruct((TILE, TILE), BF16)
-    lefts, rights = pltpu.VMEM((TILE, span), BF16), pltpu.VMEM((span, 2 * TILE), BF16)
-    total, spare, far, late_h, late_l = call(
-        functools.partial(main_kernel, steps), (whole, whole, packed, part, part), [SMEM] + [VMEM] * (2 + 2 * steps),
-        [lefts, lefts, rights, rights], flops=12 * span * TILE**2, nbytes=10 * 2**20,
-    )(place, same, other, *mine[:steps], *others[:steps])
+    with jax.named_scope("crossed"):
+        crossed = move(others[steps - 1], ("col",), lambda c: (c ^ 1,))
+    early = steps - 1
+    span = early * PART
+    part = jax.ShapeDtypeStruct((TILE, 2 * TILE), BF16)
+    lefts = jax.ShapeDtypeStruct((TILE, span), BF16)
+    rights = [pltpu.VMEM((span, TILE), BF16)] * 2
+    spare, left_h, left_l, far, late_h, late_l = call(
+        functools.partial(spare_kernel, early), (whole, lefts, lefts, packed, part, part), [VMEM] * (2 + early),
+        rights, flops=6 * span * TILE**2, nbytes=6 * 2**20,
+    )(same, other, *others[:early])
+    total = call(
+        functools.partial(main_kernel, early), whole, [VMEM] * (2 + early), rights,
+        flops=6 * span * TILE**2, nbytes=4 * 2**20,
+    )(left_h, left_l, *mine[:early])
     with jax.named_scope("spare"):
         spare = move(spare, ("col",), lambda c: (c ^ 1,))
-    rights = pltpu.VMEM((TILE, TILE), BF16)
+    rights = pltpu.VMEM((2 * TILE, TILE), BF16)
     own, away = call(
-        near_kernel, (half, half), [SMEM] + [VMEM] * 6, [rights, rights], flops=6 * TILE**3, nbytes=2**21
-    )(place, total, spare, late_h, late_l, one, two)
+        near_kernel, (half, jax.ShapeDtypeStruct((PART + 8, TILE), F32)), [VMEM] * 8, [rights, rights], flops=12 * TILE**3, nbytes=2**21
+    )(total, spare, late_h, late_l, mine[early], crossed, one, two)
     with jax.named_scope("away"):
         came = move(away, ("layer",), lambda l: (1 - l,))
     one, two = after(one, away), after(two, away)
@@ -296,8 +322,8 @@
         far_own = onward(one)
     with jax.named_scope("far_other"):
         far_other = move(two, ("row", "col", "layer"), lambda z, c, l: (z - along(c % 2), c, 1 - l))
-    return call(last_kernel, half, [SMEM] + [VMEM] * 6, flops=6 * PART * TILE * TILE, nbytes=2**20)(
-        place, keep_mask, own, came, far, far_own, far_other
+    return call(last_kernel, half, [VMEM] * 6, flops=6 * PART * TILE * TILE, nbytes=2**20)(
+        keep_mask, own, came, far, far_own, far_other
     )
 
 

time: 139 us -> 117 us (0.84)
  the two profiles are of different devices: /device:TPU:16 before, /device:TPU:1 now
where the time goes in v6:
time: 117 us; the launch traced here: 116 us
  starting transfers between devices  84.4 us (72%)
  waiting for transfers between devices  21.1 us (18%)
  Pallas kernels  9.16 us (8%)
  other arithmetic  1.2 us (1%)
    ppermute x25, starting transfers between devices, move(): lax.ppermute(value, axes, [(flat(at), flat(target(*at))) for at in points])  84.4 us
    ppermute x25, waiting for transfers between devices, move(): lax.ppermute(value, axes, [(flat(at), flat(target(*at))) for at in points])  21.1 us
    pallas_call x1, Pallas kernels, shards(): call(functools.partial(spare_kernel, early), (whole, lefts, lefts, packed...  2.78 us
  transfers between devices with their start and end apart: 25, of which 8 were waited for; matrix products, arithmetic and copies ran while one was open for 1% of the time, Pallas kernels for 4%

profile of v6, /device:TPU:1, one launch (start us, length us, event | category | flops | bytes accessed | tf_op | source)
XLA Modules:
  0.0 116.3 jit_solution(13673703773839912836)
XLA Ops:
  0.0 2.3 %shard_map.55 = (f32[576,128]{1,0:T(8,128)}, f32[192,384]{1,0:T(8,128)}) custom-call(s32[3,3]{1,0:T(4,128)} %lm_in.1, s32[3,3]{1,0:T(4,128)} %rm_in.1, f32[384,384]{1,0:T(8,128)} %left_in.1, f32[384,384]{1,0:T(8,128)} %right_in.1), custom_call_target="tpu_custom_call" | custom-call | bytes 2097152 | tf_op jit(solution)/shard_map/pallas_call | solution.py:256
  2.3 8.8 %collective-permute-start.2 = (f32[192,384]{1,0:T(8,128)}, f32[192,384]{1,0:T(8,128)S(1)}, u32[]{:S(2)}, u32[]{:S(2)}) collective-permute-start(f32[192,384]{1,0:T(8,128)} %get-tuple-element.24.refs_0_), channel_id=1, source_target_pairs={{0,2},{2,0},{4,6},{6,4},{8,10},{10,8},{12,14},{14,12},{16,18},{18,... | collective-permute-start | bytes 884744 | tf_op jit(solution)/shard_map/right_core/ppermute | solution.py:238
  11.1 5.7 %collective-permute-start.1 = (f32[192,384]{1,0:T(8,128)}, f32[192,384]{1,0:T(8,128)S(1)}, u32[]{:S(2)}, u32[]{:S(2)}) collective-permute-start(f32[192,384]{1,0:T(8,128)} %get-tuple-element.24.refs_0_), channel_id=1, source_target_pairs={{0,32},{2,482},{4,36},{6,486},{8,40},{10,490},{12,44},{14,494},{16... | collective-permute-start | bytes 884744 | tf_op jit(solution)/shard_map/own1/ppermute | solution.py:238
  16.9 4.7 %collective-permute-start = (f32[576,128]{1,0:T(8,128)}, f32[576,128]{1,0:T(8,128)S(1)}, u32[]{:S(2)}, u32[]{:S(2)}) collective-permute-start(f32[576,128]{1,0:T(8,128)} %get-tuple-element.23), channel_id=1, source_target_pairs={{0,4},{2,6},{4,0},{6,2},{8,12},{10,14},{12,8},{14,10},{16,20},{18,... | collective-permute-start | bytes 884744 | tf_op jit(solution)/shard_map/left_x/ppermute | solution.py:238
  21.5 0.0 collective-permute-done.2.refs_0_
  21.5 2.6 %collective-permute-start.3 = (f32[192,384]{1,0:T(8,128)S(1)}, f32[192,384]{1,0:T(8,128)S(1)}, u32[]{:S(2)}, u32[]{:S(2)}) collective-permute-start(f32[192,384]{1,0:T(8,128)S(1)} %collective-permute-done.2.refs_0_), channel_id=1, source_target_pairs={{0,32},{2,482},{4,36},{6,486},{8,40},{10,490},{12,44},{14,494},{16... | collective-permute-start | bytes 884744 | tf_op jit(solution)/shard_map/other1/ppermute | solution.py:238
  24.2 0.0 collective-permute-done.1.refs_1_
  24.2 2.6 %collective-permute-start.5 = (f32[192,384]{1,0:T(8,128)S(1)}, f32[192,384]{1,0:T(8,128)S(1)}, u32[]{:S(2)}, u32[]{:S(2)}) collective-permute-start(f32[192,384]{1,0:T(8,128)S(1)} %collective-permute-done.1.refs_1_), channel_id=1, source_target_pairs={{0,32},{2,482},{4,36},{6,486},{8,40},{10,490},{12,44},{14,494},{16... | collective-permute-start | bytes 884744 | tf_op jit(solution)/shard_map/own2/ppermute | solution.py:238
  26.8 0.0 collective-permute-done
  26.9 1.0 fusion
  27.9 1.4 %collective-permute-done.3.refs_1_ = f32[192,384]{1,0:T(8,128)S(1)} collective-permute-done((f32[192,384]{1,0:T(8,128)S(1)}, f32[192,384]{1,0:T(8,128)S(1)}, u32[]{:S(2)}, u32[]{:S(2)}) %collective-permute-start.3) | collective-permute-done | bytes 294944 | tf_op jit(solution)/shard_map/other1/ppermute | solution.py:238
  29.3 4.6 %collective-permute-start.4 = (f32[2,576,128]{2,1,0:T(8,128)S(1)}, f32[2,576,128]{2,1,0:T(8,128)S(1)}, u32[]{:S(2)}, u32[]{:S(2)}) collective-permute-start(f32[2,576,128]{2,1,0:T(8,128)S(1)} %get-tuple-element.25), channel_id=1, source_target_pairs={{0,8},{2,26},{4,12},{6,30},{8,16},{10,2},{12,20},{14,6},{16,24},{1... | collective-permute-start | bytes 1769480 | tf_op jit(solution)/shard_map/left_y1/ppermute | solution.py:238
  33.9 3.6 %collective-permute-start.8 = (f32[192,384]{1,0:T(8,128)S(1)}, f32[192,384]{1,0:T(8,128)S(1)}, u32[]{:S(2)}, u32[]{:S(2)}) collective-permute-start(f32[192,384]{1,0:T(8,128)S(1)} %collective-permute-done.3.refs_1_), channel_id=1, source_target_pairs={{0,32},{2,482},{4,36},{6,486},{8,40},{10,490},{12,44},{14,494},{16... | collective-permute-start | bytes 884744 | tf_op jit(solution)/shard_map/other2/ppermute | solution.py:238
  37.5 0.0 collective-permute-done.5.refs_2_
  37.5 2.3 %collective-permute-start.6 = (f32[192,384]{1,0:T(8,128)S(1)}, f32[192,384]{1,0:T(8,128)S(1)}, u32[]{:S(2)}, u32[]{:S(2)}) collective-permute-start(f32[192,384]{1,0:T(8,128)S(1)} %collective-permute-done.5.refs_2_), channel_id=1, source_target_pairs={{0,32},{2,482},{4,36},{6,486},{8,40},{10,490},{12,44},{14,494},{16... | collective-permute-start | bytes 884744 | tf_op jit(solution)/shard_map/own3/ppermute | solution.py:238
  39.8 1.9 %collective-permute-done.8.refs_2_ = f32[192,384]{1,0:T(8,128)S(1)} collective-permute-done((f32[192,384]{1,0:T(8,128)S(1)}, f32[192,384]{1,0:T(8,128)S(1)}, u32[]{:S(2)}, u32[]{:S(2)}) %collective-permute-start.8) | collective-permute-done | bytes 294944 | tf_op jit(solution)/shard_map/other2/ppermute | solution.py:238
  41.7 4.5 %collective-permute-start.12 = (f32[192,384]{1,0:T(8,128)S(1)}, f32[192,384]{1,0:T(8,128)S(1)}, u32[]{:S(2)}, u32[]{:S(2)}) collective-permute-start(f32[192,384]{1,0:T(8,128)S(1)} %collective-permute-done.8.refs_2_), channel_id=1, source_target_pairs={{0,32},{2,482},{4,36},{6,486},{8,40},{10,490},{12,44},{14,494},{16... | collective-permute-start | bytes 884744 | tf_op jit(solution)/shard_map/other3/ppermute | solution.py:238
  46.2 1.9 %collective-permute-start.9 = (f32[2,576,128]{2,1,0:T(8,128)S(1)}, f32[2,576,128]{2,1,0:T(8,128)S(1)}, u32[]{:S(2)}, u32[]{:S(2)}) collective-permute-start(f32[2,576,128]{2,1,0:T(8,128)S(1)} %get-tuple-element.25), channel_id=1, source_target_pairs={{0,24},{2,10},{4,28},{6,14},{8,0},{10,18},{12,4},{14,22},{16,8},{1... | collective-permute-start | bytes 1769480 | tf_op jit(solution)/shard_map/left_y3/ppermute | solution.py:238
  48.1 0.0 collective-permute-done.6.refs_3_
  48.1 0.0 collective-permute-done.4
  48.1 4.6 %collective-permute-start.7 = (f32[2,576,128]{2,1,0:T(8,128)S(1)}, f32[2,576,128]{2,1,0:T(8,128)S(1)}, u32[]{:S(2)}, u32[]{:S(2)}) collective-permute-start(f32[2,576,128]{2,1,0:T(8,128)S(1)} %collective-permute-done.4), channel_id=1, source_target_pairs={{0,8},{2,26},{4,12},{6,30},{8,16},{10,2},{12,20},{14,6},{16,24},{1... | collective-permute-start | bytes 1769480 | tf_op jit(solution)/shard_map/left_y2/ppermute | solution.py:238
  52.7 1.9 %collective-permute-start.10 = (f32[192,384]{1,0:T(8,128)S(1)}, f32[192,384]{1,0:T(8,128)S(1)}, u32[]{:S(2)}, u32[]{:S(2)}) collective-permute-start(f32[192,384]{1,0:T(8,128)S(1)} %collective-permute-done.6.refs_3_), channel_id=1, source_target_pairs={{0,32},{2,482},{4,36},{6,486},{8,40},{10,490},{12,44},{14,494},{16... | collective-permute-start | bytes 884744 | tf_op jit(solution)/shard_map/own4/ppermute | solution.py:238
  54.6 0.0 collective-permute-done.12.refs_3_
  54.6 2.1 %collective-permute-start.13 = (f32[192,384]{1,0:T(8,128)S(1)}, f32[192,384]{1,0:T(8,128)S(1)}, u32[]{:S(2)}, u32[]{:S(2)}) collective-permute-start(f32[192,384]{1,0:T(8,128)S(1)} %collective-permute-done.12.refs_3_), channel_id=1, source_target_pairs={{0,32},{2,482},{4,36},{6,486},{8,40},{10,490},{12,44},{14,494},{16... | collective-permute-start | bytes 884744 | tf_op jit(solution)/shard_map/other4/ppermute | solution.py:238
  56.7 3.8 %collective-permute-done.10.refs_4_ = f32[192,384]{1,0:T(8,128)S(1)} collective-permute-done((f32[192,384]{1,0:T(8,128)S(1)}, f32[192,384]{1,0:T(8,128)S(1)}, u32[]{:S(2)}, u32[]{:S(2)}) %collective-permute-start.10) | collective-permute-done | bytes 294944 | tf_op jit(solution)/shard_map/own4/ppermute | solution.py:238
  60.5 3.1 %collective-permute-start.11 = (f32[192,384]{1,0:T(8,128)S(1)}, f32[192,384]{1,0:T(8,128)S(1)}, u32[]{:S(2)}, u32[]{:S(2)}) collective-permute-start(f32[192,384]{1,0:T(8,128)S(1)} %collective-permute-done.10.refs_4_), channel_id=1, source_target_pairs={{0,32},{2,482},{4,36},{6,486},{8,40},{10,490},{12,44},{14,494},{16... | collective-permute-start | bytes 884744 | tf_op jit(solution)/shard_map/own5/ppermute | solution.py:238
  63.6 0.0 collective-permute-done.13.refs_4_
  63.6 2.9 %collective-permute-start.14 = (f32[192,384]{1,0:T(8,128)S(1)}, f32[192,384]{1,0:T(8,128)S(1)}, u32[]{:S(2)}, u32[]{:S(2)}) collective-permute-start(f32[192,384]{1,0:T(8,128)S(1)} %collective-permute-done.13.refs_4_), channel_id=1, source_target_pairs={{0,32},{2,482},{4,36},{6,486},{8,40},{10,490},{12,44},{14,494},{16... | collective-permute-start | bytes 884744 | tf_op jit(solution)/shard_map/other5/ppermute | solution.py:238
  66.5 0.0 collective-permute-done.9
  66.5 0.0 collective-permute-done.7
  66.6 0.2 pad_maximum_fusion.same
  66.7 0.0 copy-start
  66.7 1.5 %collective-permute-done.11.refs_5_ = f32[192,384]{1,0:T(8,128)S(1)} collective-permute-done((f32[192,384]{1,0:T(8,128)S(1)}, f32[192,384]{1,0:T(8,128)S(1)}, u32[]{:S(2)}, u32[]{:S(2)}) %collective-permute-start.11) | collective-permute-done | bytes 294944 | tf_op jit(solution)/shard_map/own5/ppermute | solution.py:238
  68.2 3.2 %collective-permute-done.14.refs_5_ = f32[192,384]{1,0:T(8,128)S(1)} collective-permute-done((f32[192,384]{1,0:T(8,128)S(1)}, f32[192,384]{1,0:T(8,128)S(1)}, u32[]{:S(2)}, u32[]{:S(2)}) %collective-permute-start.14) | collective-permute-done | bytes 294944 | tf_op jit(solution)/shard_map/other5/ppermute | solution.py:238
  71.4 3.2 %collective-permute-start.15 = (f32[4,2,576,128]{3,2,1,0:T(8,128)S(1)}, f32[4,2,576,128]{3,2,1,0:T(8,128)S(1)}, u32[]{:S(2)}, u32[]{:S(2)}) collective-permute-start(f32[4,2,576,128]{3,2,1,0:T(8,128)S(1)} %pad_maximum_fusion.same), channel_id=1, source_target_pairs={{0,2},{2,0},{4,6},{6,4},{8,10},{10,8},{12,14},{14,12},{16,18},{18,... | collective-permute-start | bytes 7077896 | tf_op jit(solution)/shard_map/left_core/ppermute | solution.py:238
  74.5 2.8 %collective-permute-start.17 = (f32[192,384]{1,0:T(8,128)S(1)}, f32[192,384]{1,0:T(8,128)S(1)}, u32[]{:S(2)}, u32[]{:S(2)}) collective-permute-start(f32[192,384]{1,0:T(8,128)S(1)} %collective-permute-done.11.refs_5_), channel_id=1, source_target_pairs={{0,32},{2,482},{4,36},{6,486},{8,40},{10,490},{12,44},{14,494},{16... | collective-permute-start | bytes 884744 | tf_op jit(solution)/shard_map/own6/ppermute | solution.py:238
  77.3 2.1 %collective-permute-start.18 = (f32[192,384]{1,0:T(8,128)S(1)}, f32[192,384]{1,0:T(8,128)S(1)}, u32[]{:S(2)}, u32[]{:S(2)}) collective-permute-start(f32[192,384]{1,0:T(8,128)S(1)} %collective-permute-done.14.refs_5_), channel_id=1, source_target_pairs={{0,32},{2,482},{4,36},{6,486},{8,40},{10,490},{12,44},{14,494},{16... | collective-permute-start | bytes 884744 | tf_op jit(solution)/shard_map/other6/ppermute | solution.py:238
  79.4 0.0 collective-permute-done.15.other
  79.4 2.8 %shard_map.56 = (f32[384,384]{1,0:T(8,128)S(1)}, bf16[384,1152]{1,0:T(8,128)(2,1)S(1)}, bf16[384,1152]{1,0:T(8,128)(2,1)S(1)}, f32[576,128]{1,0:T(8,128)S(1)}, b...) custom-call(f32[4,2,576,128]{3,2,1,0:T(8,128)S(1)} %pad_maximum_fusion.same, ...), custom_call_target="tpu_custom_call" | custom-call | flops 1019215872 | bytes 6291456 | tf_op jit(solution)/shard_map/pallas_call | solution.py:304
  82.2 1.9 %collective-permute-start.16 = (f32[384,384]{1,0:T(8,128)S(1)}, f32[384,384]{1,0:T(8,128)S(1)}, u32[]{:S(2)}, u32[]{:S(2)}) collective-permute-start(f32[384,384]{1,0:T(8,128)S(1)} %get-tuple-element.33), channel_id=1, source_target_pairs={{0,2},{2,0},{4,6},{6,4},{8,10},{10,8},{12,14},{14,12},{16,18},{18,... | collective-permute-start | bytes 1769480 | tf_op jit(solution)/shard_map/spare/ppermute | solution.py:238
  84.1 0.0 collective-permute-done.17.one
  84.2 4.1 %collective-permute-start.20 = (f32[192,384]{1,0:T(8,128)S(1)}, f32[192,384]{1,0:T(8,128)S(1)}, u32[]{:S(2)}, u32[]{:S(2)}) collective-permute-start(f32[192,384]{1,0:T(8,128)S(1)} %collective-permute-done.17.one), channel_id=1, source_target_pairs={{0,32},{2,482},{4,36},{6,486},{8,40},{10,490},{12,44},{14,494},{16... | collective-permute-start | bytes 884744 | tf_op jit(solution)/shard_map/own7/ppermute | solution.py:238
  88.2 0.0 collective-permute-done.18
  88.2 3.1 %collective-permute-start.21 = (f32[192,384]{1,0:T(8,128)S(1)}, f32[192,384]{1,0:T(8,128)S(1)}, u32[]{:S(2)}, u32[]{:S(2)}) collective-permute-start(f32[192,384]{1,0:T(8,128)S(1)} %collective-permute-done.18), channel_id=1, source_target_pairs={{0,34},{2,480},{4,38},{6,484},{8,42},{10,488},{12,46},{14,492},{16... | collective-permute-start | bytes 884744 | tf_op jit(solution)/shard_map/other7/ppermute | solution.py:238
  91.3 1.9 %collective-permute-start.19 = (f32[192,384]{1,0:T(8,128)S(1)}, f32[192,384]{1,0:T(8,128)S(1)}, u32[]{:S(2)}, u32[]{:S(2)}) collective-permute-start(f32[192,384]{1,0:T(8,128)S(1)} %collective-permute-done.18), channel_id=1, source_target_pairs={{0,2},{2,0},{4,6},{6,4},{8,10},{10,8},{12,14},{14,12},{16,18},{18,... | collective-permute-start | bytes 884744 | tf_op jit(solution)/shard_map/crossed/ppermute | solution.py:238
  93.3 0.0 copy-done
  93.3 1.7 %shard_map.57.total = f32[384,384]{1,0:T(8,128)S(1)} custom-call(bf16[384,1152]{1,0:T(8,128)(2,1)S(1)} %get-tuple-element.31.lh, bf16[384,1152]{1,0:T(8,128)(2,1)S(1)} %get-tuple-element.32.ll, f32[192,384]{1,0:T(8,128)S(1)} %copy-done, f32[192,384]{1,0:T(8,128)S(1)} %collective-permute-done.1.refs_1_, f32[192,384]{1,0:T(8,128)S(1)} %collective-permute-done.5.refs_2_, ...), custom_call_target="tpu_custom_call" | custom-call | flops 1019215872 | bytes 4194304 | tf_op jit(solution)/shard_map/pallas_call | solution.py:308
  95.0 0.0 copy-start.1
  95.0 0.0 collective-permute-done.20.three
  95.0 2.5 %collective-permute-done.21.four = f32[192,384]{1,0:T(8,128)S(1)} collective-permute-done((f32[192,384]{1,0:T(8,128)S(1)}, f32[192,384]{1,0:T(8,128)S(1)}, u32[]{:S(2)}, u32[]{:S(2)}) %collective-permute-start.21) | collective-permute-done | bytes 294944 | tf_op jit(solution)/shard_map/other7/ppermute | solution.py:238
  97.5 0.0 collective-permute-done.19.two
  97.5 0.0 collective-permute-done.16.spare
  97.5 1.2 %shard_map.58 = (f32[192,384]{1,0:T(8,128)S(1)}, f32[200,384]{1,0:T(8,128)S(1)}) custom-call(f32[384,384]{1,0:T(8,128)S(1)} %shard_map.57.total, f32[384,384]{1,0:T(8,128)S(1)} %collective-permute-done.16.spare, bf16[384,768]{1,0:T(8,128)(2,1)S(1)} %get-tuple-element.34.late_h, bf16[384,768]{1,0:T(8,128)(2,1)S(1)} %get-tuple-element.35.late_l, ...), custom_call_target="tpu_custom_call" | custom-call | flops 679477248 | bytes 2097152 | tf_op jit(solution)/shard_map/pallas_call | solution.py:315
  98.7 2.5 %collective-permute-start.22 = (f32[200,384]{1,0:T(8,128)S(1)}, f32[200,384]{1,0:T(8,128)S(1)}, u32[]{:S(2)}, u32[]{:S(2)}) collective-permute-start(f32[200,384]{1,0:T(8,128)S(1)} %get-tuple-element.37), channel_id=1, source_target_pairs={{0,1},{1,0},{2,3},{3,2},{4,5},{5,4},{6,7},{7,6},{8,9},{9,8},{10,11... | collective-permute-start | bytes 921608 | tf_op jit(solution)/shard_map/away/ppermute | solution.py:238
  101.2 2.3 %collective-permute-start.24 = (f32[192,384]{1,0:T(8,128)S(1)}, f32[192,384]{1,0:T(8,128)S(1)}, u32[]{:S(2)}, u32[]{:S(2)}) collective-permute-start(f32[192,384]{1,0:T(8,128)S(1)} %collective-permute-done.21.four), channel_id=1, source_target_pairs={{0,481},{1,480},{2,35},{3,34},{4,485},{5,484},{6,39},{7,38},{8,489... | collective-permute-start | bytes 884744 | tf_op jit(solution)/shard_map/far_other/ppermute | solution.py:238
  103.6 4.7 %collective-permute-start.23 = (f32[192,384]{1,0:T(8,128)S(1)}, f32[192,384]{1,0:T(8,128)S(1)}, u32[]{:S(2)}, u32[]{:S(2)}) collective-permute-start(f32[192,384]{1,0:T(8,128)S(1)} %collective-permute-done.20.three), channel_id=1, source_target_pairs={{0,32},{2,482},{4,36},{6,486},{8,40},{10,490},{12,44},{14,494},{16... | collective-permute-start | bytes 884744 | tf_op jit(solution)/shard_map/far_own/ppermute | solution.py:238
  108.3 4.5 %collective-permute-done.24.right_other = f32[192,384]{1,0:T(8,128)S(1)} collective-permute-done((f32[192,384]{1,0:T(8,128)S(1)}, f32[192,384]{1,0:T(8,128)S(1)}, u32[]{:S(2)}, u32[]{:S(2)}) %collective-permute-start.24) | collective-permute-done | bytes 294944 | tf_op jit(solution)/shard_map/far_other/ppermute | solution.py:238
  112.8 0.0 collective-permute-done.23.right_own
  112.8 2.3 %collective-permute-done.22.came = f32[200,384]{1,0:T(8,128)S(1)} collective-permute-done((f32[200,384]{1,0:T(8,128)S(1)}, f32[200,384]{1,0:T(8,128)S(1)}, u32[]{:S(2)}, u32[]{:S(2)}) %collective-permute-start.22) | collective-permute-done | bytes 307232 | tf_op jit(solution)/shard_map/away/ppermute | solution.py:238
  115.1 0.0 copy-done.1
  115.1 1.2 %shard_map.59 = f32[192,384]{1,0:T(8,128)} custom-call(s32[3,3]{1,0:T(4,128)S(1)} %copy-done.1, f32[192,384]{1,0:T(8,128)S(1)} %get-tuple-element.36.own, f32[200,384]{1,0:T(8,128)S(1)} %collective-permute-done.22.came, f32[576,128]{1,0:T(8,128)S(1)} %get-tuple-element.38.far, f32[192,384]{1,0:T(8,128)S(1)} %collective-permute-done.23.right_own, ...), custom_call_target="tpu_custom_call" | custom-call | flops 169869312 | bytes 1048576 | tf_op jit(solution)/shard_map/pallas_call | solution.py:325
Async XLA Ops:
  2.3 19.2 %collective-permute-start.2 = (f32[192,384]{1,0:T(8,128)}, f32[192,384]{1,0:T(8,128)S(1)}, u32[]{:S(2)}, u32[]{:S(2)}) collective-permute-start(f32[192,384]{1,0:T(8,128)} %get-tuple-element.24.refs_0_), channel_id=1, source_target_pairs={{0,2},{2,0},{4,6},{6,4},{8,10},{10,8},{12,14},{14,12},{16,18},{18,... | collective-permute-start | bytes 884744 | tf_op jit(solution)/shard_map/right_core/ppermute | solution.py:238
  11.1 13.1 %collective-permute-start.1 = (f32[192,384]{1,0:T(8,128)}, f32[192,384]{1,0:T(8,128)S(1)}, u32[]{:S(2)}, u32[]{:S(2)}) collective-permute-start(f32[192,384]{1,0:T(8,128)} %get-tuple-element.24.refs_0_), channel_id=1, source_target_pairs={{0,32},{2,482},{4,36},{6,486},{8,40},{10,490},{12,44},{14,494},{16... | collective-permute-start | bytes 884744 | tf_op jit(solution)/shard_map/own1/ppermute | solution.py:238
  16.9 10.0 %collective-permute-start = (f32[576,128]{1,0:T(8,128)}, f32[576,128]{1,0:T(8,128)S(1)}, u32[]{:S(2)}, u32[]{:S(2)}) collective-permute-start(f32[576,128]{1,0:T(8,128)} %get-tuple-element.23), channel_id=1, source_target_pairs={{0,4},{2,6},{4,0},{6,2},{8,12},{10,14},{12,8},{14,10},{16,20},{18,... | collective-permute-start | bytes 884744 | tf_op jit(solution)/shard_map/left_x/ppermute | solution.py:238
  21.5 7.8 %collective-permute-start.3 = (f32[192,384]{1,0:T(8,128)S(1)}, f32[192,384]{1,0:T(8,128)S(1)}, u32[]{:S(2)}, u32[]{:S(2)}) collective-permute-start(f32[192,384]{1,0:T(8,128)S(1)} %collective-permute-done.2.refs_0_), channel_id=1, source_target_pairs={{0,32},{2,482},{4,36},{6,486},{8,40},{10,490},{12,44},{14,494},{16... | collective-permute-start | bytes 884744 | tf_op jit(solution)/shard_map/other1/ppermute | solution.py:238
  24.2 13.3 %collective-permute-start.5 = (f32[192,384]{1,0:T(8,128)S(1)}, f32[192,384]{1,0:T(8,128)S(1)}, u32[]{:S(2)}, u32[]{:S(2)}) collective-permute-start(f32[192,384]{1,0:T(8,128)S(1)} %collective-permute-done.1.refs_1_), channel_id=1, source_target_pairs={{0,32},{2,482},{4,36},{6,486},{8,40},{10,490},{12,44},{14,494},{16... | collective-permute-start | bytes 884744 | tf_op jit(solution)/shard_map/own2/ppermute | solution.py:238
  29.3 18.8 %collective-permute-start.4 = (f32[2,576,128]{2,1,0:T(8,128)S(1)}, f32[2,576,128]{2,1,0:T(8,128)S(1)}, u32[]{:S(2)}, u32[]{:S(2)}) collective-permute-start(f32[2,576,128]{2,1,0:T(8,128)S(1)} %get-tuple-element.25), channel_id=1, source_target_pairs={{0,8},{2,26},{4,12},{6,30},{8,16},{10,2},{12,20},{14,6},{16,24},{1... | collective-permute-start | bytes 1769480 | tf_op jit(solution)/shard_map/left_y1/ppermute | solution.py:238
  33.9 7.8 %collective-permute-start.8 = (f32[192,384]{1,0:T(8,128)S(1)}, f32[192,384]{1,0:T(8,128)S(1)}, u32[]{:S(2)}, u32[]{:S(2)}) collective-permute-start(f32[192,384]{1,0:T(8,128)S(1)} %collective-permute-done.3.refs_1_), channel_id=1, source_target_pairs={{0,32},{2,482},{4,36},{6,486},{8,40},{10,490},{12,44},{14,494},{16... | collective-permute-start | bytes 884744 | tf_op jit(solution)/shard_map/other2/ppermute | solution.py:238
  37.5 10.6 %collective-permute-start.6 = (f32[192,384]{1,0:T(8,128)S(1)}, f32[192,384]{1,0:T(8,128)S(1)}, u32[]{:S(2)}, u32[]{:S(2)}) collective-permute-start(f32[192,384]{1,0:T(8,128)S(1)} %collective-permute-done.5.refs_2_), channel_id=1, source_target_pairs={{0,32},{2,482},{4,36},{6,486},{8,40},{10,490},{12,44},{14,494},{16... | collective-permute-start | bytes 884744 | tf_op jit(solution)/shard_map/own3/ppermute | solution.py:238
  41.7 12.9 %collective-permute-start.12 = (f32[192,384]{1,0:T(8,128)S(1)}, f32[192,384]{1,0:T(8,128)S(1)}, u32[]{:S(2)}, u32[]{:S(2)}) collective-permute-start(f32[192,384]{1,0:T(8,128)S(1)} %collective-permute-done.8.refs_2_), channel_id=1, source_target_pairs={{0,32},{2,482},{4,36},{6,486},{8,40},{10,490},{12,44},{14,494},{16... | collective-permute-start | bytes 884744 | tf_op jit(solution)/shard_map/other3/ppermute | solution.py:238
  46.2 20.4 %collective-permute-start.9 = (f32[2,576,128]{2,1,0:T(8,128)S(1)}, f32[2,576,128]{2,1,0:T(8,128)S(1)}, u32[]{:S(2)}, u32[]{:S(2)}) collective-permute-start(f32[2,576,128]{2,1,0:T(8,128)S(1)} %get-tuple-element.25), channel_id=1, source_target_pairs={{0,24},{2,10},{4,28},{6,14},{8,0},{10,18},{12,4},{14,22},{16,8},{1... | collective-permute-start | bytes 1769480 | tf_op jit(solution)/shard_map/left_y3/ppermute | solution.py:238
  48.1 18.4 %collective-permute-start.7 = (f32[2,576,128]{2,1,0:T(8,128)S(1)}, f32[2,576,128]{2,1,0:T(8,128)S(1)}, u32[]{:S(2)}, u32[]{:S(2)}) collective-permute-start(f32[2,576,128]{2,1,0:T(8,128)S(1)} %collective-permute-done.4), channel_id=1, source_target_pairs={{0,8},{2,26},{4,12},{6,30},{8,16},{10,2},{12,20},{14,6},{16,24},{1... | collective-permute-start | bytes 1769480 | tf_op jit(solution)/shard_map/left_y2/ppermute | solution.py:238
  52.7 7.8 %collective-permute-start.10 = (f32[192,384]{1,0:T(8,128)S(1)}, f32[192,384]{1,0:T(8,128)S(1)}, u32[]{:S(2)}, u32[]{:S(2)}) collective-permute-start(f32[192,384]{1,0:T(8,128)S(1)} %collective-permute-done.6.refs_3_), channel_id=1, source_target_pairs={{0,32},{2,482},{4,36},{6,486},{8,40},{10,490},{12,44},{14,494},{16... | collective-permute-start | bytes 884744 | tf_op jit(solution)/shard_map/own4/ppermute | solution.py:238
  54.6 9.0 %collective-permute-start.13 = (f32[192,384]{1,0:T(8,128)S(1)}, f32[192,384]{1,0:T(8,128)S(1)}, u32[]{:S(2)}, u32[]{:S(2)}) collective-permute-start(f32[192,384]{1,0:T(8,128)S(1)} %collective-permute-done.12.refs_3_), channel_id=1, source_target_pairs={{0,32},{2,482},{4,36},{6,486},{8,40},{10,490},{12,44},{14,494},{16... | collective-permute-start | bytes 884744 | tf_op jit(solution)/shard_map/other4/ppermute | solution.py:238
  60.5 7.8 %collective-permute-start.11 = (f32[192,384]{1,0:T(8,128)S(1)}, f32[192,384]{1,0:T(8,128)S(1)}, u32[]{:S(2)}, u32[]{:S(2)}) collective-permute-start(f32[192,384]{1,0:T(8,128)S(1)} %collective-permute-done.10.refs_4_), channel_id=1, source_target_pairs={{0,32},{2,482},{4,36},{6,486},{8,40},{10,490},{12,44},{14,494},{16... | collective-permute-start | bytes 884744 | tf_op jit(solution)/shard_map/own5/ppermute | solution.py:238
  63.6 7.8 %collective-permute-start.14 = (f32[192,384]{1,0:T(8,128)S(1)}, f32[192,384]{1,0:T(8,128)S(1)}, u32[]{:S(2)}, u32[]{:S(2)}) collective-permute-start(f32[192,384]{1,0:T(8,128)S(1)} %collective-permute-done.13.refs_4_), channel_id=1, source_target_pairs={{0,32},{2,482},{4,36},{6,486},{8,40},{10,490},{12,44},{14,494},{16... | collective-permute-start | bytes 884744 | tf_op jit(solution)/shard_map/other5/ppermute | solution.py:238
  66.7 26.5 %copy-start = (f32[192,384]{1,0:T(8,128)S(1)}, f32[192,384]{1,0:T(8,128)}, u32[]{:S(2)}) copy-start(f32[192,384]{1,0:T(8,128)} %get-tuple-element.24.refs_0_) | copy-start | bytes 884740
  71.4 8.0 %collective-permute-start.15 = (f32[4,2,576,128]{3,2,1,0:T(8,128)S(1)}, f32[4,2,576,128]{3,2,1,0:T(8,128)S(1)}, u32[]{:S(2)}, u32[]{:S(2)}) collective-permute-start(f32[4,2,576,128]{3,2,1,0:T(8,128)S(1)} %pad_maximum_fusion.same), channel_id=1, source_target_pairs={{0,2},{2,0},{4,6},{6,4},{8,10},{10,8},{12,14},{14,12},{16,18},{18,... | collective-permute-start | bytes 7077896 | tf_op jit(solution)/shard_map/left_core/ppermute | solution.py:238
  74.5 9.6 %collective-permute-start.17 = (f32[192,384]{1,0:T(8,128)S(1)}, f32[192,384]{1,0:T(8,128)S(1)}, u32[]{:S(2)}, u32[]{:S(2)}) collective-permute-start(f32[192,384]{1,0:T(8,128)S(1)} %collective-permute-done.11.refs_5_), channel_id=1, source_target_pairs={{0,32},{2,482},{4,36},{6,486},{8,40},{10,490},{12,44},{14,494},{16... | collective-permute-start | bytes 884744 | tf_op jit(solution)/shard_map/own6/ppermute | solution.py:238
  77.3 10.9 %collective-permute-start.18 = (f32[192,384]{1,0:T(8,128)S(1)}, f32[192,384]{1,0:T(8,128)S(1)}, u32[]{:S(2)}, u32[]{:S(2)}) collective-permute-start(f32[192,384]{1,0:T(8,128)S(1)} %collective-permute-done.14.refs_5_), channel_id=1, source_target_pairs={{0,32},{2,482},{4,36},{6,486},{8,40},{10,490},{12,44},{14,494},{16... | collective-permute-start | bytes 884744 | tf_op jit(solution)/shard_map/other6/ppermute | solution.py:238
  82.2 15.3 %collective-permute-start.16 = (f32[384,384]{1,0:T(8,128)S(1)}, f32[384,384]{1,0:T(8,128)S(1)}, u32[]{:S(2)}, u32[]{:S(2)}) collective-permute-start(f32[384,384]{1,0:T(8,128)S(1)} %get-tuple-element.33), channel_id=1, source_target_pairs={{0,2},{2,0},{4,6},{6,4},{8,10},{10,8},{12,14},{14,12},{16,18},{18,... | collective-permute-start | bytes 1769480 | tf_op jit(solution)/shard_map/spare/ppermute | solution.py:238
  84.2 10.8 %collective-permute-start.20 = (f32[192,384]{1,0:T(8,128)S(1)}, f32[192,384]{1,0:T(8,128)S(1)}, u32[]{:S(2)}, u32[]{:S(2)}) collective-permute-start(f32[192,384]{1,0:T(8,128)S(1)} %collective-permute-done.17.one), channel_id=1, source_target_pairs={{0,32},{2,482},{4,36},{6,486},{8,40},{10,490},{12,44},{14,494},{16... | collective-permute-start | bytes 884744 | tf_op jit(solution)/shard_map/own7/ppermute | solution.py:238
  88.2 9.3 %collective-permute-start.21 = (f32[192,384]{1,0:T(8,128)S(1)}, f32[192,384]{1,0:T(8,128)S(1)}, u32[]{:S(2)}, u32[]{:S(2)}) collective-permute-start(f32[192,384]{1,0:T(8,128)S(1)} %collective-permute-done.18), channel_id=1, source_target_pairs={{0,34},{2,480},{4,38},{6,484},{8,42},{10,488},{12,46},{14,492},{16... | collective-permute-start | bytes 884744 | tf_op jit(solution)/shard_map/other7/ppermute | solution.py:238
  91.3 6.2 %collective-permute-start.19 = (f32[192,384]{1,0:T(8,128)S(1)}, f32[192,384]{1,0:T(8,128)S(1)}, u32[]{:S(2)}, u32[]{:S(2)}) collective-permute-start(f32[192,384]{1,0:T(8,128)S(1)} %collective-permute-done.18), channel_id=1, source_target_pairs={{0,2},{2,0},{4,6},{6,4},{8,10},{10,8},{12,14},{14,12},{16,18},{18,... | collective-permute-start | bytes 884744 | tf_op jit(solution)/shard_map/crossed/ppermute | solution.py:238
  95.0 20.1 %copy-start.1 = (s32[3,3]{1,0:T(4,128)S(1)}, s32[3,3]{1,0:T(4,128)}, u32[]{:S(2)}) copy-start(s32[3,3]{1,0:T(4,128)} %keep.1) | copy-start | bytes 112
  98.7 16.4 %collective-permute-start.22 = (f32[200,384]{1,0:T(8,128)S(1)}, f32[200,384]{1,0:T(8,128)S(1)}, u32[]{:S(2)}, u32[]{:S(2)}) collective-permute-start(f32[200,384]{1,0:T(8,128)S(1)} %get-tuple-element.37), channel_id=1, source_target_pairs={{0,1},{1,0},{2,3},{3,2},{4,5},{5,4},{6,7},{7,6},{8,9},{9,8},{10,11... | collective-permute-start | bytes 921608 | tf_op jit(solution)/shard_map/away/ppermute | solution.py:238
  101.2 11.6 %collective-permute-start.24 = (f32[192,384]{1,0:T(8,128)S(1)}, f32[192,384]{1,0:T(8,128)S(1)}, u32[]{:S(2)}, u32[]{:S(2)}) collective-permute-start(f32[192,384]{1,0:T(8,128)S(1)} %collective-permute-done.21.four), channel_id=1, source_target_pairs={{0,481},{1,480},{2,35},{3,34},{4,485},{5,484},{6,39},{7,38},{8,489... | collective-permute-start | bytes 884744 | tf_op jit(solution)/shard_map/far_other/ppermute | solution.py:238
  103.6 9.3 %collective-permute-start.23 = (f32[192,384]{1,0:T(8,128)S(1)}, f32[192,384]{1,0:T(8,128)S(1)}, u32[]{:S(2)}, u32[]{:S(2)}) collective-permute-start(f32[192,384]{1,0:T(8,128)S(1)} %collective-permute-done.20.three), channel_id=1, source_target_pairs={{0,32},{2,482},{4,36},{6,486},{8,40},{10,490},{12,44},{14,494},{16... | collective-permute-start | bytes 884744 | tf_op jit(solution)/shard_map/far_own/ppermute | solution.py:238

commit v7 on v6

--- a/solution.py
+++ b/solution.py
@@ -156,23 +156,19 @@
     rh[rows, lanes], rl[rows, lanes] = split(join_right(one, two))
 
 
-def fill_rights(place, tiles, rh, rl):
-    core = lax.rem(place[1], 2)
-    for start in range(0, len(tiles), 2):
-        one = tiles[start][...]
-        if start == 0:
-            one = jnp.where(core == 0, one, jnp.zeros_like(one))
-        two = tiles[start + 1][...] if start + 1 < len(tiles) else jnp.zeros_like(one)
-        fill_right(one, two, rh, rl, start * PART)
+def fill_rights(tiles, rh, rl):
+    held = [jnp.zeros((PART, TILE), F32) if tile is None else tile[...] for tile in tiles]
+    for start in range(0, len(held), 2):
+        fill_right(held[start], held[start + 1], rh, rl, start * PART)
 
 
 def spare_kernel(steps, same, other, *refs):
     place = coordinates()
-    tiles, (spare, lh, ll, far, late_h, late_l, rh, rl) = refs[:steps], refs[steps:]
+    tiles, (spare, lh, ll, far, late_h, late_l, rh, rl) = refs[: steps - 1], refs[steps - 1 :]
     for start in range(0, steps, 2):
         two = tile_at(place, start + 1) if start + 1 < steps else None
         fill_left(place, same, other, tile_at(place, start), two, lh, ll, start * PART)
-    fill_rights(place, tiles, rh, rl)
+    fill_rights((None, *tiles), rh, rl)
     spare[...] = triple((lh[...], ll[...]), (rh[...], rl[...]))
     for number, step in enumerate((steps, steps + 1)):
         fill_left(place, same, other, tile_at(place, step), tile_at(place, -step), late_h, late_l, number * TILE)
@@ -188,9 +184,8 @@
 
 
 def main_kernel(steps, lh, ll, *refs):
-    place = coordinates()
     tiles, (total, rh, rl) = refs[:steps], refs[steps:]
-    fill_rights(place, tiles, rh, rl)
+    fill_rights(tiles, rh, rl)
     total[...] = triple((lh[...], ll[...]), (rh[...], rl[...]))
 
 
@@ -259,25 +254,27 @@
         nbytes=2**21, limit=60,
     )(left_mask, right_mask, left_values, right_values)
 
-    with jax.named_scope("right_core"):
-        right_other = move(right, ("col",), lambda c: (c ^ 1,))
     with jax.named_scope("left_x"):
         left_x = move(left, ("col",), lambda c: (c ^ 2,))
     pair = jnp.stack([left, left_x])
 
     steps = count // 2 - 1
-    mine, others = [right], [right_other]
-    one, two = right, right_other
+    mine, others = [right], [None]
+    one = two = right
     for step in range(1, steps + 1):
         if step == 3:
             one, two = after(one, pair), after(two, pair)
         with jax.named_scope(f"own{step}"):
             one = onward(one)
         with jax.named_scope(f"other{step}"):
-            if step < steps:
+            if step == 1:
+                two = move(two, ("row", "col"), lambda z, c: (z - along(c % 2), c ^ 1))
+            elif step < steps - 1:
                 two = onward(two)
+            elif step == steps - 1:
+                two = move(two, ("row", "col"), lambda z, c: (z + along(c % 2), c ^ 1))
             else:
-                two = move(two, ("row", "col"), lambda z, c: (z + along(c % 2), c ^ 1))
+                two = move(two, ("row", "col"), lambda z, c: (z - along(c % 2), c))
         mine.append(one)
         others.append(two)
         if step == 1:
@@ -294,17 +291,15 @@
                 same = after(jnp.stack([pair, left_y1, left_y2, left_y3]), one, two)
                 other = move(same, ("col",), lambda c: (c ^ 1,))
 
-    with jax.named_scope("crossed"):
-        crossed = move(others[steps - 1], ("col",), lambda c: (c ^ 1,))
     early = steps - 1
     span = early * PART
     part = jax.ShapeDtypeStruct((TILE, 2 * TILE), BF16)
     lefts = jax.ShapeDtypeStruct((TILE, span), BF16)
     rights = [pltpu.VMEM((span, TILE), BF16)] * 2
     spare, left_h, left_l, far, late_h, late_l = call(
-        functools.partial(spare_kernel, early), (whole, lefts, lefts, packed, part, part), [VMEM] * (2 + early),
+        functools.partial(spare_kernel, early), (whole, lefts, lefts, packed, part, part), [VMEM] * (1 + early),
         rights, flops=6 * span * TILE**2, nbytes=6 * 2**20,
-    )(same, other, *others[:early])
+    )(same, other, *others[1:early])
     total = call(
         functools.partial(main_kernel, early), whole, [VMEM] * (2 + early), rights,
         flops=6 * span * TILE**2, nbytes=4 * 2**20,
@@ -314,7 +309,7 @@
     rights = pltpu.VMEM((2 * TILE, TILE), BF16)
     own, away = call(
         near_kernel, (half, jax.ShapeDtypeStruct((PART + 8, TILE), F32)), [VMEM] * 8, [rights, rights], flops=12 * TILE**3, nbytes=2**21
-    )(total, spare, late_h, late_l, mine[early], crossed, one, two)
+    )(total, spare, late_h, late_l, mine[early], others[early], one, two)
     with jax.named_scope("away"):
         came = move(away, ("layer",), lambda l: (1 - l,))
     one, two = after(one, away), after(two, away)

time: 117 us -> 119 us (1.017)
  waiting for transfers between devices: 21.1 us -> 28.9 us
  starting transfers between devices: 84.4 us -> 78.3 us
    ppermute x25 -> x23, waiting for transfers between devices: 21.1 us -> 28.9 us  [move(): lax.ppermute(value, axes, [(flat(at), flat(target(*at))) for at in points])]
    ppermute x25 -> x23, starting transfers between devices: 84.4 us -> 78.3 us  [move(): lax.ppermute(value, axes, [(flat(at), flat(target(*at))) for at in points])]
  transfers between devices with their start and end apart: 25 -> 23, of which waited for: 8 -> 11; matrix products, arithmetic and copies ran while one was open for 1% -> 1% of each run, Pallas kernels for 4% -> 4%
where the time goes in v7:
time: 119 us; the launch traced here: 118 us
  starting transfers between devices  78.3 us (66%)
  waiting for transfers between devices  28.9 us (24%)
  Pallas kernels  9.13 us (8%)
  other arithmetic  1.19 us (1%)
    ppermute x23, starting transfers between devices, move(): lax.ppermute(value, axes, [(flat(at), flat(target(*at))) for at in points])  78.3 us
    ppermute x23, waiting for transfers between devices, move(): lax.ppermute(value, axes, [(flat(at), flat(target(*at))) for at in points])  28.9 us
    pallas_call x1, Pallas kernels, shards(): call(functools.partial(spare_kernel, early), (whole, lefts, lefts, packed...  2.75 us
  transfers between devices with their start and end apart: 23, of which 11 were waited for; matrix products, arithmetic and copies ran while one was open for 1% of the time, Pallas kernels for 4%

profile of v7, /device:TPU:1, one launch (start us, length us, event | category | flops | bytes accessed | tf_op | source)
XLA Modules:
  0.0 117.9 jit_solution(5824185380432672228)
XLA Ops:
  0.0 2.3 %shard_map.55 = (f32[576,128]{1,0:T(8,128)}, f32[192,384]{1,0:T(8,128)}) custom-call(s32[3,3]{1,0:T(4,128)} %lm_in.1, s32[3,3]{1,0:T(4,128)} %rm_in.1, f32[384,384]{1,0:T(8,128)} %left_in.1, f32[384,384]{1,0:T(8,128)} %right_in.1), custom_call_target="tpu_custom_call" | custom-call | bytes 2097152 | tf_op jit(solution)/shard_map/pallas_call | solution.py:251
  2.3 12.0 %collective-permute-start.1 = (f32[192,384]{1,0:T(8,128)}, f32[192,384]{1,0:T(8,128)S(1)}, u32[]{:S(2)}, u32[]{:S(2)}) collective-permute-start(f32[192,384]{1,0:T(8,128)} %get-tuple-element.24.refs_0_), channel_id=1, source_target_pairs={{0,32},{2,482},{4,36},{6,486},{8,40},{10,490},{12,44},{14,494},{16... | collective-permute-start | bytes 884744 | tf_op jit(solution)/shard_map/own1/ppermute | solution.py:233
  14.3 4.7 %collective-permute-start = (f32[576,128]{1,0:T(8,128)}, f32[576,128]{1,0:T(8,128)S(1)}, u32[]{:S(2)}, u32[]{:S(2)}) collective-permute-start(f32[576,128]{1,0:T(8,128)} %get-tuple-element.23), channel_id=1, source_target_pairs={{0,4},{2,6},{4,0},{6,2},{8,12},{10,14},{12,8},{14,10},{16,20},{18,... | collective-permute-start | bytes 884744 | tf_op jit(solution)/shard_map/left_x/ppermute | solution.py:233
  19.0 1.9 %collective-permute-start.2 = (f32[192,384]{1,0:T(8,128)}, f32[192,384]{1,0:T(8,128)S(1)}, u32[]{:S(2)}, u32[]{:S(2)}) collective-permute-start(f32[192,384]{1,0:T(8,128)} %get-tuple-element.24.refs_0_), channel_id=1, source_target_pairs={{0,482},{2,32},{4,486},{6,36},{8,490},{10,40},{12,494},{14,44},{16... | collective-permute-start | bytes 884744 | tf_op jit(solution)/shard_map/other1/ppermute | solution.py:233
  20.9 0.0 collective-permute-done.1.refs_1_
  20.9 2.6 %collective-permute-start.4 = (f32[192,384]{1,0:T(8,128)S(1)}, f32[192,384]{1,0:T(8,128)S(1)}, u32[]{:S(2)}, u32[]{:S(2)}) collective-permute-start(f32[192,384]{1,0:T(8,128)S(1)} %collective-permute-done.1.refs_1_), channel_id=1, source_target_pairs={{0,32},{2,482},{4,36},{6,486},{8,40},{10,490},{12,44},{14,494},{16... | collective-permute-start | bytes 884744 | tf_op jit(solution)/shard_map/own2/ppermute | solution.py:233
  23.5 0.4 collective-permute-done
  23.9 1.0 fusion
  25.0 4.5 %collective-permute-done.2.refs_0_ = f32[192,384]{1,0:T(8,128)S(1)} collective-permute-done((f32[192,384]{1,0:T(8,128)}, f32[192,384]{1,0:T(8,128)S(1)}, u32[]{:S(2)}, u32[]{:S(2)}) %collective-permute-start.2) | collective-permute-done | bytes 294944 | tf_op jit(solution)/shard_map/other1/ppermute | solution.py:233
  29.5 4.6 %collective-permute-start.3 = (f32[2,576,128]{2,1,0:T(8,128)S(1)}, f32[2,576,128]{2,1,0:T(8,128)S(1)}, u32[]{:S(2)}, u32[]{:S(2)}) collective-permute-start(f32[2,576,128]{2,1,0:T(8,128)S(1)} %get-tuple-element.25), channel_id=1, source_target_pairs={{0,8},{2,26},{4,12},{6,30},{8,16},{10,2},{12,20},{14,6},{16,24},{1... | collective-permute-start | bytes 1769480 | tf_op jit(solution)/shard_map/left_y1/ppermute | solution.py:233
  34.1 3.6 %collective-permute-start.7 = (f32[192,384]{1,0:T(8,128)S(1)}, f32[192,384]{1,0:T(8,128)S(1)}, u32[]{:S(2)}, u32[]{:S(2)}) collective-permute-start(f32[192,384]{1,0:T(8,128)S(1)} %collective-permute-done.2.refs_0_), channel_id=1, source_target_pairs={{0,32},{2,482},{4,36},{6,486},{8,40},{10,490},{12,44},{14,494},{16... | collective-permute-start | bytes 884744 | tf_op jit(solution)/shard_map/other2/ppermute | solution.py:233
  37.7 0.0 collective-permute-done.4.refs_2_
  37.7 1.9 %collective-permute-start.5 = (f32[192,384]{1,0:T(8,128)S(1)}, f32[192,384]{1,0:T(8,128)S(1)}, u32[]{:S(2)}, u32[]{:S(2)}) collective-permute-start(f32[192,384]{1,0:T(8,128)S(1)} %collective-permute-done.4.refs_2_), channel_id=1, source_target_pairs={{0,32},{2,482},{4,36},{6,486},{8,40},{10,490},{12,44},{14,494},{16... | collective-permute-start | bytes 884744 | tf_op jit(solution)/shard_map/own3/ppermute | solution.py:233
  39.6 2.3 %collective-permute-done.7.refs_1_ = f32[192,384]{1,0:T(8,128)S(1)} collective-permute-done((f32[192,384]{1,0:T(8,128)S(1)}, f32[192,384]{1,0:T(8,128)S(1)}, u32[]{:S(2)}, u32[]{:S(2)}) %collective-permute-start.7) | collective-permute-done | bytes 294944 | tf_op jit(solution)/shard_map/other2/ppermute | solution.py:233
  41.9 4.5 %collective-permute-start.11 = (f32[192,384]{1,0:T(8,128)S(1)}, f32[192,384]{1,0:T(8,128)S(1)}, u32[]{:S(2)}, u32[]{:S(2)}) collective-permute-start(f32[192,384]{1,0:T(8,128)S(1)} %collective-permute-done.7.refs_1_), channel_id=1, source_target_pairs={{0,32},{2,482},{4,36},{6,486},{8,40},{10,490},{12,44},{14,494},{16... | collective-permute-start | bytes 884744 | tf_op jit(solution)/shard_map/other3/ppermute | solution.py:233
  46.3 1.9 %collective-permute-start.8 = (f32[2,576,128]{2,1,0:T(8,128)S(1)}, f32[2,576,128]{2,1,0:T(8,128)S(1)}, u32[]{:S(2)}, u32[]{:S(2)}) collective-permute-start(f32[2,576,128]{2,1,0:T(8,128)S(1)} %get-tuple-element.25), channel_id=1, source_target_pairs={{0,24},{2,10},{4,28},{6,14},{8,0},{10,18},{12,4},{14,22},{16,8},{1... | collective-permute-start | bytes 1769480 | tf_op jit(solution)/shard_map/left_y3/ppermute | solution.py:233
  48.3 0.0 collective-permute-done.3
  48.3 0.0 collective-permute-done.5.refs_3_
  48.3 4.6 %collective-permute-start.6 = (f32[2,576,128]{2,1,0:T(8,128)S(1)}, f32[2,576,128]{2,1,0:T(8,128)S(1)}, u32[]{:S(2)}, u32[]{:S(2)}) collective-permute-start(f32[2,576,128]{2,1,0:T(8,128)S(1)} %collective-permute-done.3), channel_id=1, source_target_pairs={{0,8},{2,26},{4,12},{6,30},{8,16},{10,2},{12,20},{14,6},{16,24},{1... | collective-permute-start | bytes 1769480 | tf_op jit(solution)/shard_map/left_y2/ppermute | solution.py:233
  52.9 1.9 %collective-permute-start.9 = (f32[192,384]{1,0:T(8,128)S(1)}, f32[192,384]{1,0:T(8,128)S(1)}, u32[]{:S(2)}, u32[]{:S(2)}) collective-permute-start(f32[192,384]{1,0:T(8,128)S(1)} %collective-permute-done.5.refs_3_), channel_id=1, source_target_pairs={{0,32},{2,482},{4,36},{6,486},{8,40},{10,490},{12,44},{14,494},{16... | collective-permute-start | bytes 884744 | tf_op jit(solution)/shard_map/own4/ppermute | solution.py:233
  54.8 0.0 collective-permute-done.11.refs_2_
  54.8 1.9 %collective-permute-start.12 = (f32[192,384]{1,0:T(8,128)S(1)}, f32[192,384]{1,0:T(8,128)S(1)}, u32[]{:S(2)}, u32[]{:S(2)}) collective-permute-start(f32[192,384]{1,0:T(8,128)S(1)} %collective-permute-done.11.refs_2_), channel_id=1, source_target_pairs={{0,32},{2,482},{4,36},{6,486},{8,40},{10,490},{12,44},{14,494},{16... | collective-permute-start | bytes 884744 | tf_op jit(solution)/shard_map/other4/ppermute | solution.py:233
  56.7 3.9 %collective-permute-done.9.refs_4_ = f32[192,384]{1,0:T(8,128)S(1)} collective-permute-done((f32[192,384]{1,0:T(8,128)S(1)}, f32[192,384]{1,0:T(8,128)S(1)}, u32[]{:S(2)}, u32[]{:S(2)}) %collective-permute-start.9) | collective-permute-done | bytes 294944 | tf_op jit(solution)/shard_map/own4/ppermute | solution.py:233
  60.6 3.1 %collective-permute-start.10 = (f32[192,384]{1,0:T(8,128)S(1)}, f32[192,384]{1,0:T(8,128)S(1)}, u32[]{:S(2)}, u32[]{:S(2)}) collective-permute-start(f32[192,384]{1,0:T(8,128)S(1)} %collective-permute-done.9.refs_4_), channel_id=1, source_target_pairs={{0,32},{2,482},{4,36},{6,486},{8,40},{10,490},{12,44},{14,494},{16... | collective-permute-start | bytes 884744 | tf_op jit(solution)/shard_map/own5/ppermute | solution.py:233
  63.8 0.0 collective-permute-done.12.refs_3_
  63.8 2.9 %collective-permute-start.13 = (f32[192,384]{1,0:T(8,128)S(1)}, f32[192,384]{1,0:T(8,128)S(1)}, u32[]{:S(2)}, u32[]{:S(2)}) collective-permute-start(f32[192,384]{1,0:T(8,128)S(1)} %collective-permute-done.12.refs_3_), channel_id=1, source_target_pairs={{0,32},{2,482},{4,36},{6,486},{8,40},{10,490},{12,44},{14,494},{16... | collective-permute-start | bytes 884744 | tf_op jit(solution)/shard_map/other5/ppermute | solution.py:233
  66.7 0.0 collective-permute-done.8
  66.7 0.0 collective-permute-done.6
  66.7 0.2 pad_maximum_fusion.same
  66.9 0.0 copy-start
  66.9 1.5 %collective-permute-done.10.refs_5_ = f32[192,384]{1,0:T(8,128)S(1)} collective-permute-done((f32[192,384]{1,0:T(8,128)S(1)}, f32[192,384]{1,0:T(8,128)S(1)}, u32[]{:S(2)}, u32[]{:S(2)}) %collective-permute-start.10) | collective-permute-done | bytes 294944 | tf_op jit(solution)/shard_map/own5/ppermute | solution.py:233
  68.4 3.2 %collective-permute-done.13.refs_4_ = f32[192,384]{1,0:T(8,128)S(1)} collective-permute-done((f32[192,384]{1,0:T(8,128)S(1)}, f32[192,384]{1,0:T(8,128)S(1)}, u32[]{:S(2)}, u32[]{:S(2)}) %collective-permute-start.13) | collective-permute-done | bytes 294944 | tf_op jit(solution)/shard_map/other5/ppermute | solution.py:233
  71.6 2.8 %collective-permute-start.14 = (f32[4,2,576,128]{3,2,1,0:T(8,128)S(1)}, f32[4,2,576,128]{3,2,1,0:T(8,128)S(1)}, u32[]{:S(2)}, u32[]{:S(2)}) collective-permute-start(f32[4,2,576,128]{3,2,1,0:T(8,128)S(1)} %pad_maximum_fusion.same), channel_id=1, source_target_pairs={{0,2},{2,0},{4,6},{6,4},{8,10},{10,8},{12,14},{14,12},{16,18},{18,... | collective-permute-start | bytes 7077896 | tf_op jit(solution)/shard_map/left_core/ppermute | solution.py:233
  74.3 3.2 %collective-permute-start.16 = (f32[192,384]{1,0:T(8,128)S(1)}, f32[192,384]{1,0:T(8,128)S(1)}, u32[]{:S(2)}, u32[]{:S(2)}) collective-permute-start(f32[192,384]{1,0:T(8,128)S(1)} %collective-permute-done.10.refs_5_), channel_id=1, source_target_pairs={{0,32},{2,482},{4,36},{6,486},{8,40},{10,490},{12,44},{14,494},{16... | collective-permute-start | bytes 884744 | tf_op jit(solution)/shard_map/own6/ppermute | solution.py:233
  77.5 3.5 %collective-permute-start.17 = (f32[192,384]{1,0:T(8,128)S(1)}, f32[192,384]{1,0:T(8,128)S(1)}, u32[]{:S(2)}, u32[]{:S(2)}) collective-permute-start(f32[192,384]{1,0:T(8,128)S(1)} %collective-permute-done.13.refs_4_), channel_id=1, source_target_pairs={{0,34},{2,480},{4,38},{6,484},{8,42},{10,488},{12,46},{14,492},{16... | collective-permute-start | bytes 884744 | tf_op jit(solution)/shard_map/other6/ppermute | solution.py:233
  81.0 0.0 collective-permute-done.14.other
  81.0 2.8 %shard_map.56 = (f32[384,384]{1,0:T(8,128)S(1)}, bf16[384,1152]{1,0:T(8,128)(2,1)S(1)}, bf16[384,1152]{1,0:T(8,128)(2,1)S(1)}, f32[576,128]{1,0:T(8,128)S(1)}, b...) custom-call(f32[4,2,576,128]{3,2,1,0:T(8,128)S(1)} %pad_maximum_fusion.same, ...), custom_call_target="tpu_custom_call" | custom-call | flops 1019215872 | bytes 6291456 | tf_op jit(solution)/shard_map/pallas_call | solution.py:299
  83.8 1.9 %collective-permute-start.15 = (f32[384,384]{1,0:T(8,128)S(1)}, f32[384,384]{1,0:T(8,128)S(1)}, u32[]{:S(2)}, u32[]{:S(2)}) collective-permute-start(f32[384,384]{1,0:T(8,128)S(1)} %get-tuple-element.33), channel_id=1, source_target_pairs={{0,2},{2,0},{4,6},{6,4},{8,10},{10,8},{12,14},{14,12},{16,18},{18,... | collective-permute-start | bytes 1769480 | tf_op jit(solution)/shard_map/spare/ppermute | solution.py:233
  85.7 0.0 collective-permute-done.16.one
  85.7 3.4 %collective-permute-start.18 = (f32[192,384]{1,0:T(8,128)S(1)}, f32[192,384]{1,0:T(8,128)S(1)}, u32[]{:S(2)}, u32[]{:S(2)}) collective-permute-start(f32[192,384]{1,0:T(8,128)S(1)} %collective-permute-done.16.one), channel_id=1, source_target_pairs={{0,32},{2,482},{4,36},{6,486},{8,40},{10,490},{12,44},{14,494},{16... | collective-permute-start | bytes 884744 | tf_op jit(solution)/shard_map/own7/ppermute | solution.py:233
  89.1 0.0 collective-permute-done.17.two
  89.1 1.9 %collective-permute-start.19 = (f32[192,384]{1,0:T(8,128)S(1)}, f32[192,384]{1,0:T(8,128)S(1)}, u32[]{:S(2)}, u32[]{:S(2)}) collective-permute-start(f32[192,384]{1,0:T(8,128)S(1)} %collective-permute-done.17.two), channel_id=1, source_target_pairs={{0,480},{2,34},{4,484},{6,38},{8,488},{10,42},{12,492},{14,46},{16... | collective-permute-start | bytes 884744 | tf_op jit(solution)/shard_map/other7/ppermute | solution.py:233
  91.1 0.0 copy-done
  91.1 1.7 %shard_map.57.total = f32[384,384]{1,0:T(8,128)S(1)} custom-call(bf16[384,1152]{1,0:T(8,128)(2,1)S(1)} %get-tuple-element.31.lh, bf16[384,1152]{1,0:T(8,128)(2,1)S(1)} %get-tuple-element.32.ll, f32[192,384]{1,0:T(8,128)S(1)} %copy-done, f32[192,384]{1,0:T(8,128)S(1)} %collective-permute-done.1.refs_1_, f32[192,384]{1,0:T(8,128)S(1)} %collective-permute-done.4.refs_2_, ...), custom_call_target="tpu_custom_call" | custom-call | flops 1019215872 | bytes 4194304 | tf_op jit(solution)/shard_map/pallas_call | solution.py:303
  92.8 0.0 copy-start.1
  92.8 0.9 collective-permute-done.18.three
  93.7 4.8 %collective-permute-done.19.four = f32[192,384]{1,0:T(8,128)S(1)} collective-permute-done((f32[192,384]{1,0:T(8,128)S(1)}, f32[192,384]{1,0:T(8,128)S(1)}, u32[]{:S(2)}, u32[]{:S(2)}) %collective-permute-start.19) | collective-permute-done | bytes 294944 | tf_op jit(solution)/shard_map/other7/ppermute | solution.py:233
  98.5 0.0 collective-permute-done.15.spare
  98.5 1.2 shard_map.58
  99.7 1.9 %collective-permute-start.20 = (f32[200,384]{1,0:T(8,128)S(1)}, f32[200,384]{1,0:T(8,128)S(1)}, u32[]{:S(2)}, u32[]{:S(2)}) collective-permute-start(f32[200,384]{1,0:T(8,128)S(1)} %get-tuple-element.37), channel_id=1, source_target_pairs={{0,1},{1,0},{2,3},{3,2},{4,5},{5,4},{6,7},{7,6},{8,9},{9,8},{10,11... | collective-permute-start | bytes 921608 | tf_op jit(solution)/shard_map/away/ppermute | solution.py:233
  101.7 1.9 %collective-permute-start.22 = (f32[192,384]{1,0:T(8,128)S(1)}, f32[192,384]{1,0:T(8,128)S(1)}, u32[]{:S(2)}, u32[]{:S(2)}) collective-permute-start(f32[192,384]{1,0:T(8,128)S(1)} %collective-permute-done.19.four), channel_id=1, source_target_pairs={{0,481},{1,480},{2,35},{3,34},{4,485},{5,484},{6,39},{7,38},{8,489... | collective-permute-start | bytes 884744 | tf_op jit(solution)/shard_map/far_other/ppermute | solution.py:233
  103.6 5.7 %collective-permute-start.21 = (f32[192,384]{1,0:T(8,128)S(1)}, f32[192,384]{1,0:T(8,128)S(1)}, u32[]{:S(2)}, u32[]{:S(2)}) collective-permute-start(f32[192,384]{1,0:T(8,128)S(1)} %collective-permute-done.18.three), channel_id=1, source_target_pairs={{0,32},{2,482},{4,36},{6,486},{8,40},{10,490},{12,44},{14,494},{16... | collective-permute-start | bytes 884744 | tf_op jit(solution)/shard_map/far_own/ppermute | solution.py:233
  109.3 3.7 %collective-permute-done.22.right_other = f32[192,384]{1,0:T(8,128)S(1)} collective-permute-done((f32[192,384]{1,0:T(8,128)S(1)}, f32[192,384]{1,0:T(8,128)S(1)}, u32[]{:S(2)}, u32[]{:S(2)}) %collective-permute-start.22) | collective-permute-done | bytes 294944 | tf_op jit(solution)/shard_map/far_other/ppermute | solution.py:233
  113.0 1.6 %collective-permute-done.21.right_own = f32[192,384]{1,0:T(8,128)S(1)} collective-permute-done((f32[192,384]{1,0:T(8,128)S(1)}, f32[192,384]{1,0:T(8,128)S(1)}, u32[]{:S(2)}, u32[]{:S(2)}) %collective-permute-start.21) | collective-permute-done | bytes 294944 | tf_op jit(solution)/shard_map/far_own/ppermute | solution.py:233
  114.7 2.0 %collective-permute-done.20.came = f32[200,384]{1,0:T(8,128)S(1)} collective-permute-done((f32[200,384]{1,0:T(8,128)S(1)}, f32[200,384]{1,0:T(8,128)S(1)}, u32[]{:S(2)}, u32[]{:S(2)}) %collective-permute-start.20) | collective-permute-done | bytes 307232 | tf_op jit(solution)/shard_map/away/ppermute | solution.py:233
  116.7 0.0 copy-done.1
  116.7 1.2 %shard_map.59 = f32[192,384]{1,0:T(8,128)} custom-call(s32[3,3]{1,0:T(4,128)S(1)} %copy-done.1, f32[192,384]{1,0:T(8,128)S(1)} %get-tuple-element.36.own, f32[200,384]{1,0:T(8,128)S(1)} %collective-permute-done.20.came, f32[576,128]{1,0:T(8,128)S(1)} %get-tuple-element.38.far, f32[192,384]{1,0:T(8,128)S(1)} %collective-permute-done.21.right_own, ...), custom_call_target="tpu_custom_call" | custom-call | flops 169869312 | bytes 1048576 | tf_op jit(solution)/shard_map/pallas_call | solution.py:320
Async XLA Ops:
  2.3 18.5 %collective-permute-start.1 = (f32[192,384]{1,0:T(8,128)}, f32[192,384]{1,0:T(8,128)S(1)}, u32[]{:S(2)}, u32[]{:S(2)}) collective-permute-start(f32[192,384]{1,0:T(8,128)} %get-tuple-element.24.refs_0_), channel_id=1, source_target_pairs={{0,32},{2,482},{4,36},{6,486},{8,40},{10,490},{12,44},{14,494},{16... | collective-permute-start | bytes 884744 | tf_op jit(solution)/shard_map/own1/ppermute | solution.py:233
  14.3 9.6 %collective-permute-start = (f32[576,128]{1,0:T(8,128)}, f32[576,128]{1,0:T(8,128)S(1)}, u32[]{:S(2)}, u32[]{:S(2)}) collective-permute-start(f32[576,128]{1,0:T(8,128)} %get-tuple-element.23), channel_id=1, source_target_pairs={{0,4},{2,6},{4,0},{6,2},{8,12},{10,14},{12,8},{14,10},{16,20},{18,... | collective-permute-start | bytes 884744 | tf_op jit(solution)/shard_map/left_x/ppermute | solution.py:233
  19.0 10.5 %collective-permute-start.2 = (f32[192,384]{1,0:T(8,128)}, f32[192,384]{1,0:T(8,128)S(1)}, u32[]{:S(2)}, u32[]{:S(2)}) collective-permute-start(f32[192,384]{1,0:T(8,128)} %get-tuple-element.24.refs_0_), channel_id=1, source_target_pairs={{0,482},{2,32},{4,486},{6,36},{8,490},{10,40},{12,494},{14,44},{16... | collective-permute-start | bytes 884744 | tf_op jit(solution)/shard_map/other1/ppermute | solution.py:233
  20.9 16.8 %collective-permute-start.4 = (f32[192,384]{1,0:T(8,128)S(1)}, f32[192,384]{1,0:T(8,128)S(1)}, u32[]{:S(2)}, u32[]{:S(2)}) collective-permute-start(f32[192,384]{1,0:T(8,128)S(1)} %collective-permute-done.1.refs_1_), channel_id=1, source_target_pairs={{0,32},{2,482},{4,36},{6,486},{8,40},{10,490},{12,44},{14,494},{16... | collective-permute-start | bytes 884744 | tf_op jit(solution)/shard_map/own2/ppermute | solution.py:233
  29.5 18.8 %collective-permute-start.3 = (f32[2,576,128]{2,1,0:T(8,128)S(1)}, f32[2,576,128]{2,1,0:T(8,128)S(1)}, u32[]{:S(2)}, u32[]{:S(2)}) collective-permute-start(f32[2,576,128]{2,1,0:T(8,128)S(1)} %get-tuple-element.25), channel_id=1, source_target_pairs={{0,8},{2,26},{4,12},{6,30},{8,16},{10,2},{12,20},{14,6},{16,24},{1... | collective-permute-start | bytes 1769480 | tf_op jit(solution)/shard_map/left_y1/ppermute | solution.py:233
  34.1 7.8 %collective-permute-start.7 = (f32[192,384]{1,0:T(8,128)S(1)}, f32[192,384]{1,0:T(8,128)S(1)}, u32[]{:S(2)}, u32[]{:S(2)}) collective-permute-start(f32[192,384]{1,0:T(8,128)S(1)} %collective-permute-done.2.refs_0_), channel_id=1, source_target_pairs={{0,32},{2,482},{4,36},{6,486},{8,40},{10,490},{12,44},{14,494},{16... | collective-permute-start | bytes 884744 | tf_op jit(solution)/shard_map/other2/ppermute | solution.py:233
  37.7 10.6 %collective-permute-start.5 = (f32[192,384]{1,0:T(8,128)S(1)}, f32[192,384]{1,0:T(8,128)S(1)}, u32[]{:S(2)}, u32[]{:S(2)}) collective-permute-start(f32[192,384]{1,0:T(8,128)S(1)} %collective-permute-done.4.refs_2_), channel_id=1, source_target_pairs={{0,32},{2,482},{4,36},{6,486},{8,40},{10,490},{12,44},{14,494},{16... | collective-permute-start | bytes 884744 | tf_op jit(solution)/shard_map/own3/ppermute | solution.py:233
  41.9 12.9 %collective-permute-start.11 = (f32[192,384]{1,0:T(8,128)S(1)}, f32[192,384]{1,0:T(8,128)S(1)}, u32[]{:S(2)}, u32[]{:S(2)}) collective-permute-start(f32[192,384]{1,0:T(8,128)S(1)} %collective-permute-done.7.refs_1_), channel_id=1, source_target_pairs={{0,32},{2,482},{4,36},{6,486},{8,40},{10,490},{12,44},{14,494},{16... | collective-permute-start | bytes 884744 | tf_op jit(solution)/shard_map/other3/ppermute | solution.py:233
  46.3 20.4 %collective-permute-start.8 = (f32[2,576,128]{2,1,0:T(8,128)S(1)}, f32[2,576,128]{2,1,0:T(8,128)S(1)}, u32[]{:S(2)}, u32[]{:S(2)}) collective-permute-start(f32[2,576,128]{2,1,0:T(8,128)S(1)} %get-tuple-element.25), channel_id=1, source_target_pairs={{0,24},{2,10},{4,28},{6,14},{8,0},{10,18},{12,4},{14,22},{16,8},{1... | collective-permute-start | bytes 1769480 | tf_op jit(solution)/shard_map/left_y3/ppermute | solution.py:233
  48.3 18.4 %collective-permute-start.6 = (f32[2,576,128]{2,1,0:T(8,128)S(1)}, f32[2,576,128]{2,1,0:T(8,128)S(1)}, u32[]{:S(2)}, u32[]{:S(2)}) collective-permute-start(f32[2,576,128]{2,1,0:T(8,128)S(1)} %collective-permute-done.3), channel_id=1, source_target_pairs={{0,8},{2,26},{4,12},{6,30},{8,16},{10,2},{12,20},{14,6},{16,24},{1... | collective-permute-start | bytes 1769480 | tf_op jit(solution)/shard_map/left_y2/ppermute | solution.py:233
  52.9 7.8 %collective-permute-start.9 = (f32[192,384]{1,0:T(8,128)S(1)}, f32[192,384]{1,0:T(8,128)S(1)}, u32[]{:S(2)}, u32[]{:S(2)}) collective-permute-start(f32[192,384]{1,0:T(8,128)S(1)} %collective-permute-done.5.refs_3_), channel_id=1, source_target_pairs={{0,32},{2,482},{4,36},{6,486},{8,40},{10,490},{12,44},{14,494},{16... | collective-permute-start | bytes 884744 | tf_op jit(solution)/shard_map/own4/ppermute | solution.py:233
  54.8 9.0 %collective-permute-start.12 = (f32[192,384]{1,0:T(8,128)S(1)}, f32[192,384]{1,0:T(8,128)S(1)}, u32[]{:S(2)}, u32[]{:S(2)}) collective-permute-start(f32[192,384]{1,0:T(8,128)S(1)} %collective-permute-done.11.refs_2_), channel_id=1, source_target_pairs={{0,32},{2,482},{4,36},{6,486},{8,40},{10,490},{12,44},{14,494},{16... | collective-permute-start | bytes 884744 | tf_op jit(solution)/shard_map/other4/ppermute | solution.py:233
  60.6 7.8 %collective-permute-start.10 = (f32[192,384]{1,0:T(8,128)S(1)}, f32[192,384]{1,0:T(8,128)S(1)}, u32[]{:S(2)}, u32[]{:S(2)}) collective-permute-start(f32[192,384]{1,0:T(8,128)S(1)} %collective-permute-done.9.refs_4_), channel_id=1, source_target_pairs={{0,32},{2,482},{4,36},{6,486},{8,40},{10,490},{12,44},{14,494},{16... | collective-permute-start | bytes 884744 | tf_op jit(solution)/shard_map/own5/ppermute | solution.py:233
  63.8 7.8 %collective-permute-start.13 = (f32[192,384]{1,0:T(8,128)S(1)}, f32[192,384]{1,0:T(8,128)S(1)}, u32[]{:S(2)}, u32[]{:S(2)}) collective-permute-start(f32[192,384]{1,0:T(8,128)S(1)} %collective-permute-done.12.refs_3_), channel_id=1, source_target_pairs={{0,32},{2,482},{4,36},{6,486},{8,40},{10,490},{12,44},{14,494},{16... | collective-permute-start | bytes 884744 | tf_op jit(solution)/shard_map/other5/ppermute | solution.py:233
  66.9 24.2 %copy-start = (f32[192,384]{1,0:T(8,128)S(1)}, f32[192,384]{1,0:T(8,128)}, u32[]{:S(2)}) copy-start(f32[192,384]{1,0:T(8,128)} %get-tuple-element.24.refs_0_) | copy-start | bytes 884740
  71.6 9.5 %collective-permute-start.14 = (f32[4,2,576,128]{3,2,1,0:T(8,128)S(1)}, f32[4,2,576,128]{3,2,1,0:T(8,128)S(1)}, u32[]{:S(2)}, u32[]{:S(2)}) collective-permute-start(f32[4,2,576,128]{3,2,1,0:T(8,128)S(1)} %pad_maximum_fusion.same), channel_id=1, source_target_pairs={{0,2},{2,0},{4,6},{6,4},{8,10},{10,8},{12,14},{14,12},{16,18},{18,... | collective-permute-start | bytes 7077896 | tf_op jit(solution)/shard_map/left_core/ppermute | solution.py:233
  74.3 11.4 %collective-permute-start.16 = (f32[192,384]{1,0:T(8,128)S(1)}, f32[192,384]{1,0:T(8,128)S(1)}, u32[]{:S(2)}, u32[]{:S(2)}) collective-permute-start(f32[192,384]{1,0:T(8,128)S(1)} %collective-permute-done.10.refs_5_), channel_id=1, source_target_pairs={{0,32},{2,482},{4,36},{6,486},{8,40},{10,490},{12,44},{14,494},{16... | collective-permute-start | bytes 884744 | tf_op jit(solution)/shard_map/own6/ppermute | solution.py:233
  77.5 11.6 %collective-permute-start.17 = (f32[192,384]{1,0:T(8,128)S(1)}, f32[192,384]{1,0:T(8,128)S(1)}, u32[]{:S(2)}, u32[]{:S(2)}) collective-permute-start(f32[192,384]{1,0:T(8,128)S(1)} %collective-permute-done.13.refs_4_), channel_id=1, source_target_pairs={{0,34},{2,480},{4,38},{6,484},{8,42},{10,488},{12,46},{14,492},{16... | collective-permute-start | bytes 884744 | tf_op jit(solution)/shard_map/other6/ppermute | solution.py:233
  83.8 14.7 %collective-permute-start.15 = (f32[384,384]{1,0:T(8,128)S(1)}, f32[384,384]{1,0:T(8,128)S(1)}, u32[]{:S(2)}, u32[]{:S(2)}) collective-permute-start(f32[384,384]{1,0:T(8,128)S(1)} %get-tuple-element.33), channel_id=1, source_target_pairs={{0,2},{2,0},{4,6},{6,4},{8,10},{10,8},{12,14},{14,12},{16,18},{18,... | collective-permute-start | bytes 1769480 | tf_op jit(solution)/shard_map/spare/ppermute | solution.py:233
  85.7 8.0 %collective-permute-start.18 = (f32[192,384]{1,0:T(8,128)S(1)}, f32[192,384]{1,0:T(8,128)S(1)}, u32[]{:S(2)}, u32[]{:S(2)}) collective-permute-start(f32[192,384]{1,0:T(8,128)S(1)} %collective-permute-done.16.one), channel_id=1, source_target_pairs={{0,32},{2,482},{4,36},{6,486},{8,40},{10,490},{12,44},{14,494},{16... | collective-permute-start | bytes 884744 | tf_op jit(solution)/shard_map/own7/ppermute | solution.py:233
  89.1 9.4 %collective-permute-start.19 = (f32[192,384]{1,0:T(8,128)S(1)}, f32[192,384]{1,0:T(8,128)S(1)}, u32[]{:S(2)}, u32[]{:S(2)}) collective-permute-start(f32[192,384]{1,0:T(8,128)S(1)} %collective-permute-done.17.two), channel_id=1, source_target_pairs={{0,480},{2,34},{4,484},{6,38},{8,488},{10,42},{12,492},{14,46},{16... | collective-permute-start | bytes 884744 | tf_op jit(solution)/shard_map/other7/ppermute | solution.py:233
  92.8 23.9 %copy-start.1 = (s32[3,3]{1,0:T(4,128)S(1)}, s32[3,3]{1,0:T(4,128)}, u32[]{:S(2)}) copy-start(s32[3,3]{1,0:T(4,128)} %keep.1) | copy-start | bytes 112
  99.7 17.0 %collective-permute-start.20 = (f32[200,384]{1,0:T(8,128)S(1)}, f32[200,384]{1,0:T(8,128)S(1)}, u32[]{:S(2)}, u32[]{:S(2)}) collective-permute-start(f32[200,384]{1,0:T(8,128)S(1)} %get-tuple-element.37), channel_id=1, source_target_pairs={{0,1},{1,0},{2,3},{3,2},{4,5},{5,4},{6,7},{7,6},{8,9},{9,8},{10,11... | collective-permute-start | bytes 921608 | tf_op jit(solution)/shard_map/away/ppermute | solution.py:233
  101.7 11.4 %collective-permute-start.22 = (f32[192,384]{1,0:T(8,128)S(1)}, f32[192,384]{1,0:T(8,128)S(1)}, u32[]{:S(2)}, u32[]{:S(2)}) collective-permute-start(f32[192,384]{1,0:T(8,128)S(1)} %collective-permute-done.19.four), channel_id=1, source_target_pairs={{0,481},{1,480},{2,35},{3,34},{4,485},{5,484},{6,39},{7,38},{8,489... | collective-permute-start | bytes 884744 | tf_op jit(solution)/shard_map/far_other/ppermute | solution.py:233
  103.6 11.1 %collective-permute-start.21 = (f32[192,384]{1,0:T(8,128)S(1)}, f32[192,384]{1,0:T(8,128)S(1)}, u32[]{:S(2)}, u32[]{:S(2)}) collective-permute-start(f32[192,384]{1,0:T(8,128)S(1)} %collective-permute-done.18.three), channel_id=1, source_target_pairs={{0,32},{2,482},{4,36},{6,486},{8,40},{10,490},{12,44},{14,494},{16... | collective-permute-start | bytes 884744 | tf_op jit(solution)/shard_map/far_own/ppermute | solution.py:233

commit v8 on v6

--- a/solution.py
+++ b/solution.py
@@ -200,17 +200,16 @@
     fill_right(three[...], four[...], rh, rl, TILE)
     value = total[...] + spare[...] + triple((late_h[...], late_l[...]), (rh[...], rl[...]))
     layer = place[2]
-    away[PART:] = jnp.zeros((8, TILE), F32)
 
     @pl.when(layer == 0)
     def _():
         own[...] = value[:PART]
-        away[:PART] = value[PART:]
+        away[...] = value[PART:]
 
     @pl.when(layer == 1)
     def _():
         own[...] = value[PART:]
-        away[:PART] = value[:PART]
+        away[...] = value[:PART]
 
 
 def last_kernel(keep, own, came, far, right_own, right_other, out):
@@ -221,7 +220,7 @@
     low, high = jnp.where(first, mine, other), jnp.where(first, other, mine)
     right = jnp.concatenate([low, high[BLK:], high[:BLK]], 0)
     left = jnp.concatenate([far[:PART], far[PART : 2 * PART], far[2 * PART :]], 1)
-    value = own[...] + came[:PART] + triple(split(left), split(right))
+    value = own[...] + came[...] + triple(split(left), split(right))
     row = lax.broadcasted_iota(jnp.int32, (PART, BLK), 0) + layer * PART
     centre = (row >= BLK) & (row < 2 * BLK)
     for q in range(3):
@@ -313,11 +312,11 @@
         spare = move(spare, ("col",), lambda c: (c ^ 1,))
     rights = pltpu.VMEM((2 * TILE, TILE), BF16)
     own, away = call(
-        near_kernel, (half, jax.ShapeDtypeStruct((PART + 8, TILE), F32)), [VMEM] * 8, [rights, rights], flops=12 * TILE**3, nbytes=2**21
+        near_kernel, (half, half), [VMEM] * 8, [rights, rights], flops=12 * TILE**3, nbytes=2**21
     )(total, spare, late_h, late_l, mine[early], crossed, one, two)
     with jax.named_scope("away"):
         came = move(away, ("layer",), lambda l: (1 - l,))
-    one, two = after(one, away), after(two, away)
+    one, two = after(one, total), after(two, total)
     with jax.named_scope("far_own"):
         far_own = onward(one)
     with jax.named_scope("far_other"):

time: 117 us -> 118 us (level)
  transfers between devices with their start and end apart: 25 -> 25, of which waited for: 8 -> 9; matrix products, arithmetic and copies ran while one was open for 1% -> 1% of each run, Pallas kernels for 4% -> 5%
where the time goes in v8:
time: 118 us; the launch traced here: 117 us
  starting transfers between devices  85.3 us (72%)
  waiting for transfers between devices  21.3 us (18%)
  Pallas kernels  9.12 us (8%)
  other arithmetic  1.2 us (1%)
    ppermute x25, starting transfers between devices, move(): lax.ppermute(value, axes, [(flat(at), flat(target(*at))) for at in points])  85.3 us
    ppermute x25, waiting for transfers between devices, move(): lax.ppermute(value, axes, [(flat(at), flat(target(*at))) for at in points])  21.3 us
    pallas_call x1, Pallas kernels, shards(): call(functools.partial(spare_kernel, early), (whole, lefts, lefts, packed...  2.76 us
  transfers between devices with their start and end apart: 25, of which 9 were waited for; matrix products, arithmetic and copies ran while one was open for 1% of the time, Pallas kernels for 5%

profile of v8, /device:TPU:1, one launch (start us, length us, event | category | flops | bytes accessed | tf_op | source)
XLA Modules:
  0.0 117.3 jit_solution(11134030795284768446)
XLA Ops:
  0.0 2.3 %shard_map.55 = (f32[576,128]{1,0:T(8,128)}, f32[192,384]{1,0:T(8,128)}) custom-call(s32[3,3]{1,0:T(4,128)} %lm_in.1, s32[3,3]{1,0:T(4,128)} %rm_in.1, f32[384,384]{1,0:T(8,128)} %left_in.1, f32[384,384]{1,0:T(8,128)} %right_in.1), custom_call_target="tpu_custom_call" | custom-call | bytes 2097152 | tf_op jit(solution)/shard_map/pallas_call | solution.py:255
  2.3 8.8 %collective-permute-start.2 = (f32[192,384]{1,0:T(8,128)}, f32[192,384]{1,0:T(8,128)S(1)}, u32[]{:S(2)}, u32[]{:S(2)}) collective-permute-start(f32[192,384]{1,0:T(8,128)} %get-tuple-element.24.refs_0_), channel_id=1, source_target_pairs={{0,2},{2,0},{4,6},{6,4},{8,10},{10,8},{12,14},{14,12},{16,18},{18,... | collective-permute-start | bytes 884744 | tf_op jit(solution)/shard_map/right_core/ppermute | solution.py:237
  11.1 5.7 %collective-permute-start.1 = (f32[192,384]{1,0:T(8,128)}, f32[192,384]{1,0:T(8,128)S(1)}, u32[]{:S(2)}, u32[]{:S(2)}) collective-permute-start(f32[192,384]{1,0:T(8,128)} %get-tuple-element.24.refs_0_), channel_id=1, source_target_pairs={{0,32},{2,482},{4,36},{6,486},{8,40},{10,490},{12,44},{14,494},{16... | collective-permute-start | bytes 884744 | tf_op jit(solution)/shard_map/own1/ppermute | solution.py:237
  16.9 4.7 %collective-permute-start = (f32[576,128]{1,0:T(8,128)}, f32[576,128]{1,0:T(8,128)S(1)}, u32[]{:S(2)}, u32[]{:S(2)}) collective-permute-start(f32[576,128]{1,0:T(8,128)} %get-tuple-element.23), channel_id=1, source_target_pairs={{0,4},{2,6},{4,0},{6,2},{8,12},{10,14},{12,8},{14,10},{16,20},{18,... | collective-permute-start | bytes 884744 | tf_op jit(solution)/shard_map/left_x/ppermute | solution.py:237
  21.5 0.0 collective-permute-done.2.refs_0_
  21.5 2.6 %collective-permute-start.3 = (f32[192,384]{1,0:T(8,128)S(1)}, f32[192,384]{1,0:T(8,128)S(1)}, u32[]{:S(2)}, u32[]{:S(2)}) collective-permute-start(f32[192,384]{1,0:T(8,128)S(1)} %collective-permute-done.2.refs_0_), channel_id=1, source_target_pairs={{0,32},{2,482},{4,36},{6,486},{8,40},{10,490},{12,44},{14,494},{16... | collective-permute-start | bytes 884744 | tf_op jit(solution)/shard_map/other1/ppermute | solution.py:237
  24.2 0.0 collective-permute-done.1.refs_1_
  24.2 2.6 %collective-permute-start.5 = (f32[192,384]{1,0:T(8,128)S(1)}, f32[192,384]{1,0:T(8,128)S(1)}, u32[]{:S(2)}, u32[]{:S(2)}) collective-permute-start(f32[192,384]{1,0:T(8,128)S(1)} %collective-permute-done.1.refs_1_), channel_id=1, source_target_pairs={{0,32},{2,482},{4,36},{6,486},{8,40},{10,490},{12,44},{14,494},{16... | collective-permute-start | bytes 884744 | tf_op jit(solution)/shard_map/own2/ppermute | solution.py:237
  26.8 0.0 collective-permute-done
  26.9 1.0 fusion
  27.9 1.4 %collective-permute-done.3.refs_1_ = f32[192,384]{1,0:T(8,128)S(1)} collective-permute-done((f32[192,384]{1,0:T(8,128)S(1)}, f32[192,384]{1,0:T(8,128)S(1)}, u32[]{:S(2)}, u32[]{:S(2)}) %collective-permute-start.3) | collective-permute-done | bytes 294944 | tf_op jit(solution)/shard_map/other1/ppermute | solution.py:237
  29.3 4.6 %collective-permute-start.4 = (f32[2,576,128]{2,1,0:T(8,128)S(1)}, f32[2,576,128]{2,1,0:T(8,128)S(1)}, u32[]{:S(2)}, u32[]{:S(2)}) collective-permute-start(f32[2,576,128]{2,1,0:T(8,128)S(1)} %get-tuple-element.25), channel_id=1, source_target_pairs={{0,8},{2,26},{4,12},{6,30},{8,16},{10,2},{12,20},{14,6},{16,24},{1... | collective-permute-start | bytes 1769480 | tf_op jit(solution)/shard_map/left_y1/ppermute | solution.py:237
  33.9 3.6 %collective-permute-start.8 = (f32[192,384]{1,0:T(8,128)S(1)}, f32[192,384]{1,0:T(8,128)S(1)}, u32[]{:S(2)}, u32[]{:S(2)}) collective-permute-start(f32[192,384]{1,0:T(8,128)S(1)} %collective-permute-done.3.refs_1_), channel_id=1, source_target_pairs={{0,32},{2,482},{4,36},{6,486},{8,40},{10,490},{12,44},{14,494},{16... | collective-permute-start | bytes 884744 | tf_op jit(solution)/shard_map/other2/ppermute | solution.py:237
  37.5 0.0 collective-permute-done.5.refs_2_
  37.5 2.3 %collective-permute-start.6 = (f32[192,384]{1,0:T(8,128)S(1)}, f32[192,384]{1,0:T(8,128)S(1)}, u32[]{:S(2)}, u32[]{:S(2)}) collective-permute-start(f32[192,384]{1,0:T(8,128)S(1)} %collective-permute-done.5.refs_2_), channel_id=1, source_target_pairs={{0,32},{2,482},{4,36},{6,486},{8,40},{10,490},{12,44},{14,494},{16... | collective-permute-start | bytes 884744 | tf_op jit(solution)/shard_map/own3/ppermute | solution.py:237
  39.8 1.9 %collective-permute-done.8.refs_2_ = f32[192,384]{1,0:T(8,128)S(1)} collective-permute-done((f32[192,384]{1,0:T(8,128)S(1)}, f32[192,384]{1,0:T(8,128)S(1)}, u32[]{:S(2)}, u32[]{:S(2)}) %collective-permute-start.8) | collective-permute-done | bytes 294944 | tf_op jit(solution)/shard_map/other2/ppermute | solution.py:237
  41.7 4.5 %collective-permute-start.12 = (f32[192,384]{1,0:T(8,128)S(1)}, f32[192,384]{1,0:T(8,128)S(1)}, u32[]{:S(2)}, u32[]{:S(2)}) collective-permute-start(f32[192,384]{1,0:T(8,128)S(1)} %collective-permute-done.8.refs_2_), channel_id=1, source_target_pairs={{0,32},{2,482},{4,36},{6,486},{8,40},{10,490},{12,44},{14,494},{16... | collective-permute-start | bytes 884744 | tf_op jit(solution)/shard_map/other3/ppermute | solution.py:237
  46.2 1.9 %collective-permute-start.9 = (f32[2,576,128]{2,1,0:T(8,128)S(1)}, f32[2,576,128]{2,1,0:T(8,128)S(1)}, u32[]{:S(2)}, u32[]{:S(2)}) collective-permute-start(f32[2,576,128]{2,1,0:T(8,128)S(1)} %get-tuple-element.25), channel_id=1, source_target_pairs={{0,24},{2,10},{4,28},{6,14},{8,0},{10,18},{12,4},{14,22},{16,8},{1... | collective-permute-start | bytes 1769480 | tf_op jit(solution)/shard_map/left_y3/ppermute | solution.py:237
  48.1 0.0 collective-permute-done.6.refs_3_
  48.1 0.0 collective-permute-done.4
  48.1 4.6 %collective-permute-start.7 = (f32[2,576,128]{2,1,0:T(8,128)S(1)}, f32[2,576,128]{2,1,0:T(8,128)S(1)}, u32[]{:S(2)}, u32[]{:S(2)}) collective-permute-start(f32[2,576,128]{2,1,0:T(8,128)S(1)} %collective-permute-done.4), channel_id=1, source_target_pairs={{0,8},{2,26},{4,12},{6,30},{8,16},{10,2},{12,20},{14,6},{16,24},{1... | collective-permute-start | bytes 1769480 | tf_op jit(solution)/shard_map/left_y2/ppermute | solution.py:237
  52.7 1.9 %collective-permute-start.10 = (f32[192,384]{1,0:T(8,128)S(1)}, f32[192,384]{1,0:T(8,128)S(1)}, u32[]{:S(2)}, u32[]{:S(2)}) collective-permute-start(f32[192,384]{1,0:T(8,128)S(1)} %collective-permute-done.6.refs_3_), channel_id=1, source_target_pairs={{0,32},{2,482},{4,36},{6,486},{8,40},{10,490},{12,44},{14,494},{16... | collective-permute-start | bytes 884744 | tf_op jit(solution)/shard_map/own4/ppermute | solution.py:237
  54.6 0.0 collective-permute-done.12.refs_3_
  54.6 2.1 %collective-permute-start.13 = (f32[192,384]{1,0:T(8,128)S(1)}, f32[192,384]{1,0:T(8,128)S(1)}, u32[]{:S(2)}, u32[]{:S(2)}) collective-permute-start(f32[192,384]{1,0:T(8,128)S(1)} %collective-permute-done.12.refs_3_), channel_id=1, source_target_pairs={{0,32},{2,482},{4,36},{6,486},{8,40},{10,490},{12,44},{14,494},{16... | collective-permute-start | bytes 884744 | tf_op jit(solution)/shard_map/other4/ppermute | solution.py:237
  56.7 3.8 %collective-permute-done.10.refs_4_ = f32[192,384]{1,0:T(8,128)S(1)} collective-permute-done((f32[192,384]{1,0:T(8,128)S(1)}, f32[192,384]{1,0:T(8,128)S(1)}, u32[]{:S(2)}, u32[]{:S(2)}) %collective-permute-start.10) | collective-permute-done | bytes 294944 | tf_op jit(solution)/shard_map/own4/ppermute | solution.py:237
  60.5 3.1 %collective-permute-start.11 = (f32[192,384]{1,0:T(8,128)S(1)}, f32[192,384]{1,0:T(8,128)S(1)}, u32[]{:S(2)}, u32[]{:S(2)}) collective-permute-start(f32[192,384]{1,0:T(8,128)S(1)} %collective-permute-done.10.refs_4_), channel_id=1, source_target_pairs={{0,32},{2,482},{4,36},{6,486},{8,40},{10,490},{12,44},{14,494},{16... | collective-permute-start | bytes 884744 | tf_op jit(solution)/shard_map/own5/ppermute | solution.py:237
  63.6 0.0 collective-permute-done.13.refs_4_
  63.6 2.9 %collective-permute-start.14 = (f32[192,384]{1,0:T(8,128)S(1)}, f32[192,384]{1,0:T(8,128)S(1)}, u32[]{:S(2)}, u32[]{:S(2)}) collective-permute-start(f32[192,384]{1,0:T(8,128)S(1)} %collective-permute-done.13.refs_4_), channel_id=1, source_target_pairs={{0,32},{2,482},{4,36},{6,486},{8,40},{10,490},{12,44},{14,494},{16... | collective-permute-start | bytes 884744 | tf_op jit(solution)/shard_map/other5/ppermute | solution.py:237
  66.5 0.0 collective-permute-done.9
  66.5 0.0 collective-permute-done.7
  66.6 0.2 pad_maximum_fusion.same
  66.7 0.0 copy-start
  66.7 1.5 %collective-permute-done.11.refs_5_ = f32[192,384]{1,0:T(8,128)S(1)} collective-permute-done((f32[192,384]{1,0:T(8,128)S(1)}, f32[192,384]{1,0:T(8,128)S(1)}, u32[]{:S(2)}, u32[]{:S(2)}) %collective-permute-start.11) | collective-permute-done | bytes 294944 | tf_op jit(solution)/shard_map/own5/ppermute | solution.py:237
  68.2 3.2 %collective-permute-done.14.refs_5_ = f32[192,384]{1,0:T(8,128)S(1)} collective-permute-done((f32[192,384]{1,0:T(8,128)S(1)}, f32[192,384]{1,0:T(8,128)S(1)}, u32[]{:S(2)}, u32[]{:S(2)}) %collective-permute-start.14) | collective-permute-done | bytes 294944 | tf_op jit(solution)/shard_map/other5/ppermute | solution.py:237
  71.4 3.2 %collective-permute-start.15 = (f32[4,2,576,128]{3,2,1,0:T(8,128)S(1)}, f32[4,2,576,128]{3,2,1,0:T(8,128)S(1)}, u32[]{:S(2)}, u32[]{:S(2)}) collective-permute-start(f32[4,2,576,128]{3,2,1,0:T(8,128)S(1)} %pad_maximum_fusion.same), channel_id=1, source_target_pairs={{0,2},{2,0},{4,6},{6,4},{8,10},{10,8},{12,14},{14,12},{16,18},{18,... | collective-permute-start | bytes 7077896 | tf_op jit(solution)/shard_map/left_core/ppermute | solution.py:237
  74.5 2.8 %collective-permute-start.17 = (f32[192,384]{1,0:T(8,128)S(1)}, f32[192,384]{1,0:T(8,128)S(1)}, u32[]{:S(2)}, u32[]{:S(2)}) collective-permute-start(f32[192,384]{1,0:T(8,128)S(1)} %collective-permute-done.11.refs_5_), channel_id=1, source_target_pairs={{0,32},{2,482},{4,36},{6,486},{8,40},{10,490},{12,44},{14,494},{16... | collective-permute-start | bytes 884744 | tf_op jit(solution)/shard_map/own6/ppermute | solution.py:237
  77.3 2.1 %collective-permute-start.18 = (f32[192,384]{1,0:T(8,128)S(1)}, f32[192,384]{1,0:T(8,128)S(1)}, u32[]{:S(2)}, u32[]{:S(2)}) collective-permute-start(f32[192,384]{1,0:T(8,128)S(1)} %collective-permute-done.14.refs_5_), channel_id=1, source_target_pairs={{0,32},{2,482},{4,36},{6,486},{8,40},{10,490},{12,44},{14,494},{16... | collective-permute-start | bytes 884744 | tf_op jit(solution)/shard_map/other6/ppermute | solution.py:237
  79.4 0.0 collective-permute-done.15.other
  79.4 2.8 %shard_map.56 = (f32[384,384]{1,0:T(8,128)S(1)}, bf16[384,1152]{1,0:T(8,128)(2,1)S(1)}, bf16[384,1152]{1,0:T(8,128)(2,1)S(1)}, f32[576,128]{1,0:T(8,128)S(1)}, b...) custom-call(f32[4,2,576,128]{3,2,1,0:T(8,128)S(1)} %pad_maximum_fusion.same, ...), custom_call_target="tpu_custom_call" | custom-call | flops 1019215872 | bytes 6291456 | tf_op jit(solution)/shard_map/pallas_call | solution.py:303
  82.2 1.9 %collective-permute-start.16 = (f32[384,384]{1,0:T(8,128)S(1)}, f32[384,384]{1,0:T(8,128)S(1)}, u32[]{:S(2)}, u32[]{:S(2)}) collective-permute-start(f32[384,384]{1,0:T(8,128)S(1)} %get-tuple-element.33), channel_id=1, source_target_pairs={{0,2},{2,0},{4,6},{6,4},{8,10},{10,8},{12,14},{14,12},{16,18},{18,... | collective-permute-start | bytes 1769480 | tf_op jit(solution)/shard_map/spare/ppermute | solution.py:237
  84.1 1.3 %collective-permute-done.18 = f32[192,384]{1,0:T(8,128)S(1)} collective-permute-done((f32[192,384]{1,0:T(8,128)S(1)}, f32[192,384]{1,0:T(8,128)S(1)}, u32[]{:S(2)}, u32[]{:S(2)}) %collective-permute-start.18) | collective-permute-done | bytes 294944 | tf_op jit(solution)/shard_map/other6/ppermute | solution.py:237
  85.5 4.4 %collective-permute-start.21 = (f32[192,384]{1,0:T(8,128)S(1)}, f32[192,384]{1,0:T(8,128)S(1)}, u32[]{:S(2)}, u32[]{:S(2)}) collective-permute-start(f32[192,384]{1,0:T(8,128)S(1)} %collective-permute-done.18), channel_id=1, source_target_pairs={{0,34},{2,480},{4,38},{6,484},{8,42},{10,488},{12,46},{14,492},{16... | collective-permute-start | bytes 884744 | tf_op jit(solution)/shard_map/other7/ppermute | solution.py:237
  89.8 0.0 collective-permute-done.17.one
  89.8 3.6 %collective-permute-start.20 = (f32[192,384]{1,0:T(8,128)S(1)}, f32[192,384]{1,0:T(8,128)S(1)}, u32[]{:S(2)}, u32[]{:S(2)}) collective-permute-start(f32[192,384]{1,0:T(8,128)S(1)} %collective-permute-done.17.one), channel_id=1, source_target_pairs={{0,32},{2,482},{4,36},{6,486},{8,40},{10,490},{12,44},{14,494},{16... | collective-permute-start | bytes 884744 | tf_op jit(solution)/shard_map/own7/ppermute | solution.py:237
  93.5 1.9 %collective-permute-start.19 = (f32[192,384]{1,0:T(8,128)S(1)}, f32[192,384]{1,0:T(8,128)S(1)}, u32[]{:S(2)}, u32[]{:S(2)}) collective-permute-start(f32[192,384]{1,0:T(8,128)S(1)} %collective-permute-done.18), channel_id=1, source_target_pairs={{0,2},{2,0},{4,6},{6,4},{8,10},{10,8},{12,14},{14,12},{16,18},{18,... | collective-permute-start | bytes 884744 | tf_op jit(solution)/shard_map/crossed/ppermute | solution.py:237
  95.4 0.0 copy-done
  95.4 1.7 %shard_map.57.total = f32[384,384]{1,0:T(8,128)S(1)} custom-call(bf16[384,1152]{1,0:T(8,128)(2,1)S(1)} %get-tuple-element.31.lh, bf16[384,1152]{1,0:T(8,128)(2,1)S(1)} %get-tuple-element.32.ll, f32[192,384]{1,0:T(8,128)S(1)} %copy-done, f32[192,384]{1,0:T(8,128)S(1)} %collective-permute-done.1.refs_1_, f32[192,384]{1,0:T(8,128)S(1)} %collective-permute-done.5.refs_2_, ...), custom_call_target="tpu_custom_call" | custom-call | flops 1019215872 | bytes 4194304 | tf_op jit(solution)/shard_map/pallas_call | solution.py:307
  97.1 0.0 copy-start.1
  97.1 0.0 collective-permute-done.21.four
  97.1 2.1 %collective-permute-start.24 = (f32[192,384]{1,0:T(8,128)S(1)}, f32[192,384]{1,0:T(8,128)S(1)}, u32[]{:S(2)}, u32[]{:S(2)}) collective-permute-start(f32[192,384]{1,0:T(8,128)S(1)} %collective-permute-done.21.four), channel_id=1, source_target_pairs={{0,481},{1,480},{2,35},{3,34},{4,485},{5,484},{6,39},{7,38},{8,489... | collective-permute-start | bytes 884744 | tf_op jit(solution)/shard_map/far_other/ppermute | solution.py:237
  99.3 0.0 collective-permute-done.20.three
  99.3 4.7 %collective-permute-start.23 = (f32[192,384]{1,0:T(8,128)S(1)}, f32[192,384]{1,0:T(8,128)S(1)}, u32[]{:S(2)}, u32[]{:S(2)}) collective-permute-start(f32[192,384]{1,0:T(8,128)S(1)} %collective-permute-done.20.three), channel_id=1, source_target_pairs={{0,32},{2,482},{4,36},{6,486},{8,40},{10,490},{12,44},{14,494},{16... | collective-permute-start | bytes 884744 | tf_op jit(solution)/shard_map/far_own/ppermute | solution.py:237
  104.0 0.0 collective-permute-done.19.two
  104.0 0.0 collective-permute-done.16.spare
  104.0 1.1 shard_map.58
  105.2 2.8 %collective-permute-start.22 = (f32[192,384]{1,0:T(8,128)S(1)}, f32[192,384]{1,0:T(8,128)S(1)}, u32[]{:S(2)}, u32[]{:S(2)}) collective-permute-start(f32[192,384]{1,0:T(8,128)S(1)} %get-tuple-element.37), channel_id=1, source_target_pairs={{0,1},{1,0},{2,3},{3,2},{4,5},{5,4},{6,7},{7,6},{8,9},{9,8},{10,11... | collective-permute-start | bytes 884744 | tf_op jit(solution)/shard_map/away/ppermute | solution.py:237
  107.9 1.1 collective-permute-done.24.right_other
  109.1 0.8 collective-permute-done.23.right_own
  109.8 6.2 %collective-permute-done.22.came = f32[192,384]{1,0:T(8,128)S(1)} collective-permute-done((f32[192,384]{1,0:T(8,128)S(1)}, f32[192,384]{1,0:T(8,128)S(1)}, u32[]{:S(2)}, u32[]{:S(2)}) %collective-permute-start.22) | collective-permute-done | bytes 294944 | tf_op jit(solution)/shard_map/away/ppermute | solution.py:237
  116.0 0.0 copy-done.1
  116.0 1.2 %shard_map.59 = f32[192,384]{1,0:T(8,128)} custom-call(s32[3,3]{1,0:T(4,128)S(1)} %copy-done.1, f32[192,384]{1,0:T(8,128)S(1)} %get-tuple-element.36.own, f32[192,384]{1,0:T(8,128)S(1)} %collective-permute-done.22.came, f32[576,128]{1,0:T(8,128)S(1)} %get-tuple-element.38.far, f32[192,384]{1,0:T(8,128)S(1)} %collective-permute-done.23.right_own, ...), custom_call_target="tpu_custom_call" | custom-call | flops 169869312 | bytes 1048576 | tf_op jit(solution)/shard_map/pallas_call | solution.py:324
Async XLA Ops:
  2.3 19.2 %collective-permute-start.2 = (f32[192,384]{1,0:T(8,128)}, f32[192,384]{1,0:T(8,128)S(1)}, u32[]{:S(2)}, u32[]{:S(2)}) collective-permute-start(f32[192,384]{1,0:T(8,128)} %get-tuple-element.24.refs_0_), channel_id=1, source_target_pairs={{0,2},{2,0},{4,6},{6,4},{8,10},{10,8},{12,14},{14,12},{16,18},{18,... | collective-permute-start | bytes 884744 | tf_op jit(solution)/shard_map/right_core/ppermute | solution.py:237
  11.1 13.1 %collective-permute-start.1 = (f32[192,384]{1,0:T(8,128)}, f32[192,384]{1,0:T(8,128)S(1)}, u32[]{:S(2)}, u32[]{:S(2)}) collective-permute-start(f32[192,384]{1,0:T(8,128)} %get-tuple-element.24.refs_0_), channel_id=1, source_target_pairs={{0,32},{2,482},{4,36},{6,486},{8,40},{10,490},{12,44},{14,494},{16... | collective-permute-start | bytes 884744 | tf_op jit(solution)/shard_map/own1/ppermute | solution.py:237
  16.9 10.0 %collective-permute-start = (f32[576,128]{1,0:T(8,128)}, f32[576,128]{1,0:T(8,128)S(1)}, u32[]{:S(2)}, u32[]{:S(2)}) collective-permute-start(f32[576,128]{1,0:T(8,128)} %get-tuple-element.23), channel_id=1, source_target_pairs={{0,4},{2,6},{4,0},{6,2},{8,12},{10,14},{12,8},{14,10},{16,20},{18,... | collective-permute-start | bytes 884744 | tf_op jit(solution)/shard_map/left_x/ppermute | solution.py:237
  21.5 7.8 %collective-permute-start.3 = (f32[192,384]{1,0:T(8,128)S(1)}, f32[192,384]{1,0:T(8,128)S(1)}, u32[]{:S(2)}, u32[]{:S(2)}) collective-permute-start(f32[192,384]{1,0:T(8,128)S(1)} %collective-permute-done.2.refs_0_), channel_id=1, source_target_pairs={{0,32},{2,482},{4,36},{6,486},{8,40},{10,490},{12,44},{14,494},{16... | collective-permute-start | bytes 884744 | tf_op jit(solution)/shard_map/other1/ppermute | solution.py:237
  24.2 13.3 %collective-permute-start.5 = (f32[192,384]{1,0:T(8,128)S(1)}, f32[192,384]{1,0:T(8,128)S(1)}, u32[]{:S(2)}, u32[]{:S(2)}) collective-permute-start(f32[192,384]{1,0:T(8,128)S(1)} %collective-permute-done.1.refs_1_), channel_id=1, source_target_pairs={{0,32},{2,482},{4,36},{6,486},{8,40},{10,490},{12,44},{14,494},{16... | collective-permute-start | bytes 884744 | tf_op jit(solution)/shard_map/own2/ppermute | solution.py:237
  29.3 18.8 %collective-permute-start.4 = (f32[2,576,128]{2,1,0:T(8,128)S(1)}, f32[2,576,128]{2,1,0:T(8,128)S(1)}, u32[]{:S(2)}, u32[]{:S(2)}) collective-permute-start(f32[2,576,128]{2,1,0:T(8,128)S(1)} %get-tuple-element.25), channel_id=1, source_target_pairs={{0,8},{2,26},{4,12},{6,30},{8,16},{10,2},{12,20},{14,6},{16,24},{1... | collective-permute-start | bytes 1769480 | tf_op jit(solution)/shard_map/left_y1/ppermute | solution.py:237
  33.9 7.8 %collective-permute-start.8 = (f32[192,384]{1,0:T(8,128)S(1)}, f32[192,384]{1,0:T(8,128)S(1)}, u32[]{:S(2)}, u32[]{:S(2)}) collective-permute-start(f32[192,384]{1,0:T(8,128)S(1)} %collective-permute-done.3.refs_1_), channel_id=1, source_target_pairs={{0,32},{2,482},{4,36},{6,486},{8,40},{10,490},{12,44},{14,494},{16... | collective-permute-start | bytes 884744 | tf_op jit(solution)/shard_map/other2/ppermute | solution.py:237
  37.5 10.6 %collective-permute-start.6 = (f32[192,384]{1,0:T(8,128)S(1)}, f32[192,384]{1,0:T(8,128)S(1)}, u32[]{:S(2)}, u32[]{:S(2)}) collective-permute-start(f32[192,384]{1,0:T(8,128)S(1)} %collective-permute-done.5.refs_2_), channel_id=1, source_target_pairs={{0,32},{2,482},{4,36},{6,486},{8,40},{10,490},{12,44},{14,494},{16... | collective-permute-start | bytes 884744 | tf_op jit(solution)/shard_map/own3/ppermute | solution.py:237
  41.7 12.9 %collective-permute-start.12 = (f32[192,384]{1,0:T(8,128)S(1)}, f32[192,384]{1,0:T(8,128)S(1)}, u32[]{:S(2)}, u32[]{:S(2)}) collective-permute-start(f32[192,384]{1,0:T(8,128)S(1)} %collective-permute-done.8.refs_2_), channel_id=1, source_target_pairs={{0,32},{2,482},{4,36},{6,486},{8,40},{10,490},{12,44},{14,494},{16... | collective-permute-start | bytes 884744 | tf_op jit(solution)/shard_map/other3/ppermute | solution.py:237
  46.2 20.4 %collective-permute-start.9 = (f32[2,576,128]{2,1,0:T(8,128)S(1)}, f32[2,576,128]{2,1,0:T(8,128)S(1)}, u32[]{:S(2)}, u32[]{:S(2)}) collective-permute-start(f32[2,576,128]{2,1,0:T(8,128)S(1)} %get-tuple-element.25), channel_id=1, source_target_pairs={{0,24},{2,10},{4,28},{6,14},{8,0},{10,18},{12,4},{14,22},{16,8},{1... | collective-permute-start | bytes 1769480 | tf_op jit(solution)/shard_map/left_y3/ppermute | solution.py:237
  48.1 18.4 %collective-permute-start.7 = (f32[2,576,128]{2,1,0:T(8,128)S(1)}, f32[2,576,128]{2,1,0:T(8,128)S(1)}, u32[]{:S(2)}, u32[]{:S(2)}) collective-permute-start(f32[2,576,128]{2,1,0:T(8,128)S(1)} %collective-permute-done.4), channel_id=1, source_target_pairs={{0,8},{2,26},{4,12},{6,30},{8,16},{10,2},{12,20},{14,6},{16,24},{1... | collective-permute-start | bytes 1769480 | tf_op jit(solution)/shard_map/left_y2/ppermute | solution.py:237
  52.7 7.8 %collective-permute-start.10 = (f32[192,384]{1,0:T(8,128)S(1)}, f32[192,384]{1,0:T(8,128)S(1)}, u32[]{:S(2)}, u32[]{:S(2)}) collective-permute-start(f32[192,384]{1,0:T(8,128)S(1)} %collective-permute-done.6.refs_3_), channel_id=1, source_target_pairs={{0,32},{2,482},{4,36},{6,486},{8,40},{10,490},{12,44},{14,494},{16... | collective-permute-start | bytes 884744 | tf_op jit(solution)/shard_map/own4/ppermute | solution.py:237
  54.6 9.0 %collective-permute-start.13 = (f32[192,384]{1,0:T(8,128)S(1)}, f32[192,384]{1,0:T(8,128)S(1)}, u32[]{:S(2)}, u32[]{:S(2)}) collective-permute-start(f32[192,384]{1,0:T(8,128)S(1)} %collective-permute-done.12.refs_3_), channel_id=1, source_target_pairs={{0,32},{2,482},{4,36},{6,486},{8,40},{10,490},{12,44},{14,494},{16... | collective-permute-start | bytes 884744 | tf_op jit(solution)/shard_map/other4/ppermute | solution.py:237
  60.5 7.8 %collective-permute-start.11 = (f32[192,384]{1,0:T(8,128)S(1)}, f32[192,384]{1,0:T(8,128)S(1)}, u32[]{:S(2)}, u32[]{:S(2)}) collective-permute-start(f32[192,384]{1,0:T(8,128)S(1)} %collective-permute-done.10.refs_4_), channel_id=1, source_target_pairs={{0,32},{2,482},{4,36},{6,486},{8,40},{10,490},{12,44},{14,494},{16... | collective-permute-start | bytes 884744 | tf_op jit(solution)/shard_map/own5/ppermute | solution.py:237
  63.6 7.8 %collective-permute-start.14 = (f32[192,384]{1,0:T(8,128)S(1)}, f32[192,384]{1,0:T(8,128)S(1)}, u32[]{:S(2)}, u32[]{:S(2)}) collective-permute-start(f32[192,384]{1,0:T(8,128)S(1)} %collective-permute-done.13.refs_4_), channel_id=1, source_target_pairs={{0,32},{2,482},{4,36},{6,486},{8,40},{10,490},{12,44},{14,494},{16... | collective-permute-start | bytes 884744 | tf_op jit(solution)/shard_map/other5/ppermute | solution.py:237
  66.7 28.7 %copy-start = (f32[192,384]{1,0:T(8,128)S(1)}, f32[192,384]{1,0:T(8,128)}, u32[]{:S(2)}) copy-start(f32[192,384]{1,0:T(8,128)} %get-tuple-element.24.refs_0_) | copy-start | bytes 884740
  71.4 8.0 %collective-permute-start.15 = (f32[4,2,576,128]{3,2,1,0:T(8,128)S(1)}, f32[4,2,576,128]{3,2,1,0:T(8,128)S(1)}, u32[]{:S(2)}, u32[]{:S(2)}) collective-permute-start(f32[4,2,576,128]{3,2,1,0:T(8,128)S(1)} %pad_maximum_fusion.same), channel_id=1, source_target_pairs={{0,2},{2,0},{4,6},{6,4},{8,10},{10,8},{12,14},{14,12},{16,18},{18,... | collective-permute-start | bytes 7077896 | tf_op jit(solution)/shard_map/left_core/ppermute | solution.py:237
  74.5 15.3 %collective-permute-start.17 = (f32[192,384]{1,0:T(8,128)S(1)}, f32[192,384]{1,0:T(8,128)S(1)}, u32[]{:S(2)}, u32[]{:S(2)}) collective-permute-start(f32[192,384]{1,0:T(8,128)S(1)} %collective-permute-done.11.refs_5_), channel_id=1, source_target_pairs={{0,32},{2,482},{4,36},{6,486},{8,40},{10,490},{12,44},{14,494},{16... | collective-permute-start | bytes 884744 | tf_op jit(solution)/shard_map/own6/ppermute | solution.py:237
  77.3 8.1 %collective-permute-start.18 = (f32[192,384]{1,0:T(8,128)S(1)}, f32[192,384]{1,0:T(8,128)S(1)}, u32[]{:S(2)}, u32[]{:S(2)}) collective-permute-start(f32[192,384]{1,0:T(8,128)S(1)} %collective-permute-done.14.refs_5_), channel_id=1, source_target_pairs={{0,32},{2,482},{4,36},{6,486},{8,40},{10,490},{12,44},{14,494},{16... | collective-permute-start | bytes 884744 | tf_op jit(solution)/shard_map/other6/ppermute | solution.py:237
  82.2 21.8 %collective-permute-start.16 = (f32[384,384]{1,0:T(8,128)S(1)}, f32[384,384]{1,0:T(8,128)S(1)}, u32[]{:S(2)}, u32[]{:S(2)}) collective-permute-start(f32[384,384]{1,0:T(8,128)S(1)} %get-tuple-element.33), channel_id=1, source_target_pairs={{0,2},{2,0},{4,6},{6,4},{8,10},{10,8},{12,14},{14,12},{16,18},{18,... | collective-permute-start | bytes 1769480 | tf_op jit(solution)/shard_map/spare/ppermute | solution.py:237
  85.5 11.6 %collective-permute-start.21 = (f32[192,384]{1,0:T(8,128)S(1)}, f32[192,384]{1,0:T(8,128)S(1)}, u32[]{:S(2)}, u32[]{:S(2)}) collective-permute-start(f32[192,384]{1,0:T(8,128)S(1)} %collective-permute-done.18), channel_id=1, source_target_pairs={{0,34},{2,480},{4,38},{6,484},{8,42},{10,488},{12,46},{14,492},{16... | collective-permute-start | bytes 884744 | tf_op jit(solution)/shard_map/other7/ppermute | solution.py:237
  89.8 9.4 %collective-permute-start.20 = (f32[192,384]{1,0:T(8,128)S(1)}, f32[192,384]{1,0:T(8,128)S(1)}, u32[]{:S(2)}, u32[]{:S(2)}) collective-permute-start(f32[192,384]{1,0:T(8,128)S(1)} %collective-permute-done.17.one), channel_id=1, source_target_pairs={{0,32},{2,482},{4,36},{6,486},{8,40},{10,490},{12,44},{14,494},{16... | collective-permute-start | bytes 884744 | tf_op jit(solution)/shard_map/own7/ppermute | solution.py:237
  93.5 10.5 %collective-permute-start.19 = (f32[192,384]{1,0:T(8,128)S(1)}, f32[192,384]{1,0:T(8,128)S(1)}, u32[]{:S(2)}, u32[]{:S(2)}) collective-permute-start(f32[192,384]{1,0:T(8,128)S(1)} %collective-permute-done.18), channel_id=1, source_target_pairs={{0,2},{2,0},{4,6},{6,4},{8,10},{10,8},{12,14},{14,12},{16,18},{18,... | collective-permute-start | bytes 884744 | tf_op jit(solution)/shard_map/crossed/ppermute | solution.py:237
  97.1 19.0 %copy-start.1 = (s32[3,3]{1,0:T(4,128)S(1)}, s32[3,3]{1,0:T(4,128)}, u32[]{:S(2)}) copy-start(s32[3,3]{1,0:T(4,128)} %keep.1) | copy-start | bytes 112
  97.1 11.9 %collective-permute-start.24 = (f32[192,384]{1,0:T(8,128)S(1)}, f32[192,384]{1,0:T(8,128)S(1)}, u32[]{:S(2)}, u32[]{:S(2)}) collective-permute-start(f32[192,384]{1,0:T(8,128)S(1)} %collective-permute-done.21.four), channel_id=1, source_target_pairs={{0,481},{1,480},{2,35},{3,34},{4,485},{5,484},{6,39},{7,38},{8,489... | collective-permute-start | bytes 884744 | tf_op jit(solution)/shard_map/far_other/ppermute | solution.py:237
  99.3 10.6 %collective-permute-start.23 = (f32[192,384]{1,0:T(8,128)S(1)}, f32[192,384]{1,0:T(8,128)S(1)}, u32[]{:S(2)}, u32[]{:S(2)}) collective-permute-start(f32[192,384]{1,0:T(8,128)S(1)} %collective-permute-done.20.three), channel_id=1, source_target_pairs={{0,32},{2,482},{4,36},{6,486},{8,40},{10,490},{12,44},{14,494},{16... | collective-permute-start | bytes 884744 | tf_op jit(solution)/shard_map/far_own/ppermute | solution.py:237
  105.2 10.9 %collective-permute-start.22 = (f32[192,384]{1,0:T(8,128)S(1)}, f32[192,384]{1,0:T(8,128)S(1)}, u32[]{:S(2)}, u32[]{:S(2)}) collective-permute-start(f32[192,384]{1,0:T(8,128)S(1)} %get-tuple-element.37), channel_id=1, source_target_pairs={{0,1},{1,0},{2,3},{3,2},{4,5},{5,4},{6,7},{7,6},{8,9},{9,8},{10,11... | collective-permute-start | bytes 884744 | tf_op jit(solution)/shard_map/away/ppermute | solution.py:237

commit v9 on v8

--- a/solution.py
+++ b/solution.py
@@ -316,7 +316,6 @@
     )(total, spare, late_h, late_l, mine[early], crossed, one, two)
     with jax.named_scope("away"):
         came = move(away, ("layer",), lambda l: (1 - l,))
-    one, two = after(one, total), after(two, total)
     with jax.named_scope("far_own"):
         far_own = onward(one)
     with jax.named_scope("far_other"):

time: 118 us -> 116 us (0.983)
  starting transfers between devices: 85.3 us -> 83.8 us
    ppermute x25, starting transfers between devices: 85.3 us -> 83.8 us  [move(): lax.ppermute(value, axes, [(flat(at), flat(target(*at))) for at in points])]
  transfers between devices with their start and end apart: 25 -> 25, of which waited for: 9 -> 8; matrix products, arithmetic and copies ran while one was open for 1% -> 1% of each run, Pallas kernels for 5% -> 5%
where the time goes in v9:
time: 116 us; the launch traced here: 115 us
  starting transfers between devices  83.8 us (72%)
  waiting for transfers between devices  20.9 us (18%)
  Pallas kernels  9.11 us (8%)
  other arithmetic  1.2 us (1%)
    ppermute x25, starting transfers between devices, move(): lax.ppermute(value, axes, [(flat(at), flat(target(*at))) for at in points])  83.8 us
    ppermute x25, waiting for transfers between devices, move(): lax.ppermute(value, axes, [(flat(at), flat(target(*at))) for at in points])  20.9 us
    pallas_call x1, Pallas kernels, shards(): call(functools.partial(spare_kernel, early), (whole, lefts, lefts, packed...  2.76 us
  transfers between devices with their start and end apart: 25, of which 8 were waited for; matrix products, arithmetic and copies ran while one was open for 1% of the time, Pallas kernels for 5%

profile of v9, /device:TPU:1, one launch (start us, length us, event | category | flops | bytes accessed | tf_op | source)
XLA Modules:
  0.0 115.4 jit_solution(18235705183339370028)
XLA Ops:
  0.0 2.3 %shard_map.55 = (f32[576,128]{1,0:T(8,128)}, f32[192,384]{1,0:T(8,128)}) custom-call(s32[3,3]{1,0:T(4,128)} %lm_in.1, s32[3,3]{1,0:T(4,128)} %rm_in.1, f32[384,384]{1,0:T(8,128)} %left_in.1, f32[384,384]{1,0:T(8,128)} %right_in.1), custom_call_target="tpu_custom_call" | custom-call | bytes 2097152 | tf_op jit(solution)/shard_map/pallas_call | solution.py:255
  2.3 8.8 %collective-permute-start.2 = (f32[192,384]{1,0:T(8,128)}, f32[192,384]{1,0:T(8,128)S(1)}, u32[]{:S(2)}, u32[]{:S(2)}) collective-permute-start(f32[192,384]{1,0:T(8,128)} %get-tuple-element.22.refs_0_), channel_id=1, source_target_pairs={{0,2},{2,0},{4,6},{6,4},{8,10},{10,8},{12,14},{14,12},{16,18},{18,... | collective-permute-start | bytes 884744 | tf_op jit(solution)/shard_map/right_core/ppermute | solution.py:237
  11.1 5.7 %collective-permute-start.1 = (f32[192,384]{1,0:T(8,128)}, f32[192,384]{1,0:T(8,128)S(1)}, u32[]{:S(2)}, u32[]{:S(2)}) collective-permute-start(f32[192,384]{1,0:T(8,128)} %get-tuple-element.22.refs_0_), channel_id=1, source_target_pairs={{0,32},{2,482},{4,36},{6,486},{8,40},{10,490},{12,44},{14,494},{16... | collective-permute-start | bytes 884744 | tf_op jit(solution)/shard_map/own1/ppermute | solution.py:237
  16.9 4.7 %collective-permute-start = (f32[576,128]{1,0:T(8,128)}, f32[576,128]{1,0:T(8,128)S(1)}, u32[]{:S(2)}, u32[]{:S(2)}) collective-permute-start(f32[576,128]{1,0:T(8,128)} %get-tuple-element.21), channel_id=1, source_target_pairs={{0,4},{2,6},{4,0},{6,2},{8,12},{10,14},{12,8},{14,10},{16,20},{18,... | collective-permute-start | bytes 884744 | tf_op jit(solution)/shard_map/left_x/ppermute | solution.py:237
  21.5 0.0 collective-permute-done.2.refs_0_
  21.5 2.6 %collective-permute-start.3 = (f32[192,384]{1,0:T(8,128)S(1)}, f32[192,384]{1,0:T(8,128)S(1)}, u32[]{:S(2)}, u32[]{:S(2)}) collective-permute-start(f32[192,384]{1,0:T(8,128)S(1)} %collective-permute-done.2.refs_0_), channel_id=1, source_target_pairs={{0,32},{2,482},{4,36},{6,486},{8,40},{10,490},{12,44},{14,494},{16... | collective-permute-start | bytes 884744 | tf_op jit(solution)/shard_map/other1/ppermute | solution.py:237
  24.2 0.0 collective-permute-done.1.refs_1_
  24.2 2.6 %collective-permute-start.5 = (f32[192,384]{1,0:T(8,128)S(1)}, f32[192,384]{1,0:T(8,128)S(1)}, u32[]{:S(2)}, u32[]{:S(2)}) collective-permute-start(f32[192,384]{1,0:T(8,128)S(1)} %collective-permute-done.1.refs_1_), channel_id=1, source_target_pairs={{0,32},{2,482},{4,36},{6,486},{8,40},{10,490},{12,44},{14,494},{16... | collective-permute-start | bytes 884744 | tf_op jit(solution)/shard_map/own2/ppermute | solution.py:237
  26.8 0.0 collective-permute-done
  26.9 1.0 fusion
  27.9 1.4 %collective-permute-done.3.refs_1_ = f32[192,384]{1,0:T(8,128)S(1)} collective-permute-done((f32[192,384]{1,0:T(8,128)S(1)}, f32[192,384]{1,0:T(8,128)S(1)}, u32[]{:S(2)}, u32[]{:S(2)}) %collective-permute-start.3) | collective-permute-done | bytes 294944 | tf_op jit(solution)/shard_map/other1/ppermute | solution.py:237
  29.3 4.6 %collective-permute-start.4 = (f32[2,576,128]{2,1,0:T(8,128)S(1)}, f32[2,576,128]{2,1,0:T(8,128)S(1)}, u32[]{:S(2)}, u32[]{:S(2)}) collective-permute-start(f32[2,576,128]{2,1,0:T(8,128)S(1)} %get-tuple-element.23), channel_id=1, source_target_pairs={{0,8},{2,26},{4,12},{6,30},{8,16},{10,2},{12,20},{14,6},{16,24},{1... | collective-permute-start | bytes 1769480 | tf_op jit(solution)/shard_map/left_y1/ppermute | solution.py:237
  33.9 3.6 %collective-permute-start.8 = (f32[192,384]{1,0:T(8,128)S(1)}, f32[192,384]{1,0:T(8,128)S(1)}, u32[]{:S(2)}, u32[]{:S(2)}) collective-permute-start(f32[192,384]{1,0:T(8,128)S(1)} %collective-permute-done.3.refs_1_), channel_id=1, source_target_pairs={{0,32},{2,482},{4,36},{6,486},{8,40},{10,490},{12,44},{14,494},{16... | collective-permute-start | bytes 884744 | tf_op jit(solution)/shard_map/other2/ppermute | solution.py:237
  37.5 0.0 collective-permute-done.5.refs_2_
  37.5 2.3 %collective-permute-start.6 = (f32[192,384]{1,0:T(8,128)S(1)}, f32[192,384]{1,0:T(8,128)S(1)}, u32[]{:S(2)}, u32[]{:S(2)}) collective-permute-start(f32[192,384]{1,0:T(8,128)S(1)} %collective-permute-done.5.refs_2_), channel_id=1, source_target_pairs={{0,32},{2,482},{4,36},{6,486},{8,40},{10,490},{12,44},{14,494},{16... | collective-permute-start | bytes 884744 | tf_op jit(solution)/shard_map/own3/ppermute | solution.py:237
  39.8 1.9 %collective-permute-done.8.refs_2_ = f32[192,384]{1,0:T(8,128)S(1)} collective-permute-done((f32[192,384]{1,0:T(8,128)S(1)}, f32[192,384]{1,0:T(8,128)S(1)}, u32[]{:S(2)}, u32[]{:S(2)}) %collective-permute-start.8) | collective-permute-done | bytes 294944 | tf_op jit(solution)/shard_map/other2/ppermute | solution.py:237
  41.7 4.5 %collective-permute-start.12 = (f32[192,384]{1,0:T(8,128)S(1)}, f32[192,384]{1,0:T(8,128)S(1)}, u32[]{:S(2)}, u32[]{:S(2)}) collective-permute-start(f32[192,384]{1,0:T(8,128)S(1)} %collective-permute-done.8.refs_2_), channel_id=1, source_target_pairs={{0,32},{2,482},{4,36},{6,486},{8,40},{10,490},{12,44},{14,494},{16... | collective-permute-start | bytes 884744 | tf_op jit(solution)/shard_map/other3/ppermute | solution.py:237
  46.2 1.9 %collective-permute-start.9 = (f32[2,576,128]{2,1,0:T(8,128)S(1)}, f32[2,576,128]{2,1,0:T(8,128)S(1)}, u32[]{:S(2)}, u32[]{:S(2)}) collective-permute-start(f32[2,576,128]{2,1,0:T(8,128)S(1)} %get-tuple-element.23), channel_id=1, source_target_pairs={{0,24},{2,10},{4,28},{6,14},{8,0},{10,18},{12,4},{14,22},{16,8},{1... | collective-permute-start | bytes 1769480 | tf_op jit(solution)/shard_map/left_y3/ppermute | solution.py:237
  48.1 0.0 collective-permute-done.6.refs_3_
  48.1 0.0 collective-permute-done.4
  48.1 4.6 %collective-permute-start.7 = (f32[2,576,128]{2,1,0:T(8,128)S(1)}, f32[2,576,128]{2,1,0:T(8,128)S(1)}, u32[]{:S(2)}, u32[]{:S(2)}) collective-permute-start(f32[2,576,128]{2,1,0:T(8,128)S(1)} %collective-permute-done.4), channel_id=1, source_target_pairs={{0,8},{2,26},{4,12},{6,30},{8,16},{10,2},{12,20},{14,6},{16,24},{1... | collective-permute-start | bytes 1769480 | tf_op jit(solution)/shard_map/left_y2/ppermute | solution.py:237
  52.7 1.9 %collective-permute-start.10 = (f32[192,384]{1,0:T(8,128)S(1)}, f32[192,384]{1,0:T(8,128)S(1)}, u32[]{:S(2)}, u32[]{:S(2)}) collective-permute-start(f32[192,384]{1,0:T(8,128)S(1)} %collective-permute-done.6.refs_3_), channel_id=1, source_target_pairs={{0,32},{2,482},{4,36},{6,486},{8,40},{10,490},{12,44},{14,494},{16... | collective-permute-start | bytes 884744 | tf_op jit(solution)/shard_map/own4/ppermute | solution.py:237
  54.6 0.0 collective-permute-done.12.refs_3_
  54.6 2.1 %collective-permute-start.13 = (f32[192,384]{1,0:T(8,128)S(1)}, f32[192,384]{1,0:T(8,128)S(1)}, u32[]{:S(2)}, u32[]{:S(2)}) collective-permute-start(f32[192,384]{1,0:T(8,128)S(1)} %collective-permute-done.12.refs_3_), channel_id=1, source_target_pairs={{0,32},{2,482},{4,36},{6,486},{8,40},{10,490},{12,44},{14,494},{16... | collective-permute-start | bytes 884744 | tf_op jit(solution)/shard_map/other4/ppermute | solution.py:237
  56.7 3.8 %collective-permute-done.10.refs_4_ = f32[192,384]{1,0:T(8,128)S(1)} collective-permute-done((f32[192,384]{1,0:T(8,128)S(1)}, f32[192,384]{1,0:T(8,128)S(1)}, u32[]{:S(2)}, u32[]{:S(2)}) %collective-permute-start.10) | collective-permute-done | bytes 294944 | tf_op jit(solution)/shard_map/own4/ppermute | solution.py:237
  60.5 3.1 %collective-permute-start.11 = (f32[192,384]{1,0:T(8,128)S(1)}, f32[192,384]{1,0:T(8,128)S(1)}, u32[]{:S(2)}, u32[]{:S(2)}) collective-permute-start(f32[192,384]{1,0:T(8,128)S(1)} %collective-permute-done.10.refs_4_), channel_id=1, source_target_pairs={{0,32},{2,482},{4,36},{6,486},{8,40},{10,490},{12,44},{14,494},{16... | collective-permute-start | bytes 884744 | tf_op jit(solution)/shard_map/own5/ppermute | solution.py:237
  63.6 0.0 collective-permute-done.13.refs_4_
  63.6 2.9 %collective-permute-start.14 = (f32[192,384]{1,0:T(8,128)S(1)}, f32[192,384]{1,0:T(8,128)S(1)}, u32[]{:S(2)}, u32[]{:S(2)}) collective-permute-start(f32[192,384]{1,0:T(8,128)S(1)} %collective-permute-done.13.refs_4_), channel_id=1, source_target_pairs={{0,32},{2,482},{4,36},{6,486},{8,40},{10,490},{12,44},{14,494},{16... | collective-permute-start | bytes 884744 | tf_op jit(solution)/shard_map/other5/ppermute | solution.py:237
  66.5 0.0 collective-permute-done.9
  66.5 0.0 collective-permute-done.7
  66.6 0.2 pad_maximum_fusion.same
  66.7 0.0 copy-start
  66.7 1.5 %collective-permute-done.11.refs_5_ = f32[192,384]{1,0:T(8,128)S(1)} collective-permute-done((f32[192,384]{1,0:T(8,128)S(1)}, f32[192,384]{1,0:T(8,128)S(1)}, u32[]{:S(2)}, u32[]{:S(2)}) %collective-permute-start.11) | collective-permute-done | bytes 294944 | tf_op jit(solution)/shard_map/own5/ppermute | solution.py:237
  68.2 3.2 %collective-permute-done.14.refs_5_ = f32[192,384]{1,0:T(8,128)S(1)} collective-permute-done((f32[192,384]{1,0:T(8,128)S(1)}, f32[192,384]{1,0:T(8,128)S(1)}, u32[]{:S(2)}, u32[]{:S(2)}) %collective-permute-start.14) | collective-permute-done | bytes 294944 | tf_op jit(solution)/shard_map/other5/ppermute | solution.py:237
  71.4 3.2 %collective-permute-start.15 = (f32[4,2,576,128]{3,2,1,0:T(8,128)S(1)}, f32[4,2,576,128]{3,2,1,0:T(8,128)S(1)}, u32[]{:S(2)}, u32[]{:S(2)}) collective-permute-start(f32[4,2,576,128]{3,2,1,0:T(8,128)S(1)} %pad_maximum_fusion.same), channel_id=1, source_target_pairs={{0,2},{2,0},{4,6},{6,4},{8,10},{10,8},{12,14},{14,12},{16,18},{18,... | collective-permute-start | bytes 7077896 | tf_op jit(solution)/shard_map/left_core/ppermute | solution.py:237
  74.5 2.8 %collective-permute-start.17 = (f32[192,384]{1,0:T(8,128)S(1)}, f32[192,384]{1,0:T(8,128)S(1)}, u32[]{:S(2)}, u32[]{:S(2)}) collective-permute-start(f32[192,384]{1,0:T(8,128)S(1)} %collective-permute-done.11.refs_5_), channel_id=1, source_target_pairs={{0,32},{2,482},{4,36},{6,486},{8,40},{10,490},{12,44},{14,494},{16... | collective-permute-start | bytes 884744 | tf_op jit(solution)/shard_map/own6/ppermute | solution.py:237
  77.3 2.1 %collective-permute-start.18 = (f32[192,384]{1,0:T(8,128)S(1)}, f32[192,384]{1,0:T(8,128)S(1)}, u32[]{:S(2)}, u32[]{:S(2)}) collective-permute-start(f32[192,384]{1,0:T(8,128)S(1)} %collective-permute-done.14.refs_5_), channel_id=1, source_target_pairs={{0,32},{2,482},{4,36},{6,486},{8,40},{10,490},{12,44},{14,494},{16... | collective-permute-start | bytes 884744 | tf_op jit(solution)/shard_map/other6/ppermute | solution.py:237
  79.4 0.0 collective-permute-done.15.other
  79.4 2.8 %shard_map.56 = (f32[384,384]{1,0:T(8,128)S(1)}, bf16[384,1152]{1,0:T(8,128)(2,1)S(1)}, bf16[384,1152]{1,0:T(8,128)(2,1)S(1)}, f32[576,128]{1,0:T(8,128)S(1)}, b...) custom-call(f32[4,2,576,128]{3,2,1,0:T(8,128)S(1)} %pad_maximum_fusion.same, ...), custom_call_target="tpu_custom_call" | custom-call | flops 1019215872 | bytes 6291456 | tf_op jit(solution)/shard_map/pallas_call | solution.py:303
  82.2 1.9 %collective-permute-start.16 = (f32[384,384]{1,0:T(8,128)S(1)}, f32[384,384]{1,0:T(8,128)S(1)}, u32[]{:S(2)}, u32[]{:S(2)}) collective-permute-start(f32[384,384]{1,0:T(8,128)S(1)} %get-tuple-element.31), channel_id=1, source_target_pairs={{0,2},{2,0},{4,6},{6,4},{8,10},{10,8},{12,14},{14,12},{16,18},{18,... | collective-permute-start | bytes 1769480 | tf_op jit(solution)/shard_map/spare/ppermute | solution.py:237
  84.1 0.0 collective-permute-done.17.one
  84.1 4.1 %collective-permute-start.20 = (f32[192,384]{1,0:T(8,128)S(1)}, f32[192,384]{1,0:T(8,128)S(1)}, u32[]{:S(2)}, u32[]{:S(2)}) collective-permute-start(f32[192,384]{1,0:T(8,128)S(1)} %collective-permute-done.17.one), channel_id=1, source_target_pairs={{0,32},{2,482},{4,36},{6,486},{8,40},{10,490},{12,44},{14,494},{16... | collective-permute-start | bytes 884744 | tf_op jit(solution)/shard_map/own7/ppermute | solution.py:237
  88.2 0.0 collective-permute-done.18
  88.2 3.1 %collective-permute-start.21 = (f32[192,384]{1,0:T(8,128)S(1)}, f32[192,384]{1,0:T(8,128)S(1)}, u32[]{:S(2)}, u32[]{:S(2)}) collective-permute-start(f32[192,384]{1,0:T(8,128)S(1)} %collective-permute-done.18), channel_id=1, source_target_pairs={{0,34},{2,480},{4,38},{6,484},{8,42},{10,488},{12,46},{14,492},{16... | collective-permute-start | bytes 884744 | tf_op jit(solution)/shard_map/other7/ppermute | solution.py:237
  91.3 1.9 %collective-permute-start.19 = (f32[192,384]{1,0:T(8,128)S(1)}, f32[192,384]{1,0:T(8,128)S(1)}, u32[]{:S(2)}, u32[]{:S(2)}) collective-permute-start(f32[192,384]{1,0:T(8,128)S(1)} %collective-permute-done.18), channel_id=1, source_target_pairs={{0,2},{2,0},{4,6},{6,4},{8,10},{10,8},{12,14},{14,12},{16,18},{18,... | collective-permute-start | bytes 884744 | tf_op jit(solution)/shard_map/crossed/ppermute | solution.py:237
  93.2 0.0 collective-permute-done.20.three
  93.3 4.1 %collective-permute-start.23 = (f32[192,384]{1,0:T(8,128)S(1)}, f32[192,384]{1,0:T(8,128)S(1)}, u32[]{:S(2)}, u32[]{:S(2)}) collective-permute-start(f32[192,384]{1,0:T(8,128)S(1)} %collective-permute-done.20.three), channel_id=1, source_target_pairs={{0,32},{2,482},{4,36},{6,486},{8,40},{10,490},{12,44},{14,494},{16... | collective-permute-start | bytes 884744 | tf_op jit(solution)/shard_map/far_own/ppermute | solution.py:237
  97.3 0.2 collective-permute-done.21.four
  97.5 2.3 %collective-permute-start.24 = (f32[192,384]{1,0:T(8,128)S(1)}, f32[192,384]{1,0:T(8,128)S(1)}, u32[]{:S(2)}, u32[]{:S(2)}) collective-permute-start(f32[192,384]{1,0:T(8,128)S(1)} %collective-permute-done.21.four), channel_id=1, source_target_pairs={{0,481},{1,480},{2,35},{3,34},{4,485},{5,484},{6,39},{7,38},{8,489... | collective-permute-start | bytes 884744 | tf_op jit(solution)/shard_map/far_other/ppermute | solution.py:237
  99.7 0.0 copy-done
  99.7 1.7 %shard_map.57.total = f32[384,384]{1,0:T(8,128)S(1)} custom-call(bf16[384,1152]{1,0:T(8,128)(2,1)S(1)} %get-tuple-element.29.lh, bf16[384,1152]{1,0:T(8,128)(2,1)S(1)} %get-tuple-element.30.ll, f32[192,384]{1,0:T(8,128)S(1)} %copy-done, f32[192,384]{1,0:T(8,128)S(1)} %collective-permute-done.1.refs_1_, f32[192,384]{1,0:T(8,128)S(1)} %collective-permute-done.5.refs_2_, ...), custom_call_target="tpu_custom_call" | custom-call | flops 1019215872 | bytes 4194304 | tf_op jit(solution)/shard_map/pallas_call | solution.py:307
  101.5 0.0 copy-start.1
  101.5 0.0 collective-permute-done.19.two
  101.5 0.0 collective-permute-done.16.spare
  101.5 1.1 shard_map.58
  102.6 2.6 %collective-permute-start.22 = (f32[192,384]{1,0:T(8,128)S(1)}, f32[192,384]{1,0:T(8,128)S(1)}, u32[]{:S(2)}, u32[]{:S(2)}) collective-permute-start(f32[192,384]{1,0:T(8,128)S(1)} %get-tuple-element.35), channel_id=1, source_target_pairs={{0,1},{1,0},{2,3},{3,2},{4,5},{5,4},{6,7},{7,6},{8,9},{9,8},{10,11... | collective-permute-start | bytes 884744 | tf_op jit(solution)/shard_map/away/ppermute | solution.py:237
  105.2 0.0 collective-permute-done.23.right_own
  105.3 3.6 %collective-permute-done.24.right_other = f32[192,384]{1,0:T(8,128)S(1)} collective-permute-done((f32[192,384]{1,0:T(8,128)S(1)}, f32[192,384]{1,0:T(8,128)S(1)}, u32[]{:S(2)}, u32[]{:S(2)}) %collective-permute-start.24) | collective-permute-done | bytes 294944 | tf_op jit(solution)/shard_map/far_other/ppermute | solution.py:237
  108.9 5.3 %collective-permute-done.22.came = f32[192,384]{1,0:T(8,128)S(1)} collective-permute-done((f32[192,384]{1,0:T(8,128)S(1)}, f32[192,384]{1,0:T(8,128)S(1)}, u32[]{:S(2)}, u32[]{:S(2)}) %collective-permute-start.22) | collective-permute-done | bytes 294944 | tf_op jit(solution)/shard_map/away/ppermute | solution.py:237
  114.2 0.0 copy-done.1
  114.2 1.2 %shard_map.59 = f32[192,384]{1,0:T(8,128)} custom-call(s32[3,3]{1,0:T(4,128)S(1)} %copy-done.1, f32[192,384]{1,0:T(8,128)S(1)} %get-tuple-element.34.own, f32[192,384]{1,0:T(8,128)S(1)} %collective-permute-done.22.came, f32[576,128]{1,0:T(8,128)S(1)} %get-tuple-element.36.far, f32[192,384]{1,0:T(8,128)S(1)} %collective-permute-done.23.right_own, ...), custom_call_target="tpu_custom_call" | custom-call | flops 169869312 | bytes 1048576 | tf_op jit(solution)/shard_map/pallas_call | solution.py:323
Async XLA Ops:
  2.3 19.2 %collective-permute-start.2 = (f32[192,384]{1,0:T(8,128)}, f32[192,384]{1,0:T(8,128)S(1)}, u32[]{:S(2)}, u32[]{:S(2)}) collective-permute-start(f32[192,384]{1,0:T(8,128)} %get-tuple-element.22.refs_0_), channel_id=1, source_target_pairs={{0,2},{2,0},{4,6},{6,4},{8,10},{10,8},{12,14},{14,12},{16,18},{18,... | collective-permute-start | bytes 884744 | tf_op jit(solution)/shard_map/right_core/ppermute | solution.py:237
  11.1 13.1 %collective-permute-start.1 = (f32[192,384]{1,0:T(8,128)}, f32[192,384]{1,0:T(8,128)S(1)}, u32[]{:S(2)}, u32[]{:S(2)}) collective-permute-start(f32[192,384]{1,0:T(8,128)} %get-tuple-element.22.refs_0_), channel_id=1, source_target_pairs={{0,32},{2,482},{4,36},{6,486},{8,40},{10,490},{12,44},{14,494},{16... | collective-permute-start | bytes 884744 | tf_op jit(solution)/shard_map/own1/ppermute | solution.py:237
  16.9 10.0 %collective-permute-start = (f32[576,128]{1,0:T(8,128)}, f32[576,128]{1,0:T(8,128)S(1)}, u32[]{:S(2)}, u32[]{:S(2)}) collective-permute-start(f32[576,128]{1,0:T(8,128)} %get-tuple-element.21), channel_id=1, source_target_pairs={{0,4},{2,6},{4,0},{6,2},{8,12},{10,14},{12,8},{14,10},{16,20},{18,... | collective-permute-start | bytes 884744 | tf_op jit(solution)/shard_map/left_x/ppermute | solution.py:237
  21.5 7.8 %collective-permute-start.3 = (f32[192,384]{1,0:T(8,128)S(1)}, f32[192,384]{1,0:T(8,128)S(1)}, u32[]{:S(2)}, u32[]{:S(2)}) collective-permute-start(f32[192,384]{1,0:T(8,128)S(1)} %collective-permute-done.2.refs_0_), channel_id=1, source_target_pairs={{0,32},{2,482},{4,36},{6,486},{8,40},{10,490},{12,44},{14,494},{16... | collective-permute-start | bytes 884744 | tf_op jit(solution)/shard_map/other1/ppermute | solution.py:237
  24.2 13.3 %collective-permute-start.5 = (f32[192,384]{1,0:T(8,128)S(1)}, f32[192,384]{1,0:T(8,128)S(1)}, u32[]{:S(2)}, u32[]{:S(2)}) collective-permute-start(f32[192,384]{1,0:T(8,128)S(1)} %collective-permute-done.1.refs_1_), channel_id=1, source_target_pairs={{0,32},{2,482},{4,36},{6,486},{8,40},{10,490},{12,44},{14,494},{16... | collective-permute-start | bytes 884744 | tf_op jit(solution)/shard_map/own2/ppermute | solution.py:237
  29.3 18.8 %collective-permute-start.4 = (f32[2,576,128]{2,1,0:T(8,128)S(1)}, f32[2,576,128]{2,1,0:T(8,128)S(1)}, u32[]{:S(2)}, u32[]{:S(2)}) collective-permute-start(f32[2,576,128]{2,1,0:T(8,128)S(1)} %get-tuple-element.23), channel_id=1, source_target_pairs={{0,8},{2,26},{4,12},{6,30},{8,16},{10,2},{12,20},{14,6},{16,24},{1... | collective-permute-start | bytes 1769480 | tf_op jit(solution)/shard_map/left_y1/ppermute | solution.py:237
  33.9 7.8 %collective-permute-start.8 = (f32[192,384]{1,0:T(8,128)S(1)}, f32[192,384]{1,0:T(8,128)S(1)}, u32[]{:S(2)}, u32[]{:S(2)}) collective-permute-start(f32[192,384]{1,0:T(8,128)S(1)} %collective-permute-done.3.refs_1_), channel_id=1, source_target_pairs={{0,32},{2,482},{4,36},{6,486},{8,40},{10,490},{12,44},{14,494},{16... | collective-permute-start | bytes 884744 | tf_op jit(solution)/shard_map/other2/ppermute | solution.py:237
  37.5 10.6 %collective-permute-start.6 = (f32[192,384]{1,0:T(8,128)S(1)}, f32[192,384]{1,0:T(8,128)S(1)}, u32[]{:S(2)}, u32[]{:S(2)}) collective-permute-start(f32[192,384]{1,0:T(8,128)S(1)} %collective-permute-done.5.refs_2_), channel_id=1, source_target_pairs={{0,32},{2,482},{4,36},{6,486},{8,40},{10,490},{12,44},{14,494},{16... | collective-permute-start | bytes 884744 | tf_op jit(solution)/shard_map/own3/ppermute | solution.py:237
  41.7 12.9 %collective-permute-start.12 = (f32[192,384]{1,0:T(8,128)S(1)}, f32[192,384]{1,0:T(8,128)S(1)}, u32[]{:S(2)}, u32[]{:S(2)}) collective-permute-start(f32[192,384]{1,0:T(8,128)S(1)} %collective-permute-done.8.refs_2_), channel_id=1, source_target_pairs={{0,32},{2,482},{4,36},{6,486},{8,40},{10,490},{12,44},{14,494},{16... | collective-permute-start | bytes 884744 | tf_op jit(solution)/shard_map/other3/ppermute | solution.py:237
  46.2 20.4 %collective-permute-start.9 = (f32[2,576,128]{2,1,0:T(8,128)S(1)}, f32[2,576,128]{2,1,0:T(8,128)S(1)}, u32[]{:S(2)}, u32[]{:S(2)}) collective-permute-start(f32[2,576,128]{2,1,0:T(8,128)S(1)} %get-tuple-element.23), channel_id=1, source_target_pairs={{0,24},{2,10},{4,28},{6,14},{8,0},{10,18},{12,4},{14,22},{16,8},{1... | collective-permute-start | bytes 1769480 | tf_op jit(solution)/shard_map/left_y3/ppermute | solution.py:237
  48.1 18.4 %collective-permute-start.7 = (f32[2,576,128]{2,1,0:T(8,128)S(1)}, f32[2,576,128]{2,1,0:T(8,128)S(1)}, u32[]{:S(2)}, u32[]{:S(2)}) collective-permute-start(f32[2,576,128]{2,1,0:T(8,128)S(1)} %collective-permute-done.4), channel_id=1, source_target_pairs={{0,8},{2,26},{4,12},{6,30},{8,16},{10,2},{12,20},{14,6},{16,24},{1... | collective-permute-start | bytes 1769480 | tf_op jit(solution)/shard_map/left_y2/ppermute | solution.py:237
  52.7 7.8 %collective-permute-start.10 = (f32[192,384]{1,0:T(8,128)S(1)}, f32[192,384]{1,0:T(8,128)S(1)}, u32[]{:S(2)}, u32[]{:S(2)}) collective-permute-start(f32[192,384]{1,0:T(8,128)S(1)} %collective-permute-done.6.refs_3_), channel_id=1, source_target_pairs={{0,32},{2,482},{4,36},{6,486},{8,40},{10,490},{12,44},{14,494},{16... | collective-permute-start | bytes 884744 | tf_op jit(solution)/shard_map/own4/ppermute | solution.py:237
  54.6 9.0 %collective-permute-start.13 = (f32[192,384]{1,0:T(8,128)S(1)}, f32[192,384]{1,0:T(8,128)S(1)}, u32[]{:S(2)}, u32[]{:S(2)}) collective-permute-start(f32[192,384]{1,0:T(8,128)S(1)} %collective-permute-done.12.refs_3_), channel_id=1, source_target_pairs={{0,32},{2,482},{4,36},{6,486},{8,40},{10,490},{12,44},{14,494},{16... | collective-permute-start | bytes 884744 | tf_op jit(solution)/shard_map/other4/ppermute | solution.py:237
  60.5 7.8 %collective-permute-start.11 = (f32[192,384]{1,0:T(8,128)S(1)}, f32[192,384]{1,0:T(8,128)S(1)}, u32[]{:S(2)}, u32[]{:S(2)}) collective-permute-start(f32[192,384]{1,0:T(8,128)S(1)} %collective-permute-done.10.refs_4_), channel_id=1, source_target_pairs={{0,32},{2,482},{4,36},{6,486},{8,40},{10,490},{12,44},{14,494},{16... | collective-permute-start | bytes 884744 | tf_op jit(solution)/shard_map/own5/ppermute | solution.py:237
  63.6 7.8 %collective-permute-start.14 = (f32[192,384]{1,0:T(8,128)S(1)}, f32[192,384]{1,0:T(8,128)S(1)}, u32[]{:S(2)}, u32[]{:S(2)}) collective-permute-start(f32[192,384]{1,0:T(8,128)S(1)} %collective-permute-done.13.refs_4_), channel_id=1, source_target_pairs={{0,32},{2,482},{4,36},{6,486},{8,40},{10,490},{12,44},{14,494},{16... | collective-permute-start | bytes 884744 | tf_op jit(solution)/shard_map/other5/ppermute | solution.py:237
  66.7 33.0 %copy-start = (f32[192,384]{1,0:T(8,128)S(1)}, f32[192,384]{1,0:T(8,128)}, u32[]{:S(2)}) copy-start(f32[192,384]{1,0:T(8,128)} %get-tuple-element.22.refs_0_) | copy-start | bytes 884740
  71.4 8.0 %collective-permute-start.15 = (f32[4,2,576,128]{3,2,1,0:T(8,128)S(1)}, f32[4,2,576,128]{3,2,1,0:T(8,128)S(1)}, u32[]{:S(2)}, u32[]{:S(2)}) collective-permute-start(f32[4,2,576,128]{3,2,1,0:T(8,128)S(1)} %pad_maximum_fusion.same), channel_id=1, source_target_pairs={{0,2},{2,0},{4,6},{6,4},{8,10},{10,8},{12,14},{14,12},{16,18},{18,... | collective-permute-start | bytes 7077896 | tf_op jit(solution)/shard_map/left_core/ppermute | solution.py:237
  74.5 9.6 %collective-permute-start.17 = (f32[192,384]{1,0:T(8,128)S(1)}, f32[192,384]{1,0:T(8,128)S(1)}, u32[]{:S(2)}, u32[]{:S(2)}) collective-permute-start(f32[192,384]{1,0:T(8,128)S(1)} %collective-permute-done.11.refs_5_), channel_id=1, source_target_pairs={{0,32},{2,482},{4,36},{6,486},{8,40},{10,490},{12,44},{14,494},{16... | collective-permute-start | bytes 884744 | tf_op jit(solution)/shard_map/own6/ppermute | solution.py:237
  77.3 10.9 %collective-permute-start.18 = (f32[192,384]{1,0:T(8,128)S(1)}, f32[192,384]{1,0:T(8,128)S(1)}, u32[]{:S(2)}, u32[]{:S(2)}) collective-permute-start(f32[192,384]{1,0:T(8,128)S(1)} %collective-permute-done.14.refs_5_), channel_id=1, source_target_pairs={{0,32},{2,482},{4,36},{6,486},{8,40},{10,490},{12,44},{14,494},{16... | collective-permute-start | bytes 884744 | tf_op jit(solution)/shard_map/other6/ppermute | solution.py:237
  82.2 19.3 %collective-permute-start.16 = (f32[384,384]{1,0:T(8,128)S(1)}, f32[384,384]{1,0:T(8,128)S(1)}, u32[]{:S(2)}, u32[]{:S(2)}) collective-permute-start(f32[384,384]{1,0:T(8,128)S(1)} %get-tuple-element.31), channel_id=1, source_target_pairs={{0,2},{2,0},{4,6},{6,4},{8,10},{10,8},{12,14},{14,12},{16,18},{18,... | collective-permute-start | bytes 1769480 | tf_op jit(solution)/shard_map/spare/ppermute | solution.py:237
  84.1 9.1 %collective-permute-start.20 = (f32[192,384]{1,0:T(8,128)S(1)}, f32[192,384]{1,0:T(8,128)S(1)}, u32[]{:S(2)}, u32[]{:S(2)}) collective-permute-start(f32[192,384]{1,0:T(8,128)S(1)} %collective-permute-done.17.one), channel_id=1, source_target_pairs={{0,32},{2,482},{4,36},{6,486},{8,40},{10,490},{12,44},{14,494},{16... | collective-permute-start | bytes 884744 | tf_op jit(solution)/shard_map/own7/ppermute | solution.py:237
  88.2 9.3 %collective-permute-start.21 = (f32[192,384]{1,0:T(8,128)S(1)}, f32[192,384]{1,0:T(8,128)S(1)}, u32[]{:S(2)}, u32[]{:S(2)}) collective-permute-start(f32[192,384]{1,0:T(8,128)S(1)} %collective-permute-done.18), channel_id=1, source_target_pairs={{0,34},{2,480},{4,38},{6,484},{8,42},{10,488},{12,46},{14,492},{16... | collective-permute-start | bytes 884744 | tf_op jit(solution)/shard_map/other7/ppermute | solution.py:237
  91.3 10.2 %collective-permute-start.19 = (f32[192,384]{1,0:T(8,128)S(1)}, f32[192,384]{1,0:T(8,128)S(1)}, u32[]{:S(2)}, u32[]{:S(2)}) collective-permute-start(f32[192,384]{1,0:T(8,128)S(1)} %collective-permute-done.18), channel_id=1, source_target_pairs={{0,2},{2,0},{4,6},{6,4},{8,10},{10,8},{12,14},{14,12},{16,18},{18,... | collective-permute-start | bytes 884744 | tf_op jit(solution)/shard_map/crossed/ppermute | solution.py:237
  93.3 12.0 %collective-permute-start.23 = (f32[192,384]{1,0:T(8,128)S(1)}, f32[192,384]{1,0:T(8,128)S(1)}, u32[]{:S(2)}, u32[]{:S(2)}) collective-permute-start(f32[192,384]{1,0:T(8,128)S(1)} %collective-permute-done.20.three), channel_id=1, source_target_pairs={{0,32},{2,482},{4,36},{6,486},{8,40},{10,490},{12,44},{14,494},{16... | collective-permute-start | bytes 884744 | tf_op jit(solution)/shard_map/far_own/ppermute | solution.py:237
  97.5 11.4 %collective-permute-start.24 = (f32[192,384]{1,0:T(8,128)S(1)}, f32[192,384]{1,0:T(8,128)S(1)}, u32[]{:S(2)}, u32[]{:S(2)}) collective-permute-start(f32[192,384]{1,0:T(8,128)S(1)} %collective-permute-done.21.four), channel_id=1, source_target_pairs={{0,481},{1,480},{2,35},{3,34},{4,485},{5,484},{6,39},{7,38},{8,489... | collective-permute-start | bytes 884744 | tf_op jit(solution)/shard_map/far_other/ppermute | solution.py:237
  101.5 12.8 %copy-start.1 = (s32[3,3]{1,0:T(4,128)S(1)}, s32[3,3]{1,0:T(4,128)}, u32[]{:S(2)}) copy-start(s32[3,3]{1,0:T(4,128)} %keep.1) | copy-start | bytes 112
  102.6 11.6 %collective-permute-start.22 = (f32[192,384]{1,0:T(8,128)S(1)}, f32[192,384]{1,0:T(8,128)S(1)}, u32[]{:S(2)}, u32[]{:S(2)}) collective-permute-start(f32[192,384]{1,0:T(8,128)S(1)} %get-tuple-element.35), channel_id=1, source_target_pairs={{0,1},{1,0},{2,3},{3,2},{4,5},{5,4},{6,7},{7,6},{8,9},{9,8},{10,11... | collective-permute-start | bytes 884744 | tf_op jit(solution)/shard_map/away/ppermute | solution.py:237

commit v10 on v9

--- a/solution.py
+++ b/solution.py
@@ -309,7 +309,7 @@
         flops=6 * span * TILE**2, nbytes=4 * 2**20,
     )(left_h, left_l, *mine[:early])
     with jax.named_scope("spare"):
-        spare = move(spare, ("col",), lambda c: (c ^ 1,))
+        spare = move(after(spare, others[early]), ("col",), lambda c: (c ^ 1,))
     rights = pltpu.VMEM((2 * TILE, TILE), BF16)
     own, away = call(
         near_kernel, (half, half), [VMEM] * 8, [rights, rights], flops=12 * TILE**3, nbytes=2**21

time: 116 us -> 119 us (1.026)
  waiting for transfers between devices: 20.9 us -> 22.6 us
    ppermute x25, waiting for transfers between devices: 20.9 us -> 22.6 us  [move(): lax.ppermute(value, axes, [(flat(at), flat(target(*at))) for at in points])]
  transfers between devices with their start and end apart: 25 -> 25, of which waited for: 8 -> 9; matrix products, arithmetic and copies ran while one was open for 1% -> 1% of each run, Pallas kernels for 5% -> 5%
where the time goes in v10:
time: 119 us; the launch traced here: 118 us
  starting transfers between devices  84.4 us (71%)
  waiting for transfers between devices  22.6 us (19%)
  Pallas kernels  9.11 us (8%)
  other arithmetic  1.2 us (1%)
    ppermute x25, starting transfers between devices, move(): lax.ppermute(value, axes, [(flat(at), flat(target(*at))) for at in points])  84.4 us
    ppermute x25, waiting for transfers between devices, move(): lax.ppermute(value, axes, [(flat(at), flat(target(*at))) for at in points])  22.6 us
    pallas_call x1, Pallas kernels, shards(): call(functools.partial(spare_kernel, early), (whole, lefts, lefts, packed...  2.76 us
  transfers between devices with their start and end apart: 25, of which 9 were waited for; matrix products, arithmetic and copies ran while one was open for 1% of the time, Pallas kernels for 5%

profile of v10, /device:TPU:1, one launch (start us, length us, event | category | flops | bytes accessed | tf_op | source)
XLA Modules:
  0.0 117.7 jit_solution(5505182334427203412)
XLA Ops:
  0.0 2.3 %shard_map.55 = (f32[576,128]{1,0:T(8,128)}, f32[192,384]{1,0:T(8,128)}) custom-call(s32[3,3]{1,0:T(4,128)} %lm_in.1, s32[3,3]{1,0:T(4,128)} %rm_in.1, f32[384,384]{1,0:T(8,128)} %left_in.1, f32[384,384]{1,0:T(8,128)} %right_in.1), custom_call_target="tpu_custom_call" | custom-call | bytes 2097152 | tf_op jit(solution)/shard_map/pallas_call | solution.py:255
  2.3 8.8 %collective-permute-start.2 = (f32[192,384]{1,0:T(8,128)}, f32[192,384]{1,0:T(8,128)S(1)}, u32[]{:S(2)}, u32[]{:S(2)}) collective-permute-start(f32[192,384]{1,0:T(8,128)} %get-tuple-element.23.refs_0_), channel_id=1, source_target_pairs={{0,2},{2,0},{4,6},{6,4},{8,10},{10,8},{12,14},{14,12},{16,18},{18,... | collective-permute-start | bytes 884744 | tf_op jit(solution)/shard_map/right_core/ppermute | solution.py:237
  11.1 5.7 %collective-permute-start.1 = (f32[192,384]{1,0:T(8,128)}, f32[192,384]{1,0:T(8,128)S(1)}, u32[]{:S(2)}, u32[]{:S(2)}) collective-permute-start(f32[192,384]{1,0:T(8,128)} %get-tuple-element.23.refs_0_), channel_id=1, source_target_pairs={{0,32},{2,482},{4,36},{6,486},{8,40},{10,490},{12,44},{14,494},{16... | collective-permute-start | bytes 884744 | tf_op jit(solution)/shard_map/own1/ppermute | solution.py:237
  16.9 4.7 %collective-permute-start = (f32[576,128]{1,0:T(8,128)}, f32[576,128]{1,0:T(8,128)S(1)}, u32[]{:S(2)}, u32[]{:S(2)}) collective-permute-start(f32[576,128]{1,0:T(8,128)} %get-tuple-element.22), channel_id=1, source_target_pairs={{0,4},{2,6},{4,0},{6,2},{8,12},{10,14},{12,8},{14,10},{16,20},{18,... | collective-permute-start | bytes 884744 | tf_op jit(solution)/shard_map/left_x/ppermute | solution.py:237
  21.5 0.0 collective-permute-done.2.refs_0_
  21.5 2.6 %collective-permute-start.3 = (f32[192,384]{1,0:T(8,128)S(1)}, f32[192,384]{1,0:T(8,128)S(1)}, u32[]{:S(2)}, u32[]{:S(2)}) collective-permute-start(f32[192,384]{1,0:T(8,128)S(1)} %collective-permute-done.2.refs_0_), channel_id=1, source_target_pairs={{0,32},{2,482},{4,36},{6,486},{8,40},{10,490},{12,44},{14,494},{16... | collective-permute-start | bytes 884744 | tf_op jit(solution)/shard_map/other1/ppermute | solution.py:237
  24.2 0.0 collective-permute-done.1.refs_1_
  24.2 2.6 %collective-permute-start.5 = (f32[192,384]{1,0:T(8,128)S(1)}, f32[192,384]{1,0:T(8,128)S(1)}, u32[]{:S(2)}, u32[]{:S(2)}) collective-permute-start(f32[192,384]{1,0:T(8,128)S(1)} %collective-permute-done.1.refs_1_), channel_id=1, source_target_pairs={{0,32},{2,482},{4,36},{6,486},{8,40},{10,490},{12,44},{14,494},{16... | collective-permute-start | bytes 884744 | tf_op jit(solution)/shard_map/own2/ppermute | solution.py:237
  26.8 0.0 collective-permute-done
  26.9 1.0 fusion
  27.9 1.4 %collective-permute-done.3.refs_1_ = f32[192,384]{1,0:T(8,128)S(1)} collective-permute-done((f32[192,384]{1,0:T(8,128)S(1)}, f32[192,384]{1,0:T(8,128)S(1)}, u32[]{:S(2)}, u32[]{:S(2)}) %collective-permute-start.3) | collective-permute-done | bytes 294944 | tf_op jit(solution)/shard_map/other1/ppermute | solution.py:237
  29.3 4.6 %collective-permute-start.4 = (f32[2,576,128]{2,1,0:T(8,128)S(1)}, f32[2,576,128]{2,1,0:T(8,128)S(1)}, u32[]{:S(2)}, u32[]{:S(2)}) collective-permute-start(f32[2,576,128]{2,1,0:T(8,128)S(1)} %get-tuple-element.24), channel_id=1, source_target_pairs={{0,8},{2,26},{4,12},{6,30},{8,16},{10,2},{12,20},{14,6},{16,24},{1... | collective-permute-start | bytes 1769480 | tf_op jit(solution)/shard_map/left_y1/ppermute | solution.py:237
  33.9 3.6 %collective-permute-start.8 = (f32[192,384]{1,0:T(8,128)S(1)}, f32[192,384]{1,0:T(8,128)S(1)}, u32[]{:S(2)}, u32[]{:S(2)}) collective-permute-start(f32[192,384]{1,0:T(8,128)S(1)} %collective-permute-done.3.refs_1_), channel_id=1, source_target_pairs={{0,32},{2,482},{4,36},{6,486},{8,40},{10,490},{12,44},{14,494},{16... | collective-permute-start | bytes 884744 | tf_op jit(solution)/shard_map/other2/ppermute | solution.py:237
  37.5 0.0 collective-permute-done.5.refs_2_
  37.5 2.3 %collective-permute-start.6 = (f32[192,384]{1,0:T(8,128)S(1)}, f32[192,384]{1,0:T(8,128)S(1)}, u32[]{:S(2)}, u32[]{:S(2)}) collective-permute-start(f32[192,384]{1,0:T(8,128)S(1)} %collective-permute-done.5.refs_2_), channel_id=1, source_target_pairs={{0,32},{2,482},{4,36},{6,486},{8,40},{10,490},{12,44},{14,494},{16... | collective-permute-start | bytes 884744 | tf_op jit(solution)/shard_map/own3/ppermute | solution.py:237
  39.8 1.9 %collective-permute-done.8.refs_2_ = f32[192,384]{1,0:T(8,128)S(1)} collective-permute-done((f32[192,384]{1,0:T(8,128)S(1)}, f32[192,384]{1,0:T(8,128)S(1)}, u32[]{:S(2)}, u32[]{:S(2)}) %collective-permute-start.8) | collective-permute-done | bytes 294944 | tf_op jit(solution)/shard_map/other2/ppermute | solution.py:237
  41.7 4.5 %collective-permute-start.12 = (f32[192,384]{1,0:T(8,128)S(1)}, f32[192,384]{1,0:T(8,128)S(1)}, u32[]{:S(2)}, u32[]{:S(2)}) collective-permute-start(f32[192,384]{1,0:T(8,128)S(1)} %collective-permute-done.8.refs_2_), channel_id=1, source_target_pairs={{0,32},{2,482},{4,36},{6,486},{8,40},{10,490},{12,44},{14,494},{16... | collective-permute-start | bytes 884744 | tf_op jit(solution)/shard_map/other3/ppermute | solution.py:237
  46.2 1.9 %collective-permute-start.9 = (f32[2,576,128]{2,1,0:T(8,128)S(1)}, f32[2,576,128]{2,1,0:T(8,128)S(1)}, u32[]{:S(2)}, u32[]{:S(2)}) collective-permute-start(f32[2,576,128]{2,1,0:T(8,128)S(1)} %get-tuple-element.24), channel_id=1, source_target_pairs={{0,24},{2,10},{4,28},{6,14},{8,0},{10,18},{12,4},{14,22},{16,8},{1... | collective-permute-start | bytes 1769480 | tf_op jit(solution)/shard_map/left_y3/ppermute | solution.py:237
  48.1 0.0 collective-permute-done.6.refs_3_
  48.1 0.0 collective-permute-done.4
  48.1 4.6 %collective-permute-start.7 = (f32[2,576,128]{2,1,0:T(8,128)S(1)}, f32[2,576,128]{2,1,0:T(8,128)S(1)}, u32[]{:S(2)}, u32[]{:S(2)}) collective-permute-start(f32[2,576,128]{2,1,0:T(8,128)S(1)} %collective-permute-done.4), channel_id=1, source_target_pairs={{0,8},{2,26},{4,12},{6,30},{8,16},{10,2},{12,20},{14,6},{16,24},{1... | collective-permute-start | bytes 1769480 | tf_op jit(solution)/shard_map/left_y2/ppermute | solution.py:237
  52.7 1.9 %collective-permute-start.10 = (f32[192,384]{1,0:T(8,128)S(1)}, f32[192,384]{1,0:T(8,128)S(1)}, u32[]{:S(2)}, u32[]{:S(2)}) collective-permute-start(f32[192,384]{1,0:T(8,128)S(1)} %collective-permute-done.6.refs_3_), channel_id=1, source_target_pairs={{0,32},{2,482},{4,36},{6,486},{8,40},{10,490},{12,44},{14,494},{16... | collective-permute-start | bytes 884744 | tf_op jit(solution)/shard_map/own4/ppermute | solution.py:237
  54.6 0.0 collective-permute-done.12.refs_3_
  54.6 2.1 %collective-permute-start.13 = (f32[192,384]{1,0:T(8,128)S(1)}, f32[192,384]{1,0:T(8,128)S(1)}, u32[]{:S(2)}, u32[]{:S(2)}) collective-permute-start(f32[192,384]{1,0:T(8,128)S(1)} %collective-permute-done.12.refs_3_), channel_id=1, source_target_pairs={{0,32},{2,482},{4,36},{6,486},{8,40},{10,490},{12,44},{14,494},{16... | collective-permute-start | bytes 884744 | tf_op jit(solution)/shard_map/other4/ppermute | solution.py:237
  56.7 3.8 %collective-permute-done.10.refs_4_ = f32[192,384]{1,0:T(8,128)S(1)} collective-permute-done((f32[192,384]{1,0:T(8,128)S(1)}, f32[192,384]{1,0:T(8,128)S(1)}, u32[]{:S(2)}, u32[]{:S(2)}) %collective-permute-start.10) | collective-permute-done | bytes 294944 | tf_op jit(solution)/shard_map/own4/ppermute | solution.py:237
  60.5 3.1 %collective-permute-start.11 = (f32[192,384]{1,0:T(8,128)S(1)}, f32[192,384]{1,0:T(8,128)S(1)}, u32[]{:S(2)}, u32[]{:S(2)}) collective-permute-start(f32[192,384]{1,0:T(8,128)S(1)} %collective-permute-done.10.refs_4_), channel_id=1, source_target_pairs={{0,32},{2,482},{4,36},{6,486},{8,40},{10,490},{12,44},{14,494},{16... | collective-permute-start | bytes 884744 | tf_op jit(solution)/shard_map/own5/ppermute | solution.py:237
  63.6 0.0 collective-permute-done.13.refs_4_
  63.6 2.9 %collective-permute-start.14 = (f32[192,384]{1,0:T(8,128)S(1)}, f32[192,384]{1,0:T(8,128)S(1)}, u32[]{:S(2)}, u32[]{:S(2)}) collective-permute-start(f32[192,384]{1,0:T(8,128)S(1)} %collective-permute-done.13.refs_4_), channel_id=1, source_target_pairs={{0,32},{2,482},{4,36},{6,486},{8,40},{10,490},{12,44},{14,494},{16... | collective-permute-start | bytes 884744 | tf_op jit(solution)/shard_map/other5/ppermute | solution.py:237
  66.5 0.0 collective-permute-done.9
  66.5 0.0 collective-permute-done.7
  66.6 0.2 pad_maximum_fusion.same
  66.7 0.0 copy-start
  66.7 1.5 %collective-permute-done.11.refs_5_ = f32[192,384]{1,0:T(8,128)S(1)} collective-permute-done((f32[192,384]{1,0:T(8,128)S(1)}, f32[192,384]{1,0:T(8,128)S(1)}, u32[]{:S(2)}, u32[]{:S(2)}) %collective-permute-start.11) | collective-permute-done | bytes 294944 | tf_op jit(solution)/shard_map/own5/ppermute | solution.py:237
  68.2 3.2 %collective-permute-done.14.refs_5_ = f32[192,384]{1,0:T(8,128)S(1)} collective-permute-done((f32[192,384]{1,0:T(8,128)S(1)}, f32[192,384]{1,0:T(8,128)S(1)}, u32[]{:S(2)}, u32[]{:S(2)}) %collective-permute-start.14) | collective-permute-done | bytes 294944 | tf_op jit(solution)/shard_map/other5/ppermute | solution.py:237
  71.4 3.2 %collective-permute-start.15 = (f32[4,2,576,128]{3,2,1,0:T(8,128)S(1)}, f32[4,2,576,128]{3,2,1,0:T(8,128)S(1)}, u32[]{:S(2)}, u32[]{:S(2)}) collective-permute-start(f32[4,2,576,128]{3,2,1,0:T(8,128)S(1)} %pad_maximum_fusion.same), channel_id=1, source_target_pairs={{0,2},{2,0},{4,6},{6,4},{8,10},{10,8},{12,14},{14,12},{16,18},{18,... | collective-permute-start | bytes 7077896 | tf_op jit(solution)/shard_map/left_core/ppermute | solution.py:237
  74.5 2.8 %collective-permute-start.16 = (f32[192,384]{1,0:T(8,128)S(1)}, f32[192,384]{1,0:T(8,128)S(1)}, u32[]{:S(2)}, u32[]{:S(2)}) collective-permute-start(f32[192,384]{1,0:T(8,128)S(1)} %collective-permute-done.14.refs_5_), channel_id=1, source_target_pairs={{0,32},{2,482},{4,36},{6,486},{8,40},{10,490},{12,44},{14,494},{16... | collective-permute-start | bytes 884744 | tf_op jit(solution)/shard_map/other6/ppermute | solution.py:237
  77.3 2.1 %collective-permute-start.18 = (f32[192,384]{1,0:T(8,128)S(1)}, f32[192,384]{1,0:T(8,128)S(1)}, u32[]{:S(2)}, u32[]{:S(2)}) collective-permute-start(f32[192,384]{1,0:T(8,128)S(1)} %collective-permute-done.11.refs_5_), channel_id=1, source_target_pairs={{0,32},{2,482},{4,36},{6,486},{8,40},{10,490},{12,44},{14,494},{16... | collective-permute-start | bytes 884744 | tf_op jit(solution)/shard_map/own6/ppermute | solution.py:237
  79.4 0.0 collective-permute-done.15.other
  79.4 2.8 %shard_map.56 = (f32[384,384]{1,0:T(8,128)S(1)}, bf16[384,1152]{1,0:T(8,128)(2,1)S(1)}, bf16[384,1152]{1,0:T(8,128)(2,1)S(1)}, f32[576,128]{1,0:T(8,128)S(1)}, b...) custom-call(f32[4,2,576,128]{3,2,1,0:T(8,128)S(1)} %pad_maximum_fusion.same, ...), custom_call_target="tpu_custom_call" | custom-call | flops 1019215872 | bytes 6291456 | tf_op jit(solution)/shard_map/pallas_call | solution.py:303
  82.2 0.1 collective-permute-done.16
  82.3 4.0 %collective-permute-start.17 = (f32[384,384]{1,0:T(8,128)S(1)}, f32[384,384]{1,0:T(8,128)S(1)}, u32[]{:S(2)}, u32[]{:S(2)}) collective-permute-start(f32[384,384]{1,0:T(8,128)S(1)} %get-tuple-element.33), channel_id=1, source_target_pairs={{0,2},{2,0},{4,6},{6,4},{8,10},{10,8},{12,14},{14,12},{16,18},{18,... | collective-permute-start | bytes 1769480 | tf_op jit(solution)/shard_map/spare/ppermute | solution.py:237
  86.3 0.0 collective-permute-done.18.one
  86.3 2.9 %collective-permute-start.20 = (f32[192,384]{1,0:T(8,128)S(1)}, f32[192,384]{1,0:T(8,128)S(1)}, u32[]{:S(2)}, u32[]{:S(2)}) collective-permute-start(f32[192,384]{1,0:T(8,128)S(1)} %collective-permute-done.18.one), channel_id=1, source_target_pairs={{0,32},{2,482},{4,36},{6,486},{8,40},{10,490},{12,44},{14,494},{16... | collective-permute-start | bytes 884744 | tf_op jit(solution)/shard_map/own7/ppermute | solution.py:237
  89.2 5.0 %collective-permute-start.21 = (f32[192,384]{1,0:T(8,128)S(1)}, f32[192,384]{1,0:T(8,128)S(1)}, u32[]{:S(2)}, u32[]{:S(2)}) collective-permute-start(f32[192,384]{1,0:T(8,128)S(1)} %collective-permute-done.16), channel_id=1, source_target_pairs={{0,34},{2,480},{4,38},{6,484},{8,42},{10,488},{12,46},{14,492},{16... | collective-permute-start | bytes 884744 | tf_op jit(solution)/shard_map/other7/ppermute | solution.py:237
  94.2 1.9 %collective-permute-start.19 = (f32[192,384]{1,0:T(8,128)S(1)}, f32[192,384]{1,0:T(8,128)S(1)}, u32[]{:S(2)}, u32[]{:S(2)}) collective-permute-start(f32[192,384]{1,0:T(8,128)S(1)} %collective-permute-done.16), channel_id=1, source_target_pairs={{0,2},{2,0},{4,6},{6,4},{8,10},{10,8},{12,14},{14,12},{16,18},{18,... | collective-permute-start | bytes 884744 | tf_op jit(solution)/shard_map/crossed/ppermute | solution.py:237
  96.1 0.0 collective-permute-done.20.three
  96.1 2.0 %collective-permute-start.23 = (f32[192,384]{1,0:T(8,128)S(1)}, f32[192,384]{1,0:T(8,128)S(1)}, u32[]{:S(2)}, u32[]{:S(2)}) collective-permute-start(f32[192,384]{1,0:T(8,128)S(1)} %collective-permute-done.20.three), channel_id=1, source_target_pairs={{0,32},{2,482},{4,36},{6,486},{8,40},{10,490},{12,44},{14,494},{16... | collective-permute-start | bytes 884744 | tf_op jit(solution)/shard_map/far_own/ppermute | solution.py:237
  98.2 1.7 %collective-permute-done.21.four = f32[192,384]{1,0:T(8,128)S(1)} collective-permute-done((f32[192,384]{1,0:T(8,128)S(1)}, f32[192,384]{1,0:T(8,128)S(1)}, u32[]{:S(2)}, u32[]{:S(2)}) %collective-permute-start.21) | collective-permute-done | bytes 294944 | tf_op jit(solution)/shard_map/other7/ppermute | solution.py:237
  99.8 2.1 %collective-permute-start.24 = (f32[192,384]{1,0:T(8,128)S(1)}, f32[192,384]{1,0:T(8,128)S(1)}, u32[]{:S(2)}, u32[]{:S(2)}) collective-permute-start(f32[192,384]{1,0:T(8,128)S(1)} %collective-permute-done.21.four), channel_id=1, source_target_pairs={{0,481},{1,480},{2,35},{3,34},{4,485},{5,484},{6,39},{7,38},{8,489... | collective-permute-start | bytes 884744 | tf_op jit(solution)/shard_map/far_other/ppermute | solution.py:237
  101.9 0.0 copy-done
  101.9 1.7 %shard_map.57.total = f32[384,384]{1,0:T(8,128)S(1)} custom-call(bf16[384,1152]{1,0:T(8,128)(2,1)S(1)} %get-tuple-element.30.lh, bf16[384,1152]{1,0:T(8,128)(2,1)S(1)} %get-tuple-element.31.ll, f32[192,384]{1,0:T(8,128)S(1)} %copy-done, f32[192,384]{1,0:T(8,128)S(1)} %collective-permute-done.1.refs_1_, f32[192,384]{1,0:T(8,128)S(1)} %collective-permute-done.5.refs_2_, ...), custom_call_target="tpu_custom_call" | custom-call | flops 1019215872 | bytes 4194304 | tf_op jit(solution)/shard_map/pallas_call | solution.py:307
  103.6 0.0 copy-start.1
  103.6 0.0 collective-permute-done.19.two
  103.7 0.0 collective-permute-done.17.spare
  103.7 1.1 shard_map.58
  104.8 2.6 %collective-permute-start.22 = (f32[192,384]{1,0:T(8,128)S(1)}, f32[192,384]{1,0:T(8,128)S(1)}, u32[]{:S(2)}, u32[]{:S(2)}) collective-permute-start(f32[192,384]{1,0:T(8,128)S(1)} %get-tuple-element.37), channel_id=1, source_target_pairs={{0,1},{1,0},{2,3},{3,2},{4,5},{5,4},{6,7},{7,6},{8,9},{9,8},{10,11... | collective-permute-start | bytes 884744 | tf_op jit(solution)/shard_map/away/ppermute | solution.py:237
  107.5 0.0 collective-permute-done.23.right_own
  107.5 3.9 %collective-permute-done.24.right_other = f32[192,384]{1,0:T(8,128)S(1)} collective-permute-done((f32[192,384]{1,0:T(8,128)S(1)}, f32[192,384]{1,0:T(8,128)S(1)}, u32[]{:S(2)}, u32[]{:S(2)}) %collective-permute-start.24) | collective-permute-done | bytes 294944 | tf_op jit(solution)/shard_map/far_other/ppermute | solution.py:237
  111.4 5.2 %collective-permute-done.22.came = f32[192,384]{1,0:T(8,128)S(1)} collective-permute-done((f32[192,384]{1,0:T(8,128)S(1)}, f32[192,384]{1,0:T(8,128)S(1)}, u32[]{:S(2)}, u32[]{:S(2)}) %collective-permute-start.22) | collective-permute-done | bytes 294944 | tf_op jit(solution)/shard_map/away/ppermute | solution.py:237
  116.5 0.0 copy-done.1
  116.5 1.2 %shard_map.59 = f32[192,384]{1,0:T(8,128)} custom-call(s32[3,3]{1,0:T(4,128)S(1)} %copy-done.1, f32[192,384]{1,0:T(8,128)S(1)} %get-tuple-element.36.own, f32[192,384]{1,0:T(8,128)S(1)} %collective-permute-done.22.came, f32[576,128]{1,0:T(8,128)S(1)} %get-tuple-element.38.far, f32[192,384]{1,0:T(8,128)S(1)} %collective-permute-done.23.right_own, ...), custom_call_target="tpu_custom_call" | custom-call | flops 169869312 | bytes 1048576 | tf_op jit(solution)/shard_map/pallas_call | solution.py:323
Async XLA Ops:
  2.3 19.2 %collective-permute-start.2 = (f32[192,384]{1,0:T(8,128)}, f32[192,384]{1,0:T(8,128)S(1)}, u32[]{:S(2)}, u32[]{:S(2)}) collective-permute-start(f32[192,384]{1,0:T(8,128)} %get-tuple-element.23.refs_0_), channel_id=1, source_target_pairs={{0,2},{2,0},{4,6},{6,4},{8,10},{10,8},{12,14},{14,12},{16,18},{18,... | collective-permute-start | bytes 884744 | tf_op jit(solution)/shard_map/right_core/ppermute | solution.py:237
  11.1 13.1 %collective-permute-start.1 = (f32[192,384]{1,0:T(8,128)}, f32[192,384]{1,0:T(8,128)S(1)}, u32[]{:S(2)}, u32[]{:S(2)}) collective-permute-start(f32[192,384]{1,0:T(8,128)} %get-tuple-element.23.refs_0_), channel_id=1, source_target_pairs={{0,32},{2,482},{4,36},{6,486},{8,40},{10,490},{12,44},{14,494},{16... | collective-permute-start | bytes 884744 | tf_op jit(solution)/shard_map/own1/ppermute | solution.py:237
  16.9 10.0 %collective-permute-start = (f32[576,128]{1,0:T(8,128)}, f32[576,128]{1,0:T(8,128)S(1)}, u32[]{:S(2)}, u32[]{:S(2)}) collective-permute-start(f32[576,128]{1,0:T(8,128)} %get-tuple-element.22), channel_id=1, source_target_pairs={{0,4},{2,6},{4,0},{6,2},{8,12},{10,14},{12,8},{14,10},{16,20},{18,... | collective-permute-start | bytes 884744 | tf_op jit(solution)/shard_map/left_x/ppermute | solution.py:237
  21.5 7.8 %collective-permute-start.3 = (f32[192,384]{1,0:T(8,128)S(1)}, f32[192,384]{1,0:T(8,128)S(1)}, u32[]{:S(2)}, u32[]{:S(2)}) collective-permute-start(f32[192,384]{1,0:T(8,128)S(1)} %collective-permute-done.2.refs_0_), channel_id=1, source_target_pairs={{0,32},{2,482},{4,36},{6,486},{8,40},{10,490},{12,44},{14,494},{16... | collective-permute-start | bytes 884744 | tf_op jit(solution)/shard_map/other1/ppermute | solution.py:237
  24.2 13.3 %collective-permute-start.5 = (f32[192,384]{1,0:T(8,128)S(1)}, f32[192,384]{1,0:T(8,128)S(1)}, u32[]{:S(2)}, u32[]{:S(2)}) collective-permute-start(f32[192,384]{1,0:T(8,128)S(1)} %collective-permute-done.1.refs_1_), channel_id=1, source_target_pairs={{0,32},{2,482},{4,36},{6,486},{8,40},{10,490},{12,44},{14,494},{16... | collective-permute-start | bytes 884744 | tf_op jit(solution)/shard_map/own2/ppermute | solution.py:237
  29.3 18.8 %collective-permute-start.4 = (f32[2,576,128]{2,1,0:T(8,128)S(1)}, f32[2,576,128]{2,1,0:T(8,128)S(1)}, u32[]{:S(2)}, u32[]{:S(2)}) collective-permute-start(f32[2,576,128]{2,1,0:T(8,128)S(1)} %get-tuple-element.24), channel_id=1, source_target_pairs={{0,8},{2,26},{4,12},{6,30},{8,16},{10,2},{12,20},{14,6},{16,24},{1... | collective-permute-start | bytes 1769480 | tf_op jit(solution)/shard_map/left_y1/ppermute | solution.py:237
  33.9 7.8 %collective-permute-start.8 = (f32[192,384]{1,0:T(8,128)S(1)}, f32[192,384]{1,0:T(8,128)S(1)}, u32[]{:S(2)}, u32[]{:S(2)}) collective-permute-start(f32[192,384]{1,0:T(8,128)S(1)} %collective-permute-done.3.refs_1_), channel_id=1, source_target_pairs={{0,32},{2,482},{4,36},{6,486},{8,40},{10,490},{12,44},{14,494},{16... | collective-permute-start | bytes 884744 | tf_op jit(solution)/shard_map/other2/ppermute | solution.py:237
  37.5 10.6 %collective-permute-start.6 = (f32[192,384]{1,0:T(8,128)S(1)}, f32[192,384]{1,0:T(8,128)S(1)}, u32[]{:S(2)}, u32[]{:S(2)}) collective-permute-start(f32[192,384]{1,0:T(8,128)S(1)} %collective-permute-done.5.refs_2_), channel_id=1, source_target_pairs={{0,32},{2,482},{4,36},{6,486},{8,40},{10,490},{12,44},{14,494},{16... | collective-permute-start | bytes 884744 | tf_op jit(solution)/shard_map/own3/ppermute | solution.py:237
  41.7 12.9 %collective-permute-start.12 = (f32[192,384]{1,0:T(8,128)S(1)}, f32[192,384]{1,0:T(8,128)S(1)}, u32[]{:S(2)}, u32[]{:S(2)}) collective-permute-start(f32[192,384]{1,0:T(8,128)S(1)} %collective-permute-done.8.refs_2_), channel_id=1, source_target_pairs={{0,32},{2,482},{4,36},{6,486},{8,40},{10,490},{12,44},{14,494},{16... | collective-permute-start | bytes 884744 | tf_op jit(solution)/shard_map/other3/ppermute | solution.py:237
  46.2 20.4 %collective-permute-start.9 = (f32[2,576,128]{2,1,0:T(8,128)S(1)}, f32[2,576,128]{2,1,0:T(8,128)S(1)}, u32[]{:S(2)}, u32[]{:S(2)}) collective-permute-start(f32[2,576,128]{2,1,0:T(8,128)S(1)} %get-tuple-element.24), channel_id=1, source_target_pairs={{0,24},{2,10},{4,28},{6,14},{8,0},{10,18},{12,4},{14,22},{16,8},{1... | collective-permute-start | bytes 1769480 | tf_op jit(solution)/shard_map/left_y3/ppermute | solution.py:237
  48.1 18.4 %collective-permute-start.7 = (f32[2,576,128]{2,1,0:T(8,128)S(1)}, f32[2,576,128]{2,1,0:T(8,128)S(1)}, u32[]{:S(2)}, u32[]{:S(2)}) collective-permute-start(f32[2,576,128]{2,1,0:T(8,128)S(1)} %collective-permute-done.4), channel_id=1, source_target_pairs={{0,8},{2,26},{4,12},{6,30},{8,16},{10,2},{12,20},{14,6},{16,24},{1... | collective-permute-start | bytes 1769480 | tf_op jit(solution)/shard_map/left_y2/ppermute | solution.py:237
  52.7 7.8 %collective-permute-start.10 = (f32[192,384]{1,0:T(8,128)S(1)}, f32[192,384]{1,0:T(8,128)S(1)}, u32[]{:S(2)}, u32[]{:S(2)}) collective-permute-start(f32[192,384]{1,0:T(8,128)S(1)} %collective-permute-done.6.refs_3_), channel_id=1, source_target_pairs={{0,32},{2,482},{4,36},{6,486},{8,40},{10,490},{12,44},{14,494},{16... | collective-permute-start | bytes 884744 | tf_op jit(solution)/shard_map/own4/ppermute | solution.py:237
  54.6 9.0 %collective-permute-start.13 = (f32[192,384]{1,0:T(8,128)S(1)}, f32[192,384]{1,0:T(8,128)S(1)}, u32[]{:S(2)}, u32[]{:S(2)}) collective-permute-start(f32[192,384]{1,0:T(8,128)S(1)} %collective-permute-done.12.refs_3_), channel_id=1, source_target_pairs={{0,32},{2,482},{4,36},{6,486},{8,40},{10,490},{12,44},{14,494},{16... | collective-permute-start | bytes 884744 | tf_op jit(solution)/shard_map/other4/ppermute | solution.py:237
  60.5 7.8 %collective-permute-start.11 = (f32[192,384]{1,0:T(8,128)S(1)}, f32[192,384]{1,0:T(8,128)S(1)}, u32[]{:S(2)}, u32[]{:S(2)}) collective-permute-start(f32[192,384]{1,0:T(8,128)S(1)} %collective-permute-done.10.refs_4_), channel_id=1, source_target_pairs={{0,32},{2,482},{4,36},{6,486},{8,40},{10,490},{12,44},{14,494},{16... | collective-permute-start | bytes 884744 | tf_op jit(solution)/shard_map/own5/ppermute | solution.py:237
  63.6 7.8 %collective-permute-start.14 = (f32[192,384]{1,0:T(8,128)S(1)}, f32[192,384]{1,0:T(8,128)S(1)}, u32[]{:S(2)}, u32[]{:S(2)}) collective-permute-start(f32[192,384]{1,0:T(8,128)S(1)} %collective-permute-done.13.refs_4_), channel_id=1, source_target_pairs={{0,32},{2,482},{4,36},{6,486},{8,40},{10,490},{12,44},{14,494},{16... | collective-permute-start | bytes 884744 | tf_op jit(solution)/shard_map/other5/ppermute | solution.py:237
  66.7 35.2 %copy-start = (f32[192,384]{1,0:T(8,128)S(1)}, f32[192,384]{1,0:T(8,128)}, u32[]{:S(2)}) copy-start(f32[192,384]{1,0:T(8,128)} %get-tuple-element.23.refs_0_) | copy-start | bytes 884740
  71.4 8.0 %collective-permute-start.15 = (f32[4,2,576,128]{3,2,1,0:T(8,128)S(1)}, f32[4,2,576,128]{3,2,1,0:T(8,128)S(1)}, u32[]{:S(2)}, u32[]{:S(2)}) collective-permute-start(f32[4,2,576,128]{3,2,1,0:T(8,128)S(1)} %pad_maximum_fusion.same), channel_id=1, source_target_pairs={{0,2},{2,0},{4,6},{6,4},{8,10},{10,8},{12,14},{14,12},{16,18},{18,... | collective-permute-start | bytes 7077896 | tf_op jit(solution)/shard_map/left_core/ppermute | solution.py:237
  74.5 7.8 %collective-permute-start.16 = (f32[192,384]{1,0:T(8,128)S(1)}, f32[192,384]{1,0:T(8,128)S(1)}, u32[]{:S(2)}, u32[]{:S(2)}) collective-permute-start(f32[192,384]{1,0:T(8,128)S(1)} %collective-permute-done.14.refs_5_), channel_id=1, source_target_pairs={{0,32},{2,482},{4,36},{6,486},{8,40},{10,490},{12,44},{14,494},{16... | collective-permute-start | bytes 884744 | tf_op jit(solution)/shard_map/other6/ppermute | solution.py:237
  77.3 8.9 %collective-permute-start.18 = (f32[192,384]{1,0:T(8,128)S(1)}, f32[192,384]{1,0:T(8,128)S(1)}, u32[]{:S(2)}, u32[]{:S(2)}) collective-permute-start(f32[192,384]{1,0:T(8,128)S(1)} %collective-permute-done.11.refs_5_), channel_id=1, source_target_pairs={{0,32},{2,482},{4,36},{6,486},{8,40},{10,490},{12,44},{14,494},{16... | collective-permute-start | bytes 884744 | tf_op jit(solution)/shard_map/own6/ppermute | solution.py:237
  82.3 21.3 %collective-permute-start.17 = (f32[384,384]{1,0:T(8,128)S(1)}, f32[384,384]{1,0:T(8,128)S(1)}, u32[]{:S(2)}, u32[]{:S(2)}) collective-permute-start(f32[384,384]{1,0:T(8,128)S(1)} %get-tuple-element.33), channel_id=1, source_target_pairs={{0,2},{2,0},{4,6},{6,4},{8,10},{10,8},{12,14},{14,12},{16,18},{18,... | collective-permute-start | bytes 1769480 | tf_op jit(solution)/shard_map/spare/ppermute | solution.py:237
  86.3 9.8 %collective-permute-start.20 = (f32[192,384]{1,0:T(8,128)S(1)}, f32[192,384]{1,0:T(8,128)S(1)}, u32[]{:S(2)}, u32[]{:S(2)}) collective-permute-start(f32[192,384]{1,0:T(8,128)S(1)} %collective-permute-done.18.one), channel_id=1, source_target_pairs={{0,32},{2,482},{4,36},{6,486},{8,40},{10,490},{12,44},{14,494},{16... | collective-permute-start | bytes 884744 | tf_op jit(solution)/shard_map/own7/ppermute | solution.py:237
  89.2 10.7 %collective-permute-start.21 = (f32[192,384]{1,0:T(8,128)S(1)}, f32[192,384]{1,0:T(8,128)S(1)}, u32[]{:S(2)}, u32[]{:S(2)}) collective-permute-start(f32[192,384]{1,0:T(8,128)S(1)} %collective-permute-done.16), channel_id=1, source_target_pairs={{0,34},{2,480},{4,38},{6,484},{8,42},{10,488},{12,46},{14,492},{16... | collective-permute-start | bytes 884744 | tf_op jit(solution)/shard_map/other7/ppermute | solution.py:237
  94.2 9.4 %collective-permute-start.19 = (f32[192,384]{1,0:T(8,128)S(1)}, f32[192,384]{1,0:T(8,128)S(1)}, u32[]{:S(2)}, u32[]{:S(2)}) collective-permute-start(f32[192,384]{1,0:T(8,128)S(1)} %collective-permute-done.16), channel_id=1, source_target_pairs={{0,2},{2,0},{4,6},{6,4},{8,10},{10,8},{12,14},{14,12},{16,18},{18,... | collective-permute-start | bytes 884744 | tf_op jit(solution)/shard_map/crossed/ppermute | solution.py:237
  96.1 11.3 %collective-permute-start.23 = (f32[192,384]{1,0:T(8,128)S(1)}, f32[192,384]{1,0:T(8,128)S(1)}, u32[]{:S(2)}, u32[]{:S(2)}) collective-permute-start(f32[192,384]{1,0:T(8,128)S(1)} %collective-permute-done.20.three), channel_id=1, source_target_pairs={{0,32},{2,482},{4,36},{6,486},{8,40},{10,490},{12,44},{14,494},{16... | collective-permute-start | bytes 884744 | tf_op jit(solution)/shard_map/far_own/ppermute | solution.py:237
  99.8 11.5 %collective-permute-start.24 = (f32[192,384]{1,0:T(8,128)S(1)}, f32[192,384]{1,0:T(8,128)S(1)}, u32[]{:S(2)}, u32[]{:S(2)}) collective-permute-start(f32[192,384]{1,0:T(8,128)S(1)} %collective-permute-done.21.four), channel_id=1, source_target_pairs={{0,481},{1,480},{2,35},{3,34},{4,485},{5,484},{6,39},{7,38},{8,489... | collective-permute-start | bytes 884744 | tf_op jit(solution)/shard_map/far_other/ppermute | solution.py:237
  103.6 12.9 %copy-start.1 = (s32[3,3]{1,0:T(4,128)S(1)}, s32[3,3]{1,0:T(4,128)}, u32[]{:S(2)}) copy-start(s32[3,3]{1,0:T(4,128)} %keep.1) | copy-start | bytes 112
  104.8 11.7 %collective-permute-start.22 = (f32[192,384]{1,0:T(8,128)S(1)}, f32[192,384]{1,0:T(8,128)S(1)}, u32[]{:S(2)}, u32[]{:S(2)}) collective-permute-start(f32[192,384]{1,0:T(8,128)S(1)} %get-tuple-element.37), channel_id=1, source_target_pairs={{0,1},{1,0},{2,3},{3,2},{4,5},{5,4},{6,7},{7,6},{8,9},{9,8},{10,11... | collective-permute-start | bytes 884744 | tf_op jit(solution)/shard_map/away/ppermute | solution.py:237
